TPU v7x, 32 devices: a whole 2x2x4 slice. The times are simulated.
32 devices in a mesh: row: 2 (over x), col: 4 (over z), layer: 4 (over y, core).
Axes of the slice: x: 2, y: 2, z: 4, core: 2. Of those that a mesh axis runs over, the one named last changes fastest.
Arguments:
- hamiltonian: bfloat16 [2048, 2048], P('row', ('col', 'layer')), as said below
- inv_root: bfloat16 [2048, 2048], P('row', 'col'), as said below
- h_pattern: int32 [8, 8], replicated, may hold values from 0 to 1, as said below
- z_pattern: int32 [8, 8], replicated, may hold values from 0 to 1, as said below
Outputs:
- transformed: bfloat16 [2048, 2048], P('row', ('col', 'layer'))
Inputs may be any that keep to these rules, and one draw needn't show every extreme that they name: hamiltonian is symmetric. inv_root is symmetric. h_pattern is symmetric and every diagonal block is present. z_pattern is symmetric and every diagonal block is present.
All inputs are finite; a program needn't handle non-finite values.
Results may differ from a plain program's by a relative error of at most 0.005.
Values may be sent and summed in bfloat16 or wider, within the bound.
No kernel may reach another device: no remote copies, remote signals or barrier semaphores. Data moves between devices by JAX's collectives and lax.ppermute only.
A program may use at most 64 MiB of HBM per device.

v0:
```python
import jax
import jax.numpy as jnp
from jax import lax
from jax.sharding import PartitionSpec as P

BS = 256


def mask_tile(tile, pattern, row_start, col_start):
    blocks = pattern.shape[0]
    block_ids = jnp.arange(blocks, dtype=jnp.int32)
    row_ids = (row_start + jnp.arange(tile.shape[0], dtype=jnp.int32)) // BS
    col_ids = (col_start + jnp.arange(tile.shape[1], dtype=jnp.int32)) // BS
    row_pick = (row_ids[:, None] == block_ids[None, :]).astype(jnp.float32)
    col_pick = (block_ids[:, None] == col_ids[None, :]).astype(jnp.float32)
    inner = jnp.dot(pattern.astype(jnp.float32), col_pick, precision=lax.Precision.HIGHEST)
    keep = jnp.dot(row_pick, inner, precision=lax.Precision.HIGHEST)
    return jnp.where(keep > 0.5, tile, jnp.zeros_like(tile))


def accumulate(left, right):
    return jnp.dot(left, right, preferred_element_type=jnp.float32)


def local(hamiltonian, inv_root, h_pattern, z_pattern):
    rows_here = inv_root.shape[0]
    cols_here = inv_root.shape[1]
    quarter = hamiltonian.shape[1]
    layers = lax.axis_size("layer")
    per_row = lax.axis_size("col") // lax.axis_size("row")
    row_index = lax.axis_index("row")
    col_index = lax.axis_index("col")
    layer_index = lax.axis_index("layer")
    h_local = mask_tile(
        hamiltonian, h_pattern, row_index * rows_here, col_index * cols_here + layer_index * quarter
    )
    z_local = mask_tile(inv_root, z_pattern, row_index * rows_here, col_index * cols_here)
    h_whole = lax.all_gather(h_local, "col", axis=1, tiled=True)
    z_layered = z_local.reshape(per_row, layers, quarter, cols_here)
    z_part = lax.dynamic_index_in_dim(z_layered, layer_index, 1, keepdims=False).reshape(
        per_row * quarter, cols_here
    )
    columns = h_whole
    partial_y = accumulate(columns, lax.all_gather(z_part, "row", axis=0, tiled=True))
    z_quarter = lax.dynamic_slice_in_dim(z_local, layer_index * quarter, quarter, 1)
    z_rows = lax.all_gather(z_quarter, "col", axis=1, tiled=True)
    summed = lax.psum(partial_y, "layer")
    layered = summed.reshape(per_row, layers, quarter, cols_here)
    own_rows = lax.dynamic_index_in_dim(layered, layer_index, 1, keepdims=False).reshape(
        per_row * quarter, cols_here
    )
    y_own = own_rows.astype(jnp.bfloat16)
    columns = z_rows
    partial_c = accumulate(columns, lax.all_gather(y_own, "row", axis=0, tiled=True))
    result = lax.psum_scatter(partial_c, "layer", scatter_dimension=1, tiled=True)
    return result.astype(jnp.bfloat16)


def solution(mesh):
    return jax.shard_map(
        local,
        mesh=mesh,
        in_specs=(P("row", ("col", "layer")), P("row", "col"), P(), P()),
        out_specs=P("row", ("col", "layer")),
        check_vma=False,
    )
```

profile of v0, /device:TPU:0, one launch (start us, length us, event | category | flops | bytes accessed | tf_op | source)
XLA Modules:
  0.0 136.0 jit_solution(12491374444671233376)
XLA Ops:
  6.5 0.0 all-gather.5.cloned.1.call-start
  6.6 0.9 fusion.8
  7.5 2.1 %fusion = bf16[1024,128]{1,0:T(8,128)(2,1)} fusion(bf16[1024,128]{1,0:T(8,128)(2,1)} %param.4, f32[128,8]{1,0:T(8,128)S(1)} %fusion.8, s32[1024]{0:T(1024)S(1)} %add_select_fusion), kind=kOutput, calls=%fused_computation.2 | convolution fusion | flops 12853248 | bytes 532480 | tf_op jit(solution)/shard_map/dot_general | solution.py:17
  9.6 0.0 all-gather.5.cloned.1.call-update
  9.6 0.0 all-gather.3.cloned.1.call-start
  9.7 1.0 fusion.4
  10.7 2.3 %compare_select_fusion = bf16[1024,512]{1,0:T(8,128)(2,1)S(1)} fusion(bf16[1024,512]{1,0:T(8,128)(2,1)} %param.5, f32[512,8]{1,0:T(8,128)S(1)} %fusion.4, s32[1024]{0:T(1024)S(1)} %add_select_fusion), kind=kOutput, calls=%fused_computation | convolution fusion | flops 51388416 | bytes 2117632 | tf_op jit(solution)/shard_map/dot_general | solution.py:17
  13.1 0.7 constant_dynamic-slice_fusion.1
  13.8 0.0 all-gather.3.cloned.1.call-update
  13.8 0.0 reduce-scatter.2.cloned.1.call-start
  13.9 9.9 %all_gather.14 = bf16[512,512]{1,0:T(8,128)(2,1)S(1)} all-gather(bf16[256,512]{1,0:T(8,128)(2,1)S(1)} %bitcast.12), channel_id=1, replica_groups=mesh['row'=2,'col'=4,'layer'=4] {'row'}, dimensions={0}, use_global_device_ids=true | all-gather | bytes 786432 | tf_op jit(solution)/shard_map/all_gather | solution.py:44
  23.8 18.9 %all-gather.5.cloned.1.call-done = bf16[1024,512]{1,0:T(8,128)(2,1)} async-done(((bf16[1024,128]{1,0:T(8,128)(2,1)}), bf16[1024,512]{1,0:T(8,128)(2,1)}) %all-gather.5.cloned.1.call-update) | async-done | bytes 1048592 | tf_op jit(solution)/shard_map/all_gather | solution.py:38
  42.7 1.9 %fusion.19 = f32[1024,512]{1,0:T(8,128)S(1)} fusion(bf16[1024,512]{1,0:T(8,128)(2,1)} %all-gather.5.cloned.1.call-done, bf16[512,512]{1,0:T(8,128)(2,1)S(1)} %all_gather.14), kind=kOutput, calls=%fused_computation.41 | convolution fusion | flops 536870912 | bytes 3670016 | tf_op jit(solution)/shard_map/dot_general | solution.py:22
  44.6 41.0 %all-reduce.1 = bf16[2,4,128,512]{3,2,1,0:T(8,128)(2,1)S(1)} all-reduce(f32[2,4,128,512]{3,2,1,0:T(8,128)S(1)} %bitcast.10), channel_id=1, replica_groups=mesh['row'=2,'col'=4,'layer'=4] {'layer'}, use_global_device_ids=true, to_apply=%region_0.1 | all-reduce | flops 524288 | bytes 3145728 | tf_op jit(solution)/shard_map/psum | solution.py:47
  85.7 9.0 %all_gather.15 = bf16[512,512]{1,0:T(8,128)(2,1)S(1)} all-gather(bf16[256,512]{1,0:T(8,128)(2,1)S(1)} %bitcast.11), channel_id=1, replica_groups=mesh['row'=2,'col'=4,'layer'=4] {'row'}, dimensions={0}, use_global_device_ids=true | all-gather | bytes 786432 | tf_op jit(solution)/shard_map/all_gather | solution.py:54
  94.7 0.0 all-gather.3.cloned.1.call-done
  94.7 3.3 %fusion.20 = f32[1024,512]{1,0:T(8,128)} fusion(bf16[1024,512]{1,0:T(8,128)(2,1)} %all-gather.3.cloned.1.call-done, bf16[512,512]{1,0:T(8,128)(2,1)S(1)} %all_gather.15), kind=kOutput, calls=%fused_computation.42 | convolution fusion | flops 536870912 | bytes 3670016 | tf_op jit(solution)/shard_map/dot_general | solution.py:22
  97.9 0.0 reduce-scatter.2.cloned.1.call-update
  98.0 29.8 %reduce-scatter.2.cloned.1.call-done = f32[1024,128]{1,0:T(8,128)} async-done(((f32[1024,512]{1,0:T(8,128)}), f32[1024,128]{1,0:T(8,128)}) %reduce-scatter.2.cloned.1.call-update) | async-done | bytes 524304 | tf_op jit(solution)/shard_map/reduce_scatter | solution.py:55
  127.7 1.8 %convert_element_type.23 = bf16[1024,128]{1,0:T(8,128)(2,1)} convert(f32[1024,128]{1,0:T(8,128)} %reduce-scatter.2.cloned.1.call-done) | non-fusion elementwise | flops 131072 | bytes 786432 | tf_op jit(solution)/shard_map/convert_element_type | solution.py:56
  (5 shorter events, 0.1 us)
Async XLA Ops:
  6.5 36.2 %all-gather.5.cloned.1.call-start = ((), (), s32[]{:S(2)}) async-start(), calls=%async_computation.2 | async-start | bytes 1310720 | tf_op jit(solution)/shard_map/all_gather | solution.py:38
  9.6 85.0 %all-gather.3.cloned.1.call-start = ((), (), s32[]{:S(2)}) async-start(), calls=%async_computation.1 | async-start | bytes 1310720 | tf_op jit(solution)/shard_map/all_gather | solution.py:46
  13.8 113.9 %reduce-scatter.2.cloned.1.call-start = ((), (), s32[]{:S(2)}) async-start(), calls=%async_computation.3 | async-start | bytes 2621440 | tf_op jit(solution)/shard_map/reduce_scatter | solution.py:55
Sparse Core Ops, SparseCore 0:
  9.8 32.8 all-gather.4
  44.3 28.4 all-gather.2
  98.1 29.6 reduce-scatter.1
where the time goes:
time: 136 us
  blocking collectives  59.9 us (44%)
  waiting for transfers between devices  48.7 us (36%)
  between operations  13.2 us (10%)
  matrix products  11.6 us (9%)
  other arithmetic  1.8 us (1%)
    psum x1, blocking collectives, local(): summed = lax.psum(partial_y, 'layer')  41 us
    reduce_scatter x1, waiting for transfers between devices, local(): lax.psum_scatter(partial_c, 'layer', scatter_dimension=1, tiled=True)  29.8 us
    all_gather x1, waiting for transfers between devices, local(): h_whole = lax.all_gather(h_local, 'col', axis=1, tiled=True)  18.9 us
    all_gather x1, blocking collectives, local(): lax.all_gather(z_part, 'row', axis=0, tiled=True)  9.91 us
    all_gather x1, blocking collectives, local(): lax.all_gather(y_own, 'row', axis=0, tiled=True)  9 us
    dot_general x2, matrix products, accumulate(): return jnp.dot(left, right, preferred_element_type=jnp.float32)  5.18 us
    dot_general x2, matrix products, mask_tile(): keep = jnp.dot(row_pick, inner, precision=lax.Precision.HIGHEST)  4.42 us
  transfers between devices with their start and end apart: 3, of which 2 were waited for; matrix products, arithmetic and copies ran while one was open for 4% of the time, Pallas kernels for 0%

commit v1 on v0

v1 whole, which is shorter than its diff:
```python
import functools

import jax
import jax.numpy as jnp
from jax import lax
from jax.experimental import pallas as pl
from jax.experimental.pallas import tpu as pltpu
from jax.sharding import PartitionSpec as P

BS = 256
VMEM_LIMIT = 48 * 1024 * 1024


def bits_of(size):
    return [1 << b for b in reversed(range(size.bit_length() - 1))]


def flip(size, bit):
    return [(i, i ^ bit) for i in range(size)]


def mod(a, n):
    return lax.rem(a + n, n)


def keep_block(pattern, i, j, block):
    return jnp.where(pattern[i, j] > 0, block, jnp.zeros_like(block))


def first_kernel(sizes, h_offsets, *refs):
    rows, cols, layers, rows_here, cols_here = sizes
    hp, zp = refs[0], refs[1]
    z_slots = refs[2 : 2 + cols]
    h_pieces = refs[2 + cols : 2 + cols + len(h_offsets)]
    out_a, out_b, zm, hm, xs = refs[2 + cols + len(h_offsets) :]
    r, c, l = lax.axis_index("row"), lax.axis_index("col"), lax.axis_index("layer")
    quarter = cols_here // layers
    per_tile = cols_here // BS
    per_rows = rows_here // BS
    block_row = r * layers + l
    for s in range(cols):
        cc = mod(c - s, cols)
        for t in range(per_tile):
            j = cc * per_tile + t
            zm[:, pl.ds(pl.multiple_of(j * BS, BS), BS)] = keep_block(
                zp, block_row, j, z_slots[s][:, t * BS : (t + 1) * BS]
            )
    for (dr, dl), piece in zip(h_offsets, h_pieces):
        rr, ll = r ^ dr, l ^ dl
        block_col = (c * cols_here + ll * quarter) // BS
        for q in range(per_rows):
            j = rr * per_rows + q
            hm[
                pl.ds(pl.multiple_of(j * BS, BS), BS),
                pl.ds(pl.multiple_of(ll * quarter, quarter), quarter),
            ] = keep_block(hp, j, block_col, piece[q * BS : (q + 1) * BS, :])
    total = None
    order = zm.shape[1]
    chunk = min(order, 2048)
    for k in range(0, order, chunk):
        part = jnp.dot(
            zm[:, k : k + chunk], hm[k : k + chunk, :], preferred_element_type=jnp.float32
        )
        total = part if total is None else total + part
    xs[...] = total.astype(jnp.bfloat16)
    half = lax.rem(c, 2)
    out_a[...] = xs[pl.ds(pl.multiple_of(half * quarter, quarter), quarter), :]
    out_b[...] = xs[pl.ds(pl.multiple_of((1 - half) * quarter, quarter), quarter), :]


def second_kernel(sizes, z_offsets, *refs):
    rows, cols, layers, rows_here, cols_here = sizes
    zp, z_tile = refs[0], refs[1]
    n_slots = len(z_offsets) * (cols - 1)
    slots = refs[2 : 2 + n_slots]
    messages = refs[2 + n_slots : 2 + n_slots + cols]
    out, xm = refs[2 + n_slots + cols :]
    r, c, l = lax.axis_index("row"), lax.axis_index("col"), lax.axis_index("layer")
    per_tile = cols_here // BS
    index = r * 2 + lax.rem(l, 2)
    for j in range(cols):
        xm[mod(index - j, cols)] = messages[j][...]
    for n, dl in enumerate(z_offsets):
        ll = l ^ dl
        block_row = r * layers + ll
        total = None
        for s in range(cols):
            cc = mod(c - s, cols)
            if s == 0:
                piece = z_tile[pl.ds(pl.multiple_of(ll * BS, BS), BS), :]
            else:
                piece = slots[n * (cols - 1) + s - 1][...]
            masked = jnp.concatenate(
                [
                    keep_block(zp, block_row, cc * per_tile + t, piece[:, t * BS : (t + 1) * BS])
                    for t in range(per_tile)
                ],
                axis=1,
            )
            part = lax.dot_general(
                masked, xm[cc], (((1,), (1,)), ((), ())), preferred_element_type=jnp.float32
            )
            total = part if total is None else total + part
        out[pl.ds(pl.multiple_of(ll * BS, BS), BS), :] = total.astype(out.dtype)


def local(sizes, hamiltonian, inv_root, h_pattern, z_pattern):
    rows, cols, layers, rows_here, cols_here = sizes
    quarter = cols_here // layers
    order = rows * rows_here
    l = lax.axis_index("layer")
    smem = pl.BlockSpec(memory_space=pltpu.SMEM)
    vmem = pl.BlockSpec(memory_space=pltpu.VMEM)

    own = lax.dynamic_slice_in_dim(inv_root, l * BS, BS, 0)
    ring = [(i, (i + 1) % cols) for i in range(cols)]
    z_slots = [own]
    for _ in range(1, cols):
        z_slots.append(lax.ppermute(z_slots[-1], "col", ring))

    h_pieces = {(0, 0): hamiltonian}
    row_bits, layer_bits = bits_of(rows), bits_of(layers)
    steps = [("layer", layers, layer_bits[0])]
    steps += [("row", rows, b) for b in row_bits]
    steps += [("layer", layers, b) for b in layer_bits[1:]]
    for axis, size, bit in steps:
        for (dr, dl), piece in list(h_pieces.items()):
            there = (dr ^ bit, dl) if axis == "row" else (dr, dl ^ bit)
            h_pieces[there] = lax.ppermute(piece, axis, flip(size, bit))
    h_offsets = list(h_pieces)

    shared = {0: z_slots[1:]}
    for bit in layer_bits:
        for dl, pieces in list(shared.items()):
            shared[dl ^ bit] = [lax.ppermute(p, "layer", flip(layers, bit)) for p in pieces]
    z_offsets = list(shared)

    half = jax.ShapeDtypeStruct((quarter, cols_here), jnp.bfloat16)
    x_a, x_b = pl.pallas_call(
        functools.partial(first_kernel, sizes, h_offsets),
        out_shape=[half, half],
        in_specs=[smem, smem] + [vmem] * (cols + len(h_offsets)),
        out_specs=[vmem, vmem],
        scratch_shapes=[
            pltpu.VMEM((BS, order), jnp.bfloat16),
            pltpu.VMEM((order, cols_here), jnp.bfloat16),
            pltpu.VMEM((BS, cols_here), jnp.bfloat16),
        ],
        compiler_params=pltpu.CompilerParams(vmem_limit_bytes=VMEM_LIMIT),
        name="first_product",
    )(h_pattern, z_pattern, *z_slots, *[h_pieces[o] for o in h_offsets])

    per_tile = cols_here // BS
    messages = []
    for j in range(cols):
        perm = []
        for r in range(rows):
            for c in range(cols):
                for l_ in range(layers):
                    block = r * layers + l_
                    there_r, there_half = divmod((c + j) % cols, 2)
                    b, y = divmod(block, per_tile)
                    there_l = y * 2 + there_half
                    perm.append(
                        ((r * cols + c) * layers + l_, (there_r * cols + b) * layers + there_l)
                    )
        messages.append(lax.ppermute(x_b if j % 2 else x_a, ("row", "col", "layer"), perm))

    flat = [p for o in z_offsets for p in shared[o]]
    return pl.pallas_call(
        functools.partial(second_kernel, sizes, z_offsets),
        out_shape=jax.ShapeDtypeStruct(hamiltonian.shape, jnp.bfloat16),
        in_specs=[smem] + [vmem] * (1 + len(flat) + cols),
        out_specs=vmem,
        scratch_shapes=[pltpu.VMEM((cols, quarter, cols_here), jnp.bfloat16)],
        compiler_params=pltpu.CompilerParams(vmem_limit_bytes=VMEM_LIMIT),
        name="second_product",
    )(z_pattern, inv_root, *flat, *messages)


def solution(mesh):
    rows, cols, layers = (mesh.shape[a] for a in ("row", "col", "layer"))

    def whole(hamiltonian, inv_root, h_pattern, z_pattern):
        order = hamiltonian.shape[0]
        sizes = (rows, cols, layers, order // rows, order // cols)
        return jax.shard_map(
            functools.partial(local, sizes),
            mesh=mesh,
            in_specs=(P("row", ("col", "layer")), P("row", "col"), P(), P()),
            out_specs=P("row", ("col", "layer")),
            check_vma=False,
        )(hamiltonian, inv_root, h_pattern, z_pattern)

    return whole
```

time: 136 us -> 74.9 us (0.55)
  blocking collectives: 59.9 us -> 0 us
  starting transfers between devices: 0.09 us -> 32.3 us
  between operations: 13.2 us -> 0.09 us
  waiting for transfers between devices: 48.7 us -> 36.7 us
  matrix products: 11.6 us -> 0 us
  Pallas kernels: 0 us -> 4.63 us
  other arithmetic: 1.8 us -> 0 us
    psum x1 -> x0, blocking collectives: 41 us -> none  [local(): summed = lax.psum(partial_y, 'layer')]
    ppermute x0 -> x23, waiting for transfers between devices: none -> 36.7 us  [the longest x3 17.6 us: local(): z_slots.append(lax.ppermute(z_slots[-1], 'col', ring))]
    ppermute x0 -> x23, starting transfers between devices: none -> 32.3 us  [the longest x4 19.3 us: local(): lax.ppermute(x_b if j % 2 else x_a, ('row', 'col', 'layer'), perm)]
    reduce_scatter x1 -> x0, waiting for transfers between devices: 29.8 us -> none  [local(): lax.psum_scatter(partial_c, 'layer', scatter_dimension=1, tiled=True)]
    all_gather x2 -> x0, blocking collectives: 18.9 us -> none  [the longest x1 9.91 us: local(): lax.all_gather(z_part, 'row', axis=0, tiled=True)]
    all_gather x2 -> x0, waiting for transfers between devices: 18.9 us -> none  [the longest x1 18.9 us: local(): h_whole = lax.all_gather(h_local, 'col', axis=1, tiled=True)]
    dot_general x6 -> x0, matrix products: 11.6 us -> none  [the longest x2 5.18 us: accumulate(): return jnp.dot(left, right, preferred_element_type=jnp.float32)]
    pallas_call x0 -> x2, Pallas kernels: none -> 4.63 us  [the longest x1 2.66 us: local(): pl.pallas_call(functools.partial(second_kernel, sizes, z_offsets), out_sh...]
  transfers between devices with their start and end apart: 3 -> 23, of which waited for: 2 -> 5; matrix products, arithmetic and copies ran while one was open for 4% -> 0% of each run, Pallas kernels for 0% -> 3%
where the time goes in v1:
time: 74.9 us; the launch traced here: 74.7 us
  waiting for transfers between devices  36.7 us (49%)
  starting transfers between devices  32.3 us (43%)
  Pallas kernels  4.63 us (6%)
  local copies, waits for them, and re-layouts  1.03 us (1%)
    ppermute x4, starting transfers between devices, local(): lax.ppermute(x_b if j % 2 else x_a, ('row', 'col', 'layer'), perm)  19.3 us
    ppermute x3, waiting for transfers between devices, local(): z_slots.append(lax.ppermute(z_slots[-1], 'col', ring))  17.6 us
    ppermute x4, waiting for transfers between devices, local(): lax.ppermute(x_b if j % 2 else x_a, ('row', 'col', 'layer'), perm)  17 us
    ppermute x7, starting transfers between devices, local(): h_pieces[there] = lax.ppermute(piece, axis, flip(size, bit))  5.02 us
    ppermute x9, starting transfers between devices, local(): lax.ppermute(p, 'layer', flip(layers, bit))  4.88 us
    ppermute x3, starting transfers between devices, local(): z_slots.append(lax.ppermute(z_slots[-1], 'col', ring))  3.09 us
    pallas_call x1, Pallas kernels, local(): pl.pallas_call(functools.partial(second_kernel, sizes, z_offsets), out_sh...  2.66 us
    ppermute x9, waiting for transfers between devices, local(): lax.ppermute(p, 'layer', flip(layers, bit))  2.09 us
  transfers between devices with their start and end apart: 23, of which 5 were waited for; matrix products, arithmetic and copies ran while one was open for 0% of the time, Pallas kernels for 3%

profile of v1, /device:TPU:0, one launch (start us, length us, event | category | flops | bytes accessed | tf_op | source)
XLA Modules:
  0.0 74.7 jit_solution(7702893151628320273)
XLA Ops:
  0.0 1.0 %constant_dynamic-slice_fusion.refs_2_ = bf16[256,512]{1,0:T(8,128)(2,1)S(1)} fusion(bf16[1024,512]{1,0:T(8,128)(2,1)} %refs_1_.3, s32[]{:T(128)S(6)} %select_n.3), kind=kLoop, calls=%fused_computation | loop fusion | bytes 524292 | tf_op jit(solution)/shard_map/dynamic_slice | solution.py:115
  1.0 0.0 copy-start
  1.0 3.1 %collective-permute-start = (bf16[256,512]{1,0:T(8,128)(2,1)S(1)}, bf16[256,512]{1,0:T(8,128)(2,1)S(1)}, u32[]{:S(2)}, u32[]{:S(2)}) collective-permute-start(bf16[256,512]{1,0:T(8,128)(2,1)S(1)} %constant_dynamic-slice_fusion.refs_2_), channel_id=1, source_target_pairs={{0,4},{4,8},{8,12},{12,0},{1,5},{5,9},{9,13},{13,1},{2,6},{6,10},{... | collective-permute-start | bytes 786440 | tf_op jit(solution)/shard_map/ppermute | solution.py:119
  4.1 1.5 %collective-permute-start.12 = (bf16[1024,128]{1,0:T(8,128)(2,1)S(1)}, bf16[1024,128]{1,0:T(8,128)(2,1)S(1)}, u32[]{:S(2)}, u32[]{:S(2)}) collective-permute-start(bf16[1024,128]{1,0:T(8,128)(2,1)S(1)} %copy-done.1), channel_id=1, source_target_pairs={{0,2},{1,3},{2,0},{3,1},{4,6},{5,7},{6,4},{7,5},{8,10},{9,11},{10,... | collective-permute-start | bytes 786440 | tf_op jit(solution)/shard_map/ppermute | solution.py:129
  5.6 1.5 %collective-permute-start.13 = (bf16[1024,128]{1,0:T(8,128)(2,1)S(1)}, bf16[1024,128]{1,0:T(8,128)(2,1)S(1)}, u32[]{:S(2)}, u32[]{:S(2)}) collective-permute-start(bf16[1024,128]{1,0:T(8,128)(2,1)S(1)} %copy-done.1), channel_id=1, source_target_pairs={{0,16},{16,0},{1,17},{17,1},{2,18},{18,2},{3,19},{19,3},{4,20},{20... | collective-permute-start | bytes 786440 | tf_op jit(solution)/shard_map/ppermute | solution.py:129
  7.1 5.3 %collective-permute-done.refs_3_.refs_2_ = bf16[256,512]{1,0:T(8,128)(2,1)S(1)} collective-permute-done((bf16[256,512]{1,0:T(8,128)(2,1)S(1)}, bf16[256,512]{1,0:T(8,128)(2,1)S(1)}, u32[]{:S(2)}, u32[]{:S(2)}) %collective-permute-start) | collective-permute-done | bytes 262176 | tf_op jit(solution)/shard_map/ppermute | solution.py:119
  12.5 1.5 %collective-permute-start.14 = (bf16[1024,128]{1,0:T(8,128)(2,1)S(1)}, bf16[1024,128]{1,0:T(8,128)(2,1)S(1)}, u32[]{:S(2)}, u32[]{:S(2)}) collective-permute-start(bf16[1024,128]{1,0:T(8,128)(2,1)S(1)} %collective-permute-done.12.refs_7_), channel_id=1, source_target_pairs={{0,16},{16,0},{1,17},{17,1},{2,18},{18,2},{3,19},{19,3},{4,20},{20... | collective-permute-start | bytes 786440 | tf_op jit(solution)/shard_map/ppermute | solution.py:129
  14.0 0.5 collective-permute-start.17
  14.5 1.5 %collective-permute-start.3 = (bf16[256,512]{1,0:T(8,128)(2,1)S(1)}, bf16[256,512]{1,0:T(8,128)(2,1)S(1)}, u32[]{:S(2)}, u32[]{:S(2)}) collective-permute-start(bf16[256,512]{1,0:T(8,128)(2,1)S(1)} %collective-permute-done.refs_3_.refs_2_), channel_id=1, source_target_pairs={{0,2},{1,3},{2,0},{3,1},{4,6},{5,7},{6,4},{7,5},{8,10},{9,11},{10,... | collective-permute-start | bytes 786440 | tf_op jit(solution)/shard_map/ppermute | solution.py:135
  16.0 5.8 %collective-permute-done.1.refs_4_.refs_3_ = bf16[256,512]{1,0:T(8,128)(2,1)S(1)} collective-permute-done((bf16[256,512]{1,0:T(8,128)(2,1)S(1)}, bf16[256,512]{1,0:T(8,128)(2,1)S(1)}, u32[]{:S(2)}, u32[]{:S(2)}) %collective-permute-start.1) | collective-permute-done | bytes 262176 | tf_op jit(solution)/shard_map/ppermute | solution.py:119
  21.8 0.5 collective-permute-start.6
  22.3 1.3 %collective-permute-start.4 = (bf16[256,512]{1,0:T(8,128)(2,1)S(1)}, bf16[256,512]{1,0:T(8,128)(2,1)S(1)}, u32[]{:S(2)}, u32[]{:S(2)}) collective-permute-start(bf16[256,512]{1,0:T(8,128)(2,1)S(1)} %collective-permute-done.1.refs_4_.refs_3_), channel_id=1, source_target_pairs={{0,2},{1,3},{2,0},{3,1},{4,6},{5,7},{6,4},{7,5},{8,10},{9,11},{10,... | collective-permute-start | bytes 786440 | tf_op jit(solution)/shard_map/ppermute | solution.py:135
  23.5 6.6 %collective-permute-done.2.refs_5_.refs_4_ = bf16[256,512]{1,0:T(8,128)(2,1)S(1)} collective-permute-done((bf16[256,512]{1,0:T(8,128)(2,1)S(1)}, bf16[256,512]{1,0:T(8,128)(2,1)S(1)}, u32[]{:S(2)}, u32[]{:S(2)}) %collective-permute-start.2) | collective-permute-done | bytes 262176 | tf_op jit(solution)/shard_map/ppermute | solution.py:119
  30.1 1.1 %collective-permute-start.5 = (bf16[256,512]{1,0:T(8,128)(2,1)S(1)}, bf16[256,512]{1,0:T(8,128)(2,1)S(1)}, u32[]{:S(2)}, u32[]{:S(2)}) collective-permute-start(bf16[256,512]{1,0:T(8,128)(2,1)S(1)} %collective-permute-done.2.refs_5_.refs_4_), channel_id=1, source_target_pairs={{0,2},{1,3},{2,0},{3,1},{4,6},{5,7},{6,4},{7,5},{8,10},{9,11},{10,... | collective-permute-start | bytes 786440 | tf_op jit(solution)/shard_map/ppermute | solution.py:135
  31.2 2.0 %first_product.1 = (bf16[128,512]{1,0:T(8,128)(2,1)S(1)}, bf16[128,512]{1,0:T(8,128)(2,1)S(1)}) custom-call(s32[8,8]{1,0:T(8,128)S(1)} %copy-done.3, s32[8,8]{1,0:T(8,128)S(1)} %copy-done.2, bf16[256,512]{1,0:T(8,128)(2,1)S(1)} %constant_dynamic-slice_fusion.refs_2_, bf16[256,512]{1,0:T(8,128)(2,1)S(1)} %collective-permute-done.refs_3_.refs_2_, ...), custom_call_target="tpu_custom_call" | custom-call | tf_op jit(solution)/shard_map/first_product/pallas_call | solution.py:139
  33.2 0.7 collective-permute-start.19
  33.9 2.4 %collective-permute-start.20 = (bf16[128,512]{1,0:T(8,128)(2,1)S(1)}, bf16[128,512]{1,0:T(8,128)(2,1)S(1)}, u32[]{:S(2)}, u32[]{:S(2)}) collective-permute-start(bf16[128,512]{1,0:T(8,128)(2,1)S(1)} %get-tuple-element.8), channel_id=1, source_target_pairs={{0,1},{1,3},{2,5},{3,7},{4,16},{5,18},{6,20},{7,22},{8,17},{9,19},... | collective-permute-start | bytes 393224 | tf_op jit(solution)/shard_map/ppermute | solution.py:167
  36.2 0.1 collective-permute-start.8
  36.3 0.4 collective-permute-start.10
  36.8 2.1 %collective-permute-done.5.refs_7_ = bf16[256,512]{1,0:T(8,128)(2,1)S(1)} collective-permute-done((bf16[256,512]{1,0:T(8,128)(2,1)S(1)}, bf16[256,512]{1,0:T(8,128)(2,1)S(1)}, u32[]{:S(2)}, u32[]{:S(2)}) %collective-permute-start.5) | collective-permute-done | bytes 262176 | tf_op jit(solution)/shard_map/ppermute | solution.py:135
  38.8 11.6 %collective-permute-start.21 = (bf16[128,512]{1,0:T(8,128)(2,1)S(1)}, bf16[128,512]{1,0:T(8,128)(2,1)S(1)}, u32[]{:S(2)}, u32[]{:S(2)}) collective-permute-start(bf16[128,512]{1,0:T(8,128)(2,1)S(1)} %get-tuple-element.7), channel_id=1, source_target_pairs={{0,16},{1,18},{2,20},{3,22},{4,17},{5,19},{6,21},{7,23},{8,0},{9,2... | collective-permute-start | bytes 393224 | tf_op jit(solution)/shard_map/ppermute | solution.py:167
  50.4 4.7 %collective-permute-start.22 = (bf16[128,512]{1,0:T(8,128)(2,1)S(1)}, bf16[128,512]{1,0:T(8,128)(2,1)S(1)}, u32[]{:S(2)}, u32[]{:S(2)}) collective-permute-start(bf16[128,512]{1,0:T(8,128)(2,1)S(1)} %get-tuple-element.8), channel_id=1, source_target_pairs={{0,17},{1,19},{2,21},{3,23},{4,0},{5,2},{6,4},{7,6},{8,1},{9,3},{1... | collective-permute-start | bytes 393224 | tf_op jit(solution)/shard_map/ppermute | solution.py:167
  55.1 17.0 %collective-permute-done.22.refs_17_ = bf16[128,512]{1,0:T(8,128)(2,1)S(1)} collective-permute-done((bf16[128,512]{1,0:T(8,128)(2,1)S(1)}, bf16[128,512]{1,0:T(8,128)(2,1)S(1)}, u32[]{:S(2)}, u32[]{:S(2)}) %collective-permute-start.22) | collective-permute-done | bytes 131104 | tf_op jit(solution)/shard_map/ppermute | solution.py:167
  72.1 2.7 %second_product.1 = bf16[1024,128]{1,0:T(8,128)(2,1)} custom-call(s32[8,8]{1,0:T(8,128)S(1)} %copy-done.2, bf16[1024,512]{1,0:T(8,128)(2,1)S(1)} %copy-done, bf16[256,512]{1,0:T(8,128)(2,1)S(1)} %collective-permute-done.refs_3_.refs_2_, bf16[256,512]{1,0:T(8,128)(2,1)S(1)} %collective-permute-done.1.refs_4_.refs_3_, ...), custom_call_target="tpu_custom_call" | custom-call | tf_op jit(solution)/shard_map/second_product/pallas_call | solution.py:170
  (33 shorter events, 0.1 us)
Async XLA Ops:
  1.0 71.0 %copy-start = (bf16[1024,512]{1,0:T(8,128)(2,1)S(1)}, bf16[1024,512]{1,0:T(8,128)(2,1)}, u32[]{:S(2)}) copy-start(bf16[1024,512]{1,0:T(8,128)(2,1)} %refs_1_.3) | copy-start | bytes 3145732
  1.0 11.4 %collective-permute-start = (bf16[256,512]{1,0:T(8,128)(2,1)S(1)}, bf16[256,512]{1,0:T(8,128)(2,1)S(1)}, u32[]{:S(2)}, u32[]{:S(2)}) collective-permute-start(bf16[256,512]{1,0:T(8,128)(2,1)S(1)} %constant_dynamic-slice_fusion.refs_2_), channel_id=1, source_target_pairs={{0,4},{4,8},{8,12},{12,0},{1,5},{5,9},{9,13},{13,1},{2,6},{6,10},{... | collective-permute-start | bytes 786440 | tf_op jit(solution)/shard_map/ppermute | solution.py:119
  4.1 8.3 %collective-permute-start.12 = (bf16[1024,128]{1,0:T(8,128)(2,1)S(1)}, bf16[1024,128]{1,0:T(8,128)(2,1)S(1)}, u32[]{:S(2)}, u32[]{:S(2)}) collective-permute-start(bf16[1024,128]{1,0:T(8,128)(2,1)S(1)} %copy-done.1), channel_id=1, source_target_pairs={{0,2},{1,3},{2,0},{3,1},{4,6},{5,7},{6,4},{7,5},{8,10},{9,11},{10,... | collective-permute-start | bytes 786440 | tf_op jit(solution)/shard_map/ppermute | solution.py:129
  5.6 8.3 %collective-permute-start.13 = (bf16[1024,128]{1,0:T(8,128)(2,1)S(1)}, bf16[1024,128]{1,0:T(8,128)(2,1)S(1)}, u32[]{:S(2)}, u32[]{:S(2)}) collective-permute-start(bf16[1024,128]{1,0:T(8,128)(2,1)S(1)} %copy-done.1), channel_id=1, source_target_pairs={{0,16},{16,0},{1,17},{17,1},{2,18},{18,2},{3,19},{19,3},{4,20},{20... | collective-permute-start | bytes 786440 | tf_op jit(solution)/shard_map/ppermute | solution.py:129
  7.1 7.3 %collective-permute-start.15 = (bf16[1024,128]{1,0:T(8,128)(2,1)S(1)}, bf16[1024,128]{1,0:T(8,128)(2,1)S(1)}, u32[]{:S(2)}, u32[]{:S(2)}) collective-permute-start(bf16[1024,128]{1,0:T(8,128)(2,1)S(1)} %copy-done.1), channel_id=1, source_target_pairs={{0,1},{1,0},{2,3},{3,2},{4,5},{5,4},{6,7},{7,6},{8,9},{9,8},{10,11... | collective-permute-start | bytes 786440 | tf_op jit(solution)/shard_map/ppermute | solution.py:129
  12.4 9.3 %collective-permute-start.1 = (bf16[256,512]{1,0:T(8,128)(2,1)S(1)}, bf16[256,512]{1,0:T(8,128)(2,1)S(1)}, u32[]{:S(2)}, u32[]{:S(2)}) collective-permute-start(bf16[256,512]{1,0:T(8,128)(2,1)S(1)} %collective-permute-done.refs_3_.refs_2_), channel_id=1, source_target_pairs={{0,4},{4,8},{8,12},{12,0},{1,5},{5,9},{9,13},{13,1},{2,6},{6,10},{... | collective-permute-start | bytes 786440 | tf_op jit(solution)/shard_map/ppermute | solution.py:119
  12.5 9.3 %collective-permute-start.14 = (bf16[1024,128]{1,0:T(8,128)(2,1)S(1)}, bf16[1024,128]{1,0:T(8,128)(2,1)S(1)}, u32[]{:S(2)}, u32[]{:S(2)}) collective-permute-start(bf16[1024,128]{1,0:T(8,128)(2,1)S(1)} %collective-permute-done.12.refs_7_), channel_id=1, source_target_pairs={{0,16},{16,0},{1,17},{17,1},{2,18},{18,2},{3,19},{19,3},{4,20},{20... | collective-permute-start | bytes 786440 | tf_op jit(solution)/shard_map/ppermute | solution.py:129
  13.9 7.8 %collective-permute-start.16 = (bf16[1024,128]{1,0:T(8,128)(2,1)S(1)}, bf16[1024,128]{1,0:T(8,128)(2,1)S(1)}, u32[]{:S(2)}, u32[]{:S(2)}) collective-permute-start(bf16[1024,128]{1,0:T(8,128)(2,1)S(1)} %collective-permute-done.12.refs_7_), channel_id=1, source_target_pairs={{0,1},{1,0},{2,3},{3,2},{4,5},{5,4},{6,7},{7,6},{8,9},{9,8},{10,11... | collective-permute-start | bytes 786440 | tf_op jit(solution)/shard_map/ppermute | solution.py:129
  14.0 8.3 %collective-permute-start.17 = (bf16[1024,128]{1,0:T(8,128)(2,1)S(1)}, bf16[1024,128]{1,0:T(8,128)(2,1)S(1)}, u32[]{:S(2)}, u32[]{:S(2)}) collective-permute-start(bf16[1024,128]{1,0:T(8,128)(2,1)S(1)} %collective-permute-done.13.refs_8_), channel_id=1, source_target_pairs={{0,1},{1,0},{2,3},{3,2},{4,5},{5,4},{6,7},{7,6},{8,9},{9,8},{10,11... | collective-permute-start | bytes 786440 | tf_op jit(solution)/shard_map/ppermute | solution.py:129
  14.5 9.1 %collective-permute-start.3 = (bf16[256,512]{1,0:T(8,128)(2,1)S(1)}, bf16[256,512]{1,0:T(8,128)(2,1)S(1)}, u32[]{:S(2)}, u32[]{:S(2)}) collective-permute-start(bf16[256,512]{1,0:T(8,128)(2,1)S(1)} %collective-permute-done.refs_3_.refs_2_), channel_id=1, source_target_pairs={{0,2},{1,3},{2,0},{3,1},{4,6},{5,7},{6,4},{7,5},{8,10},{9,11},{10,... | collective-permute-start | bytes 786440 | tf_op jit(solution)/shard_map/ppermute | solution.py:135
  21.7 8.4 %collective-permute-start.2 = (bf16[256,512]{1,0:T(8,128)(2,1)S(1)}, bf16[256,512]{1,0:T(8,128)(2,1)S(1)}, u32[]{:S(2)}, u32[]{:S(2)}) collective-permute-start(bf16[256,512]{1,0:T(8,128)(2,1)S(1)} %collective-permute-done.1.refs_4_.refs_3_), channel_id=1, source_target_pairs={{0,4},{4,8},{8,12},{12,0},{1,5},{5,9},{9,13},{13,1},{2,6},{6,10},{... | collective-permute-start | bytes 786440 | tf_op jit(solution)/shard_map/ppermute | solution.py:119
  21.7 8.4 %collective-permute-start.18 = (bf16[1024,128]{1,0:T(8,128)(2,1)S(1)}, bf16[1024,128]{1,0:T(8,128)(2,1)S(1)}, u32[]{:S(2)}, u32[]{:S(2)}) collective-permute-start(bf16[1024,128]{1,0:T(8,128)(2,1)S(1)} %collective-permute-done.14.refs_9_), channel_id=1, source_target_pairs={{0,1},{1,0},{2,3},{3,2},{4,5},{5,4},{6,7},{7,6},{8,9},{9,8},{10,11... | collective-permute-start | bytes 786440 | tf_op jit(solution)/shard_map/ppermute | solution.py:129
  21.8 11.4 %collective-permute-start.6 = (bf16[256,512]{1,0:T(8,128)(2,1)S(1)}, bf16[256,512]{1,0:T(8,128)(2,1)S(1)}, u32[]{:S(2)}, u32[]{:S(2)}) collective-permute-start(bf16[256,512]{1,0:T(8,128)(2,1)S(1)} %collective-permute-done.refs_3_.refs_2_), channel_id=1, source_target_pairs={{0,1},{1,0},{2,3},{3,2},{4,5},{5,4},{6,7},{7,6},{8,9},{9,8},{10,11... | collective-permute-start | bytes 786440 | tf_op jit(solution)/shard_map/ppermute | solution.py:135
  22.3 11.6 %collective-permute-start.4 = (bf16[256,512]{1,0:T(8,128)(2,1)S(1)}, bf16[256,512]{1,0:T(8,128)(2,1)S(1)}, u32[]{:S(2)}, u32[]{:S(2)}) collective-permute-start(bf16[256,512]{1,0:T(8,128)(2,1)S(1)} %collective-permute-done.1.refs_4_.refs_3_), channel_id=1, source_target_pairs={{0,2},{1,3},{2,0},{3,1},{4,6},{5,7},{6,4},{7,5},{8,10},{9,11},{10,... | collective-permute-start | bytes 786440 | tf_op jit(solution)/shard_map/ppermute | solution.py:135
  23.5 12.7 %collective-permute-start.7 = (bf16[256,512]{1,0:T(8,128)(2,1)S(1)}, bf16[256,512]{1,0:T(8,128)(2,1)S(1)}, u32[]{:S(2)}, u32[]{:S(2)}) collective-permute-start(bf16[256,512]{1,0:T(8,128)(2,1)S(1)} %collective-permute-done.1.refs_4_.refs_3_), channel_id=1, source_target_pairs={{0,1},{1,0},{2,3},{3,2},{4,5},{5,4},{6,7},{7,6},{8,9},{9,8},{10,11... | collective-permute-start | bytes 786440 | tf_op jit(solution)/shard_map/ppermute | solution.py:135
  30.1 6.2 %collective-permute-start.9 = (bf16[256,512]{1,0:T(8,128)(2,1)S(1)}, bf16[256,512]{1,0:T(8,128)(2,1)S(1)}, u32[]{:S(2)}, u32[]{:S(2)}) collective-permute-start(bf16[256,512]{1,0:T(8,128)(2,1)S(1)} %collective-permute-done.3.refs_5_), channel_id=1, source_target_pairs={{0,1},{1,0},{2,3},{3,2},{4,5},{5,4},{6,7},{7,6},{8,9},{9,8},{10,11... | collective-permute-start | bytes 786440 | tf_op jit(solution)/shard_map/ppermute | solution.py:135
  30.1 8.7 %collective-permute-start.5 = (bf16[256,512]{1,0:T(8,128)(2,1)S(1)}, bf16[256,512]{1,0:T(8,128)(2,1)S(1)}, u32[]{:S(2)}, u32[]{:S(2)}) collective-permute-start(bf16[256,512]{1,0:T(8,128)(2,1)S(1)} %collective-permute-done.2.refs_5_.refs_4_), channel_id=1, source_target_pairs={{0,2},{1,3},{2,0},{3,1},{4,6},{5,7},{6,4},{7,5},{8,10},{9,11},{10,... | collective-permute-start | bytes 786440 | tf_op jit(solution)/shard_map/ppermute | solution.py:135
  33.2 5.7 %collective-permute-start.19 = (bf16[128,512]{1,0:T(8,128)(2,1)S(1)}, bf16[128,512]{1,0:T(8,128)(2,1)S(1)}, u32[]{:S(2)}, u32[]{:S(2)}) collective-permute-start(bf16[128,512]{1,0:T(8,128)(2,1)S(1)} %get-tuple-element.7), channel_id=1, source_target_pairs={{0,0},{1,2},{2,4},{3,6},{4,1},{5,3},{6,5},{7,7},{8,16},{9,18},{10,... | collective-permute-start | bytes 393224 | tf_op jit(solution)/shard_map/ppermute | solution.py:167
  33.9 16.5 %collective-permute-start.20 = (bf16[128,512]{1,0:T(8,128)(2,1)S(1)}, bf16[128,512]{1,0:T(8,128)(2,1)S(1)}, u32[]{:S(2)}, u32[]{:S(2)}) collective-permute-start(bf16[128,512]{1,0:T(8,128)(2,1)S(1)} %get-tuple-element.8), channel_id=1, source_target_pairs={{0,1},{1,3},{2,5},{3,7},{4,16},{5,18},{6,20},{7,22},{8,17},{9,19},... | collective-permute-start | bytes 393224 | tf_op jit(solution)/shard_map/ppermute | solution.py:167
  36.2 35.8 %collective-permute-start.8 = (bf16[256,512]{1,0:T(8,128)(2,1)S(1)}, bf16[256,512]{1,0:T(8,128)(2,1)S(1)}, u32[]{:S(2)}, u32[]{:S(2)}) collective-permute-start(bf16[256,512]{1,0:T(8,128)(2,1)S(1)} %collective-permute-done.2.refs_5_.refs_4_), channel_id=1, source_target_pairs={{0,1},{1,0},{2,3},{3,2},{4,5},{5,4},{6,7},{7,6},{8,9},{9,8},{10,11... | collective-permute-start | bytes 786440 | tf_op jit(solution)/shard_map/ppermute | solution.py:135
  36.3 35.7 %collective-permute-start.10 = (bf16[256,512]{1,0:T(8,128)(2,1)S(1)}, bf16[256,512]{1,0:T(8,128)(2,1)S(1)}, u32[]{:S(2)}, u32[]{:S(2)}) collective-permute-start(bf16[256,512]{1,0:T(8,128)(2,1)S(1)} %collective-permute-done.4.refs_6_), channel_id=1, source_target_pairs={{0,1},{1,0},{2,3},{3,2},{4,5},{5,4},{6,7},{7,6},{8,9},{9,8},{10,11... | collective-permute-start | bytes 786440 | tf_op jit(solution)/shard_map/ppermute | solution.py:135
  38.8 33.2 %collective-permute-start.11 = (bf16[256,512]{1,0:T(8,128)(2,1)S(1)}, bf16[256,512]{1,0:T(8,128)(2,1)S(1)}, u32[]{:S(2)}, u32[]{:S(2)}) collective-permute-start(bf16[256,512]{1,0:T(8,128)(2,1)S(1)} %collective-permute-done.5.refs_7_), channel_id=1, source_target_pairs={{0,1},{1,0},{2,3},{3,2},{4,5},{5,4},{6,7},{7,6},{8,9},{9,8},{10,11... | collective-permute-start | bytes 786440 | tf_op jit(solution)/shard_map/ppermute | solution.py:135
  38.8 16.2 %collective-permute-start.21 = (bf16[128,512]{1,0:T(8,128)(2,1)S(1)}, bf16[128,512]{1,0:T(8,128)(2,1)S(1)}, u32[]{:S(2)}, u32[]{:S(2)}) collective-permute-start(bf16[128,512]{1,0:T(8,128)(2,1)S(1)} %get-tuple-element.7), channel_id=1, source_target_pairs={{0,16},{1,18},{2,20},{3,22},{4,17},{5,19},{6,21},{7,23},{8,0},{9,2... | collective-permute-start | bytes 393224 | tf_op jit(solution)/shard_map/ppermute | solution.py:167
  50.4 21.6 %collective-permute-start.22 = (bf16[128,512]{1,0:T(8,128)(2,1)S(1)}, bf16[128,512]{1,0:T(8,128)(2,1)S(1)}, u32[]{:S(2)}, u32[]{:S(2)}) collective-permute-start(bf16[128,512]{1,0:T(8,128)(2,1)S(1)} %get-tuple-element.8), channel_id=1, source_target_pairs={{0,17},{1,19},{2,21},{3,23},{4,0},{5,2},{6,4},{7,6},{8,1},{9,3},{1... | collective-permute-start | bytes 393224 | tf_op jit(solution)/shard_map/ppermute | solution.py:167
  (3 other events, 66.5 us)

commit v2 on v1

v2 whole, which is shorter than its diff:
```python
import functools
from typing import NamedTuple

import jax
import jax.numpy as jnp
from jax import lax
from jax.experimental import pallas as pl
from jax.experimental.pallas import tpu as pltpu
from jax.sharding import PartitionSpec as P

BS = 256
VMEM_LIMIT = 48 * 1024 * 1024


class Sizes(NamedTuple):
    rows: int
    cols: int
    layers: int
    rows_here: int
    cols_here: int
    quarter: int
    per: int


def bits_of(size):
    return [1 << b for b in reversed(range(size.bit_length() - 1))]


def flip(size, bit):
    return [(i, i ^ bit) for i in range(size)]


def mod(a, n):
    return lax.rem(a + n, n)


def keep_block(pattern, i, j, block):
    return jnp.where(pattern[i, j] > 0, block, jnp.zeros_like(block))


def strip_rows(r, l, half, sizes):
    return pl.multiple_of(half * sizes.cols_here + l * sizes.quarter, sizes.quarter)


def strip_block(r, l, half, sizes):
    return (r * sizes.rows_here + half * sizes.cols_here + l * sizes.quarter) // BS


def mask_row(zp, block_row, first_block, piece):
    parts = [
        keep_block(zp, block_row, first_block + t, piece[:, t * BS : (t + 1) * BS])
        for t in range(piece.shape[1] // BS)
    ]
    return jnp.concatenate(parts, axis=1)


def first_kernel(sizes, h_offsets, *refs):
    cols, layers, quarter = sizes.cols, sizes.layers, sizes.quarter
    hp, zp = refs[0], refs[1]
    z_slots = refs[2 : 2 + cols]
    h_pieces = refs[2 + cols : 2 + cols + len(h_offsets)]
    out, zm, hm = refs[2 + cols + len(h_offsets) :]
    r, c, l = lax.axis_index("row"), lax.axis_index("col"), lax.axis_index("layer")
    per_tile = sizes.cols_here // BS
    per_rows = sizes.rows_here // BS
    for s in range(cols):
        cc = mod(c - s, cols)
        for half in range(sizes.per):
            rows = slice(half * quarter, (half + 1) * quarter)
            block_row = strip_block(r, l, half, sizes)
            zm[
                rows, pl.ds(pl.multiple_of(cc * sizes.cols_here, sizes.cols_here), sizes.cols_here)
            ] = mask_row(zp, block_row, cc * per_tile, z_slots[s][rows, :])
    for (dr, dl), piece in zip(h_offsets, h_pieces):
        rr, ll = r ^ dr, l ^ dl
        block_col = (c * sizes.cols_here + ll * quarter) // BS
        for q in range(per_rows):
            j = rr * per_rows + q
            hm[
                pl.ds(pl.multiple_of(j * BS, BS), BS),
                pl.ds(pl.multiple_of(ll * quarter, quarter), quarter),
            ] = keep_block(hp, j, block_col, piece[q * BS : (q + 1) * BS, :])
    total = None
    order = zm.shape[1]
    chunk = min(order, 2048)
    for k in range(0, order, chunk):
        part = jnp.dot(
            zm[:, k : k + chunk], hm[k : k + chunk, :], preferred_element_type=jnp.float32
        )
        total = part if total is None else total + part
    out[...] = total.astype(jnp.bfloat16)


def route_kernel(sizes, row_offsets, *refs):
    n = len(row_offsets)
    pieces, outs, table = refs[:n], refs[n:-1], refs[-1]
    r, c = lax.axis_index("row"), lax.axis_index("col")
    for dr, piece in zip(row_offsets, pieces):
        for half in range(sizes.per):
            table[(r ^ dr) * sizes.per + half] = piece[
                half * sizes.quarter : (half + 1) * sizes.quarter, :
            ]
    for d, out in enumerate(outs):
        out[...] = table[c ^ d]


def second_kernel(sizes, z_offsets, *refs):
    cols, quarter = sizes.cols, sizes.quarter
    zp, z_tile = refs[0], refs[1]
    n_slots = len(z_offsets) * (cols - 1)
    slots = refs[2 : 2 + n_slots]
    messages = refs[2 + n_slots : 2 + n_slots + cols]
    out, xm = refs[2 + n_slots + cols :]
    r, c, l = lax.axis_index("row"), lax.axis_index("col"), lax.axis_index("layer")
    per_tile = sizes.cols_here // BS
    for d in range(cols):
        xm[c ^ d] = messages[d][...]
    for n, dl in enumerate(z_offsets):
        ll = l ^ dl
        total = None
        for s in range(cols):
            cc = mod(c - s, cols)
            strips = []
            for half in range(sizes.per):
                if s == 0:
                    strip = z_tile[pl.ds(strip_rows(r, ll, half, sizes), quarter), :]
                else:
                    strip = slots[n * (cols - 1) + s - 1][half * quarter : (half + 1) * quarter, :]
                strips.append(mask_row(zp, strip_block(r, ll, half, sizes), cc * per_tile, strip))
            part = lax.dot_general(
                jnp.concatenate(strips, axis=0),
                xm[cc],
                (((1,), (1,)), ((), ())),
                preferred_element_type=jnp.float32,
            )
            total = part if total is None else total + part
        for half in range(sizes.per):
            out[pl.ds(strip_rows(r, ll, half, sizes), quarter), :] = total[
                half * quarter : (half + 1) * quarter, :
            ].astype(out.dtype)


def local(sizes, hamiltonian, inv_root, h_pattern, z_pattern):
    rows, cols, layers = sizes.rows, sizes.cols, sizes.layers
    quarter, cols_here = sizes.quarter, sizes.cols_here
    order = rows * sizes.rows_here
    strip_height = sizes.per * quarter
    l = lax.axis_index("layer")
    smem = pl.BlockSpec(memory_space=pltpu.SMEM)
    vmem = pl.BlockSpec(memory_space=pltpu.VMEM)
    params = pltpu.CompilerParams(vmem_limit_bytes=VMEM_LIMIT)

    striped = inv_root.reshape(sizes.per, layers, quarter, cols_here)
    own = lax.dynamic_index_in_dim(striped, l, 1, keepdims=False).reshape(strip_height, cols_here)
    ring = [(i, (i + 1) % cols) for i in range(cols)]
    z_slots = [own]
    for _ in range(1, cols):
        z_slots.append(lax.ppermute(z_slots[-1], "col", ring))

    h_pieces = {(0, 0): hamiltonian}
    row_bits, layer_bits = bits_of(rows), bits_of(layers)
    steps = [("layer", layers, layer_bits[0])]
    steps += [("row", rows, b) for b in row_bits]
    steps += [("layer", layers, b) for b in layer_bits[1:]]
    for axis, size, bit in steps:
        for (dr, dl), piece in list(h_pieces.items()):
            there = (dr ^ bit, dl) if axis == "row" else (dr, dl ^ bit)
            h_pieces[there] = lax.ppermute(piece, axis, flip(size, bit))
    h_offsets = list(h_pieces)

    shared = {0: z_slots[1:]}
    for bit in layer_bits:
        for dl, pieces in list(shared.items()):
            shared[dl ^ bit] = [lax.ppermute(p, "layer", flip(layers, bit)) for p in pieces]
    z_offsets = list(shared)

    product = pl.pallas_call(
        functools.partial(first_kernel, sizes, h_offsets),
        out_shape=jax.ShapeDtypeStruct((strip_height, cols_here), jnp.bfloat16),
        in_specs=[smem, smem] + [vmem] * (cols + len(h_offsets)),
        out_specs=vmem,
        scratch_shapes=[
            pltpu.VMEM((strip_height, order), jnp.bfloat16),
            pltpu.VMEM((order, cols_here), jnp.bfloat16),
        ],
        compiler_params=params,
        name="first_product",
    )(h_pattern, z_pattern, *z_slots, *[h_pieces[o] for o in h_offsets])

    gathered = {0: product}
    for bit in row_bits:
        for dr, piece in list(gathered.items()):
            gathered[dr ^ bit] = lax.ppermute(piece, "row", flip(rows, bit))
    row_offsets = list(gathered)
    strip = jax.ShapeDtypeStruct((quarter, cols_here), jnp.bfloat16)
    outgoing = pl.pallas_call(
        functools.partial(route_kernel, sizes, row_offsets),
        out_shape=[strip] * cols,
        in_specs=[vmem] * rows,
        out_specs=[vmem] * cols,
        scratch_shapes=[pltpu.VMEM((cols, quarter, cols_here), jnp.bfloat16)],
        compiler_params=params,
        name="route",
    )(*[gathered[o] for o in row_offsets])
    messages = [outgoing[0]] + [
        lax.ppermute(outgoing[d], "col", flip(cols, d)) for d in range(1, cols)
    ]

    flat = [p for o in z_offsets for p in shared[o]]
    return pl.pallas_call(
        functools.partial(second_kernel, sizes, z_offsets),
        out_shape=jax.ShapeDtypeStruct(hamiltonian.shape, jnp.bfloat16),
        in_specs=[smem] + [vmem] * (1 + len(flat) + cols),
        out_specs=vmem,
        scratch_shapes=[pltpu.VMEM((cols, quarter, cols_here), jnp.bfloat16)],
        compiler_params=params,
        name="second_product",
    )(z_pattern, inv_root, *flat, *messages)


def solution(mesh):
    rows, cols, layers = (mesh.shape[a] for a in ("row", "col", "layer"))

    def whole(hamiltonian, inv_root, h_pattern, z_pattern):
        order = hamiltonian.shape[0]
        cols_here = order // cols
        sizes = Sizes(
            rows, cols, layers, order // rows, cols_here, cols_here // layers, cols // rows
        )
        return jax.shard_map(
            functools.partial(local, sizes),
            mesh=mesh,
            in_specs=(P("row", ("col", "layer")), P("row", "col"), P(), P()),
            out_specs=P("row", ("col", "layer")),
            check_vma=False,
        )(hamiltonian, inv_root, h_pattern, z_pattern)

    return whole
```

time: 74.9 us -> 59 us (0.79)
  starting transfers between devices: 32.3 us -> 17.9 us
  waiting for transfers between devices: 36.7 us -> 35.1 us
    ppermute x4, starting transfers between devices: 19.3 us -> 5.55 us  [the longest x3 4.44 us: local(): lax.ppermute(outgoing[d], 'col', flip(cols, d))]
    ppermute x4, waiting for transfers between devices: 17 us -> 11.9 us  [the longest x3 9.91 us: local(): lax.ppermute(outgoing[d], 'col', flip(cols, d))]
    ppermute x9, waiting for transfers between devices: 2.09 us -> 4.48 us  [local(): lax.ppermute(p, 'layer', flip(layers, bit))]
    ppermute x3, waiting for transfers between devices: 17.6 us -> 18.7 us  [local(): z_slots.append(lax.ppermute(z_slots[-1], 'col', ring))]
  transfers between devices with their start and end apart: 23 -> 23, of which waited for: 5 -> 8; matrix products, arithmetic and copies ran while one was open for 0% -> 0% of each run, Pallas kernels for 3% -> 3%
where the time goes in v2:
time: 59 us; the launch traced here: 58.9 us
  waiting for transfers between devices  35.1 us (59%)
  starting transfers between devices  17.9 us (30%)
  Pallas kernels  4.73 us (8%)
  local copies, waits for them, and re-layouts  1.03 us (2%)
    ppermute x3, waiting for transfers between devices, local(): z_slots.append(lax.ppermute(z_slots[-1], 'col', ring))  18.7 us
    ppermute x3, waiting for transfers between devices, local(): lax.ppermute(outgoing[d], 'col', flip(cols, d))  9.91 us
    ppermute x7, starting transfers between devices, local(): h_pieces[there] = lax.ppermute(piece, axis, flip(size, bit))  5.02 us
    ppermute x9, waiting for transfers between devices, local(): lax.ppermute(p, 'layer', flip(layers, bit))  4.48 us
    ppermute x3, starting transfers between devices, local(): lax.ppermute(outgoing[d], 'col', flip(cols, d))  4.44 us
    ppermute x9, starting transfers between devices, local(): lax.ppermute(p, 'layer', flip(layers, bit))  4.29 us
    ppermute x3, starting transfers between devices, local(): z_slots.append(lax.ppermute(z_slots[-1], 'col', ring))  3.09 us
    pallas_call x1, Pallas kernels, local(): pl.pallas_call(functools.partial(second_kernel, sizes, z_offsets), out_sh...  2.67 us
  transfers between devices with their start and end apart: 23, of which 8 were waited for; matrix products, arithmetic and copies ran while one was open for 0% of the time, Pallas kernels for 3%

profile of v2, /device:TPU:0, one launch (start us, length us, event | category | flops | bytes accessed | tf_op | source)
XLA Modules:
  0.0 58.9 jit_solution(1000242533373282774)
XLA Ops:
  0.0 1.0 %constant_dynamic-slice_fusion = bf16[2,1,128,512]{3,2,1,0:T(8,128)(2,1)S(1)} fusion(bf16[2,4,128,512]{3,2,1,0:T(8,128)(2,1)} %bitcast.4, s32[]{:T(128)S(6)} %select_n.4), kind=kLoop, calls=%fused_computation | loop fusion | bytes 524292 | tf_op jit(solution)/shard_map/jit(dynamic_index_in_dim)/dynamic_slice | solution.py:154
  1.0 3.1 %collective-permute-start = (bf16[256,512]{1,0:T(8,128)(2,1)S(1)}, bf16[256,512]{1,0:T(8,128)(2,1)S(1)}, u32[]{:S(2)}, u32[]{:S(2)}) collective-permute-start(bf16[256,512]{1,0:T(8,128)(2,1)S(1)} %bitcast.5), channel_id=1, source_target_pairs={{0,4},{4,8},{8,12},{12,0},{1,5},{5,9},{9,13},{13,1},{2,6},{6,10},{... | collective-permute-start | bytes 786440 | tf_op jit(solution)/shard_map/ppermute | solution.py:158
  4.1 1.5 %collective-permute-start.12 = (bf16[1024,128]{1,0:T(8,128)(2,1)S(1)}, bf16[1024,128]{1,0:T(8,128)(2,1)S(1)}, u32[]{:S(2)}, u32[]{:S(2)}) collective-permute-start(bf16[1024,128]{1,0:T(8,128)(2,1)S(1)} %copy-done.1), channel_id=1, source_target_pairs={{0,2},{1,3},{2,0},{3,1},{4,6},{5,7},{6,4},{7,5},{8,10},{9,11},{10,... | collective-permute-start | bytes 786440 | tf_op jit(solution)/shard_map/ppermute | solution.py:168
  5.6 1.5 %collective-permute-start.13 = (bf16[1024,128]{1,0:T(8,128)(2,1)S(1)}, bf16[1024,128]{1,0:T(8,128)(2,1)S(1)}, u32[]{:S(2)}, u32[]{:S(2)}) collective-permute-start(bf16[1024,128]{1,0:T(8,128)(2,1)S(1)} %copy-done.1), channel_id=1, source_target_pairs={{0,16},{16,0},{1,17},{17,1},{2,18},{18,2},{3,19},{19,3},{4,20},{20... | collective-permute-start | bytes 786440 | tf_op jit(solution)/shard_map/ppermute | solution.py:168
  7.1 5.3 %collective-permute-done.refs_3_.refs_2_ = bf16[256,512]{1,0:T(8,128)(2,1)S(1)} collective-permute-done((bf16[256,512]{1,0:T(8,128)(2,1)S(1)}, bf16[256,512]{1,0:T(8,128)(2,1)S(1)}, u32[]{:S(2)}, u32[]{:S(2)}) %collective-permute-start) | collective-permute-done | bytes 262176 | tf_op jit(solution)/shard_map/ppermute | solution.py:158
  12.4 1.5 %collective-permute-start.14 = (bf16[1024,128]{1,0:T(8,128)(2,1)S(1)}, bf16[1024,128]{1,0:T(8,128)(2,1)S(1)}, u32[]{:S(2)}, u32[]{:S(2)}) collective-permute-start(bf16[1024,128]{1,0:T(8,128)(2,1)S(1)} %collective-permute-done.12.refs_7_), channel_id=1, source_target_pairs={{0,16},{16,0},{1,17},{17,1},{2,18},{18,2},{3,19},{19,3},{4,20},{20... | collective-permute-start | bytes 786440 | tf_op jit(solution)/shard_map/ppermute | solution.py:168
  13.9 0.5 collective-permute-start.16
  14.5 7.3 %collective-permute-done.1.refs_4_.refs_3_ = bf16[256,512]{1,0:T(8,128)(2,1)S(1)} collective-permute-done((bf16[256,512]{1,0:T(8,128)(2,1)S(1)}, bf16[256,512]{1,0:T(8,128)(2,1)S(1)}, u32[]{:S(2)}, u32[]{:S(2)}) %collective-permute-start.1) | collective-permute-done | bytes 262176 | tf_op jit(solution)/shard_map/ppermute | solution.py:158
  21.8 1.3 %collective-permute-start.3 = (bf16[256,512]{1,0:T(8,128)(2,1)S(1)}, bf16[256,512]{1,0:T(8,128)(2,1)S(1)}, u32[]{:S(2)}, u32[]{:S(2)}) collective-permute-start(bf16[256,512]{1,0:T(8,128)(2,1)S(1)} %collective-permute-done.refs_3_.refs_2_), channel_id=1, source_target_pairs={{0,2},{1,3},{2,0},{3,1},{4,6},{5,7},{6,4},{7,5},{8,10},{9,11},{10,... | collective-permute-start | bytes 786440 | tf_op jit(solution)/shard_map/ppermute | solution.py:174
  23.1 0.2 collective-permute-start.6
  23.3 0.8 %collective-permute-start.4 = (bf16[256,512]{1,0:T(8,128)(2,1)S(1)}, bf16[256,512]{1,0:T(8,128)(2,1)S(1)}, u32[]{:S(2)}, u32[]{:S(2)}) collective-permute-start(bf16[256,512]{1,0:T(8,128)(2,1)S(1)} %collective-permute-done.1.refs_4_.refs_3_), channel_id=1, source_target_pairs={{0,2},{1,3},{2,0},{3,1},{4,6},{5,7},{6,4},{7,5},{8,10},{9,11},{10,... | collective-permute-start | bytes 786440 | tf_op jit(solution)/shard_map/ppermute | solution.py:174
  24.0 6.1 %collective-permute-done.2.refs_5_.refs_4_ = bf16[256,512]{1,0:T(8,128)(2,1)S(1)} collective-permute-done((bf16[256,512]{1,0:T(8,128)(2,1)S(1)}, bf16[256,512]{1,0:T(8,128)(2,1)S(1)}, u32[]{:S(2)}, u32[]{:S(2)}) %collective-permute-start.2) | collective-permute-done | bytes 262176 | tf_op jit(solution)/shard_map/ppermute | solution.py:158
  30.1 2.0 %first_product.1.refs_0_ = bf16[256,512]{1,0:T(8,128)(2,1)S(1)} custom-call(s32[8,8]{1,0:T(8,128)S(1)} %copy-done.3, s32[8,8]{1,0:T(8,128)S(1)} %copy-done.2, bf16[256,512]{1,0:T(8,128)(2,1)S(1)} %bitcast.6, bf16[256,512]{1,0:T(8,128)(2,1)S(1)} %collective-permute-done.refs_3_.refs_2_, bf16[256,512]{1,0:T(8,128)(2,1)S(1)} %collective-permute-done.1.refs_4_.refs_3_, ...), custom_call_target="tpu_custom_call" | custom-call | tf_op jit(solution)/shard_map/first_product/pallas_call | solution.py:177
  32.1 1.1 %collective-permute-start.19 = (bf16[256,512]{1,0:T(8,128)(2,1)S(1)}, bf16[256,512]{1,0:T(8,128)(2,1)S(1)}, u32[]{:S(2)}, u32[]{:S(2)}) collective-permute-start(bf16[256,512]{1,0:T(8,128)(2,1)S(1)} %first_product.1.refs_0_), channel_id=1, source_target_pairs={{0,16},{16,0},{1,17},{17,1},{2,18},{18,2},{3,19},{19,3},{4,20},{20... | collective-permute-start | bytes 786440 | tf_op jit(solution)/shard_map/ppermute | solution.py:193
  33.2 1.5 %collective-permute-start.5 = (bf16[256,512]{1,0:T(8,128)(2,1)S(1)}, bf16[256,512]{1,0:T(8,128)(2,1)S(1)}, u32[]{:S(2)}, u32[]{:S(2)}) collective-permute-start(bf16[256,512]{1,0:T(8,128)(2,1)S(1)} %collective-permute-done.2.refs_5_.refs_4_), channel_id=1, source_target_pairs={{0,2},{1,3},{2,0},{3,1},{4,6},{5,7},{6,4},{7,5},{8,10},{9,11},{10,... | collective-permute-start | bytes 786440 | tf_op jit(solution)/shard_map/ppermute | solution.py:174
  34.7 0.5 collective-permute-start.9
  35.2 1.3 %collective-permute-done.4.refs_6_ = bf16[256,512]{1,0:T(8,128)(2,1)S(1)} collective-permute-done((bf16[256,512]{1,0:T(8,128)(2,1)S(1)}, bf16[256,512]{1,0:T(8,128)(2,1)S(1)}, u32[]{:S(2)}, u32[]{:S(2)}) %collective-permute-start.4) | collective-permute-done | bytes 262176 | tf_op jit(solution)/shard_map/ppermute | solution.py:174
  36.5 2.0 %collective-permute-done.19.refs_1_ = bf16[256,512]{1,0:T(8,128)(2,1)S(1)} collective-permute-done((bf16[256,512]{1,0:T(8,128)(2,1)S(1)}, bf16[256,512]{1,0:T(8,128)(2,1)S(1)}, u32[]{:S(2)}, u32[]{:S(2)}) %collective-permute-start.19) | collective-permute-done | bytes 262176 | tf_op jit(solution)/shard_map/ppermute | solution.py:193
  38.5 3.2 %collective-permute-done.5.refs_7_ = bf16[256,512]{1,0:T(8,128)(2,1)S(1)} collective-permute-done((bf16[256,512]{1,0:T(8,128)(2,1)S(1)}, bf16[256,512]{1,0:T(8,128)(2,1)S(1)}, u32[]{:S(2)}, u32[]{:S(2)}) %collective-permute-start.5) | collective-permute-done | bytes 262176 | tf_op jit(solution)/shard_map/ppermute | solution.py:174
  41.7 0.1 route.1
  41.9 4.3 %collective-permute-start.21 = (bf16[128,512]{1,0:T(8,128)(2,1)S(1)}, bf16[128,512]{1,0:T(8,128)(2,1)S(1)}, u32[]{:S(2)}, u32[]{:S(2)}) collective-permute-start(bf16[128,512]{1,0:T(8,128)(2,1)S(1)} %get-tuple-element.11), channel_id=1, source_target_pairs={{0,8},{4,12},{8,0},{12,4},{1,9},{5,13},{9,1},{13,5},{2,10},{6,14},... | collective-permute-start | bytes 393224 | tf_op jit(solution)/shard_map/ppermute | solution.py:206
  46.3 4.0 %collective-permute-done.20.refs_15_ = bf16[128,512]{1,0:T(8,128)(2,1)S(1)} collective-permute-done((bf16[128,512]{1,0:T(8,128)(2,1)S(1)}, bf16[128,512]{1,0:T(8,128)(2,1)S(1)}, u32[]{:S(2)}, u32[]{:S(2)}) %collective-permute-start.20) | collective-permute-done | bytes 131104 | tf_op jit(solution)/shard_map/ppermute | solution.py:206
  50.3 5.9 %collective-permute-done.21.refs_16_ = bf16[128,512]{1,0:T(8,128)(2,1)S(1)} collective-permute-done((bf16[128,512]{1,0:T(8,128)(2,1)S(1)}, bf16[128,512]{1,0:T(8,128)(2,1)S(1)}, u32[]{:S(2)}, u32[]{:S(2)}) %collective-permute-start.21) | collective-permute-done | bytes 131104 | tf_op jit(solution)/shard_map/ppermute | solution.py:206
  56.2 2.7 %second_product.1 = bf16[1024,128]{1,0:T(8,128)(2,1)} custom-call(s32[8,8]{1,0:T(8,128)S(1)} %copy-done.2, bf16[1024,512]{1,0:T(8,128)(2,1)S(1)} %copy-done, bf16[256,512]{1,0:T(8,128)(2,1)S(1)} %collective-permute-done.refs_3_.refs_2_, bf16[256,512]{1,0:T(8,128)(2,1)S(1)} %collective-permute-done.1.refs_4_.refs_3_, ...), custom_call_target="tpu_custom_call" | custom-call | tf_op jit(solution)/shard_map/second_product/pallas_call | solution.py:210
  (34 shorter events, 0.2 us)
Async XLA Ops:
  0.0 30.1 %copy-start.3 = (s32[8,8]{1,0:T(8,128)S(1)}, s32[8,8]{1,0:T(8,128)}, u32[]{:S(2)}) copy-start(s32[8,8]{1,0:T(8,128)} %refs_0_.2) | copy-start | bytes 772
  1.0 11.4 %collective-permute-start = (bf16[256,512]{1,0:T(8,128)(2,1)S(1)}, bf16[256,512]{1,0:T(8,128)(2,1)S(1)}, u32[]{:S(2)}, u32[]{:S(2)}) collective-permute-start(bf16[256,512]{1,0:T(8,128)(2,1)S(1)} %bitcast.5), channel_id=1, source_target_pairs={{0,4},{4,8},{8,12},{12,0},{1,5},{5,9},{9,13},{13,1},{2,6},{6,10},{... | collective-permute-start | bytes 786440 | tf_op jit(solution)/shard_map/ppermute | solution.py:158
  4.1 8.3 %collective-permute-start.12 = (bf16[1024,128]{1,0:T(8,128)(2,1)S(1)}, bf16[1024,128]{1,0:T(8,128)(2,1)S(1)}, u32[]{:S(2)}, u32[]{:S(2)}) collective-permute-start(bf16[1024,128]{1,0:T(8,128)(2,1)S(1)} %copy-done.1), channel_id=1, source_target_pairs={{0,2},{1,3},{2,0},{3,1},{4,6},{5,7},{6,4},{7,5},{8,10},{9,11},{10,... | collective-permute-start | bytes 786440 | tf_op jit(solution)/shard_map/ppermute | solution.py:168
  5.6 8.8 %collective-permute-start.13 = (bf16[1024,128]{1,0:T(8,128)(2,1)S(1)}, bf16[1024,128]{1,0:T(8,128)(2,1)S(1)}, u32[]{:S(2)}, u32[]{:S(2)}) collective-permute-start(bf16[1024,128]{1,0:T(8,128)(2,1)S(1)} %copy-done.1), channel_id=1, source_target_pairs={{0,16},{16,0},{1,17},{17,1},{2,18},{18,2},{3,19},{19,3},{4,20},{20... | collective-permute-start | bytes 786440 | tf_op jit(solution)/shard_map/ppermute | solution.py:168
  12.4 9.3 %collective-permute-start.1 = (bf16[256,512]{1,0:T(8,128)(2,1)S(1)}, bf16[256,512]{1,0:T(8,128)(2,1)S(1)}, u32[]{:S(2)}, u32[]{:S(2)}) collective-permute-start(bf16[256,512]{1,0:T(8,128)(2,1)S(1)} %collective-permute-done.refs_3_.refs_2_), channel_id=1, source_target_pairs={{0,4},{4,8},{8,12},{12,0},{1,5},{5,9},{9,13},{13,1},{2,6},{6,10},{... | collective-permute-start | bytes 786440 | tf_op jit(solution)/shard_map/ppermute | solution.py:158
  12.4 9.3 %collective-permute-start.14 = (bf16[1024,128]{1,0:T(8,128)(2,1)S(1)}, bf16[1024,128]{1,0:T(8,128)(2,1)S(1)}, u32[]{:S(2)}, u32[]{:S(2)}) collective-permute-start(bf16[1024,128]{1,0:T(8,128)(2,1)S(1)} %collective-permute-done.12.refs_7_), channel_id=1, source_target_pairs={{0,16},{16,0},{1,17},{17,1},{2,18},{18,2},{3,19},{19,3},{4,20},{20... | collective-permute-start | bytes 786440 | tf_op jit(solution)/shard_map/ppermute | solution.py:168
  13.9 7.8 %collective-permute-start.15 = (bf16[1024,128]{1,0:T(8,128)(2,1)S(1)}, bf16[1024,128]{1,0:T(8,128)(2,1)S(1)}, u32[]{:S(2)}, u32[]{:S(2)}) collective-permute-start(bf16[1024,128]{1,0:T(8,128)(2,1)S(1)} %copy-done.1), channel_id=1, source_target_pairs={{0,1},{1,0},{2,3},{3,2},{4,5},{5,4},{6,7},{7,6},{8,9},{9,8},{10,11... | collective-permute-start | bytes 786440 | tf_op jit(solution)/shard_map/ppermute | solution.py:168
  13.9 9.2 %collective-permute-start.16 = (bf16[1024,128]{1,0:T(8,128)(2,1)S(1)}, bf16[1024,128]{1,0:T(8,128)(2,1)S(1)}, u32[]{:S(2)}, u32[]{:S(2)}) collective-permute-start(bf16[1024,128]{1,0:T(8,128)(2,1)S(1)} %collective-permute-done.12.refs_7_), channel_id=1, source_target_pairs={{0,1},{1,0},{2,3},{3,2},{4,5},{5,4},{6,7},{7,6},{8,9},{9,8},{10,11... | collective-permute-start | bytes 786440 | tf_op jit(solution)/shard_map/ppermute | solution.py:168
  14.5 8.8 %collective-permute-start.17 = (bf16[1024,128]{1,0:T(8,128)(2,1)S(1)}, bf16[1024,128]{1,0:T(8,128)(2,1)S(1)}, u32[]{:S(2)}, u32[]{:S(2)}) collective-permute-start(bf16[1024,128]{1,0:T(8,128)(2,1)S(1)} %collective-permute-done.13.refs_8_), channel_id=1, source_target_pairs={{0,1},{1,0},{2,3},{3,2},{4,5},{5,4},{6,7},{7,6},{8,9},{9,8},{10,11... | collective-permute-start | bytes 786440 | tf_op jit(solution)/shard_map/ppermute | solution.py:168
  21.7 8.4 %collective-permute-start.2 = (bf16[256,512]{1,0:T(8,128)(2,1)S(1)}, bf16[256,512]{1,0:T(8,128)(2,1)S(1)}, u32[]{:S(2)}, u32[]{:S(2)}) collective-permute-start(bf16[256,512]{1,0:T(8,128)(2,1)S(1)} %collective-permute-done.1.refs_4_.refs_3_), channel_id=1, source_target_pairs={{0,4},{4,8},{8,12},{12,0},{1,5},{5,9},{9,13},{13,1},{2,6},{6,10},{... | collective-permute-start | bytes 786440 | tf_op jit(solution)/shard_map/ppermute | solution.py:158
  21.7 8.4 %collective-permute-start.18 = (bf16[1024,128]{1,0:T(8,128)(2,1)S(1)}, bf16[1024,128]{1,0:T(8,128)(2,1)S(1)}, u32[]{:S(2)}, u32[]{:S(2)}) collective-permute-start(bf16[1024,128]{1,0:T(8,128)(2,1)S(1)} %collective-permute-done.14.refs_9_), channel_id=1, source_target_pairs={{0,1},{1,0},{2,3},{3,2},{4,5},{5,4},{6,7},{7,6},{8,9},{9,8},{10,11... | collective-permute-start | bytes 786440 | tf_op jit(solution)/shard_map/ppermute | solution.py:168
  21.8 13.0 %collective-permute-start.3 = (bf16[256,512]{1,0:T(8,128)(2,1)S(1)}, bf16[256,512]{1,0:T(8,128)(2,1)S(1)}, u32[]{:S(2)}, u32[]{:S(2)}) collective-permute-start(bf16[256,512]{1,0:T(8,128)(2,1)S(1)} %collective-permute-done.refs_3_.refs_2_), channel_id=1, source_target_pairs={{0,2},{1,3},{2,0},{3,1},{4,6},{5,7},{6,4},{7,5},{8,10},{9,11},{10,... | collective-permute-start | bytes 786440 | tf_op jit(solution)/shard_map/ppermute | solution.py:174
  23.1 11.6 %collective-permute-start.6 = (bf16[256,512]{1,0:T(8,128)(2,1)S(1)}, bf16[256,512]{1,0:T(8,128)(2,1)S(1)}, u32[]{:S(2)}, u32[]{:S(2)}) collective-permute-start(bf16[256,512]{1,0:T(8,128)(2,1)S(1)} %collective-permute-done.refs_3_.refs_2_), channel_id=1, source_target_pairs={{0,1},{1,0},{2,3},{3,2},{4,5},{5,4},{6,7},{7,6},{8,9},{9,8},{10,11... | collective-permute-start | bytes 786440 | tf_op jit(solution)/shard_map/ppermute | solution.py:174
  23.3 13.3 %collective-permute-start.4 = (bf16[256,512]{1,0:T(8,128)(2,1)S(1)}, bf16[256,512]{1,0:T(8,128)(2,1)S(1)}, u32[]{:S(2)}, u32[]{:S(2)}) collective-permute-start(bf16[256,512]{1,0:T(8,128)(2,1)S(1)} %collective-permute-done.1.refs_4_.refs_3_), channel_id=1, source_target_pairs={{0,2},{1,3},{2,0},{3,1},{4,6},{5,7},{6,4},{7,5},{8,10},{9,11},{10,... | collective-permute-start | bytes 786440 | tf_op jit(solution)/shard_map/ppermute | solution.py:174
  32.1 6.4 %collective-permute-start.19 = (bf16[256,512]{1,0:T(8,128)(2,1)S(1)}, bf16[256,512]{1,0:T(8,128)(2,1)S(1)}, u32[]{:S(2)}, u32[]{:S(2)}) collective-permute-start(bf16[256,512]{1,0:T(8,128)(2,1)S(1)} %first_product.1.refs_0_), channel_id=1, source_target_pairs={{0,16},{16,0},{1,17},{17,1},{2,18},{18,2},{3,19},{19,3},{4,20},{20... | collective-permute-start | bytes 786440 | tf_op jit(solution)/shard_map/ppermute | solution.py:193
  33.2 8.5 %collective-permute-start.5 = (bf16[256,512]{1,0:T(8,128)(2,1)S(1)}, bf16[256,512]{1,0:T(8,128)(2,1)S(1)}, u32[]{:S(2)}, u32[]{:S(2)}) collective-permute-start(bf16[256,512]{1,0:T(8,128)(2,1)S(1)} %collective-permute-done.2.refs_5_.refs_4_), channel_id=1, source_target_pairs={{0,2},{1,3},{2,0},{3,1},{4,6},{5,7},{6,4},{7,5},{8,10},{9,11},{10,... | collective-permute-start | bytes 786440 | tf_op jit(solution)/shard_map/ppermute | solution.py:174
  34.7 7.1 %collective-permute-start.7 = (bf16[256,512]{1,0:T(8,128)(2,1)S(1)}, bf16[256,512]{1,0:T(8,128)(2,1)S(1)}, u32[]{:S(2)}, u32[]{:S(2)}) collective-permute-start(bf16[256,512]{1,0:T(8,128)(2,1)S(1)} %collective-permute-done.1.refs_4_.refs_3_), channel_id=1, source_target_pairs={{0,1},{1,0},{2,3},{3,2},{4,5},{5,4},{6,7},{7,6},{8,9},{9,8},{10,11... | collective-permute-start | bytes 786440 | tf_op jit(solution)/shard_map/ppermute | solution.py:174
  34.7 7.2 %collective-permute-start.9 = (bf16[256,512]{1,0:T(8,128)(2,1)S(1)}, bf16[256,512]{1,0:T(8,128)(2,1)S(1)}, u32[]{:S(2)}, u32[]{:S(2)}) collective-permute-start(bf16[256,512]{1,0:T(8,128)(2,1)S(1)} %collective-permute-done.3.refs_5_), channel_id=1, source_target_pairs={{0,1},{1,0},{2,3},{3,2},{4,5},{5,4},{6,7},{7,6},{8,9},{9,8},{10,11... | collective-permute-start | bytes 786440 | tf_op jit(solution)/shard_map/ppermute | solution.py:174
  36.5 9.7 %collective-permute-start.8 = (bf16[256,512]{1,0:T(8,128)(2,1)S(1)}, bf16[256,512]{1,0:T(8,128)(2,1)S(1)}, u32[]{:S(2)}, u32[]{:S(2)}) collective-permute-start(bf16[256,512]{1,0:T(8,128)(2,1)S(1)} %collective-permute-done.2.refs_5_.refs_4_), channel_id=1, source_target_pairs={{0,1},{1,0},{2,3},{3,2},{4,5},{5,4},{6,7},{7,6},{8,9},{9,8},{10,11... | collective-permute-start | bytes 786440 | tf_op jit(solution)/shard_map/ppermute | solution.py:174
  38.5 7.7 %collective-permute-start.10 = (bf16[256,512]{1,0:T(8,128)(2,1)S(1)}, bf16[256,512]{1,0:T(8,128)(2,1)S(1)}, u32[]{:S(2)}, u32[]{:S(2)}) collective-permute-start(bf16[256,512]{1,0:T(8,128)(2,1)S(1)} %collective-permute-done.4.refs_6_), channel_id=1, source_target_pairs={{0,1},{1,0},{2,3},{3,2},{4,5},{5,4},{6,7},{7,6},{8,9},{9,8},{10,11... | collective-permute-start | bytes 786440 | tf_op jit(solution)/shard_map/ppermute | solution.py:174
  41.7 14.5 %collective-permute-start.11 = (bf16[256,512]{1,0:T(8,128)(2,1)S(1)}, bf16[256,512]{1,0:T(8,128)(2,1)S(1)}, u32[]{:S(2)}, u32[]{:S(2)}) collective-permute-start(bf16[256,512]{1,0:T(8,128)(2,1)S(1)} %collective-permute-done.5.refs_7_), channel_id=1, source_target_pairs={{0,1},{1,0},{2,3},{3,2},{4,5},{5,4},{6,7},{7,6},{8,9},{9,8},{10,11... | collective-permute-start | bytes 786440 | tf_op jit(solution)/shard_map/ppermute | solution.py:174
  41.8 8.5 %collective-permute-start.20 = (bf16[128,512]{1,0:T(8,128)(2,1)S(1)}, bf16[128,512]{1,0:T(8,128)(2,1)S(1)}, u32[]{:S(2)}, u32[]{:S(2)}) collective-permute-start(bf16[128,512]{1,0:T(8,128)(2,1)S(1)} %get-tuple-element.10), channel_id=1, source_target_pairs={{0,4},{4,0},{8,12},{12,8},{1,5},{5,1},{9,13},{13,9},{2,6},{6,2},{1... | collective-permute-start | bytes 393224 | tf_op jit(solution)/shard_map/ppermute | solution.py:206
  41.9 14.3 %collective-permute-start.21 = (bf16[128,512]{1,0:T(8,128)(2,1)S(1)}, bf16[128,512]{1,0:T(8,128)(2,1)S(1)}, u32[]{:S(2)}, u32[]{:S(2)}) collective-permute-start(bf16[128,512]{1,0:T(8,128)(2,1)S(1)} %get-tuple-element.11), channel_id=1, source_target_pairs={{0,8},{4,12},{8,0},{12,4},{1,9},{5,13},{9,1},{13,5},{2,10},{6,14},... | collective-permute-start | bytes 393224 | tf_op jit(solution)/shard_map/ppermute | solution.py:206
  46.3 9.9 %collective-permute-start.22 = (bf16[128,512]{1,0:T(8,128)(2,1)S(1)}, bf16[128,512]{1,0:T(8,128)(2,1)S(1)}, u32[]{:S(2)}, u32[]{:S(2)}) collective-permute-start(bf16[128,512]{1,0:T(8,128)(2,1)S(1)} %get-tuple-element.12), channel_id=1, source_target_pairs={{0,12},{4,8},{8,4},{12,0},{1,13},{5,9},{9,5},{13,1},{2,14},{6,10},... | collective-permute-start | bytes 393224 | tf_op jit(solution)/shard_map/ppermute | solution.py:206
  (3 other events, 60.3 us)

commit v3 on v2

v3 whole, which is shorter than its diff:
```python
import functools
from typing import NamedTuple

import jax
import jax.numpy as jnp
from jax import lax
from jax.experimental import pallas as pl
from jax.experimental.pallas import tpu as pltpu
from jax.sharding import PartitionSpec as P

BS = 256
VMEM_LIMIT = 48 * 1024 * 1024


class Sizes(NamedTuple):
    rows: int
    cols: int
    layers: int
    rows_here: int
    cols_here: int
    quarter: int
    per: int
    sub: int


def bits_of(size):
    return [1 << b for b in reversed(range(size.bit_length() - 1))]


def flip(size, bit):
    return [(i, i ^ bit) for i in range(size)]


def mod(a, n):
    return lax.rem(a + n, n)


def keep_block(pattern, i, j, block):
    return jnp.where(pattern[i, j] > 0, block, jnp.zeros_like(block))


def strip_rows(l, half, part, sizes):
    start = half * sizes.cols_here + l * sizes.quarter + part * sizes.sub
    return pl.multiple_of(start, sizes.sub)


def strip_block(r, l, half, sizes):
    return (r * sizes.rows_here + half * sizes.cols_here + l * sizes.quarter) // BS


def mask_row(zp, block_row, first_block, piece):
    parts = [
        keep_block(zp, block_row, first_block + t, piece[:, t * BS : (t + 1) * BS])
        for t in range(piece.shape[1] // BS)
    ]
    return jnp.concatenate(parts, axis=1)


def mask_part(zp, r, l, cc, piece, sizes):
    first_block = cc * (sizes.cols_here // BS)
    return jnp.concatenate(
        [
            mask_row(
                zp,
                strip_block(r, l, half, sizes),
                first_block,
                piece[half * sizes.sub : (half + 1) * sizes.sub, :],
            )
            for half in range(sizes.per)
        ],
        axis=0,
    )


def columns_of(cc, sizes):
    return pl.ds(pl.multiple_of(cc * sizes.cols_here, sizes.cols_here), sizes.cols_here)


def cut_kernel(sizes, z_ref, h_ref, *refs):
    outs, sems = refs[:3], refs[3]
    l = lax.axis_index("layer")
    copies = [pltpu.make_async_copy(h_ref, outs[2], sems.at[2 * sizes.per])]
    copies[0].start()
    for part in range(2):
        for half in range(sizes.per):
            copy = pltpu.make_async_copy(
                z_ref.at[pl.ds(strip_rows(l, half, part, sizes), sizes.sub), :],
                outs[part].at[pl.ds(half * sizes.sub, sizes.sub), :],
                sems.at[part * sizes.per + half],
            )
            copy.start()
            copies.append(copy)
    for copy in copies:
        copy.wait()


def pack_kernel(n, *refs):
    out, row = refs[-1], 0
    for ref in refs[:n]:
        out[row : row + ref.shape[0], :] = ref[...]
        row += ref.shape[0]


def pack(pieces, after=()):
    height = sum(p.shape[0] for p in pieces)
    return pl.pallas_call(
        functools.partial(pack_kernel, len(pieces)),
        out_shape=jax.ShapeDtypeStruct((height, pieces[0].shape[1]), pieces[0].dtype),
        in_specs=[pl.BlockSpec(memory_space=pltpu.VMEM)] * len(pieces)
        + [pl.BlockSpec(memory_space=pl.ANY)] * len(after),
        out_specs=pl.BlockSpec(memory_space=pltpu.VMEM),
        compiler_params=pltpu.CompilerParams(vmem_limit_bytes=VMEM_LIMIT),
        name="pack",
    )(*pieces, *after)


def first_kernel(sizes, h_table, n_early, *refs):
    cols, quarter, height = sizes.cols, sizes.quarter, sizes.per * sizes.sub
    hp, zp = refs[0], refs[1]
    parts = (refs[2 : 2 + n_early], refs[2 + n_early : 2 + 2 * n_early])
    h_refs = refs[2 + 2 * n_early : -3]
    hm, total, zm = refs[-3:]
    r, c, l = lax.axis_index("row"), lax.axis_index("col"), lax.axis_index("layer")
    per_rows = sizes.rows_here // BS
    for part, sign in ((0, -1), (1, 1)):
        rows = slice(part * height, (part + 1) * height)
        for s in range(n_early):
            cc = mod(c + sign * s, cols)
            zm[rows, columns_of(cc, sizes)] = mask_part(zp, r, l, cc, parts[part][s][...], sizes)
        for s in range(n_early, cols):
            cc = mod(c + sign * s, cols)
            zm[rows, columns_of(cc, sizes)] = jnp.zeros((height, sizes.cols_here), zm.dtype)
    for index, row, dr, dl in h_table:
        piece = h_refs[index]
        rr, ll = r ^ dr, l ^ dl
        block_col = (c * sizes.cols_here + ll * quarter) // BS
        for q in range(per_rows):
            j = rr * per_rows + q
            hm[
                pl.ds(pl.multiple_of(j * BS, BS), BS),
                pl.ds(pl.multiple_of(ll * quarter, quarter), quarter),
            ] = keep_block(hp, j, block_col, piece[row + q * BS : row + (q + 1) * BS, :])
    order = zm.shape[1]
    chunk = min(order, 2048)
    acc = None
    for k in range(0, order, chunk):
        part = jnp.dot(
            zm[:, k : k + chunk], hm[k : k + chunk, :], preferred_element_type=jnp.float32
        )
        acc = part if acc is None else acc + part
    total[...] = acc


def finish_kernel(sizes, zp, hm, total, right, left, out):
    cols, height = sizes.cols, sizes.per * sizes.sub
    r, c, l = lax.axis_index("row"), lax.axis_index("col"), lax.axis_index("layer")
    for part, sign, piece in ((0, -1, right), (1, 1, left)):
        cc = mod(c + sign * (cols - 1), cols)
        rows = slice(part * height, (part + 1) * height)
        added = jnp.dot(
            mask_part(zp, r, l, cc, piece[...], sizes),
            hm[columns_of(cc, sizes), :],
            preferred_element_type=jnp.float32,
        )
        out[rows, :] = (total[rows, :] + added).astype(out.dtype)


def route_kernel(sizes, row_offsets, *refs):
    n = len(row_offsets)
    pieces, table = refs[:n], refs[n]
    r = lax.axis_index("row")
    sub, height = sizes.sub, sizes.per * sizes.sub
    for dr, piece in zip(row_offsets, pieces):
        for half in range(sizes.per):
            for part in range(2):
                first = part * height + half * sub
                table[(r ^ dr) * sizes.per + half, part * sub : (part + 1) * sub, :] = piece[
                    first : first + sub, :
                ]


def place_rows(out, ll, rows, first, sizes):
    for part in range(2):
        for half in range(sizes.per):
            out[pl.ds(strip_rows(ll, half, part, sizes), sizes.sub), :] = rows[
                first : first + sizes.sub, :
            ].astype(out.dtype)
            first += sizes.sub


def second_kernel(sizes, z_table, offsets, ready, *refs):
    cols, sub, height = sizes.cols, sizes.sub, sizes.per * sizes.sub
    zp, z_tile, xm = refs[:3]
    out = refs[-1]
    held = refs[4:-1] if ready else refs[3:-1]
    r, c, l = lax.axis_index("row"), lax.axis_index("col"), lax.axis_index("layer")
    for n, dl in enumerate(ready):
        place_rows(out, l ^ dl, refs[3], n * 2 * height, sizes)
    for n, dl in enumerate(offsets):
        ll = l ^ dl
        total = None
        for s in range(cols):
            cc = mod(c - s, cols)
            parts = []
            for part in range(2):
                if s == 0:
                    piece = jnp.concatenate(
                        [
                            z_tile[pl.ds(strip_rows(ll, half, part, sizes), sub), :]
                            for half in range(sizes.per)
                        ],
                        axis=0,
                    )
                else:
                    index, row = z_table[dl, s if part == 0 else cols - s, part]
                    piece = held[index][row : row + height, :]
                parts.append(mask_part(zp, r, ll, cc, piece, sizes))
            part = lax.dot_general(
                jnp.concatenate(parts, axis=0),
                xm[cc],
                (((1,), (1,)), ((), ())),
                preferred_element_type=jnp.float32,
            )
            total = part if total is None else total + part
        if ready:
            place_rows(out, ll, total, 0, sizes)
        else:
            out[n * 2 * height : (n + 1) * 2 * height, :] = total.astype(out.dtype)


def local(sizes, hamiltonian, inv_root, h_pattern, z_pattern):
    rows, cols, layers = sizes.rows, sizes.cols, sizes.layers
    quarter, cols_here = sizes.quarter, sizes.cols_here
    order = rows * sizes.rows_here
    height = sizes.per * sizes.sub
    smem = pl.BlockSpec(memory_space=pltpu.SMEM)
    vmem = pl.BlockSpec(memory_space=pltpu.VMEM)
    params = pltpu.CompilerParams(vmem_limit_bytes=VMEM_LIMIT)
    row_bits, layer_bits = bits_of(rows), bits_of(layers)

    own = pl.pallas_call(
        functools.partial(cut_kernel, sizes),
        out_shape=[jax.ShapeDtypeStruct((height, cols_here), jnp.bfloat16)] * 2
        + [jax.ShapeDtypeStruct(hamiltonian.shape, jnp.bfloat16)],
        in_specs=[pl.BlockSpec(memory_space=pl.ANY)] * 2,
        out_specs=[vmem] * 3,
        scratch_shapes=[pltpu.SemaphoreType.DMA((2 * sizes.per + 1,))],
        compiler_params=params,
        name="cut",
    )(inv_root, hamiltonian)
    rings = [[(i, (i + step) % cols) for i in range(cols)] for step in (1, -1)]
    slots = [[own[0]], [own[1]]]
    for _ in range(1, cols):
        for part in range(2):
            slots[part].append(lax.ppermute(slots[part][-1], "col", rings[part]))

    top, rest = layer_bits[0], layer_bits[1:]
    h_arrays, h_table = [own[2]], [(0, 0, 0, 0)]
    steps = [("row", b) for b in row_bits] + [("layer", top)]
    for axis, bit in steps:
        for index, _, dr, dl in list(h_table):
            there = (dr ^ bit, dl) if axis == "row" else (dr, dl ^ bit)
            size = rows if axis == "row" else layers
            h_table.append((len(h_arrays), 0) + there)
            source = h_arrays[index]
            if index:
                source = pack([source], [slots[0][1], slots[1][1]])
            h_arrays.append(lax.ppermute(source, axis, flip(size, bit)))
    for bit in rest:
        packed = pack(h_arrays, [slots[0][-2], slots[1][-2]])
        place, starts = 0, []
        for array in h_arrays:
            starts.append(place)
            place += array.shape[0]
        h_table += [
            (len(h_arrays), starts[index] + row, dr, dl ^ bit) for index, row, dr, dl in h_table
        ]
        h_arrays = h_arrays + [lax.ppermute(packed, "layer", flip(layers, bit))]

    n_early = cols - 1
    hm, total = pl.pallas_call(
        functools.partial(first_kernel, sizes, h_table, n_early),
        out_shape=[
            jax.ShapeDtypeStruct((order, cols_here), jnp.bfloat16),
            jax.ShapeDtypeStruct((2 * height, cols_here), jnp.float32),
        ],
        in_specs=[smem, smem] + [vmem] * (2 * n_early + len(h_arrays)),
        out_specs=[vmem, vmem],
        scratch_shapes=[pltpu.VMEM((2 * height, order), jnp.bfloat16)],
        compiler_params=params,
        cost_estimate=pl.CostEstimate(
            flops=0, bytes_accessed=order * cols_here, transcendentals=0
        ),
        name="first_product",
    )(h_pattern, z_pattern, *slots[0][:n_early], *slots[1][:n_early], *h_arrays)
    product = pl.pallas_call(
        functools.partial(finish_kernel, sizes),
        out_shape=jax.ShapeDtypeStruct((2 * height, cols_here), jnp.bfloat16),
        in_specs=[smem] + [vmem] * 4,
        out_specs=vmem,
        compiler_params=params,
        name="finish_product",
    )(z_pattern, hm, total, slots[0][-1], slots[1][-1])

    gathered = {0: product}
    for bit in row_bits:
        for dr, piece in list(gathered.items()):
            gathered[dr ^ bit] = lax.ppermute(piece, "row", flip(rows, bit))
    row_offsets = list(gathered)
    outgoing = pl.pallas_call(
        functools.partial(route_kernel, sizes, row_offsets),
        out_shape=jax.ShapeDtypeStruct((cols, quarter, cols_here), jnp.bfloat16),
        in_specs=[vmem] * rows,
        out_specs=vmem,
        compiler_params=params,
        name="route",
    )(*[gathered[o] for o in row_offsets])
    messages = lax.all_to_all(outgoing, "col", 0, 0, tiled=True)

    held, z_table = [], {}
    for group, gates in (
        (range(1, cols - 1), [[h_arrays[-1]], [outgoing]]),
        (range(cols - 1, cols), [[product], [messages]]),
    ):
        mine = pack([slots[part][s] for s in group for part in range(2)], gates[0])
        arrays, table = [mine], []
        for n, s in enumerate(group):
            for part in range(2):
                table.append((0, (2 * n + part) * height, 0, s, part))
        for step, bit in enumerate(layer_bits):
            packed = pack(arrays, gates[1]) if step else mine
            place, starts = 0, []
            for array in arrays:
                starts.append(place)
                place += array.shape[0]
            table += [
                (len(arrays), starts[index] + row, dl ^ bit, s, part)
                for index, row, dl, s, part in table
            ]
            arrays = arrays + [lax.ppermute(packed, "layer", flip(layers, bit))]
        for index, row, dl, s, part in table:
            z_table[dl, s, part] = (len(held) + index, row)
        held += arrays

    early = [dl for dl in range(layers) if not dl & layer_bits[-1]]
    late = [dl for dl in range(layers) if dl & layer_bits[-1]]
    result = None
    for offsets in (early, late):
        chosen = sorted({z_table[key][0] for key in z_table if key[0] in offsets})
        table = {
            key: (chosen.index(index), row)
            for key, (index, row) in z_table.items()
            if key[0] in offsets
        }
        shape = (len(early) * 2 * height, quarter) if result is None else hamiltonian.shape
        before = [] if result is None else [result]
        result = pl.pallas_call(
            functools.partial(
                second_kernel, sizes, table, offsets, [] if result is None else early
            ),
            out_shape=jax.ShapeDtypeStruct(shape, jnp.bfloat16),
            in_specs=[smem] + [vmem] * (2 + len(before) + len(chosen)),
            out_specs=vmem,
            compiler_params=params,
            name="second_product",
        )(z_pattern, inv_root, messages, *before, *[held[n] for n in chosen])
    return result


def solution(mesh):
    rows, cols, layers = (mesh.shape[a] for a in ("row", "col", "layer"))

    def whole(hamiltonian, inv_root, h_pattern, z_pattern):
        order = hamiltonian.shape[0]
        cols_here = order // cols
        quarter = cols_here // layers
        sizes = Sizes(
            rows, cols, layers, order // rows, cols_here, quarter, cols // rows, quarter // 2
        )
        return jax.shard_map(
            functools.partial(local, sizes),
            mesh=mesh,
            in_specs=(P("row", ("col", "layer")), P("row", "col"), P(), P()),
            out_specs=P("row", ("col", "layer")),
            check_vma=False,
        )(hamiltonian, inv_root, h_pattern, z_pattern)

    return whole
```

time: 59 us -> 65.4 us (1.11)
  starting transfers between devices: 17.9 us -> 24 us
  waiting for transfers between devices: 35.1 us -> 29.5 us
  Pallas kernels: 4.73 us -> 9.34 us
  local copies, waits for them, and re-layouts: 1.03 us -> 2.18 us
    ppermute x22 -> x14, waiting for transfers between devices: 33.1 us -> 20.8 us  [the longest x6 11.3 us: local(): slots[part].append(lax.ppermute(slots[part][-1], 'col', rings[part]))]
    all_to_all x0 -> x1, starting transfers between devices: none -> 4.27 us  [local(): messages = lax.all_to_all(outgoing, 'col', 0, 0, tiled=True)]
    ppermute x1, waiting for transfers between devices: 1.99 us -> 6.03 us  [local(): gathered[dr ^ bit] = lax.ppermute(piece, 'row', flip(rows, bit))]
    pallas_call x2 -> x11, Pallas kernels: 4.64 us -> 8.51 us  [the longest x2 3.97 us: local(): pl.pallas_call(functools.partial(second_kernel, sizes, table, offsets, []...]
    all_to_all x0 -> x1, waiting for transfers between devices: none -> 2.66 us  [local(): messages = lax.all_to_all(outgoing, 'col', 0, 0, tiled=True)]
    ppermute x22 -> x14, starting transfers between devices: 16.8 us -> 19.1 us  [the longest x6 11.5 us: local(): slots[part].append(lax.ppermute(slots[part][-1], 'col', rings[part]))]
    unnamed x8 -> x10, local copies, waits for them, and re-layouts: 0.02 us -> 2.18 us
    dynamic_slice x1 -> x0, local copies, waits for them, and re-layouts: 1.01 us -> none  [local(): lax.dynamic_index_in_dim(striped, l, 1, keepdims=False)]
  transfers between devices with their start and end apart: 23 -> 16, of which waited for: 8 -> 11; matrix products, arithmetic and copies ran while one was open for 0% -> 0% of each run, Pallas kernels for 3% -> 8%
where the time goes in v3:
time: 65.4 us; the launch traced here: 65.2 us
  waiting for transfers between devices  29.5 us (45%)
  starting transfers between devices  24 us (37%)
  Pallas kernels  9.34 us (14%)
  local copies, waits for them, and re-layouts  2.18 us (3%)
    ppermute x6, starting transfers between devices, local(): slots[part].append(lax.ppermute(slots[part][-1], 'col', rings[part]))  11.5 us
    ppermute x6, waiting for transfers between devices, local(): slots[part].append(lax.ppermute(slots[part][-1], 'col', rings[part]))  11.3 us
    ppermute x4, waiting for transfers between devices, local(): arrays = arrays + [lax.ppermute(packed, 'layer', flip(layers, bit))]  9.56 us
    ppermute x3, starting transfers between devices, local(): h_arrays.append(lax.ppermute(source, axis, flip(size, bit)))  6.11 us
    ppermute x1, waiting for transfers between devices, local(): gathered[dr ^ bit] = lax.ppermute(piece, 'row', flip(rows, bit))  6.03 us
    all_to_all x1, starting transfers between devices, local(): messages = lax.all_to_all(outgoing, 'col', 0, 0, tiled=True)  4.27 us
    pallas_call x2, Pallas kernels, local(): pl.pallas_call(functools.partial(second_kernel, sizes, table, offsets, []...  3.97 us
    all_to_all x1, waiting for transfers between devices, local(): messages = lax.all_to_all(outgoing, 'col', 0, 0, tiled=True)  2.66 us
  transfers between devices with their start and end apart: 16, of which 11 were waited for; matrix products, arithmetic and copies ran while one was open for 0% of the time, Pallas kernels for 8%

profile of v3, /device:TPU:0, one launch (start us, length us, event | category | flops | bytes accessed | tf_op | source)
XLA Modules:
  0.0 65.2 jit_solution(4758658378640406930)
XLA Ops:
  0.0 1.2 %copy-done = bf16[1024,512]{1,0:T(8,128)(2,1)S(1)} copy-done((bf16[1024,512]{1,0:T(8,128)(2,1)S(1)}, bf16[1024,512]{1,0:T(8,128)(2,1)}, u32[]{:S(2)}) %copy-start) | copy-done | bytes 1048600
  1.2 0.9 %copy-done.2 = bf16[1024,128]{1,0:T(8,128)(2,1)S(1)} copy-done((bf16[1024,128]{1,0:T(8,128)(2,1)S(1)}, bf16[1024,128]{1,0:T(8,128)(2,1)}, u32[]{:S(2)}) %copy-start.2) | copy-done | bytes 262168
  2.6 3.0 %collective-permute-start.4 = (bf16[1024,128]{1,0:T(8,128)(2,1)S(1)}, bf16[1024,128]{1,0:T(8,128)(2,1)S(1)}, u32[]{:S(2)}, u32[]{:S(2)}) collective-permute-start(bf16[1024,128]{1,0:T(8,128)(2,1)S(1)} %get-tuple-element.12.refs_0_.refs_8_), channel_id=1, source_target_pairs={{0,16},{16,0},{1,17},{17,1},{2,18},{18,2},{3,19},{19,3},{4,20},{20... | collective-permute-start | bytes 786440 | tf_op jit(solution)/shard_map/ppermute | solution.py:268
  5.6 1.6 %collective-permute-start = (bf16[128,512]{1,0:T(8,128)(2,1)S(1)}, bf16[128,512]{1,0:T(8,128)(2,1)S(1)}, u32[]{:S(2)}, u32[]{:S(2)}) collective-permute-start(bf16[128,512]{1,0:T(8,128)(2,1)S(1)} %get-tuple-element.10.refs_2_), channel_id=1, source_target_pairs={{0,4},{4,8},{8,12},{12,0},{1,5},{5,9},{9,13},{13,1},{2,6},{6,10},{... | collective-permute-start | bytes 393224 | tf_op jit(solution)/shard_map/ppermute | solution.py:255
  7.2 2.2 %collective-permute-start.2 = (bf16[128,512]{1,0:T(8,128)(2,1)S(1)}, bf16[128,512]{1,0:T(8,128)(2,1)S(1)}, u32[]{:S(2)}, u32[]{:S(2)}) collective-permute-start(bf16[128,512]{1,0:T(8,128)(2,1)S(1)} %get-tuple-element.11.refs_5_), channel_id=1, source_target_pairs={{0,12},{4,0},{8,4},{12,8},{1,13},{5,1},{9,5},{13,9},{2,14},{6,2},{... | collective-permute-start | bytes 393224 | tf_op jit(solution)/shard_map/ppermute | solution.py:255
  9.4 1.5 %collective-permute-start.5 = (bf16[1024,128]{1,0:T(8,128)(2,1)S(1)}, bf16[1024,128]{1,0:T(8,128)(2,1)S(1)}, u32[]{:S(2)}, u32[]{:S(2)}) collective-permute-start(bf16[1024,128]{1,0:T(8,128)(2,1)S(1)} %get-tuple-element.12.refs_0_.refs_8_), channel_id=1, source_target_pairs={{0,2},{1,3},{2,0},{3,1},{4,6},{5,7},{6,4},{7,5},{8,10},{9,11},{10,... | collective-permute-start | bytes 786440 | tf_op jit(solution)/shard_map/ppermute | solution.py:268
  10.9 2.8 %collective-permute-done.refs_1_.refs_3_.refs_0_ = bf16[128,512]{1,0:T(8,128)(2,1)S(1)} collective-permute-done((bf16[128,512]{1,0:T(8,128)(2,1)S(1)}, bf16[128,512]{1,0:T(8,128)(2,1)S(1)}, u32[]{:S(2)}, u32[]{:S(2)}) %collective-permute-start) | collective-permute-done | bytes 131104 | tf_op jit(solution)/shard_map/ppermute | solution.py:255
  13.8 0.9 %collective-permute-done.2.refs_2_.refs_6_.refs_1_ = bf16[128,512]{1,0:T(8,128)(2,1)S(1)} collective-permute-done((bf16[128,512]{1,0:T(8,128)(2,1)S(1)}, bf16[128,512]{1,0:T(8,128)(2,1)S(1)}, u32[]{:S(2)}, u32[]{:S(2)}) %collective-permute-start.2) | collective-permute-done | bytes 131104 | tf_op jit(solution)/shard_map/ppermute | solution.py:255
  14.7 1.6 %collective-permute-start.6 = (bf16[1024,128]{1,0:T(8,128)(2,1)S(1)}, bf16[1024,128]{1,0:T(8,128)(2,1)S(1)}, u32[]{:S(2)}, u32[]{:S(2)}) collective-permute-start(bf16[1024,128]{1,0:T(8,128)(2,1)S(1)} %pack.6), channel_id=1, source_target_pairs={{0,2},{1,3},{2,0},{3,1},{4,6},{5,7},{6,4},{7,5},{8,10},{9,11},{10,... | collective-permute-start | bytes 786440 | tf_op jit(solution)/shard_map/ppermute | solution.py:268
  16.3 1.1 %collective-permute-start.1 = (bf16[128,512]{1,0:T(8,128)(2,1)S(1)}, bf16[128,512]{1,0:T(8,128)(2,1)S(1)}, u32[]{:S(2)}, u32[]{:S(2)}) collective-permute-start(bf16[128,512]{1,0:T(8,128)(2,1)S(1)} %collective-permute-done.refs_1_.refs_3_.refs_0_), channel_id=1, source_target_pairs={{0,4},{4,8},{8,12},{12,0},{1,5},{5,9},{9,13},{13,1},{2,6},{6,10},{... | collective-permute-start | bytes 393224 | tf_op jit(solution)/shard_map/ppermute | solution.py:255
  17.4 2.7 %collective-permute-start.3 = (bf16[128,512]{1,0:T(8,128)(2,1)S(1)}, bf16[128,512]{1,0:T(8,128)(2,1)S(1)}, u32[]{:S(2)}, u32[]{:S(2)}) collective-permute-start(bf16[128,512]{1,0:T(8,128)(2,1)S(1)} %collective-permute-done.2.refs_2_.refs_6_.refs_1_), channel_id=1, source_target_pairs={{0,12},{4,0},{8,4},{12,8},{1,13},{5,1},{9,5},{13,9},{2,14},{6,2},{... | collective-permute-start | bytes 393224 | tf_op jit(solution)/shard_map/ppermute | solution.py:255
  20.1 4.0 %collective-permute-done.1.refs_4_.refs_2_ = bf16[128,512]{1,0:T(8,128)(2,1)S(1)} collective-permute-done((bf16[128,512]{1,0:T(8,128)(2,1)S(1)}, bf16[128,512]{1,0:T(8,128)(2,1)S(1)}, u32[]{:S(2)}, u32[]{:S(2)}) %collective-permute-start.1) | collective-permute-done | bytes 131104 | tf_op jit(solution)/shard_map/ppermute | solution.py:255
  25.3 3.5 %collective-permute-start.9 = (bf16[128,512]{1,0:T(8,128)(2,1)S(1)}, bf16[128,512]{1,0:T(8,128)(2,1)S(1)}, u32[]{:S(2)}, u32[]{:S(2)}) collective-permute-start(bf16[128,512]{1,0:T(8,128)(2,1)S(1)} %collective-permute-done.3.refs_5_.refs_7_.refs_3_), channel_id=1, source_target_pairs={{0,12},{4,0},{8,4},{12,8},{1,13},{5,1},{9,5},{13,9},{2,14},{6,2},{... | collective-permute-start | bytes 393224 | tf_op jit(solution)/shard_map/ppermute | solution.py:255
  28.9 2.0 %first_product.1 = (bf16[2048,512]{1,0:T(8,128)(2,1)S(1)}, f32[256,512]{1,0:T(8,128)S(1)}) custom-call(s32[8,8]{1,0:T(8,128)S(1)} %copy-done.4, s32[8,8]{1,0:T(8,128)S(1)} %copy-done.3, bf16[128,512]{1,0:T(8,128)(2,1)S(1)} %get-tuple-element.10.refs_2_, bf16[128,512]{1,0:T(8,128)(2,1)S(1)} %collective-permute-done.refs_1_.refs_3_.refs_0_, ...), custom_call_target="tpu_custom_call" | custom-call | bytes 1048576 | tf_op jit(solution)/shard_map/first_product/pallas_call | solution.py:281
  30.9 2.3 %collective-permute-done.8.right.refs_0_ = bf16[128,512]{1,0:T(8,128)(2,1)S(1)} collective-permute-done((bf16[128,512]{1,0:T(8,128)(2,1)S(1)}, bf16[128,512]{1,0:T(8,128)(2,1)S(1)}, u32[]{:S(2)}, u32[]{:S(2)}) %collective-permute-start.8) | collective-permute-done | bytes 131104 | tf_op jit(solution)/shard_map/ppermute | solution.py:255
  33.7 0.9 %finish_product.1.refs_0_.refs_2_ = bf16[256,512]{1,0:T(8,128)(2,1)S(1)} custom-call(s32[8,8]{1,0:T(8,128)S(1)} %copy-done.3, bf16[2048,512]{1,0:T(8,128)(2,1)S(1)} %get-tuple-element.13.hm, f32[256,512]{1,0:T(8,128)S(1)} %get-tuple-element.14.total, bf16[128,512]{1,0:T(8,128)(2,1)S(1)} %collective-permute-done.8.right.refs_0_, ...), custom_call_target="tpu_custom_call" | custom-call | tf_op jit(solution)/shard_map/finish_product/pallas_call | solution.py:296
  35.9 6.0 %collective-permute-done.10.refs_1_ = bf16[256,512]{1,0:T(8,128)(2,1)S(1)} collective-permute-done((bf16[256,512]{1,0:T(8,128)(2,1)S(1)}, bf16[256,512]{1,0:T(8,128)(2,1)S(1)}, u32[]{:S(2)}, u32[]{:S(2)}) %collective-permute-start.10) | collective-permute-done | bytes 262176 | tf_op jit(solution)/shard_map/ppermute | solution.py:308
  42.8 4.3 %all-to-all-start = ((bf16[4,128,512]{2,1,0:T(8,128)(2,1)}), bf16[4,128,512]{2,1,0:T(8,128)(2,1)S(1)}, u32[]{:S(2)}, u32[]{:S(2)}) async-start(bf16[4,128,512]{2,1,0:T(8,128)(2,1)} %route.1.refs_2_), calls=%async_computation | async-start | bytes 1048576 | tf_op jit(solution)/shard_map/all_to_all | solution.py:318
  47.1 0.9 %collective-permute-done.11.refs_4_.refs_1_ = bf16[512,512]{1,0:T(8,128)(2,1)S(1)} collective-permute-done((bf16[512,512]{1,0:T(8,128)(2,1)S(1)}, bf16[512,512]{1,0:T(8,128)(2,1)S(1)}, u32[]{:S(2)}, u32[]{:S(2)}) %collective-permute-start.11) | collective-permute-done | bytes 524320 | tf_op jit(solution)/shard_map/ppermute | solution.py:340
  47.9 1.1 %pack.10 = bf16[1024,512]{1,0:T(8,128)(2,1)} custom-call(bf16[512,512]{1,0:T(8,128)(2,1)S(1)} %pack.8.refs_3_.refs_0_, bf16[512,512]{1,0:T(8,128)(2,1)S(1)} %collective-permute-done.11.refs_4_.refs_1_, bf16[4,128,512]{2,1,0:T(8,128)(2,1)} %route.1.refs_2_), custom_call_target="tpu_custom_call" | custom-call | tf_op jit(solution)/shard_map/pack/pallas_call | solution.py:106
  49.7 8.1 %collective-permute-done.12.refs_6_.refs_1_ = bf16[256,512]{1,0:T(8,128)(2,1)S(1)} collective-permute-done((bf16[256,512]{1,0:T(8,128)(2,1)S(1)}, bf16[256,512]{1,0:T(8,128)(2,1)S(1)}, u32[]{:S(2)}, u32[]{:S(2)}) %collective-permute-start.12) | collective-permute-done | bytes 262176 | tf_op jit(solution)/shard_map/ppermute | solution.py:340
  57.8 2.7 %all-to-all-done.refs_2_ = bf16[4,128,512]{2,1,0:T(8,128)(2,1)S(1)} async-done(((bf16[4,128,512]{2,1,0:T(8,128)(2,1)}), bf16[4,128,512]{2,1,0:T(8,128)(2,1)S(1)}, u32[]{:S(2)}, u32[]{:S(2)}) %all-to-all-start) | async-done | bytes 524320 | tf_op jit(solution)/shard_map/all_to_all | solution.py:318
  60.6 1.3 %second_product.2.refs_3_ = bf16[512,128]{1,0:T(8,128)(2,1)S(1)} custom-call(s32[8,8]{1,0:T(8,128)S(1)} %copy-done.3, bf16[1024,512]{1,0:T(8,128)(2,1)S(1)} %copy-done.1, bf16[4,128,512]{2,1,0:T(8,128)(2,1)S(1)} %all-to-all-done.refs_2_, bf16[512,512]{1,0:T(8,128)(2,1)S(1)} %pack.8.refs_3_.refs_0_, ...), custom_call_target="tpu_custom_call" | custom-call | tf_op jit(solution)/shard_map/second_product/pallas_call | solution.py:357
  62.5 2.7 %second_product.3 = bf16[1024,128]{1,0:T(8,128)(2,1)} custom-call(s32[8,8]{1,0:T(8,128)S(1)} %copy-done.3, bf16[1024,512]{1,0:T(8,128)(2,1)S(1)} %copy-done.1, bf16[4,128,512]{2,1,0:T(8,128)(2,1)S(1)} %all-to-all-done.refs_2_, bf16[512,128]{1,0:T(8,128)(2,1)S(1)} %second_product.2.refs_3_, bf16[1024,512]{1,0:T(8,128)(2,1)} %collective-permute-done.13.refs_4_, ...), custom_call_target="tpu_custom_call" | custom-call | tf_op jit(solution)/shard_map/second_product/pallas_call | solution.py:357
  (30 shorter events, 5.7 us)
Async XLA Ops:
  0.0 1.2 %copy-start = (bf16[1024,512]{1,0:T(8,128)(2,1)S(1)}, bf16[1024,512]{1,0:T(8,128)(2,1)}, u32[]{:S(2)}) copy-start(bf16[1024,512]{1,0:T(8,128)(2,1)} %refs_1_.5) | copy-start | bytes 3145732
  1.2 0.9 %copy-start.2 = (bf16[1024,128]{1,0:T(8,128)(2,1)S(1)}, bf16[1024,128]{1,0:T(8,128)(2,1)}, u32[]{:S(2)}) copy-start(bf16[1024,128]{1,0:T(8,128)(2,1)} %h_ref.1) | copy-start | bytes 786436
  2.2 26.7 %copy-start.3 = (s32[8,8]{1,0:T(8,128)S(1)}, s32[8,8]{1,0:T(8,128)}, u32[]{:S(2)}) copy-start(s32[8,8]{1,0:T(8,128)} %refs_0_.5) | copy-start | bytes 772
  2.2 26.7 %copy-start.4 = (s32[8,8]{1,0:T(8,128)S(1)}, s32[8,8]{1,0:T(8,128)}, u32[]{:S(2)}) copy-start(s32[8,8]{1,0:T(8,128)} %refs_0_.3) | copy-start | bytes 772
  2.6 12.1 %collective-permute-start.4 = (bf16[1024,128]{1,0:T(8,128)(2,1)S(1)}, bf16[1024,128]{1,0:T(8,128)(2,1)S(1)}, u32[]{:S(2)}, u32[]{:S(2)}) collective-permute-start(bf16[1024,128]{1,0:T(8,128)(2,1)S(1)} %get-tuple-element.12.refs_0_.refs_8_), channel_id=1, source_target_pairs={{0,16},{16,0},{1,17},{17,1},{2,18},{18,2},{3,19},{19,3},{4,20},{20... | collective-permute-start | bytes 786440 | tf_op jit(solution)/shard_map/ppermute | solution.py:268
  5.6 8.2 %collective-permute-start = (bf16[128,512]{1,0:T(8,128)(2,1)S(1)}, bf16[128,512]{1,0:T(8,128)(2,1)S(1)}, u32[]{:S(2)}, u32[]{:S(2)}) collective-permute-start(bf16[128,512]{1,0:T(8,128)(2,1)S(1)} %get-tuple-element.10.refs_2_), channel_id=1, source_target_pairs={{0,4},{4,8},{8,12},{12,0},{1,5},{5,9},{9,13},{13,1},{2,6},{6,10},{... | collective-permute-start | bytes 393224 | tf_op jit(solution)/shard_map/ppermute | solution.py:255
  7.2 7.5 %collective-permute-start.2 = (bf16[128,512]{1,0:T(8,128)(2,1)S(1)}, bf16[128,512]{1,0:T(8,128)(2,1)S(1)}, u32[]{:S(2)}, u32[]{:S(2)}) collective-permute-start(bf16[128,512]{1,0:T(8,128)(2,1)S(1)} %get-tuple-element.11.refs_5_), channel_id=1, source_target_pairs={{0,12},{4,0},{8,4},{12,8},{1,13},{5,1},{9,5},{13,9},{2,14},{6,2},{... | collective-permute-start | bytes 393224 | tf_op jit(solution)/shard_map/ppermute | solution.py:255
  9.4 15.4 %collective-permute-start.5 = (bf16[1024,128]{1,0:T(8,128)(2,1)S(1)}, bf16[1024,128]{1,0:T(8,128)(2,1)S(1)}, u32[]{:S(2)}, u32[]{:S(2)}) collective-permute-start(bf16[1024,128]{1,0:T(8,128)(2,1)S(1)} %get-tuple-element.12.refs_0_.refs_8_), channel_id=1, source_target_pairs={{0,2},{1,3},{2,0},{3,1},{4,6},{5,7},{6,4},{7,5},{8,10},{9,11},{10,... | collective-permute-start | bytes 786440 | tf_op jit(solution)/shard_map/ppermute | solution.py:268
  14.7 10.1 %collective-permute-start.6 = (bf16[1024,128]{1,0:T(8,128)(2,1)S(1)}, bf16[1024,128]{1,0:T(8,128)(2,1)S(1)}, u32[]{:S(2)}, u32[]{:S(2)}) collective-permute-start(bf16[1024,128]{1,0:T(8,128)(2,1)S(1)} %pack.6), channel_id=1, source_target_pairs={{0,2},{1,3},{2,0},{3,1},{4,6},{5,7},{6,4},{7,5},{8,10},{9,11},{10,... | collective-permute-start | bytes 786440 | tf_op jit(solution)/shard_map/ppermute | solution.py:268
  16.3 7.8 %collective-permute-start.1 = (bf16[128,512]{1,0:T(8,128)(2,1)S(1)}, bf16[128,512]{1,0:T(8,128)(2,1)S(1)}, u32[]{:S(2)}, u32[]{:S(2)}) collective-permute-start(bf16[128,512]{1,0:T(8,128)(2,1)S(1)} %collective-permute-done.refs_1_.refs_3_.refs_0_), channel_id=1, source_target_pairs={{0,4},{4,8},{8,12},{12,0},{1,5},{5,9},{9,13},{13,1},{2,6},{6,10},{... | collective-permute-start | bytes 393224 | tf_op jit(solution)/shard_map/ppermute | solution.py:255
  17.4 7.4 %collective-permute-start.3 = (bf16[128,512]{1,0:T(8,128)(2,1)S(1)}, bf16[128,512]{1,0:T(8,128)(2,1)S(1)}, u32[]{:S(2)}, u32[]{:S(2)}) collective-permute-start(bf16[128,512]{1,0:T(8,128)(2,1)S(1)} %collective-permute-done.2.refs_2_.refs_6_.refs_1_), channel_id=1, source_target_pairs={{0,12},{4,0},{8,4},{12,8},{1,13},{5,1},{9,5},{13,9},{2,14},{6,2},{... | collective-permute-start | bytes 393224 | tf_op jit(solution)/shard_map/ppermute | solution.py:255
  24.9 4.0 %collective-permute-start.7 = (bf16[4096,128]{1,0:T(8,128)(2,1)S(1)}, bf16[4096,128]{1,0:T(8,128)(2,1)S(1)}, u32[]{:S(2)}, u32[]{:S(2)}) collective-permute-start(bf16[4096,128]{1,0:T(8,128)(2,1)S(1)} %pack.7), channel_id=1, source_target_pairs={{0,1},{1,0},{2,3},{3,2},{4,5},{5,4},{6,7},{7,6},{8,9},{9,8},{10,11... | collective-permute-start | bytes 3145736 | tf_op jit(solution)/shard_map/ppermute | solution.py:278
  25.0 8.2 %collective-permute-start.8 = (bf16[128,512]{1,0:T(8,128)(2,1)S(1)}, bf16[128,512]{1,0:T(8,128)(2,1)S(1)}, u32[]{:S(2)}, u32[]{:S(2)}) collective-permute-start(bf16[128,512]{1,0:T(8,128)(2,1)S(1)} %collective-permute-done.1.refs_4_.refs_2_), channel_id=1, source_target_pairs={{0,4},{4,8},{8,12},{12,0},{1,5},{5,9},{9,13},{13,1},{2,6},{6,10},{... | collective-permute-start | bytes 393224 | tf_op jit(solution)/shard_map/ppermute | solution.py:255
  25.3 8.4 %collective-permute-start.9 = (bf16[128,512]{1,0:T(8,128)(2,1)S(1)}, bf16[128,512]{1,0:T(8,128)(2,1)S(1)}, u32[]{:S(2)}, u32[]{:S(2)}) collective-permute-start(bf16[128,512]{1,0:T(8,128)(2,1)S(1)} %collective-permute-done.3.refs_5_.refs_7_.refs_3_), channel_id=1, source_target_pairs={{0,12},{4,0},{8,4},{12,8},{1,13},{5,1},{9,5},{13,9},{2,14},{6,2},{... | collective-permute-start | bytes 393224 | tf_op jit(solution)/shard_map/ppermute | solution.py:255
  34.6 7.3 %collective-permute-start.10 = (bf16[256,512]{1,0:T(8,128)(2,1)S(1)}, bf16[256,512]{1,0:T(8,128)(2,1)S(1)}, u32[]{:S(2)}, u32[]{:S(2)}) collective-permute-start(bf16[256,512]{1,0:T(8,128)(2,1)S(1)} %finish_product.1.refs_0_.refs_2_), channel_id=1, source_target_pairs={{0,16},{16,0},{1,17},{17,1},{2,18},{18,2},{3,19},{19,3},{4,20},{20... | collective-permute-start | bytes 786440 | tf_op jit(solution)/shard_map/ppermute | solution.py:308
  35.3 12.7 %collective-permute-start.11 = (bf16[512,512]{1,0:T(8,128)(2,1)S(1)}, bf16[512,512]{1,0:T(8,128)(2,1)S(1)}, u32[]{:S(2)}, u32[]{:S(2)}) collective-permute-start(bf16[512,512]{1,0:T(8,128)(2,1)S(1)} %pack.8.refs_3_.refs_0_), channel_id=1, source_target_pairs={{0,2},{1,3},{2,0},{3,1},{4,6},{5,7},{6,4},{7,5},{8,10},{9,11},{10,... | collective-permute-start | bytes 1572872 | tf_op jit(solution)/shard_map/ppermute | solution.py:340
  42.8 17.7 %all-to-all-start = ((bf16[4,128,512]{2,1,0:T(8,128)(2,1)}), bf16[4,128,512]{2,1,0:T(8,128)(2,1)S(1)}, u32[]{:S(2)}, u32[]{:S(2)}) async-start(bf16[4,128,512]{2,1,0:T(8,128)(2,1)} %route.1.refs_2_), calls=%async_computation | async-start | bytes 1048576 | tf_op jit(solution)/shard_map/all_to_all | solution.py:318
  47.1 13.5 %copy-start.1 = (bf16[1024,512]{1,0:T(8,128)(2,1)S(1)}, bf16[1024,512]{1,0:T(8,128)(2,1)}, u32[]{:S(2)}) copy-start(bf16[1024,512]{1,0:T(8,128)(2,1)} %refs_1_.5) | copy-start | bytes 3145732
  49.0 13.5 %collective-permute-start.13 = (bf16[1024,512]{1,0:T(8,128)(2,1)}, bf16[1024,512]{1,0:T(8,128)(2,1)}, u32[]{:S(2)}, u32[]{:S(2)}) collective-permute-start(bf16[1024,512]{1,0:T(8,128)(2,1)} %pack.10), channel_id=1, source_target_pairs={{0,1},{1,0},{2,3},{3,2},{4,5},{5,4},{6,7},{7,6},{8,9},{9,8},{10,11... | collective-permute-start | bytes 3145736 | tf_op jit(solution)/shard_map/ppermute | solution.py:340
  49.0 8.8 %collective-permute-start.12 = (bf16[256,512]{1,0:T(8,128)(2,1)S(1)}, bf16[256,512]{1,0:T(8,128)(2,1)S(1)}, u32[]{:S(2)}, u32[]{:S(2)}) collective-permute-start(bf16[256,512]{1,0:T(8,128)(2,1)S(1)} %pack.9.refs_5_.refs_0_), channel_id=1, source_target_pairs={{0,2},{1,3},{2,0},{3,1},{4,6},{5,7},{6,4},{7,5},{8,10},{9,11},{10,... | collective-permute-start | bytes 786440 | tf_op jit(solution)/shard_map/ppermute | solution.py:340
  60.5 2.0 %collective-permute-start.14 = (bf16[512,512]{1,0:T(8,128)(2,1)S(1)}, bf16[512,512]{1,0:T(8,128)(2,1)S(1)}, u32[]{:S(2)}, u32[]{:S(2)}) collective-permute-start(bf16[512,512]{1,0:T(8,128)(2,1)S(1)} %pack.11), channel_id=1, source_target_pairs={{0,1},{1,0},{2,3},{3,2},{4,5},{5,4},{6,7},{7,6},{8,9},{9,8},{10,11... | collective-permute-start | bytes 1572872 | tf_op jit(solution)/shard_map/ppermute | solution.py:340

commit v4 on v0

v4 whole, which is shorter than its diff:
```python
import functools
from typing import NamedTuple

import jax
import jax.numpy as jnp
from jax import lax
from jax.experimental import pallas as pl
from jax.experimental.pallas import tpu as pltpu
from jax.sharding import PartitionSpec as P

BS = 256
MARGIN = 4 * 1024 * 1024


class Sizes(NamedTuple):
    rows: int
    cols: int
    layers: int
    rows_here: int
    cols_here: int
    quarter: int
    per: int


def bits_of(size):
    return [1 << b for b in reversed(range(size.bit_length() - 1))]


def flip(size, bit):
    return [(i, i ^ bit) for i in range(size)]


def mod(a, n):
    return lax.rem(a + n, n)


def place():
    return lax.axis_index("row"), lax.axis_index("col"), lax.axis_index("layer")


def run(kernel, name, outs, arrays, smem=(), after=(), scratch=(), flops=0):
    size = sum(a.size * a.dtype.itemsize for a in arrays)
    size += sum(o.size * o.dtype.itemsize for o in outs)
    for kept in scratch:
        size += kept.shape[0] * kept.shape[1] * jnp.dtype(kept.dtype).itemsize
    skip = len(smem) + len(arrays)

    def body(*refs):
        kernel(*refs[:skip], *refs[skip + len(after) :])

    return pl.pallas_call(
        body,
        out_shape=list(outs),
        in_specs=[pl.BlockSpec(memory_space=pltpu.SMEM)] * len(smem)
        + [pl.BlockSpec(memory_space=pltpu.VMEM)] * len(arrays)
        + [pl.BlockSpec(memory_space=pl.ANY)] * len(after),
        out_specs=[pl.BlockSpec(memory_space=pltpu.VMEM)] * len(outs),
        scratch_shapes=list(scratch),
        compiler_params=pltpu.CompilerParams(vmem_limit_bytes=size + MARGIN),
        cost_estimate=pl.CostEstimate(flops=flops, bytes_accessed=size, transcendentals=0),
        name=name,
    )(*smem, *arrays, *after)


def shape(rows, columns, dtype=jnp.bfloat16):
    return jax.ShapeDtypeStruct((rows, columns), dtype)


def keep_block(pattern, i, j, block):
    return jnp.where(pattern[i, j] > 0, block, jnp.zeros_like(block))


def strip_start(l, half, sizes):
    return pl.multiple_of(half * sizes.cols_here + l * sizes.quarter, sizes.quarter)


def columns_of(cc, sizes):
    return pl.ds(pl.multiple_of(cc * sizes.cols_here, sizes.cols_here), sizes.cols_here)


def mask_strip(zp, r, l, half, cc, strip, sizes):
    block_row = (r * sizes.rows_here + half * sizes.cols_here + l * sizes.quarter) // BS
    first = cc * (sizes.cols_here // BS)
    return jnp.concatenate(
        [
            keep_block(zp, block_row, first + t, strip[:, t * BS : (t + 1) * BS])
            for t in range(sizes.cols_here // BS)
        ],
        axis=1,
    )


def mask_piece(zp, r, l, cc, piece, sizes):
    q = sizes.quarter
    return jnp.concatenate(
        [
            mask_strip(zp, r, l, half, cc, piece[half * q : (half + 1) * q, :], sizes)
            for half in range(sizes.per)
        ],
        axis=0,
    )


def pack_kernel(*refs):
    out, row = refs[-1], 0
    for ref in refs[:-1]:
        out[row : row + ref.shape[0], :] = ref[...]
        row += ref.shape[0]


def pack(pieces, after=()):
    height = sum(p.shape[0] for p in pieces)
    out = shape(height, pieces[0].shape[1])
    return run(pack_kernel, "pack", [out], pieces, after=after)[0]


def pick_kernel(choose, *refs):
    for condition, ref in zip(choose(lax.axis_index("col")), refs[:-1]):

        @pl.when(condition)
        def _(ref=ref):
            refs[-1][...] = ref[...]


def pick(choose, pieces, after=()):
    return run(
        functools.partial(pick_kernel, choose), "pick", [shape(*pieces[0].shape)], pieces,
        after=after,
    )[0]


def first_kernel(sizes, h_table, n_h, hp, zp, own, *refs):
    cols, q = sizes.cols, sizes.quarter
    n = cols - 2
    rights, lefts, h_refs = refs[:n], refs[n : 2 * n], refs[2 * n : 2 * n + n_h]
    hm, total, *strips, zm = refs[2 * n + n_h :]
    r, c, l = place()
    zm[...] = jnp.zeros_like(zm)
    zm[:, columns_of(c, sizes)] = mask_piece(zp, r, l, c, own[...], sizes)
    for s in range(1, n + 1):

        @pl.when(c >= s)
        def _(s=s):
            zm[:, columns_of(c - s, sizes)] = mask_piece(
                zp, r, l, c - s, rights[s - 1][...], sizes
            )

        @pl.when(c + s < cols)
        def _(s=s):
            zm[:, columns_of(c + s, sizes)] = mask_piece(
                zp, r, l, c + s, lefts[s - 1][...], sizes
            )

    per_rows = sizes.rows_here // BS
    for index, row, dr, dl in h_table:
        rr, ll = r ^ dr, l ^ dl
        block_col = (c * sizes.cols_here + ll * q) // BS
        for t in range(per_rows):
            j = rr * per_rows + t
            hm[pl.ds(pl.multiple_of(j * BS, BS), BS), pl.ds(pl.multiple_of(ll * q, q), q)] = (
                keep_block(hp, j, block_col, h_refs[index][row + t * BS : row + (t + 1) * BS, :])
            )
    order = zm.shape[1]
    chunk = min(order, 2048)
    acc = None
    for k in range(0, order, chunk):
        part = jnp.dot(
            zm[:, k : k + chunk], hm[k : k + chunk, :], preferred_element_type=jnp.float32
        )
        acc = part if acc is None else acc + part
    total[...] = acc
    for half, strip in enumerate(strips):
        strip[...] = acc[half * q : (half + 1) * q, :].astype(strip.dtype)


def finish_kernel(sizes, zp, hm, total, last, *strips):
    q = sizes.quarter
    r, c, l = place()
    cc = jnp.where(c == 0, sizes.cols - 1, 0)
    acc = total[...] + jnp.dot(
        mask_piece(zp, r, l, cc, last[...], sizes),
        hm[columns_of(cc, sizes), :],
        preferred_element_type=jnp.float32,
    )
    for half, strip in enumerate(strips):
        strip[...] = acc[half * q : (half + 1) * q, :].astype(strip.dtype)


def layers_kernel(sizes, z_table, zp, z_tile, *refs):
    cols, q = sizes.cols, sizes.quarter
    held, out = refs[:-1], refs[-1]
    r, c, l = place()
    sign = jnp.where(c < cols // 2, 1, -1)
    for dl in range(sizes.layers):
        ll = l ^ dl
        for half in range(sizes.per):
            rows = pl.ds(strip_start(ll, half, sizes), q)
            for s in range(cols - 1):
                cc = mod(c + sign * s, cols)
                if s == 0:
                    strip = z_tile[rows, :]
                else:
                    index, row = z_table[dl, s]
                    strip = held[index][row + half * q : row + (half + 1) * q, :]
                out[rows, columns_of(cc, sizes)] = mask_strip(zp, r, ll, half, cc, strip, sizes)
            cc = mod(c + sign * (cols - 1), cols)
            out[rows, columns_of(cc, sizes)] = jnp.zeros((q, sizes.cols_here), out.dtype)


def second_kernel(sizes, *refs):
    per, width = sizes.per, sizes.cols_here
    outside, inside, z_full, xm, total = refs
    r, c, l = place()
    first, second = (
        pl.ds(pl.multiple_of(mod(group - lax.rem(r, per), per) * width, width), width)
        for group in range(2)
    )
    xm[:, first] = outside[...]
    xm[:, second] = inside[...]
    total[...] = jnp.dot(xm[...], z_full[...], preferred_element_type=jnp.float32)


def rest_kernel(sizes, z_table, zp, xm, total, *refs):
    cols, q, wide = sizes.cols, sizes.quarter, sizes.rows_here
    *held, keep = refs[: -1 - sizes.rows]
    *sends, z_last, rest = refs[-1 - sizes.rows :]
    r, c, l = place()
    cc = mod(c + jnp.where(c < cols // 2, 1, -1) * (cols - 1), cols)
    for dl in range(sizes.layers):
        index, row = z_table[dl, cols - 1]
        for half in range(sizes.per):
            strip = held[index][row + half * q : row + (half + 1) * q, :]
            z_last[pl.ds(strip_start(l ^ dl, half, sizes), q), :] = mask_strip(
                zp, r, l ^ dl, half, cc, strip, sizes
            )
    rest[...] = total[...]
    rest[:, columns_of(cc, sizes)] = jnp.dot(
        xm[...], z_last[...], preferred_element_type=jnp.float32
    )
    for dr, out in enumerate([keep, *sends]):
        start = pl.multiple_of((r ^ dr) * wide, wide)
        out[...] = rest[:, pl.ds(start, wide)].astype(out.dtype)


def sum_kernel(*refs):
    keep, received, out = refs[0], refs[1:-1], refs[-1]
    total = keep[...]
    for part in received:
        total = total + part[...].astype(jnp.float32)
    out[...] = total.T.astype(out.dtype)


def local(sizes, hamiltonian, inv_root, h_pattern, z_pattern):
    rows, cols, layers, per = sizes.rows, sizes.cols, sizes.layers, sizes.per
    q, cols_here, rows_here = sizes.quarter, sizes.cols_here, sizes.rows_here
    order = rows * rows_here
    height = per * q
    row_bits, layer_bits = bits_of(rows), bits_of(layers)
    f32 = jnp.float32

    striped = inv_root.reshape(per, layers, q, cols_here)
    l = lax.axis_index("layer")
    own = lax.dynamic_index_in_dim(striped, l, 1, keepdims=False).reshape(height, cols_here)
    rights, lefts = [own], [own]
    for s in range(1, cols - 1):
        to_right = [(i, i + 1) for i in range(s - 1, cols - 1)]
        to_left = [(i, i - 1) for i in range(1, cols - s + 1)]
        rights.append(lax.ppermute(rights[-1], "col", to_right))
        lefts.append(lax.ppermute(lefts[-1], "col", to_left))
    inner = pick(
        lambda c: [c >= cols // 2, c < cols // 2], [rights[-1], lefts[-1]]
    )
    last = lax.ppermute(inner, "col", [(cols - 2, cols - 1), (1, 0)])

    def slot(s, after):
        if s <= cols // 2:
            pieces = [lefts[s], rights[s]]
            return pick(lambda c: [c < cols // 2, c >= cols // 2], pieces, after)
        left = lefts[s] if s < cols - 1 else last
        right = rights[s] if s < cols - 1 else last
        return pick(
            lambda c: [
                (c < cols // 2) & (c + s < cols),
                (c < cols // 2) & (c + s >= cols),
                (c >= cols // 2) & (c >= s),
                (c >= cols // 2) & (c < s),
            ],
            [left, rights[cols - s], right, lefts[cols - s]],
            after,
        )

    def cross(s, after=()):
        mine = slot(s, after)
        return [mine, lax.ppermute(mine, "layer", flip(layers, layer_bits[0]))]

    def share(slots, crossed, gate):
        arrays, table = [], []
        for s, pair in zip(slots, crossed):
            table += [(len(arrays), 0, 0, s), (len(arrays) + 1, 0, layer_bits[0], s)]
            arrays += pair
        for bit in layer_bits[1:]:
            packed = pack(arrays, gate)
            starts = [0]
            for array in arrays:
                starts.append(starts[-1] + array.shape[0])
            table += [
                (len(arrays), starts[index] + row, dl ^ bit, s) for index, row, dl, s in table
            ]
            arrays = arrays + [lax.ppermute(packed, "layer", flip(layers, bit))]
        return arrays, {(dl, s): (index, row) for index, row, dl, s in table}

    crossed = [cross(s) for s in range(1, cols - 1)]

    h_arrays, h_table = [hamiltonian], [(0, 0, 0, 0)]
    for axis, bit in [("layer", layer_bits[0])] + [("row", b) for b in row_bits]:
        for index, _, dr, dl in list(h_table):
            there = (dr ^ bit, dl) if axis == "row" else (dr, dl ^ bit)
            source = h_arrays[index]
            if index:
                source = pack([source], [rights[1], lefts[1]])
            h_table.append((len(h_arrays), 0) + there)
            h_arrays.append(
                lax.ppermute(source, axis, flip(rows if axis == "row" else layers, bit))
            )
    for bit in layer_bits[1:]:
        packed = pack(h_arrays, [rights[-1], lefts[-1], crossed[0][1]])
        starts = [0]
        for array in h_arrays:
            starts.append(starts[-1] + array.shape[0])
        h_table += [
            (len(h_arrays), starts[index] + row, dr, dl ^ bit) for index, row, dr, dl in h_table
        ]
        h_arrays = h_arrays + [lax.ppermute(packed, "layer", flip(layers, bit))]

    strip = shape(q, cols_here)
    hm, total, *early = run(
        functools.partial(first_kernel, sizes, h_table, len(h_arrays)),
        "first_product",
        [shape(order, cols_here), shape(height, cols_here, f32)] + [strip] * per,
        [own, *rights[1:], *lefts[1:], *h_arrays],
        smem=[h_pattern, z_pattern],
        scratch=[pltpu.VMEM((height, order), jnp.bfloat16)],
    )
    late = run(
        functools.partial(finish_kernel, sizes),
        "finish_product",
        [strip] * per,
        [hm, total, last],
        smem=[z_pattern],
        after=[crossed[-1][1]],
    )

    messages = []
    for group, strips in ((1, early), (0, late)):
        part = []
        for half in range(per):
            perm = []
            for r in range(rows):
                for c in range(cols):
                    if (c // per + c) % per != group:
                        continue
                    for k in range(layers):
                        perm.append(
                            (
                                (r * cols + c) * layers + k,
                                ((c // per) * cols + r * per + half) * layers + k,
                            )
                        )
            part.append(lax.ppermute(strips[half], ("row", "col", "layer"), perm))
        messages = part + messages

    from_inside = pick(lambda c: [c % per == half for half in range(per)], messages[per:], late[:1])
    held, z_table = share(range(1, cols - 1), crossed, [from_inside])
    z_full = run(
        functools.partial(layers_kernel, sizes, z_table),
        "layers",
        [shape(rows_here, order)],
        [inv_root, *held],
        smem=[z_pattern],
    )[0]
    from_outside = pick(
        lambda c: [c % per == half for half in range(per)], messages[:per], [z_full]
    )
    xm, total = run(
        functools.partial(second_kernel, sizes),
        "second_product",
        [shape(q, rows_here), shape(q, order, f32)],
        [from_outside, from_inside, z_full],
    )
    held, z_table = share([cols - 1], [cross(cols - 1, late[:1])], [xm])
    keep, *sends = run(
        functools.partial(rest_kernel, sizes, z_table),
        "rest_product",
        [shape(q, rows_here, f32)] + [shape(q, rows_here)] * (rows - 1),
        [xm, total, *held],
        smem=[z_pattern],
        scratch=[pltpu.VMEM((rows_here, cols_here), jnp.bfloat16), pltpu.VMEM((q, order), f32)],
    )
    received = [lax.ppermute(sends[d - 1], "row", flip(rows, d)) for d in range(1, rows)]
    return run(sum_kernel, "sum", [shape(*hamiltonian.shape)], [keep, *received])[0]


def solution(mesh):
    rows, cols, layers = (mesh.shape[a] for a in ("row", "col", "layer"))

    def whole(hamiltonian, inv_root, h_pattern, z_pattern):
        order = hamiltonian.shape[0]
        cols_here = order // cols
        sizes = Sizes(
            rows, cols, layers, order // rows, cols_here, cols_here // layers, cols // rows
        )
        return jax.shard_map(
            functools.partial(local, sizes),
            mesh=mesh,
            in_specs=(P("row", ("col", "layer")), P("row", "col"), P(), P()),
            out_specs=P("row", ("col", "layer")),
            check_vma=False,
        )(hamiltonian, inv_root, h_pattern, z_pattern)

    return whole
```

time: 136 us -> 74.2 us (0.55)
  blocking collectives: 59.9 us -> 0 us
  starting transfers between devices: 0.09 us -> 31.8 us
  waiting for transfers between devices: 48.7 us -> 32.5 us
  between operations: 13.2 us -> 0.25 us
  matrix products: 11.6 us -> 0 us
  Pallas kernels: 0 us -> 7.29 us
  other arithmetic: 1.8 us -> 0 us
    psum x1 -> x0, blocking collectives: 41 us -> none  [local(): summed = lax.psum(partial_y, 'layer')]
    ppermute x0 -> x19, waiting for transfers between devices: none -> 32.5 us  [the longest x1 10.1 us: local(): last = lax.ppermute(inner, 'col', [(cols - 2, cols - 1), (1, 0)])]
    ppermute x0 -> x19, starting transfers between devices: none -> 31.8 us  [the longest x1 9.22 us: local(): lax.ppermute(sends[d - 1], 'row', flip(rows, d))]
    reduce_scatter x1 -> x0, waiting for transfers between devices: 29.8 us -> none  [local(): lax.psum_scatter(partial_c, 'layer', scatter_dimension=1, tiled=True)]
    all_gather x2 -> x0, blocking collectives: 18.9 us -> none  [the longest x1 9.91 us: local(): lax.all_gather(z_part, 'row', axis=0, tiled=True)]
    all_gather x2 -> x0, waiting for transfers between devices: 18.9 us -> none  [the longest x1 18.9 us: local(): h_whole = lax.all_gather(h_local, 'col', axis=1, tiled=True)]
    dot_general x6 -> x0, matrix products: 11.6 us -> none  [the longest x2 5.18 us: accumulate(): return jnp.dot(left, right, preferred_element_type=jnp.float32)]
    pallas_call x0 -> x16, Pallas kernels: none -> 7.29 us  [run(): pl.pallas_call(body, out_shape=list(outs), in_specs=[pl.BlockSpec(memory_...]
  transfers between devices with their start and end apart: 3 -> 19, of which waited for: 2 -> 11; matrix products, arithmetic and copies ran while one was open for 4% -> 0% of each run, Pallas kernels for 0% -> 7%
where the time goes in v4:
time: 74.2 us; the launch traced here: 73.9 us
  waiting for transfers between devices  32.5 us (44%)
  starting transfers between devices  31.8 us (43%)
  Pallas kernels  7.29 us (10%)
  local copies, waits for them, and re-layouts  1.97 us (3%)
    ppermute x1, waiting for transfers between devices, local(): last = lax.ppermute(inner, 'col', [(cols - 2, cols - 1), (1, 0)])  10.1 us
    ppermute x1, starting transfers between devices, local(): lax.ppermute(sends[d - 1], 'row', flip(rows, d))  9.22 us
    pallas_call x16, Pallas kernels, run(): pl.pallas_call(body, out_shape=list(outs), in_specs=[pl.BlockSpec(memory_...  7.29 us
    ppermute x1, waiting for transfers between devices, local(): lax.ppermute(sends[d - 1], 'row', flip(rows, d))  6.6 us
    ppermute x2, waiting for transfers between devices, local(): lefts.append(lax.ppermute(lefts[-1], 'col', to_left))  6.45 us
    ppermute x2, starting transfers between devices, local(): rights.append(lax.ppermute(rights[-1], 'col', to_right))  6.26 us
    ppermute x3, starting transfers between devices, local(): lax.ppermute(source, axis, flip(rows if axis == 'row' else layers, bit))  5.09 us
    ppermute x4, starting transfers between devices, local(): part.append(lax.ppermute(strips[half], ('row', 'col', 'layer'), perm))  4.2 us
  transfers between devices with their start and end apart: 19, of which 11 were waited for; matrix products, arithmetic and copies ran while one was open for 0% of the time, Pallas kernels for 7%

profile of v4, /device:TPU:0, one launch (start us, length us, event | category | flops | bytes accessed | tf_op | source)
XLA Modules:
  0.0 73.9 jit_solution(6073093643943556558)
XLA Ops:
  0.0 1.0 %constant_dynamic-slice_fusion = bf16[2,1,128,512]{3,2,1,0:T(8,128)(2,1)S(1)} fusion(bf16[2,4,128,512]{3,2,1,0:T(8,128)(2,1)} %bitcast.4, s32[]{:T(128)S(6)} %select_n.4), kind=kLoop, calls=%fused_computation | loop fusion | bytes 524292 | tf_op jit(solution)/shard_map/jit(dynamic_index_in_dim)/dynamic_slice | solution.py:263
  1.0 1.3 %collective-permute-start.2 = (bf16[256,512]{1,0:T(8,128)(2,1)S(1)}, bf16[256,512]{1,0:T(8,128)(2,1)S(1)}, u32[]{:S(2)}, u32[]{:S(2)}) collective-permute-start(bf16[256,512]{1,0:T(8,128)(2,1)S(1)} %bitcast.5), channel_id=1, source_target_pairs={{4,0},{8,4},{12,8},{5,1},{9,5},{13,9},{6,2},{10,6},{14,10},{7,3},{... | collective-permute-start | bytes 786440 | tf_op jit(solution)/shard_map/ppermute | solution.py:269
  2.3 5.6 %collective-permute-start = (bf16[256,512]{1,0:T(8,128)(2,1)S(1)}, bf16[256,512]{1,0:T(8,128)(2,1)S(1)}, u32[]{:S(2)}, u32[]{:S(2)}) collective-permute-start(bf16[256,512]{1,0:T(8,128)(2,1)S(1)} %bitcast.6), channel_id=1, source_target_pairs={{0,4},{4,8},{8,12},{1,5},{5,9},{9,13},{2,6},{6,10},{10,14},{3,7},{... | collective-permute-start | bytes 786440 | tf_op jit(solution)/shard_map/ppermute | solution.py:268
  7.9 2.0 %collective-permute-start.4 = (bf16[1024,128]{1,0:T(8,128)(2,1)}, bf16[1024,128]{1,0:T(8,128)(2,1)S(1)}, u32[]{:S(2)}, u32[]{:S(2)}) collective-permute-start(bf16[1024,128]{1,0:T(8,128)(2,1)} %refs_7_.1), channel_id=1, source_target_pairs={{0,2},{1,3},{2,0},{3,1},{4,6},{5,7},{6,4},{7,5},{8,10},{9,11},{10,... | collective-permute-start | bytes 786440 | tf_op jit(solution)/shard_map/ppermute | solution.py:323
  9.9 1.5 %collective-permute-start.5 = (bf16[1024,128]{1,0:T(8,128)(2,1)}, bf16[1024,128]{1,0:T(8,128)(2,1)S(1)}, u32[]{:S(2)}, u32[]{:S(2)}) collective-permute-start(bf16[1024,128]{1,0:T(8,128)(2,1)} %refs_7_.1), channel_id=1, source_target_pairs={{0,16},{16,0},{1,17},{17,1},{2,18},{18,2},{3,19},{19,3},{4,20},{20... | collective-permute-start | bytes 786440 | tf_op jit(solution)/shard_map/ppermute | solution.py:323
  12.3 1.2 %collective-permute-done.refs_1_.refs_3_ = bf16[256,512]{1,0:T(8,128)(2,1)S(1)} collective-permute-done((bf16[256,512]{1,0:T(8,128)(2,1)S(1)}, bf16[256,512]{1,0:T(8,128)(2,1)S(1)}, u32[]{:S(2)}, u32[]{:S(2)}) %collective-permute-start) | collective-permute-done | bytes 262176 | tf_op jit(solution)/shard_map/ppermute | solution.py:268
  13.5 1.7 %collective-permute-start.7 = (bf16[256,512]{1,0:T(8,128)(2,1)S(1)}, bf16[256,512]{1,0:T(8,128)(2,1)S(1)}, u32[]{:S(2)}, u32[]{:S(2)}) collective-permute-start(bf16[256,512]{1,0:T(8,128)(2,1)S(1)} %pick.6.refs_0_.refs_2_), channel_id=1, source_target_pairs={{0,2},{1,3},{2,0},{3,1},{4,6},{5,7},{6,4},{7,5},{8,10},{9,11},{10,... | collective-permute-start | bytes 786440 | tf_op jit(solution)/shard_map/ppermute | solution.py:294
  15.2 1.3 %collective-permute-start.3 = (bf16[256,512]{1,0:T(8,128)(2,1)S(1)}, bf16[256,512]{1,0:T(8,128)(2,1)S(1)}, u32[]{:S(2)}, u32[]{:S(2)}) collective-permute-start(bf16[256,512]{1,0:T(8,128)(2,1)S(1)} %collective-permute-done.2.refs_2_.refs_0_.refs_5_.refs_3_), channel_id=1, source_target_pairs={{4,0},{8,4},{5,1},{9,5},{6,2},{10,6},{7,3},{11,7},{20,16},{24,20},... | collective-permute-start | bytes 786440 | tf_op jit(solution)/shard_map/ppermute | solution.py:269
  17.2 1.6 %collective-permute-start.6 = (bf16[1024,128]{1,0:T(8,128)(2,1)S(1)}, bf16[1024,128]{1,0:T(8,128)(2,1)S(1)}, u32[]{:S(2)}, u32[]{:S(2)}) collective-permute-start(bf16[1024,128]{1,0:T(8,128)(2,1)S(1)} %pack.4), channel_id=1, source_target_pairs={{0,16},{16,0},{1,17},{17,1},{2,18},{18,2},{3,19},{19,3},{4,20},{20... | collective-permute-start | bytes 786440 | tf_op jit(solution)/shard_map/ppermute | solution.py:323
  18.8 5.6 %collective-permute-done.3.refs_5_.refs_6_.refs_1_.refs_0_ = bf16[256,512]{1,0:T(8,128)(2,1)S(1)} collective-permute-done((bf16[256,512]{1,0:T(8,128)(2,1)S(1)}, bf16[256,512]{1,0:T(8,128)(2,1)S(1)}, u32[]{:S(2)}, u32[]{:S(2)}) %collective-permute-start.3) | collective-permute-done | bytes 262176 | tf_op jit(solution)/shard_map/ppermute | solution.py:269
  24.4 0.9 %copy-done.1 = bf16[1024,128]{1,0:T(8,128)(2,1)S(1)} copy-done((bf16[1024,128]{1,0:T(8,128)(2,1)S(1)}, bf16[1024,128]{1,0:T(8,128)(2,1)}, u32[]{:S(2)}) %copy-start.1) | copy-done | bytes 262168
  25.6 1.3 %collective-permute-start.9 = (bf16[256,512]{1,0:T(8,128)(2,1)S(1)}, bf16[256,512]{1,0:T(8,128)(2,1)S(1)}, u32[]{:S(2)}, u32[]{:S(2)}) collective-permute-start(bf16[256,512]{1,0:T(8,128)(2,1)S(1)} %pick.7), channel_id=1, source_target_pairs={{8,12},{4,0},{9,13},{5,1},{10,14},{6,2},{11,15},{7,3},{24,28},{20,... | collective-permute-start | bytes 786440 | tf_op jit(solution)/shard_map/ppermute | solution.py:273
  28.2 2.0 %first_product.1 = (bf16[2048,512]{1,0:T(8,128)(2,1)S(1)}, f32[256,512]{1,0:T(8,128)S(1)}, bf16[128,512]{1,0:T(8,128)(2,1)S(1)}, bf16[128,512]{1,0:T(8,128)(2,1)S(1)}) custom-call(s32[8,8]{1,0:T(8,128)S(1)} %copy-done.4, s32[8,8]{1,0:T(8,128)S(1)} %copy-done.3, bf16[256,512]{1,0:T(8,128)(2,1)S(1)} %bitcast.7, ...), custom_call_target="tpu_custom_call" | custom-call | bytes 7340032 | tf_op jit(solution)/shard_map/first_product/pallas_call | solution.py:51
  30.3 1.4 %collective-permute-start.13 = (bf16[128,512]{1,0:T(8,128)(2,1)S(1)}, bf16[128,512]{1,0:T(8,128)(2,1)S(1)}, u32[]{:S(2)}, u32[]{:S(2)}) collective-permute-start(bf16[128,512]{1,0:T(8,128)(2,1)S(1)} %get-tuple-element.19), channel_id=1, source_target_pairs={{4,0},{5,1},{6,2},{7,3},{8,16},{9,17},{10,18},{11,19},{20,8},{21,9... | collective-permute-start | bytes 393224 | tf_op jit(solution)/shard_map/ppermute | solution.py:369
  32.4 10.1 %collective-permute-done.9.refs_3_.refs_0_.refs_2_ = bf16[256,512]{1,0:T(8,128)(2,1)S(1)} collective-permute-done((bf16[256,512]{1,0:T(8,128)(2,1)S(1)}, bf16[256,512]{1,0:T(8,128)(2,1)S(1)}, u32[]{:S(2)}, u32[]{:S(2)}) %collective-permute-start.9) | collective-permute-done | bytes 262176 | tf_op jit(solution)/shard_map/ppermute | solution.py:273
  43.3 1.7 %collective-permute-done.13.refs_0_ = bf16[128,512]{1,0:T(8,128)(2,1)S(1)} collective-permute-done((bf16[128,512]{1,0:T(8,128)(2,1)S(1)}, bf16[128,512]{1,0:T(8,128)(2,1)S(1)}, u32[]{:S(2)}, u32[]{:S(2)}) %collective-permute-start.13) | collective-permute-done | bytes 131104 | tf_op jit(solution)/shard_map/ppermute | solution.py:369
  45.7 1.4 %collective-permute-start.12 = (bf16[128,512]{1,0:T(8,128)(2,1)S(1)}, bf16[128,512]{1,0:T(8,128)(2,1)S(1)}, u32[]{:S(2)}, u32[]{:S(2)}) collective-permute-start(bf16[128,512]{1,0:T(8,128)(2,1)S(1)} %get-tuple-element.18), channel_id=1, source_target_pairs={{0,4},{1,5},{2,6},{3,7},{12,20},{13,21},{14,22},{15,23},{16,12},{1... | collective-permute-start | bytes 393224 | tf_op jit(solution)/shard_map/ppermute | solution.py:369
  47.9 1.3 %layers.1.refs_2_ = bf16[1024,2048]{1,0:T(8,128)(2,1)S(1)} custom-call(s32[8,8]{1,0:T(8,128)S(1)} %copy-done.3, bf16[1024,512]{1,0:T(8,128)(2,1)S(1)} %copy-done, bf16[256,512]{1,0:T(8,128)(2,1)S(1)} %pick.6.refs_0_.refs_2_, bf16[256,512]{1,0:T(8,128)(2,1)S(1)} %collective-permute-done.7.refs_6_.refs_1_.refs_3_, bf16[256,512]{1,0:T(8,128)(2,1)S(1)} %pick.8.refs_2_.refs_4_, ...), custom_call_target="tpu_custom_call" | custom-call | bytes 7340032 | tf_op jit(solution)/shard_map/layers/pallas_call | solution.py:51
  49.1 1.2 %collective-permute-done.12.refs_1_ = bf16[128,512]{1,0:T(8,128)(2,1)S(1)} collective-permute-done((bf16[128,512]{1,0:T(8,128)(2,1)S(1)}, bf16[128,512]{1,0:T(8,128)(2,1)S(1)}, u32[]{:S(2)}, u32[]{:S(2)}) %collective-permute-start.12) | collective-permute-done | bytes 131104 | tf_op jit(solution)/shard_map/ppermute | solution.py:369
  51.1 2.9 %collective-permute-done.16.refs_1_.refs_4_ = bf16[256,512]{1,0:T(8,128)(2,1)S(1)} collective-permute-done((bf16[256,512]{1,0:T(8,128)(2,1)S(1)}, bf16[256,512]{1,0:T(8,128)(2,1)S(1)}, u32[]{:S(2)}, u32[]{:S(2)}) %collective-permute-start.16) | collective-permute-done | bytes 262176 | tf_op jit(solution)/shard_map/ppermute | solution.py:294
  54.1 1.9 %collective-permute-done.17.refs_5_ = bf16[512,512]{1,0:T(8,128)(2,1)S(1)} collective-permute-done((bf16[512,512]{1,0:T(8,128)(2,1)S(1)}, bf16[512,512]{1,0:T(8,128)(2,1)S(1)}, u32[]{:S(2)}, u32[]{:S(2)}) %collective-permute-start.17) | collective-permute-done | bytes 524320 | tf_op jit(solution)/shard_map/ppermute | solution.py:309
  56.0 1.2 %rest_product.1 = (f32[128,1024]{1,0:T(8,128)S(1)}, bf16[128,1024]{1,0:T(8,128)(2,1)S(1)}) custom-call(s32[8,8]{1,0:T(8,128)S(1)} %copy-done.3, bf16[128,1024]{1,0:T(8,128)(2,1)S(1)} %get-tuple-element.21.refs_2_.refs_1_, f32[128,2048]{1,0:T(8,128)S(1)} %get-tuple-element.22.refs_2_, bf16[256,512]{1,0:T(8,128)(2,1)S(1)} %pick.11.refs_0_.refs_3_, ...), custom_call_target="tpu_custom_call" | custom-call | bytes 5242880 | tf_op jit(solution)/shard_map/rest_product/pallas_call | solution.py:51
  57.2 9.2 %collective-permute-start.18 = (bf16[128,1024]{1,0:T(8,128)(2,1)S(1)}, bf16[128,1024]{1,0:T(8,128)(2,1)S(1)}, u32[]{:S(2)}, u32[]{:S(2)}) collective-permute-start(bf16[128,1024]{1,0:T(8,128)(2,1)S(1)} %get-tuple-element.24), channel_id=1, source_target_pairs={{0,16},{16,0},{1,17},{17,1},{2,18},{18,2},{3,19},{19,3},{4,20},{20... | collective-permute-start | bytes 786440 | tf_op jit(solution)/shard_map/ppermute | solution.py:399
  66.4 6.6 %collective-permute-done.18.refs_1_ = bf16[128,1024]{1,0:T(8,128)(2,1)S(1)} collective-permute-done((bf16[128,1024]{1,0:T(8,128)(2,1)S(1)}, bf16[128,1024]{1,0:T(8,128)(2,1)S(1)}, u32[]{:S(2)}, u32[]{:S(2)}) %collective-permute-start.18) | collective-permute-done | bytes 262176 | tf_op jit(solution)/shard_map/ppermute | solution.py:399
  (41 shorter events, 7.7 us)
Async XLA Ops:
  0.0 28.2 %copy-start.2 = (bf16[1024,128]{1,0:T(8,128)(2,1)S(1)}, bf16[1024,128]{1,0:T(8,128)(2,1)}, u32[]{:S(2)}) copy-start(bf16[1024,128]{1,0:T(8,128)(2,1)} %refs_7_.1) | copy-start | bytes 786436
  0.0 28.2 %copy-start.3 = (s32[8,8]{1,0:T(8,128)S(1)}, s32[8,8]{1,0:T(8,128)}, u32[]{:S(2)}) copy-start(s32[8,8]{1,0:T(8,128)} %refs_0_.9) | copy-start | bytes 772
  0.0 28.2 %copy-start.4 = (s32[8,8]{1,0:T(8,128)S(1)}, s32[8,8]{1,0:T(8,128)}, u32[]{:S(2)}) copy-start(s32[8,8]{1,0:T(8,128)} %refs_0_.6) | copy-start | bytes 772
  1.0 11.2 %collective-permute-start.2 = (bf16[256,512]{1,0:T(8,128)(2,1)S(1)}, bf16[256,512]{1,0:T(8,128)(2,1)S(1)}, u32[]{:S(2)}, u32[]{:S(2)}) collective-permute-start(bf16[256,512]{1,0:T(8,128)(2,1)S(1)} %bitcast.5), channel_id=1, source_target_pairs={{4,0},{8,4},{12,8},{5,1},{9,5},{13,9},{6,2},{10,6},{14,10},{7,3},{... | collective-permute-start | bytes 786440 | tf_op jit(solution)/shard_map/ppermute | solution.py:269
  2.3 11.1 %collective-permute-start = (bf16[256,512]{1,0:T(8,128)(2,1)S(1)}, bf16[256,512]{1,0:T(8,128)(2,1)S(1)}, u32[]{:S(2)}, u32[]{:S(2)}) collective-permute-start(bf16[256,512]{1,0:T(8,128)(2,1)S(1)} %bitcast.6), channel_id=1, source_target_pairs={{0,4},{4,8},{8,12},{1,5},{5,9},{9,13},{2,6},{6,10},{10,14},{3,7},{... | collective-permute-start | bytes 786440 | tf_op jit(solution)/shard_map/ppermute | solution.py:268
  7.9 9.3 %collective-permute-start.4 = (bf16[1024,128]{1,0:T(8,128)(2,1)}, bf16[1024,128]{1,0:T(8,128)(2,1)S(1)}, u32[]{:S(2)}, u32[]{:S(2)}) collective-permute-start(bf16[1024,128]{1,0:T(8,128)(2,1)} %refs_7_.1), channel_id=1, source_target_pairs={{0,2},{1,3},{2,0},{3,1},{4,6},{5,7},{6,4},{7,5},{8,10},{9,11},{10,... | collective-permute-start | bytes 786440 | tf_op jit(solution)/shard_map/ppermute | solution.py:323
  9.9 8.9 %collective-permute-start.5 = (bf16[1024,128]{1,0:T(8,128)(2,1)}, bf16[1024,128]{1,0:T(8,128)(2,1)S(1)}, u32[]{:S(2)}, u32[]{:S(2)}) collective-permute-start(bf16[1024,128]{1,0:T(8,128)(2,1)} %refs_7_.1), channel_id=1, source_target_pairs={{0,16},{16,0},{1,17},{17,1},{2,18},{18,2},{3,19},{19,3},{4,20},{20... | collective-permute-start | bytes 786440 | tf_op jit(solution)/shard_map/ppermute | solution.py:323
  13.5 11.0 %collective-permute-start.7 = (bf16[256,512]{1,0:T(8,128)(2,1)S(1)}, bf16[256,512]{1,0:T(8,128)(2,1)S(1)}, u32[]{:S(2)}, u32[]{:S(2)}) collective-permute-start(bf16[256,512]{1,0:T(8,128)(2,1)S(1)} %pick.6.refs_0_.refs_2_), channel_id=1, source_target_pairs={{0,2},{1,3},{2,0},{3,1},{4,6},{5,7},{6,4},{7,5},{8,10},{9,11},{10,... | collective-permute-start | bytes 786440 | tf_op jit(solution)/shard_map/ppermute | solution.py:294
  15.2 9.2 %collective-permute-start.3 = (bf16[256,512]{1,0:T(8,128)(2,1)S(1)}, bf16[256,512]{1,0:T(8,128)(2,1)S(1)}, u32[]{:S(2)}, u32[]{:S(2)}) collective-permute-start(bf16[256,512]{1,0:T(8,128)(2,1)S(1)} %collective-permute-done.2.refs_2_.refs_0_.refs_5_.refs_3_), channel_id=1, source_target_pairs={{4,0},{8,4},{5,1},{9,5},{6,2},{10,6},{7,3},{11,7},{20,16},{24,20},... | collective-permute-start | bytes 786440 | tf_op jit(solution)/shard_map/ppermute | solution.py:269
  16.5 7.9 %collective-permute-start.1 = (bf16[256,512]{1,0:T(8,128)(2,1)S(1)}, bf16[256,512]{1,0:T(8,128)(2,1)S(1)}, u32[]{:S(2)}, u32[]{:S(2)}) collective-permute-start(bf16[256,512]{1,0:T(8,128)(2,1)S(1)} %collective-permute-done.refs_1_.refs_3_), channel_id=1, source_target_pairs={{4,8},{8,12},{5,9},{9,13},{6,10},{10,14},{7,11},{11,15},{20,24},{2... | collective-permute-start | bytes 786440 | tf_op jit(solution)/shard_map/ppermute | solution.py:268
  17.2 7.2 %collective-permute-start.6 = (bf16[1024,128]{1,0:T(8,128)(2,1)S(1)}, bf16[1024,128]{1,0:T(8,128)(2,1)S(1)}, u32[]{:S(2)}, u32[]{:S(2)}) collective-permute-start(bf16[1024,128]{1,0:T(8,128)(2,1)S(1)} %pack.4), channel_id=1, source_target_pairs={{0,16},{16,0},{1,17},{17,1},{2,18},{18,2},{3,19},{19,3},{4,20},{20... | collective-permute-start | bytes 786440 | tf_op jit(solution)/shard_map/ppermute | solution.py:323
  24.4 1.0 %copy-start.1 = (bf16[1024,128]{1,0:T(8,128)(2,1)S(1)}, bf16[1024,128]{1,0:T(8,128)(2,1)}, u32[]{:S(2)}) copy-start(bf16[1024,128]{1,0:T(8,128)(2,1)} %refs_7_.1) | copy-start | bytes 786436
  25.5 2.7 %collective-permute-start.8 = (bf16[4096,128]{1,0:T(8,128)(2,1)S(1)}, bf16[4096,128]{1,0:T(8,128)(2,1)S(1)}, u32[]{:S(2)}, u32[]{:S(2)}) collective-permute-start(bf16[4096,128]{1,0:T(8,128)(2,1)S(1)} %pack.5), channel_id=1, source_target_pairs={{0,1},{1,0},{2,3},{3,2},{4,5},{5,4},{6,7},{7,6},{8,9},{9,8},{10,11... | collective-permute-start | bytes 3145736 | tf_op jit(solution)/shard_map/ppermute | solution.py:333
  25.6 16.8 %collective-permute-start.9 = (bf16[256,512]{1,0:T(8,128)(2,1)S(1)}, bf16[256,512]{1,0:T(8,128)(2,1)S(1)}, u32[]{:S(2)}, u32[]{:S(2)}) collective-permute-start(bf16[256,512]{1,0:T(8,128)(2,1)S(1)} %pick.7), channel_id=1, source_target_pairs={{8,12},{4,0},{9,13},{5,1},{10,14},{6,2},{11,15},{7,3},{24,28},{20,... | collective-permute-start | bytes 786440 | tf_op jit(solution)/shard_map/ppermute | solution.py:273
  26.9 15.5 %collective-permute-start.10 = (bf16[256,512]{1,0:T(8,128)(2,1)S(1)}, bf16[256,512]{1,0:T(8,128)(2,1)S(1)}, u32[]{:S(2)}, u32[]{:S(2)}) collective-permute-start(bf16[256,512]{1,0:T(8,128)(2,1)S(1)} %pick.8.refs_2_.refs_4_), channel_id=1, source_target_pairs={{0,2},{1,3},{2,0},{3,1},{4,6},{5,7},{6,4},{7,5},{8,10},{9,11},{10,... | collective-permute-start | bytes 786440 | tf_op jit(solution)/shard_map/ppermute | solution.py:294
  30.2 17.6 %copy-start = (bf16[1024,512]{1,0:T(8,128)(2,1)S(1)}, bf16[1024,512]{1,0:T(8,128)(2,1)}, u32[]{:S(2)}) copy-start(bf16[1024,512]{1,0:T(8,128)(2,1)} %refs_1_.3) | copy-start | bytes 3145732
  30.3 14.8 %collective-permute-start.13 = (bf16[128,512]{1,0:T(8,128)(2,1)S(1)}, bf16[128,512]{1,0:T(8,128)(2,1)S(1)}, u32[]{:S(2)}, u32[]{:S(2)}) collective-permute-start(bf16[128,512]{1,0:T(8,128)(2,1)S(1)} %get-tuple-element.19), channel_id=1, source_target_pairs={{4,0},{5,1},{6,2},{7,3},{8,16},{9,17},{10,18},{11,19},{20,8},{21,9... | collective-permute-start | bytes 393224 | tf_op jit(solution)/shard_map/ppermute | solution.py:369
  31.7 13.3 %collective-permute-start.14 = (bf16[128,512]{1,0:T(8,128)(2,1)S(1)}, bf16[128,512]{1,0:T(8,128)(2,1)S(1)}, u32[]{:S(2)}, u32[]{:S(2)}) collective-permute-start(bf16[128,512]{1,0:T(8,128)(2,1)S(1)} %get-tuple-element.20), channel_id=1, source_target_pairs={{4,4},{5,5},{6,6},{7,7},{8,20},{9,21},{10,22},{11,23},{20,12},{21,... | collective-permute-start | bytes 393224 | tf_op jit(solution)/shard_map/ppermute | solution.py:369
  45.1 2.7 %collective-permute-start.15 = (bf16[1024,512]{1,0:T(8,128)(2,1)S(1)}, bf16[1024,512]{1,0:T(8,128)(2,1)S(1)}, u32[]{:S(2)}, u32[]{:S(2)}) collective-permute-start(bf16[1024,512]{1,0:T(8,128)(2,1)S(1)} %pack.6), channel_id=1, source_target_pairs={{0,1},{1,0},{2,3},{3,2},{4,5},{5,4},{6,7},{7,6},{8,9},{9,8},{10,11... | collective-permute-start | bytes 3145736 | tf_op jit(solution)/shard_map/ppermute | solution.py:309
  45.3 8.8 %collective-permute-start.16 = (bf16[256,512]{1,0:T(8,128)(2,1)S(1)}, bf16[256,512]{1,0:T(8,128)(2,1)S(1)}, u32[]{:S(2)}, u32[]{:S(2)}) collective-permute-start(bf16[256,512]{1,0:T(8,128)(2,1)S(1)} %pick.11.refs_0_.refs_3_), channel_id=1, source_target_pairs={{0,2},{1,3},{2,0},{3,1},{4,6},{5,7},{6,4},{7,5},{8,10},{9,11},{10,... | collective-permute-start | bytes 786440 | tf_op jit(solution)/shard_map/ppermute | solution.py:294
  45.7 4.7 %collective-permute-start.12 = (bf16[128,512]{1,0:T(8,128)(2,1)S(1)}, bf16[128,512]{1,0:T(8,128)(2,1)S(1)}, u32[]{:S(2)}, u32[]{:S(2)}) collective-permute-start(bf16[128,512]{1,0:T(8,128)(2,1)S(1)} %get-tuple-element.18), channel_id=1, source_target_pairs={{0,4},{1,5},{2,6},{3,7},{12,20},{13,21},{14,22},{15,23},{16,12},{1... | collective-permute-start | bytes 393224 | tf_op jit(solution)/shard_map/ppermute | solution.py:369
  47.1 3.2 %collective-permute-start.11 = (bf16[128,512]{1,0:T(8,128)(2,1)S(1)}, bf16[128,512]{1,0:T(8,128)(2,1)S(1)}, u32[]{:S(2)}, u32[]{:S(2)}) collective-permute-start(bf16[128,512]{1,0:T(8,128)(2,1)S(1)} %get-tuple-element.17.refs_2_.refs_4_), channel_id=1, source_target_pairs={{0,0},{1,1},{2,2},{3,3},{12,16},{13,17},{14,18},{15,19},{16,8},{17... | collective-permute-start | bytes 393224 | tf_op jit(solution)/shard_map/ppermute | solution.py:369
  54.0 2.0 %collective-permute-start.17 = (bf16[512,512]{1,0:T(8,128)(2,1)S(1)}, bf16[512,512]{1,0:T(8,128)(2,1)S(1)}, u32[]{:S(2)}, u32[]{:S(2)}) collective-permute-start(bf16[512,512]{1,0:T(8,128)(2,1)S(1)} %pack.7), channel_id=1, source_target_pairs={{0,1},{1,0},{2,3},{3,2},{4,5},{5,4},{6,7},{7,6},{8,9},{9,8},{10,11... | collective-permute-start | bytes 1572872 | tf_op jit(solution)/shard_map/ppermute | solution.py:309
  57.2 15.8 %collective-permute-start.18 = (bf16[128,1024]{1,0:T(8,128)(2,1)S(1)}, bf16[128,1024]{1,0:T(8,128)(2,1)S(1)}, u32[]{:S(2)}, u32[]{:S(2)}) collective-permute-start(bf16[128,1024]{1,0:T(8,128)(2,1)S(1)} %get-tuple-element.24), channel_id=1, source_target_pairs={{0,16},{16,0},{1,17},{17,1},{2,18},{18,2},{3,19},{19,3},{4,20},{20... | collective-permute-start | bytes 786440 | tf_op jit(solution)/shard_map/ppermute | solution.py:399

commit v5 on v4

v5 whole, which is shorter than its diff:
```python
import functools
from typing import NamedTuple

import jax
import jax.numpy as jnp
from jax import lax
from jax.experimental import pallas as pl
from jax.experimental.pallas import tpu as pltpu
from jax.sharding import PartitionSpec as P

BS = 256
MARGIN = 4 * 1024 * 1024


class Sizes(NamedTuple):
    rows: int
    cols: int
    layers: int
    rows_here: int
    cols_here: int
    quarter: int
    per: int


def bits_of(size):
    return [1 << b for b in reversed(range(size.bit_length() - 1))]


def flip(size, bit):
    return [(i, i ^ bit) for i in range(size)]


def mod(a, n):
    return lax.rem(a + n, n)


def place():
    return lax.axis_index("row"), lax.axis_index("col"), lax.axis_index("layer")


def run(kernel, name, outs, arrays, smem=(), after=(), scratch=(), flops=0):
    size = sum(a.size * a.dtype.itemsize for a in arrays)
    size += sum(o.size * o.dtype.itemsize for o in outs)
    for kept in scratch:
        size += kept.shape[0] * kept.shape[1] * jnp.dtype(kept.dtype).itemsize
    skip = len(smem) + len(arrays)

    def body(*refs):
        kernel(*refs[:skip], *refs[skip + len(after) :])

    return pl.pallas_call(
        body,
        out_shape=list(outs),
        in_specs=[pl.BlockSpec(memory_space=pltpu.SMEM)] * len(smem)
        + [pl.BlockSpec(memory_space=pltpu.VMEM)] * len(arrays)
        + [pl.BlockSpec(memory_space=pl.ANY)] * len(after),
        out_specs=[pl.BlockSpec(memory_space=pltpu.VMEM)] * len(outs),
        scratch_shapes=list(scratch),
        compiler_params=pltpu.CompilerParams(vmem_limit_bytes=size + MARGIN),
        cost_estimate=pl.CostEstimate(flops=flops, bytes_accessed=size, transcendentals=0),
        name=name,
    )(*smem, *arrays, *after)


def shape(rows, columns, dtype=jnp.bfloat16):
    return jax.ShapeDtypeStruct((rows, columns), dtype)


def keep_block(pattern, i, j, block):
    return jnp.where(pattern[i, j] > 0, block, jnp.zeros_like(block))


def strip_start(l, half, sizes):
    return pl.multiple_of(half * sizes.cols_here + l * sizes.quarter, sizes.quarter)


def columns_of(cc, sizes):
    return pl.ds(pl.multiple_of(cc * sizes.cols_here, sizes.cols_here), sizes.cols_here)


def mask_strip(zp, r, l, half, cc, strip, sizes):
    block_row = (r * sizes.rows_here + half * sizes.cols_here + l * sizes.quarter) // BS
    first = cc * (sizes.cols_here // BS)
    return jnp.concatenate(
        [
            keep_block(zp, block_row, first + t, strip[:, t * BS : (t + 1) * BS])
            for t in range(sizes.cols_here // BS)
        ],
        axis=1,
    )


def mask_piece(zp, r, l, cc, piece, sizes):
    q = sizes.quarter
    return jnp.concatenate(
        [
            mask_strip(zp, r, l, half, cc, piece[half * q : (half + 1) * q, :], sizes)
            for half in range(sizes.per)
        ],
        axis=0,
    )


def pack_kernel(*refs):
    out, row = refs[-1], 0
    for ref in refs[:-1]:
        out[row : row + ref.shape[0], :] = ref[...]
        row += ref.shape[0]


def pack(pieces, after=()):
    height = sum(p.shape[0] for p in pieces)
    out = shape(height, pieces[0].shape[1])
    return run(pack_kernel, "pack", [out], pieces, after=after)[0]


def ring_place(c, cols):
    return jnp.where(c % 2 == 0, c // 2, cols - 1 - c // 2)


def ring_column(p, cols):
    return jnp.where(p < cols // 2, 2 * p, 2 * (cols - 1 - p) + 1)


def slot_column(c, s, cols):
    return ring_column(mod(ring_place(c, cols) - s, cols), cols)


def first_kernel(sizes, h_table, n_h, hp, zp, *refs):
    cols, q = sizes.cols, sizes.quarter
    slots, h_refs = refs[: cols - 1], refs[cols - 1 : cols - 1 + n_h]
    hm, total, zm = refs[cols - 1 + n_h :]
    r, c, l = place()
    for s in range(cols - 1):
        cc = slot_column(c, s, cols)
        zm[:, columns_of(cc, sizes)] = mask_piece(zp, r, l, cc, slots[s][...], sizes)
    zm[:, columns_of(slot_column(c, cols - 1, cols), sizes)] = jnp.zeros(
        (zm.shape[0], sizes.cols_here), zm.dtype
    )
    per_rows = sizes.rows_here // BS
    for index, row, dr, dl in h_table:
        rr, ll = r ^ dr, l ^ dl
        block_col = (c * sizes.cols_here + ll * q) // BS
        for t in range(per_rows):
            j = rr * per_rows + t
            hm[pl.ds(pl.multiple_of(j * BS, BS), BS), pl.ds(pl.multiple_of(ll * q, q), q)] = (
                keep_block(hp, j, block_col, h_refs[index][row + t * BS : row + (t + 1) * BS, :])
            )
    order = zm.shape[1]
    chunk = min(order, 2048)
    acc = None
    for k in range(0, order, chunk):
        part = jnp.dot(
            zm[:, k : k + chunk], hm[k : k + chunk, :], preferred_element_type=jnp.float32
        )
        acc = part if acc is None else acc + part
    total[...] = acc


def finish_kernel(sizes, zp, hm, total, last, out):
    r, c, l = place()
    cc = slot_column(c, sizes.cols - 1, sizes.cols)
    out[...] = (
        total[...]
        + jnp.dot(
            mask_piece(zp, r, l, cc, last[...], sizes),
            hm[columns_of(cc, sizes), :],
            preferred_element_type=jnp.float32,
        )
    ).astype(out.dtype)


def route_kernel(sizes, row_offsets, *refs):
    n = len(row_offsets)
    pieces, outs, table = refs[:n], refs[n:-1], refs[-1]
    r, c, _ = place()
    q = sizes.quarter
    for dr, piece in zip(row_offsets, pieces):
        for half in range(sizes.per):
            start = pl.multiple_of(((r ^ dr) * sizes.per + half) * q, q)
            table[pl.ds(start, q), :] = piece[half * q : (half + 1) * q, :]
    for d, out in enumerate(outs):
        out[...] = table[pl.ds(pl.multiple_of((c ^ d) * q, q), q), :]


def layers_kernel(sizes, z_table, slots, zp, *refs):
    cols, q = sizes.cols, sizes.quarter
    out, held = refs[-1], refs[:-1]
    r, c, l = place()
    for dl in range(sizes.layers):
        ll = l ^ dl
        for half in range(sizes.per):
            rows = pl.ds(strip_start(ll, half, sizes), q)
            for s in slots:
                cc = slot_column(c, s, cols)
                if s == 0:
                    strip = held[0][rows, :]
                else:
                    index, row = z_table[dl, s]
                    strip = held[index][row + half * q : row + (half + 1) * q, :]
                columns = columns_of(cc, sizes) if len(slots) > 1 else slice(None)
                out[rows, columns] = mask_strip(zp, r, ll, half, cc, strip, sizes)


def second_kernel(sizes, z_early, z_late, *refs):
    cols, width = sizes.cols, sizes.cols_here
    messages, out, xm = refs[:cols], refs[cols], refs[cols + 1]
    r, c, l = place()
    for d in range(cols):
        xm[:, columns_of(c ^ d, sizes)] = messages[d][...]
    cc = slot_column(c, cols - 1, cols)
    turned = (((1,), (1,)), ((), ()))
    total = lax.dot_general(
        z_late[...], xm[:, columns_of(cc, sizes)], turned, preferred_element_type=jnp.float32
    )
    for s in range(cols - 1):
        columns = columns_of(slot_column(c, s, cols), sizes)
        total += lax.dot_general(
            z_early[:, columns], xm[:, columns], turned, preferred_element_type=jnp.float32
        )
    out[...] = total.astype(out.dtype)


def local(sizes, hamiltonian, inv_root, h_pattern, z_pattern):
    rows, cols, layers, per = sizes.rows, sizes.cols, sizes.layers, sizes.per
    q, cols_here, rows_here = sizes.quarter, sizes.cols_here, sizes.rows_here
    order = rows * rows_here
    height = per * q
    row_bits, layer_bits = bits_of(rows), bits_of(layers)
    f32 = jnp.float32

    striped = inv_root.reshape(per, layers, q, cols_here)
    l = lax.axis_index("layer")
    own = lax.dynamic_index_in_dim(striped, l, 1, keepdims=False).reshape(height, cols_here)
    trip = list(range(0, cols, 2)) + list(range(cols - 1, 0, -2))
    ring = [(trip[i], trip[(i + 1) % cols]) for i in range(cols)]
    slots = [own]
    for _ in range(1, cols):
        slots.append(lax.ppermute(slots[-1], "col", ring))

    def offsets(arrays):
        starts = [0]
        for array in arrays:
            starts.append(starts[-1] + array.shape[0])
        return starts

    crossed = [lax.ppermute(slots[s], "layer", flip(layers, layer_bits[0])) for s in range(1, cols)]

    h_arrays, h_table = [hamiltonian], [(0, 0, 0, 0)]
    for axis, bit in [("layer", layer_bits[0])] + [("row", b) for b in row_bits]:
        for index, _, dr, dl in list(h_table):
            there = (dr ^ bit, dl) if axis == "row" else (dr, dl ^ bit)
            source = h_arrays[index]
            if index:
                source = pack([source], [slots[1]])
            h_table.append((len(h_arrays), 0) + there)
            h_arrays.append(
                lax.ppermute(source, axis, flip(rows if axis == "row" else layers, bit))
            )
    for bit in layer_bits[1:]:
        packed, starts = pack(h_arrays, [slots[-2], crossed[0]]), offsets(h_arrays)
        h_table += [
            (len(h_arrays), starts[index] + row, dr, dl ^ bit) for index, row, dr, dl in h_table
        ]
        h_arrays = h_arrays + [lax.ppermute(packed, "layer", flip(layers, bit))]

    hm, total = run(
        functools.partial(first_kernel, sizes, h_table, len(h_arrays)),
        "first_product",
        [shape(order, cols_here), shape(height, cols_here, f32)],
        [*slots[:-1], *h_arrays],
        smem=[h_pattern, z_pattern],
        scratch=[pltpu.VMEM((height, order), jnp.bfloat16)],
    )
    product = run(
        functools.partial(finish_kernel, sizes),
        "finish_product",
        [shape(height, cols_here)],
        [hm, total, slots[-1]],
        smem=[z_pattern],
    )[0]

    gathered = {0: product}
    for bit in row_bits:
        for dr, piece in list(gathered.items()):
            gathered[dr ^ bit] = lax.ppermute(piece, "row", flip(rows, bit))
    row_offsets = list(gathered)
    outgoing = run(
        functools.partial(route_kernel, sizes, row_offsets),
        "route",
        [shape(q, cols_here)] * cols,
        [gathered[o] for o in row_offsets],
        after=[crossed[-1]],
        scratch=[pltpu.VMEM((cols * q, cols_here), jnp.bfloat16)],
    )
    messages = [outgoing[0]] + [
        lax.ppermute(outgoing[d], "col", flip(cols, d)) for d in range(1, cols)
    ]

    def share(group, gate):
        arrays, table = [], []
        for s in group:
            table += [(len(arrays), 0, 0, s), (len(arrays) + 1, 0, layer_bits[0], s)]
            arrays += [slots[s], crossed[s - 1]]
        for bit in layer_bits[1:]:
            packed, starts = pack(arrays, gate), offsets(arrays)
            table += [
                (len(arrays), starts[index] + row, dl ^ bit, s) for index, row, dl, s in table
            ]
            arrays = arrays + [lax.ppermute(packed, "layer", flip(layers, bit))]
        return arrays, table

    def lay_out(group, tile, gate):
        arrays, table = share([s for s in group if s], gate)
        place_of = {(dl, s): (index + len(tile), row) for index, row, dl, s in table}
        return run(
            functools.partial(layers_kernel, sizes, place_of, group),
            "layers",
            [shape(rows_here, order if len(group) > 1 else cols_here)],
            [*tile, *arrays],
            smem=[z_pattern],
        )[0]

    z_early = lay_out(list(range(cols - 1)), [inv_root], [product])
    z_late = lay_out([cols - 1], [], [outgoing[0]])
    return run(
        functools.partial(second_kernel, sizes),
        "second_product",
        [shape(*hamiltonian.shape)],
        [z_early, z_late, *messages],
        scratch=[pltpu.VMEM((q, order), jnp.bfloat16)],
    )[0]


def solution(mesh):
    rows, cols, layers = (mesh.shape[a] for a in ("row", "col", "layer"))

    def whole(hamiltonian, inv_root, h_pattern, z_pattern):
        order = hamiltonian.shape[0]
        cols_here = order // cols
        sizes = Sizes(
            rows, cols, layers, order // rows, cols_here, cols_here // layers, cols // rows
        )
        return jax.shard_map(
            functools.partial(local, sizes),
            mesh=mesh,
            in_specs=(P("row", ("col", "layer")), P("row", "col"), P(), P()),
            out_specs=P("row", ("col", "layer")),
            check_vma=False,
        )(hamiltonian, inv_root, h_pattern, z_pattern)

    return whole
```

time: 74.2 us -> 58.5 us (0.79)
  starting transfers between devices: 31.8 us -> 21.9 us
  waiting for transfers between devices: 32.5 us -> 24.7 us
  local copies, waits for them, and re-layouts: 1.97 us -> 4.25 us
    ppermute x13 -> x10, starting transfers between devices: 26.5 us -> 17.2 us  [the longest x3 8.61 us: local(): slots.append(lax.ppermute(slots[-1], 'col', ring))]
    ppermute x13 -> x10, waiting for transfers between devices: 30.1 us -> 21.4 us  [the longest x3 8.2 us: local(): lax.ppermute(slots[s], 'layer', flip(layers, layer_bits[0]))]
    unnamed x10 -> x12, local copies, waits for them, and re-layouts: 0.96 us -> 3.28 us
    ppermute x3, waiting for transfers between devices: 0.01 us -> 2.3 us  [local(): lax.ppermute(source, axis, flip(rows if axis == 'row' else layers, bit))]
    ppermute x2, waiting for transfers between devices: 1.95 us -> 0.01 us  [share(): arrays = arrays + [lax.ppermute(packed, 'layer', flip(layers, bit))]]
    pallas_call x16 -> x10, Pallas kernels: 7.29 us -> 7.22 us  [run(): pl.pallas_call(body, out_shape=list(outs), in_specs=[pl.BlockSpec(memory_...]
  transfers between devices with their start and end apart: 19 -> 16, of which waited for: 11 -> 10; matrix products, arithmetic and copies ran while one was open for 0% -> 0% of each run, Pallas kernels for 7% -> 9%
where the time goes in v5:
time: 58.5 us; the launch traced here: 58.3 us
  waiting for transfers between devices  24.7 us (42%)
  starting transfers between devices  21.9 us (37%)
  Pallas kernels  7.22 us (12%)
  local copies, waits for them, and re-layouts  4.25 us (7%)
    ppermute x3, starting transfers between devices, local(): slots.append(lax.ppermute(slots[-1], 'col', ring))  8.61 us
    ppermute x3, waiting for transfers between devices, local(): lax.ppermute(slots[s], 'layer', flip(layers, layer_bits[0]))  8.2 us
    ppermute x3, waiting for transfers between devices, local(): lax.ppermute(outgoing[d], 'col', flip(cols, d))  7.43 us
    pallas_call x10, Pallas kernels, run(): pl.pallas_call(body, out_shape=list(outs), in_specs=[pl.BlockSpec(memory_...  7.22 us
    ppermute x3, waiting for transfers between devices, local(): slots.append(lax.ppermute(slots[-1], 'col', ring))  5.57 us
    ppermute x3, starting transfers between devices, local(): lax.ppermute(source, axis, flip(rows if axis == 'row' else layers, bit))  4.57 us
    ppermute x3, starting transfers between devices, local(): lax.ppermute(outgoing[d], 'col', flip(cols, d))  4.45 us
    unnamed x12, local copies, waits for them, and re-layouts  3.28 us
  transfers between devices with their start and end apart: 16, of which 10 were waited for; matrix products, arithmetic and copies ran while one was open for 0% of the time, Pallas kernels for 9%

profile of v5, /device:TPU:0, one launch (start us, length us, event | category | flops | bytes accessed | tf_op | source)
XLA Modules:
  0.0 58.3 jit_solution(396674625696698266)
XLA Ops:
  0.0 1.0 %constant_dynamic-slice_fusion = bf16[2,1,128,512]{3,2,1,0:T(8,128)(2,1)S(1)} fusion(bf16[2,4,128,512]{3,2,1,0:T(8,128)(2,1)} %bitcast.4, s32[]{:T(128)S(6)} %select_n.4), kind=kLoop, calls=%fused_computation | loop fusion | bytes 524292 | tf_op jit(solution)/shard_map/jit(dynamic_index_in_dim)/dynamic_slice | solution.py:234
  1.0 4.1 %collective-permute-start = (bf16[256,512]{1,0:T(8,128)(2,1)S(1)}, bf16[256,512]{1,0:T(8,128)(2,1)S(1)}, u32[]{:S(2)}, u32[]{:S(2)}) collective-permute-start(bf16[256,512]{1,0:T(8,128)(2,1)S(1)} %bitcast.5), channel_id=1, source_target_pairs={{0,8},{8,12},{12,4},{4,0},{1,9},{9,13},{13,5},{5,1},{2,10},{10,14}... | collective-permute-start | bytes 786440 | tf_op jit(solution)/shard_map/ppermute | solution.py:239
  5.1 1.5 %collective-permute-start.4 = (bf16[1024,128]{1,0:T(8,128)(2,1)}, bf16[1024,128]{1,0:T(8,128)(2,1)S(1)}, u32[]{:S(2)}, u32[]{:S(2)}) collective-permute-start(bf16[1024,128]{1,0:T(8,128)(2,1)} %refs_5_.1), channel_id=1, source_target_pairs={{0,2},{1,3},{2,0},{3,1},{4,6},{5,7},{6,4},{7,5},{8,10},{9,11},{10,... | collective-permute-start | bytes 786440 | tf_op jit(solution)/shard_map/ppermute | solution.py:258
  6.6 1.5 %collective-permute-start.5 = (bf16[1024,128]{1,0:T(8,128)(2,1)}, bf16[1024,128]{1,0:T(8,128)(2,1)S(1)}, u32[]{:S(2)}, u32[]{:S(2)}) collective-permute-start(bf16[1024,128]{1,0:T(8,128)(2,1)} %refs_5_.1), channel_id=1, source_target_pairs={{0,16},{16,0},{1,17},{17,1},{2,18},{18,2},{3,19},{19,3},{4,20},{20... | collective-permute-start | bytes 786440 | tf_op jit(solution)/shard_map/ppermute | solution.py:258
  8.1 2.6 %collective-permute-done.refs_1_.refs_3_.refs_0_.refs_2_ = bf16[256,512]{1,0:T(8,128)(2,1)S(1)} collective-permute-done((bf16[256,512]{1,0:T(8,128)(2,1)S(1)}, bf16[256,512]{1,0:T(8,128)(2,1)S(1)}, u32[]{:S(2)}, u32[]{:S(2)}) %collective-permute-start) | collective-permute-done | bytes 262176 | tf_op jit(solution)/shard_map/ppermute | solution.py:239
  10.6 1.5 %collective-permute-start.1 = (bf16[256,512]{1,0:T(8,128)(2,1)S(1)}, bf16[256,512]{1,0:T(8,128)(2,1)S(1)}, u32[]{:S(2)}, u32[]{:S(2)}) collective-permute-start(bf16[256,512]{1,0:T(8,128)(2,1)S(1)} %collective-permute-done.refs_1_.refs_3_.refs_0_.refs_2_), channel_id=1, source_target_pairs={{0,2},{1,3},{2,0},{3,1},{4,6},{5,7},{6,4},{7,5},{8,10},{9,11},{10,... | collective-permute-start | bytes 786440 | tf_op jit(solution)/shard_map/ppermute | solution.py:247
  12.1 3.4 %collective-permute-start.2 = (bf16[256,512]{1,0:T(8,128)(2,1)S(1)}, bf16[256,512]{1,0:T(8,128)(2,1)S(1)}, u32[]{:S(2)}, u32[]{:S(2)}) collective-permute-start(bf16[256,512]{1,0:T(8,128)(2,1)S(1)} %collective-permute-done.refs_1_.refs_3_.refs_0_.refs_2_), channel_id=1, source_target_pairs={{0,8},{8,12},{12,4},{4,0},{1,9},{9,13},{13,5},{5,1},{2,10},{10,14}... | collective-permute-start | bytes 786440 | tf_op jit(solution)/shard_map/ppermute | solution.py:239
  15.6 1.6 %collective-permute-start.6 = (bf16[1024,128]{1,0:T(8,128)(2,1)S(1)}, bf16[1024,128]{1,0:T(8,128)(2,1)S(1)}, u32[]{:S(2)}, u32[]{:S(2)}) collective-permute-start(bf16[1024,128]{1,0:T(8,128)(2,1)S(1)} %pack.4), channel_id=1, source_target_pairs={{0,16},{16,0},{1,17},{17,1},{2,18},{18,2},{3,19},{19,3},{4,20},{20... | collective-permute-start | bytes 786440 | tf_op jit(solution)/shard_map/ppermute | solution.py:258
  17.1 1.5 %collective-permute-done.1.refs_5_.refs_1_.refs_3_ = bf16[256,512]{1,0:T(8,128)(2,1)S(1)} collective-permute-done((bf16[256,512]{1,0:T(8,128)(2,1)S(1)}, bf16[256,512]{1,0:T(8,128)(2,1)S(1)}, u32[]{:S(2)}, u32[]{:S(2)}) %collective-permute-start.1) | collective-permute-done | bytes 262176 | tf_op jit(solution)/shard_map/ppermute | solution.py:247
  18.7 1.3 %collective-permute-done.2.refs_4_.refs_2_ = bf16[256,512]{1,0:T(8,128)(2,1)S(1)} collective-permute-done((bf16[256,512]{1,0:T(8,128)(2,1)S(1)}, bf16[256,512]{1,0:T(8,128)(2,1)S(1)}, u32[]{:S(2)}, u32[]{:S(2)}) %collective-permute-start.2) | collective-permute-done | bytes 262176 | tf_op jit(solution)/shard_map/ppermute | solution.py:239
  19.9 2.3 %collective-permute-done.6.refs_3_.refs_8_ = bf16[1024,128]{1,0:T(8,128)(2,1)S(1)} collective-permute-done((bf16[1024,128]{1,0:T(8,128)(2,1)S(1)}, bf16[1024,128]{1,0:T(8,128)(2,1)S(1)}, u32[]{:S(2)}, u32[]{:S(2)}) %collective-permute-start.6) | collective-permute-done | bytes 262176 | tf_op jit(solution)/shard_map/ppermute | solution.py:258
  23.3 1.1 %collective-permute-start.8 = (bf16[256,512]{1,0:T(8,128)(2,1)S(1)}, bf16[256,512]{1,0:T(8,128)(2,1)S(1)}, u32[]{:S(2)}, u32[]{:S(2)}) collective-permute-start(bf16[256,512]{1,0:T(8,128)(2,1)S(1)} %collective-permute-done.2.refs_4_.refs_2_), channel_id=1, source_target_pairs={{0,8},{8,12},{12,4},{4,0},{1,9},{9,13},{13,5},{5,1},{2,10},{10,14}... | collective-permute-start | bytes 786440 | tf_op jit(solution)/shard_map/ppermute | solution.py:239
  25.0 1.0 %collective-permute-done.7.refs_9_ = bf16[4096,128]{1,0:T(8,128)(2,1)S(1)} collective-permute-done((bf16[4096,128]{1,0:T(8,128)(2,1)S(1)}, bf16[4096,128]{1,0:T(8,128)(2,1)S(1)}, u32[]{:S(2)}, u32[]{:S(2)}) %collective-permute-start.7) | collective-permute-done | bytes 1048608 | tf_op jit(solution)/shard_map/ppermute | solution.py:265
  28.3 2.0 %first_product.1 = (bf16[2048,512]{1,0:T(8,128)(2,1)S(1)}, f32[256,512]{1,0:T(8,128)S(1)}) custom-call(s32[8,8]{1,0:T(8,128)S(1)} %copy-done.5, s32[8,8]{1,0:T(8,128)S(1)} %copy-done.3, bf16[256,512]{1,0:T(8,128)(2,1)S(1)} %bitcast.6, bf16[256,512]{1,0:T(8,128)(2,1)S(1)} %collective-permute-done.refs_1_.refs_3_.refs_0_.refs_2_, ...), custom_call_target="tpu_custom_call" | custom-call | bytes 6553600 | tf_op jit(solution)/shard_map/first_product/pallas_call | solution.py:51
  30.3 1.7 %collective-permute-done.8.refs_3_.refs_0_.refs_1_ = bf16[256,512]{1,0:T(8,128)(2,1)S(1)} collective-permute-done((bf16[256,512]{1,0:T(8,128)(2,1)S(1)}, bf16[256,512]{1,0:T(8,128)(2,1)S(1)}, u32[]{:S(2)}, u32[]{:S(2)}) %collective-permute-start.8) | collective-permute-done | bytes 262176 | tf_op jit(solution)/shard_map/ppermute | solution.py:239
  33.7 1.5 %collective-permute-start.11 = (bf16[256,512]{1,0:T(8,128)(2,1)S(1)}, bf16[256,512]{1,0:T(8,128)(2,1)S(1)}, u32[]{:S(2)}, u32[]{:S(2)}) collective-permute-start(bf16[256,512]{1,0:T(8,128)(2,1)S(1)} %finish_product.1.refs_4_.refs_0_), channel_id=1, source_target_pairs={{0,16},{16,0},{1,17},{17,1},{2,18},{18,2},{3,19},{19,3},{4,20},{20... | collective-permute-start | bytes 786440 | tf_op jit(solution)/shard_map/ppermute | solution.py:286
  35.2 6.7 %collective-permute-done.10.refs_2_.refs_1_ = bf16[256,512]{1,0:T(8,128)(2,1)S(1)} collective-permute-done((bf16[256,512]{1,0:T(8,128)(2,1)S(1)}, bf16[256,512]{1,0:T(8,128)(2,1)S(1)}, u32[]{:S(2)}, u32[]{:S(2)}) %collective-permute-start.10) | collective-permute-done | bytes 262176 | tf_op jit(solution)/shard_map/ppermute | solution.py:247
  42.3 1.0 %collective-permute-start.13 = (bf16[128,512]{1,0:T(8,128)(2,1)S(1)}, bf16[128,512]{1,0:T(8,128)(2,1)S(1)}, u32[]{:S(2)}, u32[]{:S(2)}) collective-permute-start(bf16[128,512]{1,0:T(8,128)(2,1)S(1)} %get-tuple-element.14), channel_id=1, source_target_pairs={{0,4},{4,0},{8,12},{12,8},{1,5},{5,1},{9,13},{13,9},{2,6},{6,2},{1... | collective-permute-start | bytes 393224 | tf_op jit(solution)/shard_map/ppermute | solution.py:297
  43.3 1.1 %collective-permute-start.14 = (bf16[128,512]{1,0:T(8,128)(2,1)S(1)}, bf16[128,512]{1,0:T(8,128)(2,1)S(1)}, u32[]{:S(2)}, u32[]{:S(2)}) collective-permute-start(bf16[128,512]{1,0:T(8,128)(2,1)S(1)} %get-tuple-element.15), channel_id=1, source_target_pairs={{0,8},{4,12},{8,0},{12,4},{1,9},{5,13},{9,1},{13,5},{2,10},{6,14},... | collective-permute-start | bytes 393224 | tf_op jit(solution)/shard_map/ppermute | solution.py:297
  44.4 2.3 %collective-permute-start.15 = (bf16[128,512]{1,0:T(8,128)(2,1)S(1)}, bf16[128,512]{1,0:T(8,128)(2,1)S(1)}, u32[]{:S(2)}, u32[]{:S(2)}) collective-permute-start(bf16[128,512]{1,0:T(8,128)(2,1)S(1)} %get-tuple-element.16), channel_id=1, source_target_pairs={{0,12},{4,8},{8,4},{12,0},{1,13},{5,9},{9,5},{13,1},{2,14},{6,10},... | collective-permute-start | bytes 393224 | tf_op jit(solution)/shard_map/ppermute | solution.py:297
  47.6 1.2 %layers.2.refs_0_ = bf16[1024,2048]{1,0:T(8,128)(2,1)S(1)} custom-call(s32[8,8]{1,0:T(8,128)S(1)} %copy-done.4, bf16[1024,512]{1,0:T(8,128)(2,1)S(1)} %copy-done, bf16[256,512]{1,0:T(8,128)(2,1)S(1)} %collective-permute-done.refs_1_.refs_3_.refs_0_.refs_2_, bf16[256,512]{1,0:T(8,128)(2,1)S(1)} %collective-permute-done.1.refs_5_.refs_1_.refs_3_, ...), custom_call_target="tpu_custom_call" | custom-call | bytes 7340032 | tf_op jit(solution)/shard_map/layers/pallas_call | solution.py:51
  48.8 1.8 %collective-permute-done.13.refs_3_ = bf16[128,512]{1,0:T(8,128)(2,1)S(1)} collective-permute-done((bf16[128,512]{1,0:T(8,128)(2,1)S(1)}, bf16[128,512]{1,0:T(8,128)(2,1)S(1)}, u32[]{:S(2)}, u32[]{:S(2)}) %collective-permute-start.13) | collective-permute-done | bytes 131104 | tf_op jit(solution)/shard_map/ppermute | solution.py:297
  50.6 5.7 %collective-permute-done.14.refs_4_ = bf16[128,512]{1,0:T(8,128)(2,1)S(1)} collective-permute-done((bf16[128,512]{1,0:T(8,128)(2,1)S(1)}, bf16[128,512]{1,0:T(8,128)(2,1)S(1)}, u32[]{:S(2)}, u32[]{:S(2)}) %collective-permute-start.14) | collective-permute-done | bytes 131104 | tf_op jit(solution)/shard_map/ppermute | solution.py:297
  56.3 2.0 %second_product.1 = bf16[1024,128]{1,0:T(8,128)(2,1)} custom-call(bf16[1024,2048]{1,0:T(8,128)(2,1)S(1)} %layers.2.refs_0_, bf16[1024,512]{1,0:T(8,128)(2,1)S(1)} %layers.3.refs_1_, bf16[128,512]{1,0:T(8,128)(2,1)S(1)} %get-tuple-element.13.refs_2_, bf16[128,512]{1,0:T(8,128)(2,1)S(1)} %collective-permute-done.13.refs_3_, ...), custom_call_target="tpu_custom_call" | custom-call | bytes 6553600 | tf_op jit(solution)/shard_map/second_product/pallas_call | solution.py:51
  (31 shorter events, 6.8 us)
Async XLA Ops:
  1.0 9.7 %collective-permute-start = (bf16[256,512]{1,0:T(8,128)(2,1)S(1)}, bf16[256,512]{1,0:T(8,128)(2,1)S(1)}, u32[]{:S(2)}, u32[]{:S(2)}) collective-permute-start(bf16[256,512]{1,0:T(8,128)(2,1)S(1)} %bitcast.5), channel_id=1, source_target_pairs={{0,8},{8,12},{12,4},{4,0},{1,9},{9,13},{13,5},{5,1},{2,10},{10,14}... | collective-permute-start | bytes 786440 | tf_op jit(solution)/shard_map/ppermute | solution.py:239
  5.1 10.5 %collective-permute-start.4 = (bf16[1024,128]{1,0:T(8,128)(2,1)}, bf16[1024,128]{1,0:T(8,128)(2,1)S(1)}, u32[]{:S(2)}, u32[]{:S(2)}) collective-permute-start(bf16[1024,128]{1,0:T(8,128)(2,1)} %refs_5_.1), channel_id=1, source_target_pairs={{0,2},{1,3},{2,0},{3,1},{4,6},{5,7},{6,4},{7,5},{8,10},{9,11},{10,... | collective-permute-start | bytes 786440 | tf_op jit(solution)/shard_map/ppermute | solution.py:258
  6.6 10.5 %collective-permute-start.5 = (bf16[1024,128]{1,0:T(8,128)(2,1)}, bf16[1024,128]{1,0:T(8,128)(2,1)S(1)}, u32[]{:S(2)}, u32[]{:S(2)}) collective-permute-start(bf16[1024,128]{1,0:T(8,128)(2,1)} %refs_5_.1), channel_id=1, source_target_pairs={{0,16},{16,0},{1,17},{17,1},{2,18},{18,2},{3,19},{19,3},{4,20},{20... | collective-permute-start | bytes 786440 | tf_op jit(solution)/shard_map/ppermute | solution.py:258
  10.6 8.0 %collective-permute-start.1 = (bf16[256,512]{1,0:T(8,128)(2,1)S(1)}, bf16[256,512]{1,0:T(8,128)(2,1)S(1)}, u32[]{:S(2)}, u32[]{:S(2)}) collective-permute-start(bf16[256,512]{1,0:T(8,128)(2,1)S(1)} %collective-permute-done.refs_1_.refs_3_.refs_0_.refs_2_), channel_id=1, source_target_pairs={{0,2},{1,3},{2,0},{3,1},{4,6},{5,7},{6,4},{7,5},{8,10},{9,11},{10,... | collective-permute-start | bytes 786440 | tf_op jit(solution)/shard_map/ppermute | solution.py:247
  12.1 7.8 %collective-permute-start.2 = (bf16[256,512]{1,0:T(8,128)(2,1)S(1)}, bf16[256,512]{1,0:T(8,128)(2,1)S(1)}, u32[]{:S(2)}, u32[]{:S(2)}) collective-permute-start(bf16[256,512]{1,0:T(8,128)(2,1)S(1)} %collective-permute-done.refs_1_.refs_3_.refs_0_.refs_2_), channel_id=1, source_target_pairs={{0,8},{8,12},{12,4},{4,0},{1,9},{9,13},{13,5},{5,1},{2,10},{10,14}... | collective-permute-start | bytes 786440 | tf_op jit(solution)/shard_map/ppermute | solution.py:239
  15.6 6.7 %collective-permute-start.6 = (bf16[1024,128]{1,0:T(8,128)(2,1)S(1)}, bf16[1024,128]{1,0:T(8,128)(2,1)S(1)}, u32[]{:S(2)}, u32[]{:S(2)}) collective-permute-start(bf16[1024,128]{1,0:T(8,128)(2,1)S(1)} %pack.4), channel_id=1, source_target_pairs={{0,16},{16,0},{1,17},{17,1},{2,18},{18,2},{3,19},{19,3},{4,20},{20... | collective-permute-start | bytes 786440 | tf_op jit(solution)/shard_map/ppermute | solution.py:258
  22.2 1.0 %copy-start.1 = (bf16[1024,128]{1,0:T(8,128)(2,1)S(1)}, bf16[1024,128]{1,0:T(8,128)(2,1)}, u32[]{:S(2)}) copy-start(bf16[1024,128]{1,0:T(8,128)(2,1)} %refs_5_.1) | copy-start | bytes 786436
  23.3 2.7 %collective-permute-start.7 = (bf16[4096,128]{1,0:T(8,128)(2,1)S(1)}, bf16[4096,128]{1,0:T(8,128)(2,1)S(1)}, u32[]{:S(2)}, u32[]{:S(2)}) collective-permute-start(bf16[4096,128]{1,0:T(8,128)(2,1)S(1)} %pack.5), channel_id=1, source_target_pairs={{0,1},{1,0},{2,3},{3,2},{4,5},{5,4},{6,7},{7,6},{8,9},{9,8},{10,11... | collective-permute-start | bytes 3145736 | tf_op jit(solution)/shard_map/ppermute | solution.py:265
  23.3 8.7 %collective-permute-start.8 = (bf16[256,512]{1,0:T(8,128)(2,1)S(1)}, bf16[256,512]{1,0:T(8,128)(2,1)S(1)}, u32[]{:S(2)}, u32[]{:S(2)}) collective-permute-start(bf16[256,512]{1,0:T(8,128)(2,1)S(1)} %collective-permute-done.2.refs_4_.refs_2_), channel_id=1, source_target_pairs={{0,8},{8,12},{12,4},{4,0},{1,9},{9,13},{13,5},{5,1},{2,10},{10,14}... | collective-permute-start | bytes 786440 | tf_op jit(solution)/shard_map/ppermute | solution.py:239
  24.5 8.5 %collective-permute-start.3 = (bf16[256,512]{1,0:T(8,128)(2,1)S(1)}, bf16[256,512]{1,0:T(8,128)(2,1)S(1)}, u32[]{:S(2)}, u32[]{:S(2)}) collective-permute-start(bf16[256,512]{1,0:T(8,128)(2,1)S(1)} %collective-permute-done.2.refs_4_.refs_2_), channel_id=1, source_target_pairs={{0,2},{1,3},{2,0},{3,1},{4,6},{5,7},{6,4},{7,5},{8,10},{9,11},{10,... | collective-permute-start | bytes 786440 | tf_op jit(solution)/shard_map/ppermute | solution.py:247
  26.0 1.0 %copy-start.2 = (bf16[1024,128]{1,0:T(8,128)(2,1)S(1)}, bf16[1024,128]{1,0:T(8,128)(2,1)}, u32[]{:S(2)}) copy-start(bf16[1024,128]{1,0:T(8,128)(2,1)} %refs_5_.1) | copy-start | bytes 786436
  26.9 0.7 %copy-start.3 = (s32[8,8]{1,0:T(8,128)S(1)}, s32[8,8]{1,0:T(8,128)}, u32[]{:S(2)}) copy-start(s32[8,8]{1,0:T(8,128)} %refs_0_.9) | copy-start | bytes 772
  27.6 0.7 %copy-start.5 = (s32[8,8]{1,0:T(8,128)S(1)}, s32[8,8]{1,0:T(8,128)}, u32[]{:S(2)}) copy-start(s32[8,8]{1,0:T(8,128)} %refs_0_.6) | copy-start | bytes 772
  30.3 16.5 %copy-start.4 = (s32[8,8]{1,0:T(8,128)S(1)}, s32[8,8]{1,0:T(8,128)}, u32[]{:S(2)}) copy-start(s32[8,8]{1,0:T(8,128)} %refs_0_.9) | copy-start | bytes 772
  32.0 15.5 %copy-start = (bf16[1024,512]{1,0:T(8,128)(2,1)S(1)}, bf16[1024,512]{1,0:T(8,128)(2,1)}, u32[]{:S(2)}) copy-start(bf16[1024,512]{1,0:T(8,128)(2,1)} %refs_1_.3) | copy-start | bytes 3145732
  33.1 14.5 %collective-permute-start.9 = (bf16[1024,512]{1,0:T(8,128)(2,1)S(1)}, bf16[1024,512]{1,0:T(8,128)(2,1)S(1)}, u32[]{:S(2)}, u32[]{:S(2)}) collective-permute-start(bf16[1024,512]{1,0:T(8,128)(2,1)S(1)} %pack.6), channel_id=1, source_target_pairs={{0,1},{1,0},{2,3},{3,2},{4,5},{5,4},{6,7},{7,6},{8,9},{9,8},{10,11... | collective-permute-start | bytes 3145736 | tf_op jit(solution)/shard_map/ppermute | solution.py:310
  33.1 8.7 %collective-permute-start.10 = (bf16[256,512]{1,0:T(8,128)(2,1)S(1)}, bf16[256,512]{1,0:T(8,128)(2,1)S(1)}, u32[]{:S(2)}, u32[]{:S(2)}) collective-permute-start(bf16[256,512]{1,0:T(8,128)(2,1)S(1)} %collective-permute-done.8.refs_3_.refs_0_.refs_1_), channel_id=1, source_target_pairs={{0,2},{1,3},{2,0},{3,1},{4,6},{5,7},{6,4},{7,5},{8,10},{9,11},{10,... | collective-permute-start | bytes 786440 | tf_op jit(solution)/shard_map/ppermute | solution.py:247
  33.7 8.4 %collective-permute-start.11 = (bf16[256,512]{1,0:T(8,128)(2,1)S(1)}, bf16[256,512]{1,0:T(8,128)(2,1)S(1)}, u32[]{:S(2)}, u32[]{:S(2)}) collective-permute-start(bf16[256,512]{1,0:T(8,128)(2,1)S(1)} %finish_product.1.refs_4_.refs_0_), channel_id=1, source_target_pairs={{0,16},{16,0},{1,17},{17,1},{2,18},{18,2},{3,19},{19,3},{4,20},{20... | collective-permute-start | bytes 786440 | tf_op jit(solution)/shard_map/ppermute | solution.py:286
  42.2 4.5 %collective-permute-start.12 = (bf16[512,512]{1,0:T(8,128)(2,1)S(1)}, bf16[512,512]{1,0:T(8,128)(2,1)S(1)}, u32[]{:S(2)}, u32[]{:S(2)}) collective-permute-start(bf16[512,512]{1,0:T(8,128)(2,1)S(1)} %pack.7), channel_id=1, source_target_pairs={{0,1},{1,0},{2,3},{3,2},{4,5},{5,4},{6,7},{7,6},{8,9},{9,8},{10,11... | collective-permute-start | bytes 1572872 | tf_op jit(solution)/shard_map/ppermute | solution.py:310
  42.3 8.3 %collective-permute-start.13 = (bf16[128,512]{1,0:T(8,128)(2,1)S(1)}, bf16[128,512]{1,0:T(8,128)(2,1)S(1)}, u32[]{:S(2)}, u32[]{:S(2)}) collective-permute-start(bf16[128,512]{1,0:T(8,128)(2,1)S(1)} %get-tuple-element.14), channel_id=1, source_target_pairs={{0,4},{4,0},{8,12},{12,8},{1,5},{5,1},{9,13},{13,9},{2,6},{6,2},{1... | collective-permute-start | bytes 393224 | tf_op jit(solution)/shard_map/ppermute | solution.py:297
  43.3 12.9 %collective-permute-start.14 = (bf16[128,512]{1,0:T(8,128)(2,1)S(1)}, bf16[128,512]{1,0:T(8,128)(2,1)S(1)}, u32[]{:S(2)}, u32[]{:S(2)}) collective-permute-start(bf16[128,512]{1,0:T(8,128)(2,1)S(1)} %get-tuple-element.15), channel_id=1, source_target_pairs={{0,8},{4,12},{8,0},{12,4},{1,9},{5,13},{9,1},{13,5},{2,10},{6,14},... | collective-permute-start | bytes 393224 | tf_op jit(solution)/shard_map/ppermute | solution.py:297
  44.4 11.8 %collective-permute-start.15 = (bf16[128,512]{1,0:T(8,128)(2,1)S(1)}, bf16[128,512]{1,0:T(8,128)(2,1)S(1)}, u32[]{:S(2)}, u32[]{:S(2)}) collective-permute-start(bf16[128,512]{1,0:T(8,128)(2,1)S(1)} %get-tuple-element.16), channel_id=1, source_target_pairs={{0,12},{4,8},{8,4},{12,0},{1,13},{5,9},{9,5},{13,1},{2,14},{6,10},... | collective-permute-start | bytes 393224 | tf_op jit(solution)/shard_map/ppermute | solution.py:297

commit v6 on v5

v6 whole, which is shorter than its diff:
```python
import functools
from typing import NamedTuple

import jax
import jax.numpy as jnp
from jax import lax
from jax.experimental import pallas as pl
from jax.experimental.pallas import tpu as pltpu
from jax.sharding import PartitionSpec as P

BS = 256
MARGIN = 4 * 1024 * 1024


class Sizes(NamedTuple):
    rows: int
    cols: int
    layers: int
    rows_here: int
    cols_here: int
    quarter: int
    per: int


def bits_of(size):
    return [1 << b for b in reversed(range(size.bit_length() - 1))]


def flip(size, bit):
    return [(i, i ^ bit) for i in range(size)]


def mod(a, n):
    return lax.rem(a + n, n)


def place():
    return lax.axis_index("row"), lax.axis_index("col"), lax.axis_index("layer")


def run(kernel, name, outs, arrays, smem=(), after=(), scratch=(), flops=0):
    size = sum(a.size * a.dtype.itemsize for a in arrays)
    size += sum(o.size * o.dtype.itemsize for o in outs)
    for kept in scratch:
        size += kept.shape[0] * kept.shape[1] * jnp.dtype(kept.dtype).itemsize
    skip = len(smem) + len(arrays)

    def body(*refs):
        kernel(*refs[:skip], *refs[skip + len(after) :])

    return pl.pallas_call(
        body,
        out_shape=list(outs),
        in_specs=[pl.BlockSpec(memory_space=pltpu.SMEM)] * len(smem)
        + [pl.BlockSpec(memory_space=pltpu.VMEM)] * len(arrays)
        + [pl.BlockSpec(memory_space=pl.ANY)] * len(after),
        out_specs=[pl.BlockSpec(memory_space=pltpu.VMEM)] * len(outs),
        scratch_shapes=list(scratch),
        compiler_params=pltpu.CompilerParams(vmem_limit_bytes=size + MARGIN),
        cost_estimate=pl.CostEstimate(flops=flops, bytes_accessed=size, transcendentals=0),
        name=name,
    )(*smem, *arrays, *after)


def shape(rows, columns, dtype=jnp.bfloat16):
    return jax.ShapeDtypeStruct((rows, columns), dtype)


def keep_block(pattern, i, j, block):
    return jnp.where(pattern[i, j] > 0, block, jnp.zeros_like(block))


def strip_start(l, half, sizes):
    return pl.multiple_of(half * sizes.cols_here + l * sizes.quarter, sizes.quarter)


def columns_of(cc, sizes):
    return pl.ds(pl.multiple_of(cc * sizes.cols_here, sizes.cols_here), sizes.cols_here)


def mask_strip(zp, r, l, half, cc, strip, sizes):
    block_row = (r * sizes.rows_here + half * sizes.cols_here + l * sizes.quarter) // BS
    first = cc * (sizes.cols_here // BS)
    return jnp.concatenate(
        [
            keep_block(zp, block_row, first + t, strip[:, t * BS : (t + 1) * BS])
            for t in range(sizes.cols_here // BS)
        ],
        axis=1,
    )


def mask_piece(zp, r, l, cc, piece, sizes):
    q = sizes.quarter
    return jnp.concatenate(
        [
            mask_strip(zp, r, l, half, cc, piece[half * q : (half + 1) * q, :], sizes)
            for half in range(sizes.per)
        ],
        axis=0,
    )


def pack_kernel(*refs):
    out, row = refs[-1], 0
    for ref in refs[:-1]:
        out[row : row + ref.shape[0], :] = ref[...]
        row += ref.shape[0]


def pack(pieces, after=()):
    height = sum(p.shape[0] for p in pieces)
    out = shape(height, pieces[0].shape[1])
    return run(pack_kernel, "pack", [out], pieces, after=after)[0]


def ring_place(c, cols):
    return jnp.where(c % 2 == 0, c // 2, cols - 1 - c // 2)


def ring_column(p, cols):
    return jnp.where(p < cols // 2, 2 * p, 2 * (cols - 1 - p) + 1)


def slot_column(c, s, cols):
    return ring_column(mod(ring_place(c, cols) - s, cols), cols)


def mask_kernel(sizes, numbers, zp, *refs):
    slots, before, out = refs[: len(numbers)], refs[len(numbers) : -1], refs[-1]
    r, c, l = place()
    if before:
        out[...] = before[0][...]
    for s, slot in zip(numbers, slots):
        cc = slot_column(c, s, sizes.cols)
        out[:, columns_of(cc, sizes)] = mask_piece(zp, r, l, cc, slot[...], sizes)


def first_kernel(sizes, top, zm, h_own, h_other, out):
    q, (_, _, l) = sizes.quarter, place()
    for side, h in ((l, h_own), (l ^ 1, h_other)):
        part = jnp.dot(zm[...], h[...], preferred_element_type=jnp.float32).astype(out.dtype)
        for n, ll in enumerate((side, side ^ top)):
            out[:, pl.ds(pl.multiple_of(ll * q, q), q)] = part[:, n * q : (n + 1) * q]


def bring_kernel(sizes, h_table, hp, *refs):
    *pieces, piece, hm, piece_out = refs
    r, c, l = place()
    q, per_rows = sizes.quarter, sizes.rows_here // BS
    for h, (dr, dl) in zip(pieces, h_table):
        n = 1 if dl else 0
        block_col = (c * sizes.cols_here + (l ^ dl) * q) // BS
        for t in range(per_rows):
            j = (r ^ dr) * per_rows + t
            hm[pl.ds(pl.multiple_of(j * BS, BS), BS), n * q : (n + 1) * q] = keep_block(
                hp, j, block_col, h[t * BS : (t + 1) * BS, :]
            )
    piece_out[...] = piece[...]


def route_kernel(sizes, row_offsets, *refs):
    table, (r, _, _), q = refs[-1], place(), sizes.quarter
    for dr, piece in zip(row_offsets, refs[:-1]):
        for half in range(sizes.per):
            start = pl.multiple_of(((r ^ dr) * sizes.per + half) * q, q)
            table[pl.ds(start, q), :] = piece[half * q : (half + 1) * q, :]


def cut_kernel(sizes, table, *outs):
    c, q = lax.axis_index("col"), sizes.quarter
    for d, out in enumerate(outs):
        out[...] = table[pl.ds(pl.multiple_of((c ^ d) * q, q), q), :]


def layers_kernel(sizes, z_table, zp, *refs):
    cols, q = sizes.cols, sizes.quarter
    out, held = refs[-1], refs[:-1]
    r, c, l = place()
    for dl in range(sizes.layers):
        ll = l ^ dl
        for half in range(sizes.per):
            rows = pl.ds(strip_start(ll, half, sizes), q)
            for s in range(cols):
                cc = slot_column(c, s, cols)
                if s == 0:
                    strip = held[0][rows, :]
                else:
                    index, row = z_table[dl, s]
                    strip = held[index][row + half * q : row + (half + 1) * q, :]
                out[rows, columns_of(cc, sizes)] = mask_strip(zp, r, ll, half, cc, strip, sizes)


def second_kernel(sizes, part, z_full, *refs):
    messages, before, out = refs[: len(part)], refs[len(part) : -1], refs[-1]
    c = lax.axis_index("col")
    total = before[0][...] if before else None
    for d, message in zip(part, messages):
        added = lax.dot_general(
            z_full[:, columns_of(c ^ d, sizes)],
            message[...],
            (((1,), (1,)), ((), ())),
            preferred_element_type=jnp.float32,
        )
        total = added if total is None else total + added
    out[...] = total.astype(out.dtype)


def local(sizes, hamiltonian, inv_root, h_pattern, z_pattern):
    rows, cols, layers, per = sizes.rows, sizes.cols, sizes.layers, sizes.per
    q, cols_here, rows_here = sizes.quarter, sizes.cols_here, sizes.rows_here
    order = rows * rows_here
    height = per * q
    row_bits, layer_bits = bits_of(rows), bits_of(layers)
    f32 = jnp.float32

    striped = inv_root.reshape(per, layers, q, cols_here)
    l = lax.axis_index("layer")
    own = lax.dynamic_index_in_dim(striped, l, 1, keepdims=False).reshape(height, cols_here)
    trip = list(range(0, cols, 2)) + list(range(cols - 1, 0, -2))
    ring = [(trip[i], trip[(i + 1) % cols]) for i in range(cols)]
    slots = [own]
    for _ in range(1, cols):
        slots.append(lax.ppermute(slots[-1], "col", ring))

    def offsets(arrays):
        starts = [0]
        for array in arrays:
            starts.append(starts[-1] + array.shape[0])
        return starts

    top, low = layer_bits
    h_pieces, h_table = [hamiltonian], [(0, 0)]
    for dr in range(rows):
        for dl in (0, top):
            if dr or dl:
                perm = [
                    (r * layers + k, (r ^ dr) * layers + (k ^ dl))
                    for r in range(rows)
                    for k in range(layers)
                ]
                h_pieces.append(lax.ppermute(hamiltonian, ("row", "layer"), perm))
                h_table.append((dr, dl))
    h_own, first_slot = run(
        functools.partial(bring_kernel, sizes, h_table),
        "bring",
        [shape(order, 2 * q), shape(height, cols_here)],
        [*h_pieces, slots[1]],
        smem=[h_pattern],
    )

    def cross(piece):
        return lax.ppermute(piece, "layer", flip(layers, top))

    crossed = [cross(first_slot)] + [cross(slots[s]) for s in range(2, cols - 1)]
    h_sent = pack([h_own], [slots[-2]])
    h_other = lax.ppermute(h_sent, "layer", flip(layers, low))

    zm = []
    for numbers, after in ((range(cols - 1), [crossed[0]]), ([cols - 1], [])):
        zm = run(
            functools.partial(mask_kernel, sizes, numbers),
            "mask",
            [shape(height, order)],
            [*(slots[s] for s in numbers), *zm],
            smem=[z_pattern],
            after=after,
            flops=0 if after else 0,
        )
    product = run(
        functools.partial(first_kernel, sizes, top),
        "first_product",
        [shape(height, cols_here)],
        [*zm, h_sent, h_other],
    )[0]

    gathered = {0: product}
    for bit in row_bits:
        for dr, piece in list(gathered.items()):
            gathered[dr ^ bit] = lax.ppermute(piece, "row", flip(rows, bit))
    row_offsets = list(gathered)
    crossed.append(cross(pack([slots[-1]], [product])))
    table = run(
        functools.partial(route_kernel, sizes, row_offsets),
        "route",
        [shape(cols * q, cols_here)],
        [gathered[o] for o in row_offsets],
    )[0]
    outgoing = run(
        functools.partial(cut_kernel, sizes),
        "cut",
        [shape(q, cols_here)] * cols,
        [table],
        after=[crossed[-1]],
    )
    messages = [outgoing[0]] + [
        lax.ppermute(outgoing[d], "col", flip(cols, d)) for d in range(1, cols)
    ]

    def share(group, gate):
        arrays, table = [], []
        for s in group:
            table += [(len(arrays), 0, 0, s), (len(arrays) + 1, 0, layer_bits[0], s)]
            arrays += [slots[s], crossed[s - 1]]
        for bit in layer_bits[1:]:
            packed, starts = pack(arrays, gate), offsets(arrays)
            table += [
                (len(arrays), starts[index] + row, dl ^ bit, s) for index, row, dl, s in table
            ]
            arrays = arrays + [lax.ppermute(packed, "layer", flip(layers, bit))]
        return arrays, table

    held, z_table = [inv_root], {}
    for group, gate in ((range(1, cols - 1), [product]), ([cols - 1], [outgoing[0]])):
        arrays, entries = share(group, gate)
        for index, row, dl, s in entries:
            z_table[dl, s] = (index + len(held), row)
        held += arrays
    z_full = run(
        functools.partial(layers_kernel, sizes, z_table),
        "layers",
        [shape(rows_here, order)],
        held,
        smem=[z_pattern],
    )[0]
    total = []
    for part in (range(cols // 2), range(cols // 2, cols)):
        last_part = part[-1] == cols - 1
        total = run(
            functools.partial(second_kernel, sizes, part),
            "second_product",
            [shape(*hamiltonian.shape, jnp.bfloat16 if last_part else f32)],
            [z_full, *[messages[d] for d in part], *total],
        )
    return total[0]


def solution(mesh):
    rows, cols, layers = (mesh.shape[a] for a in ("row", "col", "layer"))

    def whole(hamiltonian, inv_root, h_pattern, z_pattern):
        order = hamiltonian.shape[0]
        cols_here = order // cols
        sizes = Sizes(
            rows, cols, layers, order // rows, cols_here, cols_here // layers, cols // rows
        )
        return jax.shard_map(
            functools.partial(local, sizes),
            mesh=mesh,
            in_specs=(P("row", ("col", "layer")), P("row", "col"), P(), P()),
            out_specs=P("row", ("col", "layer")),
            check_vma=False,
        )(hamiltonian, inv_root, h_pattern, z_pattern)

    return whole
```

time: 58.5 us -> 61.7 us (1.055)
  waiting for transfers between devices: 24.7 us -> 30.3 us
  local copies, waits for them, and re-layouts: 4.25 us -> 2.63 us
    ppermute x1, waiting for transfers between devices: 0.23 us -> 6.52 us  [local(): gathered[dr ^ bit] = lax.ppermute(piece, 'row', flip(rows, bit))]
    ppermute x7, waiting for transfers between devices: 11.5 us -> 15.3 us  [the longest x3 9.39 us: cross(): return lax.ppermute(piece, 'layer', flip(layers, top))]
    ppermute x3, waiting for transfers between devices: 5.57 us -> 2.1 us  [local(): slots.append(lax.ppermute(slots[-1], 'col', ring))]
    unnamed x12 -> x8, local copies, waits for them, and re-layouts: 3.28 us -> 1.65 us
    ppermute x3, waiting for transfers between devices: 7.43 us -> 6.43 us  [local(): lax.ppermute(outgoing[d], 'col', flip(cols, d))]
    ppermute x7, starting transfers between devices: 7.24 us -> 6.54 us  [the longest x3 3.49 us: local(): h_pieces.append(lax.ppermute(hamiltonian, ('row', 'layer'), perm))]
    pallas_call x10 -> x13, Pallas kernels: 7.22 us -> 6.87 us  [run(): pl.pallas_call(body, out_shape=list(outs), in_specs=[pl.BlockSpec(memory_...]
  transfers between devices with their start and end apart: 16 -> 16, of which waited for: 10 -> 9; matrix products, arithmetic and copies ran while one was open for 0% -> 0% of each run, Pallas kernels for 9% -> 9%
where the time goes in v6:
time: 61.7 us; the launch traced here: 61.4 us
  waiting for transfers between devices  30.3 us (49%)
  starting transfers between devices  21.5 us (35%)
  Pallas kernels  6.87 us (11%)
  local copies, waits for them, and re-layouts  2.63 us (4%)
    ppermute x3, waiting for transfers between devices, cross(): return lax.ppermute(piece, 'layer', flip(layers, top))  9.39 us
    ppermute x3, starting transfers between devices, local(): slots.append(lax.ppermute(slots[-1], 'col', ring))  9.05 us
    pallas_call x13, Pallas kernels, run(): pl.pallas_call(body, out_shape=list(outs), in_specs=[pl.BlockSpec(memory_...  6.87 us
    ppermute x1, waiting for transfers between devices, local(): gathered[dr ^ bit] = lax.ppermute(piece, 'row', flip(rows, bit))  6.52 us
    ppermute x3, waiting for transfers between devices, local(): lax.ppermute(outgoing[d], 'col', flip(cols, d))  6.43 us
    ppermute x3, waiting for transfers between devices, local(): h_pieces.append(lax.ppermute(hamiltonian, ('row', 'layer'), perm))  5.86 us
    ppermute x3, starting transfers between devices, local(): lax.ppermute(outgoing[d], 'col', flip(cols, d))  4.44 us
    ppermute x3, starting transfers between devices, local(): h_pieces.append(lax.ppermute(hamiltonian, ('row', 'layer'), perm))  3.49 us
  transfers between devices with their start and end apart: 16, of which 9 were waited for; matrix products, arithmetic and copies ran while one was open for 0% of the time, Pallas kernels for 9%

profile of v6, /device:TPU:0, one launch (start us, length us, event | category | flops | bytes accessed | tf_op | source)
XLA Modules:
  0.0 61.4 jit_solution(3517934957436245000)
XLA Ops:
  0.0 1.0 %constant_dynamic-slice_fusion = bf16[2,1,128,512]{3,2,1,0:T(8,128)(2,1)S(1)} fusion(bf16[2,4,128,512]{3,2,1,0:T(8,128)(2,1)} %bitcast.4, s32[]{:T(128)S(6)} %select_n.4), kind=kLoop, calls=%fused_computation | loop fusion | bytes 524292 | tf_op jit(solution)/shard_map/jit(dynamic_index_in_dim)/dynamic_slice | solution.py:219
  1.0 4.1 %collective-permute-start = (bf16[256,512]{1,0:T(8,128)(2,1)S(1)}, bf16[256,512]{1,0:T(8,128)(2,1)S(1)}, u32[]{:S(2)}, u32[]{:S(2)}) collective-permute-start(bf16[256,512]{1,0:T(8,128)(2,1)S(1)} %bitcast.5), channel_id=1, source_target_pairs={{0,8},{8,12},{12,4},{4,0},{1,9},{9,13},{13,5},{5,1},{2,10},{10,14}... | collective-permute-start | bytes 786440 | tf_op jit(solution)/shard_map/ppermute | solution.py:224
  5.1 1.5 %collective-permute-start.2 = (bf16[1024,128]{1,0:T(8,128)(2,1)}, bf16[1024,128]{1,0:T(8,128)(2,1)S(1)}, u32[]{:S(2)}, u32[]{:S(2)}) collective-permute-start(bf16[1024,128]{1,0:T(8,128)(2,1)} %refs_1_.2), channel_id=1, source_target_pairs={{0,16},{1,17},{2,18},{3,19},{16,0},{17,1},{18,2},{19,3},{4,20},{5,... | collective-permute-start | bytes 786440 | tf_op jit(solution)/shard_map/ppermute | solution.py:242
  6.6 1.5 %collective-permute-start.1 = (bf16[1024,128]{1,0:T(8,128)(2,1)}, bf16[1024,128]{1,0:T(8,128)(2,1)S(1)}, u32[]{:S(2)}, u32[]{:S(2)}) collective-permute-start(bf16[1024,128]{1,0:T(8,128)(2,1)} %refs_1_.2), channel_id=1, source_target_pairs={{0,2},{1,3},{2,0},{3,1},{16,18},{17,19},{18,16},{19,17},{4,6},{5,7... | collective-permute-start | bytes 786440 | tf_op jit(solution)/shard_map/ppermute | solution.py:242
  8.6 2.1 %collective-permute-done.refs_5_.refs_2_.refs_0_ = bf16[256,512]{1,0:T(8,128)(2,1)S(1)} collective-permute-done((bf16[256,512]{1,0:T(8,128)(2,1)S(1)}, bf16[256,512]{1,0:T(8,128)(2,1)S(1)}, u32[]{:S(2)}, u32[]{:S(2)}) %collective-permute-start) | collective-permute-done | bytes 262176 | tf_op jit(solution)/shard_map/ppermute | solution.py:224
  10.6 3.4 %collective-permute-start.5 = (bf16[256,512]{1,0:T(8,128)(2,1)S(1)}, bf16[256,512]{1,0:T(8,128)(2,1)S(1)}, u32[]{:S(2)}, u32[]{:S(2)}) collective-permute-start(bf16[256,512]{1,0:T(8,128)(2,1)S(1)} %collective-permute-done.refs_5_.refs_2_.refs_0_), channel_id=1, source_target_pairs={{0,8},{8,12},{12,4},{4,0},{1,9},{9,13},{13,5},{5,1},{2,10},{10,14}... | collective-permute-start | bytes 786440 | tf_op jit(solution)/shard_map/ppermute | solution.py:224
  14.5 5.4 %collective-permute-done.1.refs_2_ = bf16[1024,128]{1,0:T(8,128)(2,1)S(1)} collective-permute-done((bf16[1024,128]{1,0:T(8,128)(2,1)}, bf16[1024,128]{1,0:T(8,128)(2,1)S(1)}, u32[]{:S(2)}, u32[]{:S(2)}) %collective-permute-start.1) | collective-permute-done | bytes 262176 | tf_op jit(solution)/shard_map/ppermute | solution.py:242
  19.9 0.9 %copy-done.1 = bf16[1024,128]{1,0:T(8,128)(2,1)S(1)} copy-done((bf16[1024,128]{1,0:T(8,128)(2,1)S(1)}, bf16[1024,128]{1,0:T(8,128)(2,1)}, u32[]{:S(2)}) %copy-start.1) | copy-done | bytes 262168
  21.5 0.9 %bring.1 = (bf16[2048,256]{1,0:T(8,128)(2,1)S(1)}, bf16[256,512]{1,0:T(8,128)(2,1)S(1)}) custom-call(s32[8,8]{1,0:T(8,128)S(1)} %copy-done.3, bf16[1024,128]{1,0:T(8,128)(2,1)S(1)} %copy-done.1, bf16[1024,128]{1,0:T(8,128)(2,1)S(1)} %collective-permute-done.1.refs_2_, bf16[1024,128]{1,0:T(8,128)(2,1)S(1)} %collective-permute-done.2.refs_3_, ...), custom_call_target="tpu_custom_call" | custom-call | bytes 2621440 | tf_op jit(solution)/shard_map/bring/pallas_call | solution.py:51
  22.6 1.6 %collective-permute-start.4 = (bf16[256,512]{1,0:T(8,128)(2,1)S(1)}, bf16[256,512]{1,0:T(8,128)(2,1)S(1)}, u32[]{:S(2)}, u32[]{:S(2)}) collective-permute-start(bf16[256,512]{1,0:T(8,128)(2,1)S(1)} %get-tuple-element.11), channel_id=1, source_target_pairs={{0,2},{1,3},{2,0},{3,1},{4,6},{5,7},{6,4},{7,5},{8,10},{9,11},{10,... | collective-permute-start | bytes 786440 | tf_op jit(solution)/shard_map/ppermute | solution.py:253
  24.2 1.6 %collective-permute-start.7 = (bf16[256,512]{1,0:T(8,128)(2,1)S(1)}, bf16[256,512]{1,0:T(8,128)(2,1)S(1)}, u32[]{:S(2)}, u32[]{:S(2)}) collective-permute-start(bf16[256,512]{1,0:T(8,128)(2,1)S(1)} %collective-permute-done.5.refs_3_.refs_1_.refs_2_.refs_4_), channel_id=1, source_target_pairs={{0,8},{8,12},{12,4},{4,0},{1,9},{9,13},{13,5},{5,1},{2,10},{10,14}... | collective-permute-start | bytes 786440 | tf_op jit(solution)/shard_map/ppermute | solution.py:224
  26.2 5.5 %collective-permute-done.4.refs_4_.refs_1_.refs_3_ = bf16[256,512]{1,0:T(8,128)(2,1)S(1)} collective-permute-done((bf16[256,512]{1,0:T(8,128)(2,1)S(1)}, bf16[256,512]{1,0:T(8,128)(2,1)S(1)}, u32[]{:S(2)}, u32[]{:S(2)}) %collective-permute-start.4) | collective-permute-done | bytes 262176 | tf_op jit(solution)/shard_map/ppermute | solution.py:253
  31.7 0.8 %mask.2.refs_2_ = bf16[256,2048]{1,0:T(8,128)(2,1)S(1)} custom-call(s32[8,8]{1,0:T(8,128)S(1)} %copy-done.2, bf16[256,512]{1,0:T(8,128)(2,1)S(1)} %bitcast.6, bf16[256,512]{1,0:T(8,128)(2,1)S(1)} %collective-permute-done.refs_5_.refs_2_.refs_0_, bf16[256,512]{1,0:T(8,128)(2,1)S(1)} %collective-permute-done.5.refs_3_.refs_1_.refs_2_.refs_4_, ...), custom_call_target="tpu_custom_call" | custom-call | bytes 1835008 | tf_op jit(solution)/shard_map/mask/pallas_call | solution.py:51
  34.0 2.9 %collective-permute-done.6.refs_3_.refs_5_ = bf16[256,512]{1,0:T(8,128)(2,1)S(1)} collective-permute-done((bf16[256,512]{1,0:T(8,128)(2,1)S(1)}, bf16[256,512]{1,0:T(8,128)(2,1)S(1)}, u32[]{:S(2)}, u32[]{:S(2)}) %collective-permute-start.6) | collective-permute-done | bytes 262176 | tf_op jit(solution)/shard_map/ppermute | solution.py:253
  37.1 1.3 %collective-permute-start.11 = (bf16[256,512]{1,0:T(8,128)(2,1)S(1)}, bf16[256,512]{1,0:T(8,128)(2,1)S(1)}, u32[]{:S(2)}, u32[]{:S(2)}) collective-permute-start(bf16[256,512]{1,0:T(8,128)(2,1)S(1)} %first_product.1.refs_4_.refs_1_.refs_0_), channel_id=1, source_target_pairs={{0,16},{16,0},{1,17},{17,1},{2,18},{18,2},{3,19},{19,3},{4,20},{20... | collective-permute-start | bytes 786440 | tf_op jit(solution)/shard_map/ppermute | solution.py:280
  38.4 0.9 %collective-permute-start.10 = (bf16[256,512]{1,0:T(8,128)(2,1)S(1)}, bf16[256,512]{1,0:T(8,128)(2,1)S(1)}, u32[]{:S(2)}, u32[]{:S(2)}) collective-permute-start(bf16[256,512]{1,0:T(8,128)(2,1)S(1)} %pack.6), channel_id=1, source_target_pairs={{0,2},{1,3},{2,0},{3,1},{4,6},{5,7},{6,4},{7,5},{8,10},{9,11},{10,... | collective-permute-start | bytes 786440 | tf_op jit(solution)/shard_map/ppermute | solution.py:253
  39.3 6.5 %collective-permute-done.11.refs_1_ = bf16[256,512]{1,0:T(8,128)(2,1)S(1)} collective-permute-done((bf16[256,512]{1,0:T(8,128)(2,1)S(1)}, bf16[256,512]{1,0:T(8,128)(2,1)S(1)}, u32[]{:S(2)}, u32[]{:S(2)}) %collective-permute-start.11) | collective-permute-done | bytes 262176 | tf_op jit(solution)/shard_map/ppermute | solution.py:280
  45.8 1.0 %collective-permute-done.10.refs_1_.refs_8_ = bf16[256,512]{1,0:T(8,128)(2,1)S(1)} collective-permute-done((bf16[256,512]{1,0:T(8,128)(2,1)S(1)}, bf16[256,512]{1,0:T(8,128)(2,1)S(1)}, u32[]{:S(2)}, u32[]{:S(2)}) %collective-permute-start.10) | collective-permute-done | bytes 262176 | tf_op jit(solution)/shard_map/ppermute | solution.py:253
  47.1 1.9 %collective-permute-start.13 = (bf16[128,512]{1,0:T(8,128)(2,1)S(1)}, bf16[128,512]{1,0:T(8,128)(2,1)S(1)}, u32[]{:S(2)}, u32[]{:S(2)}) collective-permute-start(bf16[128,512]{1,0:T(8,128)(2,1)S(1)} %get-tuple-element.14), channel_id=1, source_target_pairs={{0,8},{4,12},{8,0},{12,4},{1,9},{5,13},{9,1},{13,5},{2,10},{6,14},... | collective-permute-start | bytes 393224 | tf_op jit(solution)/shard_map/ppermute | solution.py:297
  49.0 2.5 %collective-permute-start.14 = (bf16[128,512]{1,0:T(8,128)(2,1)S(1)}, bf16[128,512]{1,0:T(8,128)(2,1)S(1)}, u32[]{:S(2)}, u32[]{:S(2)}) collective-permute-start(bf16[128,512]{1,0:T(8,128)(2,1)S(1)} %get-tuple-element.15), channel_id=1, source_target_pairs={{0,12},{4,8},{8,4},{12,0},{1,13},{5,9},{9,5},{13,1},{2,14},{6,10},... | collective-permute-start | bytes 393224 | tf_op jit(solution)/shard_map/ppermute | solution.py:297
  51.5 1.4 %layers.1.refs_0_ = bf16[1024,2048]{1,0:T(8,128)(2,1)S(1)} custom-call(s32[8,8]{1,0:T(8,128)S(1)} %copy-done.2, bf16[1024,512]{1,0:T(8,128)(2,1)S(1)} %copy-done, bf16[256,512]{1,0:T(8,128)(2,1)S(1)} %collective-permute-done.refs_5_.refs_2_.refs_0_, bf16[256,512]{1,0:T(8,128)(2,1)S(1)} %collective-permute-done.4.refs_4_.refs_1_.refs_3_, ...), custom_call_target="tpu_custom_call" | custom-call | bytes 8388608 | tf_op jit(solution)/shard_map/layers/pallas_call | solution.py:51
  52.9 2.7 %collective-permute-done.15.refs_2_ = bf16[128,512]{1,0:T(8,128)(2,1)S(1)} collective-permute-done((bf16[128,512]{1,0:T(8,128)(2,1)S(1)}, bf16[128,512]{1,0:T(8,128)(2,1)S(1)}, u32[]{:S(2)}, u32[]{:S(2)}) %collective-permute-start.15) | collective-permute-done | bytes 131104 | tf_op jit(solution)/shard_map/ppermute | solution.py:297
  56.2 3.8 %collective-permute-done.13.refs_1_ = bf16[128,512]{1,0:T(8,128)(2,1)S(1)} collective-permute-done((bf16[128,512]{1,0:T(8,128)(2,1)S(1)}, bf16[128,512]{1,0:T(8,128)(2,1)S(1)}, u32[]{:S(2)}, u32[]{:S(2)}) %collective-permute-start.13) | collective-permute-done | bytes 131104 | tf_op jit(solution)/shard_map/ppermute | solution.py:297
  60.0 1.4 %second_product.3 = bf16[1024,128]{1,0:T(8,128)(2,1)} custom-call(bf16[1024,2048]{1,0:T(8,128)(2,1)S(1)} %layers.1.refs_0_, bf16[128,512]{1,0:T(8,128)(2,1)S(1)} %collective-permute-done.13.refs_1_, bf16[128,512]{1,0:T(8,128)(2,1)S(1)} %collective-permute-done.14.refs_2_, f32[1024,128]{1,0:T(8,128)S(1)} %second_product.2.refs_3_), custom_call_target="tpu_custom_call" | custom-call | bytes 5242880 | tf_op jit(solution)/shard_map/second_product/pallas_call | solution.py:51
  (30 shorter events, 4.9 us)
Async XLA Ops:
  0.0 31.7 %copy-start.2 = (s32[8,8]{1,0:T(8,128)S(1)}, s32[8,8]{1,0:T(8,128)}, u32[]{:S(2)}) copy-start(s32[8,8]{1,0:T(8,128)} %refs_0_.7) | copy-start | bytes 772
  1.0 9.7 %collective-permute-start = (bf16[256,512]{1,0:T(8,128)(2,1)S(1)}, bf16[256,512]{1,0:T(8,128)(2,1)S(1)}, u32[]{:S(2)}, u32[]{:S(2)}) collective-permute-start(bf16[256,512]{1,0:T(8,128)(2,1)S(1)} %bitcast.5), channel_id=1, source_target_pairs={{0,8},{8,12},{12,4},{4,0},{1,9},{9,13},{13,5},{5,1},{2,10},{10,14}... | collective-permute-start | bytes 786440 | tf_op jit(solution)/shard_map/ppermute | solution.py:224
  5.1 9.4 %collective-permute-start.2 = (bf16[1024,128]{1,0:T(8,128)(2,1)}, bf16[1024,128]{1,0:T(8,128)(2,1)S(1)}, u32[]{:S(2)}, u32[]{:S(2)}) collective-permute-start(bf16[1024,128]{1,0:T(8,128)(2,1)} %refs_1_.2), channel_id=1, source_target_pairs={{0,16},{1,17},{2,18},{3,19},{16,0},{17,1},{18,2},{19,3},{4,20},{5,... | collective-permute-start | bytes 786440 | tf_op jit(solution)/shard_map/ppermute | solution.py:242
  6.6 13.3 %collective-permute-start.1 = (bf16[1024,128]{1,0:T(8,128)(2,1)}, bf16[1024,128]{1,0:T(8,128)(2,1)S(1)}, u32[]{:S(2)}, u32[]{:S(2)}) collective-permute-start(bf16[1024,128]{1,0:T(8,128)(2,1)} %refs_1_.2), channel_id=1, source_target_pairs={{0,2},{1,3},{2,0},{3,1},{16,18},{17,19},{18,16},{19,17},{4,6},{5,7... | collective-permute-start | bytes 786440 | tf_op jit(solution)/shard_map/ppermute | solution.py:242
  8.1 11.8 %collective-permute-start.3 = (bf16[1024,128]{1,0:T(8,128)(2,1)}, bf16[1024,128]{1,0:T(8,128)(2,1)S(1)}, u32[]{:S(2)}, u32[]{:S(2)}) collective-permute-start(bf16[1024,128]{1,0:T(8,128)(2,1)} %refs_1_.2), channel_id=1, source_target_pairs={{0,18},{1,19},{2,16},{3,17},{16,2},{17,3},{18,0},{19,1},{4,22},{5,... | collective-permute-start | bytes 786440 | tf_op jit(solution)/shard_map/ppermute | solution.py:242
  10.6 11.8 %collective-permute-start.5 = (bf16[256,512]{1,0:T(8,128)(2,1)S(1)}, bf16[256,512]{1,0:T(8,128)(2,1)S(1)}, u32[]{:S(2)}, u32[]{:S(2)}) collective-permute-start(bf16[256,512]{1,0:T(8,128)(2,1)S(1)} %collective-permute-done.refs_5_.refs_2_.refs_0_), channel_id=1, source_target_pairs={{0,8},{8,12},{12,4},{4,0},{1,9},{9,13},{13,5},{5,1},{2,10},{10,14}... | collective-permute-start | bytes 786440 | tf_op jit(solution)/shard_map/ppermute | solution.py:224
  19.9 1.0 %copy-start.1 = (bf16[1024,128]{1,0:T(8,128)(2,1)S(1)}, bf16[1024,128]{1,0:T(8,128)(2,1)}, u32[]{:S(2)}) copy-start(bf16[1024,128]{1,0:T(8,128)(2,1)} %refs_1_.2) | copy-start | bytes 786436
  20.8 0.7 %copy-start.3 = (s32[8,8]{1,0:T(8,128)S(1)}, s32[8,8]{1,0:T(8,128)}, u32[]{:S(2)}) copy-start(s32[8,8]{1,0:T(8,128)} %refs_0_.4) | copy-start | bytes 772
  22.5 10.8 %collective-permute-start.8 = (bf16[2048,256]{1,0:T(8,128)(2,1)S(1)}, bf16[2048,256]{1,0:T(8,128)(2,1)S(1)}, u32[]{:S(2)}, u32[]{:S(2)}) collective-permute-start(bf16[2048,256]{1,0:T(8,128)(2,1)S(1)} %pack.4.refs_1_), channel_id=1, source_target_pairs={{0,1},{1,0},{2,3},{3,2},{4,5},{5,4},{6,7},{7,6},{8,9},{9,8},{10,11... | collective-permute-start | bytes 3145736 | tf_op jit(solution)/shard_map/ppermute | solution.py:257
  22.6 9.2 %collective-permute-start.4 = (bf16[256,512]{1,0:T(8,128)(2,1)S(1)}, bf16[256,512]{1,0:T(8,128)(2,1)S(1)}, u32[]{:S(2)}, u32[]{:S(2)}) collective-permute-start(bf16[256,512]{1,0:T(8,128)(2,1)S(1)} %get-tuple-element.11), channel_id=1, source_target_pairs={{0,2},{1,3},{2,0},{3,1},{4,6},{5,7},{6,4},{7,5},{8,10},{9,11},{10,... | collective-permute-start | bytes 786440 | tf_op jit(solution)/shard_map/ppermute | solution.py:253
  24.2 8.4 %collective-permute-start.7 = (bf16[256,512]{1,0:T(8,128)(2,1)S(1)}, bf16[256,512]{1,0:T(8,128)(2,1)S(1)}, u32[]{:S(2)}, u32[]{:S(2)}) collective-permute-start(bf16[256,512]{1,0:T(8,128)(2,1)S(1)} %collective-permute-done.5.refs_3_.refs_1_.refs_2_.refs_4_), channel_id=1, source_target_pairs={{0,8},{8,12},{12,4},{4,0},{1,9},{9,13},{13,5},{5,1},{2,10},{10,14}... | collective-permute-start | bytes 786440 | tf_op jit(solution)/shard_map/ppermute | solution.py:224
  25.7 11.2 %collective-permute-start.6 = (bf16[256,512]{1,0:T(8,128)(2,1)S(1)}, bf16[256,512]{1,0:T(8,128)(2,1)S(1)}, u32[]{:S(2)}, u32[]{:S(2)}) collective-permute-start(bf16[256,512]{1,0:T(8,128)(2,1)S(1)} %collective-permute-done.5.refs_3_.refs_1_.refs_2_.refs_4_), channel_id=1, source_target_pairs={{0,2},{1,3},{2,0},{3,1},{4,6},{5,7},{6,4},{7,5},{8,10},{9,11},{10,... | collective-permute-start | bytes 786440 | tf_op jit(solution)/shard_map/ppermute | solution.py:253
  33.2 18.2 %copy-start = (bf16[1024,512]{1,0:T(8,128)(2,1)S(1)}, bf16[1024,512]{1,0:T(8,128)(2,1)}, u32[]{:S(2)}) copy-start(bf16[1024,512]{1,0:T(8,128)(2,1)} %refs_1_.3) | copy-start | bytes 3145732
  37.0 14.5 %collective-permute-start.9 = (bf16[1024,512]{1,0:T(8,128)(2,1)S(1)}, bf16[1024,512]{1,0:T(8,128)(2,1)S(1)}, u32[]{:S(2)}, u32[]{:S(2)}) collective-permute-start(bf16[1024,512]{1,0:T(8,128)(2,1)S(1)} %pack.5), channel_id=1, source_target_pairs={{0,1},{1,0},{2,3},{3,2},{4,5},{5,4},{6,7},{7,6},{8,9},{9,8},{10,11... | collective-permute-start | bytes 3145736 | tf_op jit(solution)/shard_map/ppermute | solution.py:310
  37.1 8.7 %collective-permute-start.11 = (bf16[256,512]{1,0:T(8,128)(2,1)S(1)}, bf16[256,512]{1,0:T(8,128)(2,1)S(1)}, u32[]{:S(2)}, u32[]{:S(2)}) collective-permute-start(bf16[256,512]{1,0:T(8,128)(2,1)S(1)} %first_product.1.refs_4_.refs_1_.refs_0_), channel_id=1, source_target_pairs={{0,16},{16,0},{1,17},{17,1},{2,18},{18,2},{3,19},{19,3},{4,20},{20... | collective-permute-start | bytes 786440 | tf_op jit(solution)/shard_map/ppermute | solution.py:280
  38.4 8.4 %collective-permute-start.10 = (bf16[256,512]{1,0:T(8,128)(2,1)S(1)}, bf16[256,512]{1,0:T(8,128)(2,1)S(1)}, u32[]{:S(2)}, u32[]{:S(2)}) collective-permute-start(bf16[256,512]{1,0:T(8,128)(2,1)S(1)} %pack.6), channel_id=1, source_target_pairs={{0,2},{1,3},{2,0},{3,1},{4,6},{5,7},{6,4},{7,5},{8,10},{9,11},{10,... | collective-permute-start | bytes 786440 | tf_op jit(solution)/shard_map/ppermute | solution.py:253
  46.9 4.5 %collective-permute-start.12 = (bf16[512,512]{1,0:T(8,128)(2,1)S(1)}, bf16[512,512]{1,0:T(8,128)(2,1)S(1)}, u32[]{:S(2)}, u32[]{:S(2)}) collective-permute-start(bf16[512,512]{1,0:T(8,128)(2,1)S(1)} %pack.7), channel_id=1, source_target_pairs={{0,1},{1,0},{2,3},{3,2},{4,5},{5,4},{6,7},{7,6},{8,9},{9,8},{10,11... | collective-permute-start | bytes 1572872 | tf_op jit(solution)/shard_map/ppermute | solution.py:310
  47.0 8.5 %collective-permute-start.15 = (bf16[128,512]{1,0:T(8,128)(2,1)S(1)}, bf16[128,512]{1,0:T(8,128)(2,1)S(1)}, u32[]{:S(2)}, u32[]{:S(2)}) collective-permute-start(bf16[128,512]{1,0:T(8,128)(2,1)S(1)} %get-tuple-element.16), channel_id=1, source_target_pairs={{0,4},{4,0},{8,12},{12,8},{1,5},{5,1},{9,13},{13,9},{2,6},{6,2},{1... | collective-permute-start | bytes 393224 | tf_op jit(solution)/shard_map/ppermute | solution.py:297
  47.1 12.9 %collective-permute-start.13 = (bf16[128,512]{1,0:T(8,128)(2,1)S(1)}, bf16[128,512]{1,0:T(8,128)(2,1)S(1)}, u32[]{:S(2)}, u32[]{:S(2)}) collective-permute-start(bf16[128,512]{1,0:T(8,128)(2,1)S(1)} %get-tuple-element.14), channel_id=1, source_target_pairs={{0,8},{4,12},{8,0},{12,4},{1,9},{5,13},{9,1},{13,5},{2,10},{6,14},... | collective-permute-start | bytes 393224 | tf_op jit(solution)/shard_map/ppermute | solution.py:297
  49.0 11.0 %collective-permute-start.14 = (bf16[128,512]{1,0:T(8,128)(2,1)S(1)}, bf16[128,512]{1,0:T(8,128)(2,1)S(1)}, u32[]{:S(2)}, u32[]{:S(2)}) collective-permute-start(bf16[128,512]{1,0:T(8,128)(2,1)S(1)} %get-tuple-element.15), channel_id=1, source_target_pairs={{0,12},{4,8},{8,4},{12,0},{1,13},{5,9},{9,5},{13,1},{2,14},{6,10},... | collective-permute-start | bytes 393224 | tf_op jit(solution)/shard_map/ppermute | solution.py:297

commit v7 on v5

--- a/solution.py
+++ b/solution.py
@@ -122,8 +122,51 @@
     return jnp.where(p < cols // 2, 2 * p, 2 * (cols - 1 - p) + 1)
 
 
+def inner(c):
+    return (c == 1) | (c == 2)
+
+
 def slot_column(c, s, cols):
+    if cols == 4:
+        near, far = jnp.where(inner(c), c ^ 3, c ^ 2), jnp.where(inner(c), c ^ 2, c ^ 3)
+        return (c, c ^ 1, near, far)[s]
     return ring_column(mod(ring_place(c, cols) - s, cols), cols)
+
+
+def pick_kernel(inside, outside, out):
+    c = lax.axis_index("col")
+
+    @pl.when(inner(c))
+    def _():
+        out[...] = inside[...]
+
+    @pl.when(jnp.logical_not(inner(c)))
+    def _():
+        out[...] = outside[...]
+
+
+def pick(inside, outside):
+    return run(pick_kernel, "pick", [shape(*inside.shape)], [inside, outside])[0]
+
+
+def send(piece, *pairs):
+    return lax.ppermute(piece, "col", pairs)
+
+
+def gather_columns(own, cols):
+    if cols == 4:
+        first = send(own, (0, 1), (1, 0), (2, 3), (3, 2))
+        middle = send(own, (1, 2), (2, 1))
+        across = send(first, (1, 2), (2, 1))
+        outer = send(middle, (1, 0), (2, 3))
+        last = send(across, (1, 0), (2, 3))
+        return [own, first, pick(middle, outer), pick(across, last)], [middle], [across, outer]
+    trip = list(range(0, cols, 2)) + list(range(cols - 1, 0, -2))
+    ring = [(trip[i], trip[(i + 1) % cols]) for i in range(cols)]
+    slots = [own]
+    for _ in range(1, cols):
+        slots.append(lax.ppermute(slots[-1], "col", ring))
+    return slots, [slots[1]], [slots[-2]]
 
 
 def first_kernel(sizes, h_table, n_h, hp, zp, *refs):
@@ -183,7 +226,12 @@
         out[...] = table[pl.ds(pl.multiple_of((c ^ d) * q, q), q), :]
 
 
-def layers_kernel(sizes, z_table, slots, zp, *refs):
+def bring_kernel(hp, zp, h, piece, h_out, piece_out):
+    h_out[...] = h[...]
+    piece_out[...] = piece[...]
+
+
+def layers_kernel(sizes, z_table, zp, *refs):
     cols, q = sizes.cols, sizes.quarter
     out, held = refs[-1], refs[:-1]
     r, c, l = place()
@@ -191,33 +239,28 @@
         ll = l ^ dl
         for half in range(sizes.per):
             rows = pl.ds(strip_start(ll, half, sizes), q)
-            for s in slots:
+            for s in range(cols):
                 cc = slot_column(c, s, cols)
                 if s == 0:
                     strip = held[0][rows, :]
                 else:
                     index, row = z_table[dl, s]
                     strip = held[index][row + half * q : row + (half + 1) * q, :]
-                columns = columns_of(cc, sizes) if len(slots) > 1 else slice(None)
-                out[rows, columns] = mask_strip(zp, r, ll, half, cc, strip, sizes)
-
-
-def second_kernel(sizes, z_early, z_late, *refs):
-    cols, width = sizes.cols, sizes.cols_here
-    messages, out, xm = refs[:cols], refs[cols], refs[cols + 1]
-    r, c, l = place()
-    for d in range(cols):
-        xm[:, columns_of(c ^ d, sizes)] = messages[d][...]
-    cc = slot_column(c, cols - 1, cols)
-    turned = (((1,), (1,)), ((), ()))
-    total = lax.dot_general(
-        z_late[...], xm[:, columns_of(cc, sizes)], turned, preferred_element_type=jnp.float32
-    )
-    for s in range(cols - 1):
-        columns = columns_of(slot_column(c, s, cols), sizes)
-        total += lax.dot_general(
-            z_early[:, columns], xm[:, columns], turned, preferred_element_type=jnp.float32
-        )
+                out[rows, columns_of(cc, sizes)] = mask_strip(zp, r, ll, half, cc, strip, sizes)
+
+
+def second_kernel(sizes, part, z_full, *refs):
+    messages, before, out = refs[: len(part)], refs[len(part) : -1], refs[-1]
+    c = lax.axis_index("col")
+    total = before[0][...] if before else None
+    for d, message in zip(part, messages):
+        added = lax.dot_general(
+            z_full[:, columns_of(c ^ d, sizes)],
+            message[...],
+            (((1,), (1,)), ((), ())),
+            preferred_element_type=jnp.float32,
+        )
+        total = added if total is None else total + added
     out[...] = total.astype(out.dtype)
 
 
@@ -232,11 +275,7 @@
     striped = inv_root.reshape(per, layers, q, cols_here)
     l = lax.axis_index("layer")
     own = lax.dynamic_index_in_dim(striped, l, 1, keepdims=False).reshape(height, cols_here)
-    trip = list(range(0, cols, 2)) + list(range(cols - 1, 0, -2))
-    ring = [(trip[i], trip[(i + 1) % cols]) for i in range(cols)]
-    slots = [own]
-    for _ in range(1, cols):
-        slots.append(lax.ppermute(slots[-1], "col", ring))
+    slots, step_one, step_two = gather_columns(own, cols)
 
     def offsets(arrays):
         starts = [0]
@@ -244,25 +283,32 @@
             starts.append(starts[-1] + array.shape[0])
         return starts
 
-    crossed = [lax.ppermute(slots[s], "layer", flip(layers, layer_bits[0])) for s in range(1, cols)]
+    top, low = layer_bits
+    crossed = [lax.ppermute(slots[s], "layer", flip(layers, top)) for s in range(1, cols)]
 
     h_arrays, h_table = [hamiltonian], [(0, 0, 0, 0)]
-    for axis, bit in [("layer", layer_bits[0])] + [("row", b) for b in row_bits]:
+    for axis, bit in [("layer", top)] + [("row", b) for b in row_bits]:
         for index, _, dr, dl in list(h_table):
             there = (dr ^ bit, dl) if axis == "row" else (dr, dl ^ bit)
             source = h_arrays[index]
-            if index:
-                source = pack([source], [slots[1]])
+            if index == 1:
+                h_arrays[0], source = run(
+                    bring_kernel,
+                    "bring",
+                    [shape(*hamiltonian.shape)] * 2,
+                    [hamiltonian, source],
+                    smem=[h_pattern, z_pattern],
+                    after=[slots[1], *step_one],
+                )
             h_table.append((len(h_arrays), 0) + there)
             h_arrays.append(
                 lax.ppermute(source, axis, flip(rows if axis == "row" else layers, bit))
             )
-    for bit in layer_bits[1:]:
-        packed, starts = pack(h_arrays, [slots[-2], crossed[0]]), offsets(h_arrays)
-        h_table += [
-            (len(h_arrays), starts[index] + row, dr, dl ^ bit) for index, row, dr, dl in h_table
-        ]
-        h_arrays = h_arrays + [lax.ppermute(packed, "layer", flip(layers, bit))]
+    packed, starts = pack(h_arrays, [*step_two, crossed[0]]), offsets(h_arrays)
+    h_table += [
+        (len(h_arrays), starts[index] + row, dr, dl ^ low) for index, row, dr, dl in h_table
+    ]
+    h_arrays = h_arrays + [lax.ppermute(packed, "layer", flip(layers, low))]
 
     hm, total = run(
         functools.partial(first_kernel, sizes, h_table, len(h_arrays)),
@@ -297,39 +343,38 @@
         lax.ppermute(outgoing[d], "col", flip(cols, d)) for d in range(1, cols)
     ]
 
+    held, z_table = [inv_root], {}
+
     def share(group, gate):
         arrays, table = [], []
         for s in group:
-            table += [(len(arrays), 0, 0, s), (len(arrays) + 1, 0, layer_bits[0], s)]
+            table += [(len(arrays), 0, 0, s), (len(arrays) + 1, 0, top, s)]
             arrays += [slots[s], crossed[s - 1]]
-        for bit in layer_bits[1:]:
-            packed, starts = pack(arrays, gate), offsets(arrays)
-            table += [
-                (len(arrays), starts[index] + row, dl ^ bit, s) for index, row, dl, s in table
-            ]
-            arrays = arrays + [lax.ppermute(packed, "layer", flip(layers, bit))]
-        return arrays, table
-
-    def lay_out(group, tile, gate):
-        arrays, table = share([s for s in group if s], gate)
-        place_of = {(dl, s): (index + len(tile), row) for index, row, dl, s in table}
-        return run(
-            functools.partial(layers_kernel, sizes, place_of, group),
-            "layers",
-            [shape(rows_here, order if len(group) > 1 else cols_here)],
-            [*tile, *arrays],
-            smem=[z_pattern],
-        )[0]
-
-    z_early = lay_out(list(range(cols - 1)), [inv_root], [product])
-    z_late = lay_out([cols - 1], [], [outgoing[0]])
-    return run(
-        functools.partial(second_kernel, sizes),
-        "second_product",
-        [shape(*hamiltonian.shape)],
-        [z_early, z_late, *messages],
-        scratch=[pltpu.VMEM((q, order), jnp.bfloat16)],
+        starts = offsets(arrays)
+        table += [(len(arrays), starts[index] + row, dl ^ low, s) for index, row, dl, s in table]
+        for index, row, dl, s in table:
+            z_table[dl, s] = (index + len(held), row)
+        return arrays + [lax.ppermute(pack(arrays, gate), "layer", flip(layers, low))]
+
+    held += share(range(1, cols - 1), [product])
+    held += share([cols - 1], [outgoing[0]])
+    z_full = run(
+        functools.partial(layers_kernel, sizes, z_table),
+        "layers",
+        [shape(rows_here, order)],
+        held,
+        smem=[z_pattern],
     )[0]
+    total = []
+    for part in (range(cols // 2), range(cols // 2, cols)):
+        last_part = part[-1] == cols - 1
+        total = run(
+            functools.partial(second_kernel, sizes, part),
+            "second_product",
+            [shape(*hamiltonian.shape, jnp.bfloat16 if last_part else f32)],
+            [z_full, *[messages[d] for d in part], *total],
+        )
+    return total[0]
 
 
 def solution(mesh):

time: 58.5 us -> 63.6 us (1.087)
  waiting for transfers between devices: 24.7 us -> 31.6 us
  starting transfers between devices: 21.9 us -> 20.8 us
  local copies, waits for them, and re-layouts: 4.25 us -> 3.31 us
    ppermute x9 -> x11, waiting for transfers between devices: 14.8 us -> 24.1 us  [the longest x5 17.5 us: send(): return lax.ppermute(piece, 'col', pairs)]
    ppermute x3, waiting for transfers between devices: 2.3 us -> 0.77 us  [local(): lax.ppermute(source, axis, flip(rows if axis == 'row' else layers, bit))]
    ppermute x9 -> x11, starting transfers between devices: 11.4 us -> 10.3 us  [the longest x5 6.99 us: send(): return lax.ppermute(piece, 'col', pairs)]
    ppermute x3, waiting for transfers between devices: 7.43 us -> 6.44 us  [local(): lax.ppermute(outgoing[d], 'col', flip(cols, d))]
    unnamed x12 -> x10, local copies, waits for them, and re-layouts: 3.28 us -> 2.33 us
    pallas_call x10 -> x12, Pallas kernels: 7.22 us -> 7.4 us  [run(): pl.pallas_call(body, out_shape=list(outs), in_specs=[pl.BlockSpec(memory_...]
  transfers between devices with their start and end apart: 16 -> 18, of which waited for: 10 -> 8; matrix products, arithmetic and copies ran while one was open for 0% -> 0% of each run, Pallas kernels for 9% -> 9%
where the time goes in v7:
time: 63.6 us; the launch traced here: 63.3 us
  waiting for transfers between devices  31.6 us (50%)
  starting transfers between devices  20.8 us (33%)
  Pallas kernels  7.4 us (12%)
  local copies, waits for them, and re-layouts  3.31 us (5%)
    ppermute x5, waiting for transfers between devices, send(): return lax.ppermute(piece, 'col', pairs)  17.5 us
    pallas_call x12, Pallas kernels, run(): pl.pallas_call(body, out_shape=list(outs), in_specs=[pl.BlockSpec(memory_...  7.4 us
    ppermute x5, starting transfers between devices, send(): return lax.ppermute(piece, 'col', pairs)  6.99 us
    ppermute x3, waiting for transfers between devices, local(): lax.ppermute(slots[s], 'layer', flip(layers, top))  6.66 us
    ppermute x3, waiting for transfers between devices, local(): lax.ppermute(outgoing[d], 'col', flip(cols, d))  6.44 us
    ppermute x3, starting transfers between devices, local(): lax.ppermute(source, axis, flip(rows if axis == 'row' else layers, bit))  4.63 us
    ppermute x3, starting transfers between devices, local(): lax.ppermute(outgoing[d], 'col', flip(cols, d))  4.44 us
    ppermute x3, starting transfers between devices, local(): lax.ppermute(slots[s], 'layer', flip(layers, top))  3.05 us
  transfers between devices with their start and end apart: 18, of which 8 were waited for; matrix products, arithmetic and copies ran while one was open for 0% of the time, Pallas kernels for 9%

profile of v7, /device:TPU:0, one launch (start us, length us, event | category | flops | bytes accessed | tf_op | source)
XLA Modules:
  0.0 63.3 jit_solution(12341167230226181180)
XLA Ops:
  0.0 1.0 %constant_dynamic-slice_fusion = bf16[2,1,128,512]{3,2,1,0:T(8,128)(2,1)S(1)} fusion(bf16[2,4,128,512]{3,2,1,0:T(8,128)(2,1)} %bitcast.4, s32[]{:T(128)S(6)} %select_n.4), kind=kLoop, calls=%fused_computation | loop fusion | bytes 524292 | tf_op jit(solution)/shard_map/jit(dynamic_index_in_dim)/dynamic_slice | solution.py:277
  1.0 3.1 %collective-permute-start = (bf16[256,512]{1,0:T(8,128)(2,1)S(1)}, bf16[256,512]{1,0:T(8,128)(2,1)S(1)}, u32[]{:S(2)}, u32[]{:S(2)}) collective-permute-start(bf16[256,512]{1,0:T(8,128)(2,1)S(1)} %bitcast.5), channel_id=1, source_target_pairs={{0,4},{4,0},{8,12},{12,8},{1,5},{5,1},{9,13},{13,9},{2,6},{6,2},{1... | collective-permute-start | bytes 786440 | tf_op jit(solution)/shard_map/ppermute | solution.py:153
  4.7 1.6 %collective-permute-start.5 = (bf16[1024,128]{1,0:T(8,128)(2,1)}, bf16[1024,128]{1,0:T(8,128)(2,1)S(1)}, u32[]{:S(2)}, u32[]{:S(2)}) collective-permute-start(bf16[1024,128]{1,0:T(8,128)(2,1)} %refs_2_.1), channel_id=1, source_target_pairs={{0,2},{1,3},{2,0},{3,1},{4,6},{5,7},{6,4},{7,5},{8,10},{9,11},{10,... | collective-permute-start | bytes 786440 | tf_op jit(solution)/shard_map/ppermute | solution.py:305
  6.3 1.5 %collective-permute-start.6 = (bf16[1024,128]{1,0:T(8,128)(2,1)}, bf16[1024,128]{1,0:T(8,128)(2,1)S(1)}, u32[]{:S(2)}, u32[]{:S(2)}) collective-permute-start(bf16[1024,128]{1,0:T(8,128)(2,1)} %refs_2_.1), channel_id=1, source_target_pairs={{0,16},{16,0},{1,17},{17,1},{2,18},{18,2},{3,19},{19,3},{4,20},{20... | collective-permute-start | bytes 786440 | tf_op jit(solution)/shard_map/ppermute | solution.py:305
  7.8 2.6 %collective-permute-done.refs_4_.refs_3_.refs_0_.refs_2_ = bf16[256,512]{1,0:T(8,128)(2,1)S(1)} collective-permute-done((bf16[256,512]{1,0:T(8,128)(2,1)S(1)}, bf16[256,512]{1,0:T(8,128)(2,1)S(1)}, u32[]{:S(2)}, u32[]{:S(2)}) %collective-permute-start) | collective-permute-done | bytes 262176 | tf_op jit(solution)/shard_map/ppermute | solution.py:153
  11.1 1.7 %collective-permute-start.1 = (bf16[256,512]{1,0:T(8,128)(2,1)S(1)}, bf16[256,512]{1,0:T(8,128)(2,1)S(1)}, u32[]{:S(2)}, u32[]{:S(2)}) collective-permute-start(bf16[256,512]{1,0:T(8,128)(2,1)S(1)} %collective-permute-done.refs_4_.refs_3_.refs_0_.refs_2_), channel_id=1, source_target_pairs={{0,2},{1,3},{2,0},{3,1},{4,6},{5,7},{6,4},{7,5},{8,10},{9,11},{10,... | collective-permute-start | bytes 786440 | tf_op jit(solution)/shard_map/ppermute | solution.py:287
  12.8 1.3 %collective-permute-start.3 = (bf16[256,512]{1,0:T(8,128)(2,1)S(1)}, bf16[256,512]{1,0:T(8,128)(2,1)S(1)}, u32[]{:S(2)}, u32[]{:S(2)}) collective-permute-start(bf16[256,512]{1,0:T(8,128)(2,1)S(1)} %collective-permute-done.2.refs_0_.refs_5_), channel_id=1, source_target_pairs={{4,0},{8,12},{5,1},{9,13},{6,2},{10,14},{7,3},{11,15},{20,16},{24,... | collective-permute-start | bytes 786440 | tf_op jit(solution)/shard_map/ppermute | solution.py:153
  14.1 0.9 %copy-done.1 = bf16[1024,128]{1,0:T(8,128)(2,1)S(1)} copy-done((bf16[1024,128]{1,0:T(8,128)(2,1)S(1)}, bf16[1024,128]{1,0:T(8,128)(2,1)}, u32[]{:S(2)}) %copy-start.1) | copy-done | bytes 262168
  17.1 1.6 %collective-permute-start.7 = (bf16[1024,128]{1,0:T(8,128)(2,1)S(1)}, bf16[1024,128]{1,0:T(8,128)(2,1)S(1)}, u32[]{:S(2)}, u32[]{:S(2)}) collective-permute-start(bf16[1024,128]{1,0:T(8,128)(2,1)S(1)} %get-tuple-element.14), channel_id=1, source_target_pairs={{0,16},{16,0},{1,17},{17,1},{2,18},{18,2},{3,19},{19,3},{4,20},{20... | collective-permute-start | bytes 786440 | tf_op jit(solution)/shard_map/ppermute | solution.py:305
  18.7 4.6 %collective-permute-done.3.refs_1_.refs_5_ = bf16[256,512]{1,0:T(8,128)(2,1)S(1)} collective-permute-done((bf16[256,512]{1,0:T(8,128)(2,1)S(1)}, bf16[256,512]{1,0:T(8,128)(2,1)S(1)}, u32[]{:S(2)}, u32[]{:S(2)}) %collective-permute-start.3) | collective-permute-done | bytes 262176 | tf_op jit(solution)/shard_map/ppermute | solution.py:153
  23.3 0.8 %collective-permute-done.7.refs_3_.refs_8_ = bf16[1024,128]{1,0:T(8,128)(2,1)S(1)} collective-permute-done((bf16[1024,128]{1,0:T(8,128)(2,1)S(1)}, bf16[1024,128]{1,0:T(8,128)(2,1)S(1)}, u32[]{:S(2)}, u32[]{:S(2)}) %collective-permute-start.7) | collective-permute-done | bytes 262176 | tf_op jit(solution)/shard_map/ppermute | solution.py:305
  24.2 1.3 %collective-permute-start.10 = (bf16[256,512]{1,0:T(8,128)(2,1)S(1)}, bf16[256,512]{1,0:T(8,128)(2,1)S(1)}, u32[]{:S(2)}, u32[]{:S(2)}) collective-permute-start(bf16[256,512]{1,0:T(8,128)(2,1)S(1)} %collective-permute-done.8.refs_4_.refs_0_), channel_id=1, source_target_pairs={{4,0},{8,12},{5,1},{9,13},{6,2},{10,14},{7,3},{11,15},{20,16},{24,... | collective-permute-start | bytes 786440 | tf_op jit(solution)/shard_map/ppermute | solution.py:153
  25.6 0.7 %collective-permute-start.4 = (bf16[256,512]{1,0:T(8,128)(2,1)S(1)}, bf16[256,512]{1,0:T(8,128)(2,1)S(1)}, u32[]{:S(2)}, u32[]{:S(2)}) collective-permute-start(bf16[256,512]{1,0:T(8,128)(2,1)S(1)} %pick.2.refs_4_.refs_2_), channel_id=1, source_target_pairs={{0,2},{1,3},{2,0},{3,1},{4,6},{5,7},{6,4},{7,5},{8,10},{9,11},{10,... | collective-permute-start | bytes 786440 | tf_op jit(solution)/shard_map/ppermute | solution.py:287
  26.3 10.3 %collective-permute-done.10.refs_1_ = bf16[256,512]{1,0:T(8,128)(2,1)S(1)} collective-permute-done((bf16[256,512]{1,0:T(8,128)(2,1)S(1)}, bf16[256,512]{1,0:T(8,128)(2,1)S(1)}, u32[]{:S(2)}, u32[]{:S(2)}) %collective-permute-start.10) | collective-permute-done | bytes 262176 | tf_op jit(solution)/shard_map/ppermute | solution.py:153
  36.6 2.0 %first_product.1 = (bf16[2048,512]{1,0:T(8,128)(2,1)S(1)}, f32[256,512]{1,0:T(8,128)S(1)}) custom-call(s32[8,8]{1,0:T(8,128)S(1)} %copy-done.4, s32[8,8]{1,0:T(8,128)S(1)} %copy-done.3, bf16[256,512]{1,0:T(8,128)(2,1)S(1)} %bitcast.7, bf16[256,512]{1,0:T(8,128)(2,1)S(1)} %collective-permute-done.refs_4_.refs_3_.refs_0_.refs_2_, ...), custom_call_target="tpu_custom_call" | custom-call | bytes 6553600 | tf_op jit(solution)/shard_map/first_product/pallas_call | solution.py:51
  38.6 0.9 %finish_product.1.refs_4_.refs_0_ = bf16[256,512]{1,0:T(8,128)(2,1)S(1)} custom-call(s32[8,8]{1,0:T(8,128)S(1)} %copy-done.3, bf16[2048,512]{1,0:T(8,128)(2,1)S(1)} %get-tuple-element.15.refs_1_, f32[256,512]{1,0:T(8,128)S(1)} %get-tuple-element.16.refs_2_, bf16[256,512]{1,0:T(8,128)(2,1)S(1)} %pick.3.refs_3_.refs_0_.refs_7_), custom_call_target="tpu_custom_call" | custom-call | bytes 3145728 | tf_op jit(solution)/shard_map/finish_product/pallas_call | solution.py:51
  40.3 1.5 %collective-permute-start.13 = (bf16[256,512]{1,0:T(8,128)(2,1)S(1)}, bf16[256,512]{1,0:T(8,128)(2,1)S(1)}, u32[]{:S(2)}, u32[]{:S(2)}) collective-permute-start(bf16[256,512]{1,0:T(8,128)(2,1)S(1)} %finish_product.1.refs_4_.refs_0_), channel_id=1, source_target_pairs={{0,16},{16,0},{1,17},{17,1},{2,18},{18,2},{3,19},{19,3},{4,20},{20... | collective-permute-start | bytes 786440 | tf_op jit(solution)/shard_map/ppermute | solution.py:332
  41.8 6.7 %collective-permute-done.12.refs_2_.refs_1_.refs_8_ = bf16[256,512]{1,0:T(8,128)(2,1)S(1)} collective-permute-done((bf16[256,512]{1,0:T(8,128)(2,1)S(1)}, bf16[256,512]{1,0:T(8,128)(2,1)S(1)}, u32[]{:S(2)}, u32[]{:S(2)}) %collective-permute-start.12) | collective-permute-done | bytes 262176 | tf_op jit(solution)/shard_map/ppermute | solution.py:287
  49.0 2.4 %collective-permute-start.15 = (bf16[128,512]{1,0:T(8,128)(2,1)S(1)}, bf16[128,512]{1,0:T(8,128)(2,1)S(1)}, u32[]{:S(2)}, u32[]{:S(2)}) collective-permute-start(bf16[128,512]{1,0:T(8,128)(2,1)S(1)} %get-tuple-element.18), channel_id=1, source_target_pairs={{0,8},{4,12},{8,0},{12,4},{1,9},{5,13},{9,1},{13,5},{2,10},{6,14},... | collective-permute-start | bytes 393224 | tf_op jit(solution)/shard_map/ppermute | solution.py:343
  51.4 2.0 %collective-permute-start.16 = (bf16[128,512]{1,0:T(8,128)(2,1)S(1)}, bf16[128,512]{1,0:T(8,128)(2,1)S(1)}, u32[]{:S(2)}, u32[]{:S(2)}) collective-permute-start(bf16[128,512]{1,0:T(8,128)(2,1)S(1)} %get-tuple-element.19), channel_id=1, source_target_pairs={{0,12},{4,8},{8,4},{12,0},{1,13},{5,9},{9,5},{13,1},{2,14},{6,10},... | collective-permute-start | bytes 393224 | tf_op jit(solution)/shard_map/ppermute | solution.py:343
  53.3 1.4 %layers.1.refs_0_ = bf16[1024,2048]{1,0:T(8,128)(2,1)S(1)} custom-call(s32[8,8]{1,0:T(8,128)S(1)} %copy-done.3, bf16[1024,512]{1,0:T(8,128)(2,1)S(1)} %copy-done, bf16[256,512]{1,0:T(8,128)(2,1)S(1)} %collective-permute-done.refs_4_.refs_3_.refs_0_.refs_2_, bf16[256,512]{1,0:T(8,128)(2,1)S(1)} %collective-permute-done.1.refs_6_.refs_1_.refs_3_, ...), custom_call_target="tpu_custom_call" | custom-call | bytes 8388608 | tf_op jit(solution)/shard_map/layers/pallas_call | solution.py:51
  54.8 2.1 %collective-permute-done.17.refs_2_ = bf16[128,512]{1,0:T(8,128)(2,1)S(1)} collective-permute-done((bf16[128,512]{1,0:T(8,128)(2,1)S(1)}, bf16[128,512]{1,0:T(8,128)(2,1)S(1)}, u32[]{:S(2)}, u32[]{:S(2)}) %collective-permute-start.17) | collective-permute-done | bytes 131104 | tf_op jit(solution)/shard_map/ppermute | solution.py:343
  57.6 4.3 %collective-permute-done.15.refs_1_ = bf16[128,512]{1,0:T(8,128)(2,1)S(1)} collective-permute-done((bf16[128,512]{1,0:T(8,128)(2,1)S(1)}, bf16[128,512]{1,0:T(8,128)(2,1)S(1)}, u32[]{:S(2)}, u32[]{:S(2)}) %collective-permute-start.15) | collective-permute-done | bytes 131104 | tf_op jit(solution)/shard_map/ppermute | solution.py:343
  61.9 1.4 %second_product.3 = bf16[1024,128]{1,0:T(8,128)(2,1)} custom-call(bf16[1024,2048]{1,0:T(8,128)(2,1)S(1)} %layers.1.refs_0_, bf16[128,512]{1,0:T(8,128)(2,1)S(1)} %collective-permute-done.15.refs_1_, bf16[128,512]{1,0:T(8,128)(2,1)S(1)} %collective-permute-done.16.refs_2_, f32[1024,128]{1,0:T(8,128)S(1)} %second_product.2.refs_3_), custom_call_target="tpu_custom_call" | custom-call | bytes 5242880 | tf_op jit(solution)/shard_map/second_product/pallas_call | solution.py:51
  (35 shorter events, 5.5 us)
Async XLA Ops:
  0.0 36.6 %copy-start.3 = (s32[8,8]{1,0:T(8,128)S(1)}, s32[8,8]{1,0:T(8,128)}, u32[]{:S(2)}) copy-start(s32[8,8]{1,0:T(8,128)} %refs_0_.7) | copy-start | bytes 772
  1.0 9.4 %collective-permute-start = (bf16[256,512]{1,0:T(8,128)(2,1)S(1)}, bf16[256,512]{1,0:T(8,128)(2,1)S(1)}, u32[]{:S(2)}, u32[]{:S(2)}) collective-permute-start(bf16[256,512]{1,0:T(8,128)(2,1)S(1)} %bitcast.5), channel_id=1, source_target_pairs={{0,4},{4,0},{8,12},{12,8},{1,5},{5,1},{9,13},{13,9},{2,6},{6,2},{1... | collective-permute-start | bytes 786440 | tf_op jit(solution)/shard_map/ppermute | solution.py:153
  4.1 8.7 %collective-permute-start.2 = (bf16[256,512]{1,0:T(8,128)(2,1)S(1)}, bf16[256,512]{1,0:T(8,128)(2,1)S(1)}, u32[]{:S(2)}, u32[]{:S(2)}) collective-permute-start(bf16[256,512]{1,0:T(8,128)(2,1)S(1)} %bitcast.6), channel_id=1, source_target_pairs={{4,8},{8,4},{5,9},{9,5},{6,10},{10,6},{7,11},{11,7},{20,24},{24,20... | collective-permute-start | bytes 786440 | tf_op jit(solution)/shard_map/ppermute | solution.py:153
  4.7 9.3 %collective-permute-start.5 = (bf16[1024,128]{1,0:T(8,128)(2,1)}, bf16[1024,128]{1,0:T(8,128)(2,1)S(1)}, u32[]{:S(2)}, u32[]{:S(2)}) collective-permute-start(bf16[1024,128]{1,0:T(8,128)(2,1)} %refs_2_.1), channel_id=1, source_target_pairs={{0,2},{1,3},{2,0},{3,1},{4,6},{5,7},{6,4},{7,5},{8,10},{9,11},{10,... | collective-permute-start | bytes 786440 | tf_op jit(solution)/shard_map/ppermute | solution.py:305
  6.3 12.4 %collective-permute-start.6 = (bf16[1024,128]{1,0:T(8,128)(2,1)}, bf16[1024,128]{1,0:T(8,128)(2,1)S(1)}, u32[]{:S(2)}, u32[]{:S(2)}) collective-permute-start(bf16[1024,128]{1,0:T(8,128)(2,1)} %refs_2_.1), channel_id=1, source_target_pairs={{0,16},{16,0},{1,17},{17,1},{2,18},{18,2},{3,19},{19,3},{4,20},{20... | collective-permute-start | bytes 786440 | tf_op jit(solution)/shard_map/ppermute | solution.py:305
  10.4 12.9 %collective-permute-start.8 = (bf16[256,512]{1,0:T(8,128)(2,1)S(1)}, bf16[256,512]{1,0:T(8,128)(2,1)S(1)}, u32[]{:S(2)}, u32[]{:S(2)}) collective-permute-start(bf16[256,512]{1,0:T(8,128)(2,1)S(1)} %collective-permute-done.refs_4_.refs_3_.refs_0_.refs_2_), channel_id=1, source_target_pairs={{4,8},{8,4},{5,9},{9,5},{6,10},{10,6},{7,11},{11,7},{20,24},{24,20... | collective-permute-start | bytes 786440 | tf_op jit(solution)/shard_map/ppermute | solution.py:153
  11.1 12.3 %collective-permute-start.1 = (bf16[256,512]{1,0:T(8,128)(2,1)S(1)}, bf16[256,512]{1,0:T(8,128)(2,1)S(1)}, u32[]{:S(2)}, u32[]{:S(2)}) collective-permute-start(bf16[256,512]{1,0:T(8,128)(2,1)S(1)} %collective-permute-done.refs_4_.refs_3_.refs_0_.refs_2_), channel_id=1, source_target_pairs={{0,2},{1,3},{2,0},{3,1},{4,6},{5,7},{6,4},{7,5},{8,10},{9,11},{10,... | collective-permute-start | bytes 786440 | tf_op jit(solution)/shard_map/ppermute | solution.py:287
  12.8 10.5 %collective-permute-start.3 = (bf16[256,512]{1,0:T(8,128)(2,1)S(1)}, bf16[256,512]{1,0:T(8,128)(2,1)S(1)}, u32[]{:S(2)}, u32[]{:S(2)}) collective-permute-start(bf16[256,512]{1,0:T(8,128)(2,1)S(1)} %collective-permute-done.2.refs_0_.refs_5_), channel_id=1, source_target_pairs={{4,0},{8,12},{5,1},{9,13},{6,2},{10,14},{7,3},{11,15},{20,16},{24,... | collective-permute-start | bytes 786440 | tf_op jit(solution)/shard_map/ppermute | solution.py:153
  14.1 1.0 %copy-start.1 = (bf16[1024,128]{1,0:T(8,128)(2,1)S(1)}, bf16[1024,128]{1,0:T(8,128)(2,1)}, u32[]{:S(2)}) copy-start(bf16[1024,128]{1,0:T(8,128)(2,1)} %refs_2_.1) | copy-start | bytes 786436
  15.1 0.7 %copy-start.2 = (s32[8,8]{1,0:T(8,128)S(1)}, s32[8,8]{1,0:T(8,128)}, u32[]{:S(2)}) copy-start(s32[8,8]{1,0:T(8,128)} %refs_0_.7) | copy-start | bytes 772
  15.7 0.7 %copy-start.4 = (s32[8,8]{1,0:T(8,128)S(1)}, s32[8,8]{1,0:T(8,128)}, u32[]{:S(2)}) copy-start(s32[8,8]{1,0:T(8,128)} %refs_0_.5) | copy-start | bytes 772
  17.1 7.0 %collective-permute-start.7 = (bf16[1024,128]{1,0:T(8,128)(2,1)S(1)}, bf16[1024,128]{1,0:T(8,128)(2,1)S(1)}, u32[]{:S(2)}, u32[]{:S(2)}) collective-permute-start(bf16[1024,128]{1,0:T(8,128)(2,1)S(1)} %get-tuple-element.14), channel_id=1, source_target_pairs={{0,16},{16,0},{1,17},{17,1},{2,18},{18,2},{3,19},{19,3},{4,20},{20... | collective-permute-start | bytes 786440 | tf_op jit(solution)/shard_map/ppermute | solution.py:305
  24.2 12.5 %collective-permute-start.9 = (bf16[4096,128]{1,0:T(8,128)(2,1)S(1)}, bf16[4096,128]{1,0:T(8,128)(2,1)S(1)}, u32[]{:S(2)}, u32[]{:S(2)}) collective-permute-start(bf16[4096,128]{1,0:T(8,128)(2,1)S(1)} %pack.3), channel_id=1, source_target_pairs={{0,1},{1,0},{2,3},{3,2},{4,5},{5,4},{6,7},{7,6},{8,9},{9,8},{10,11... | collective-permute-start | bytes 3145736 | tf_op jit(solution)/shard_map/ppermute | solution.py:311
  24.2 12.3 %collective-permute-start.10 = (bf16[256,512]{1,0:T(8,128)(2,1)S(1)}, bf16[256,512]{1,0:T(8,128)(2,1)S(1)}, u32[]{:S(2)}, u32[]{:S(2)}) collective-permute-start(bf16[256,512]{1,0:T(8,128)(2,1)S(1)} %collective-permute-done.8.refs_4_.refs_0_), channel_id=1, source_target_pairs={{4,0},{8,12},{5,1},{9,13},{6,2},{10,14},{7,3},{11,15},{20,16},{24,... | collective-permute-start | bytes 786440 | tf_op jit(solution)/shard_map/ppermute | solution.py:153
  25.6 14.0 %collective-permute-start.4 = (bf16[256,512]{1,0:T(8,128)(2,1)S(1)}, bf16[256,512]{1,0:T(8,128)(2,1)S(1)}, u32[]{:S(2)}, u32[]{:S(2)}) collective-permute-start(bf16[256,512]{1,0:T(8,128)(2,1)S(1)} %pick.2.refs_4_.refs_2_), channel_id=1, source_target_pairs={{0,2},{1,3},{2,0},{3,1},{4,6},{5,7},{6,4},{7,5},{8,10},{9,11},{10,... | collective-permute-start | bytes 786440 | tf_op jit(solution)/shard_map/ppermute | solution.py:287
  38.6 14.7 %copy-start = (bf16[1024,512]{1,0:T(8,128)(2,1)S(1)}, bf16[1024,512]{1,0:T(8,128)(2,1)}, u32[]{:S(2)}) copy-start(bf16[1024,512]{1,0:T(8,128)(2,1)} %refs_1_.5) | copy-start | bytes 3145732
  39.6 13.7 %collective-permute-start.11 = (bf16[1024,512]{1,0:T(8,128)(2,1)S(1)}, bf16[1024,512]{1,0:T(8,128)(2,1)S(1)}, u32[]{:S(2)}, u32[]{:S(2)}) collective-permute-start(bf16[1024,512]{1,0:T(8,128)(2,1)S(1)} %pack.4), channel_id=1, source_target_pairs={{0,1},{1,0},{2,3},{3,2},{4,5},{5,4},{6,7},{7,6},{8,9},{9,8},{10,11... | collective-permute-start | bytes 3145736 | tf_op jit(solution)/shard_map/ppermute | solution.py:357
  39.7 8.7 %collective-permute-start.12 = (bf16[256,512]{1,0:T(8,128)(2,1)S(1)}, bf16[256,512]{1,0:T(8,128)(2,1)S(1)}, u32[]{:S(2)}, u32[]{:S(2)}) collective-permute-start(bf16[256,512]{1,0:T(8,128)(2,1)S(1)} %pick.3.refs_3_.refs_0_.refs_7_), channel_id=1, source_target_pairs={{0,2},{1,3},{2,0},{3,1},{4,6},{5,7},{6,4},{7,5},{8,10},{9,11},{10,... | collective-permute-start | bytes 786440 | tf_op jit(solution)/shard_map/ppermute | solution.py:287
  40.3 8.4 %collective-permute-start.13 = (bf16[256,512]{1,0:T(8,128)(2,1)S(1)}, bf16[256,512]{1,0:T(8,128)(2,1)S(1)}, u32[]{:S(2)}, u32[]{:S(2)}) collective-permute-start(bf16[256,512]{1,0:T(8,128)(2,1)S(1)} %finish_product.1.refs_4_.refs_0_), channel_id=1, source_target_pairs={{0,16},{16,0},{1,17},{17,1},{2,18},{18,2},{3,19},{19,3},{4,20},{20... | collective-permute-start | bytes 786440 | tf_op jit(solution)/shard_map/ppermute | solution.py:332
  48.8 4.5 %collective-permute-start.14 = (bf16[512,512]{1,0:T(8,128)(2,1)S(1)}, bf16[512,512]{1,0:T(8,128)(2,1)S(1)}, u32[]{:S(2)}, u32[]{:S(2)}) collective-permute-start(bf16[512,512]{1,0:T(8,128)(2,1)S(1)} %pack.5), channel_id=1, source_target_pairs={{0,1},{1,0},{2,3},{3,2},{4,5},{5,4},{6,7},{7,6},{8,9},{9,8},{10,11... | collective-permute-start | bytes 1572872 | tf_op jit(solution)/shard_map/ppermute | solution.py:357
  48.9 8.0 %collective-permute-start.17 = (bf16[128,512]{1,0:T(8,128)(2,1)S(1)}, bf16[128,512]{1,0:T(8,128)(2,1)S(1)}, u32[]{:S(2)}, u32[]{:S(2)}) collective-permute-start(bf16[128,512]{1,0:T(8,128)(2,1)S(1)} %get-tuple-element.20), channel_id=1, source_target_pairs={{0,4},{4,0},{8,12},{12,8},{1,5},{5,1},{9,13},{13,9},{2,6},{6,2},{1... | collective-permute-start | bytes 393224 | tf_op jit(solution)/shard_map/ppermute | solution.py:343
  49.0 12.9 %collective-permute-start.15 = (bf16[128,512]{1,0:T(8,128)(2,1)S(1)}, bf16[128,512]{1,0:T(8,128)(2,1)S(1)}, u32[]{:S(2)}, u32[]{:S(2)}) collective-permute-start(bf16[128,512]{1,0:T(8,128)(2,1)S(1)} %get-tuple-element.18), channel_id=1, source_target_pairs={{0,8},{4,12},{8,0},{12,4},{1,9},{5,13},{9,1},{13,5},{2,10},{6,14},... | collective-permute-start | bytes 393224 | tf_op jit(solution)/shard_map/ppermute | solution.py:343
  51.4 10.5 %collective-permute-start.16 = (bf16[128,512]{1,0:T(8,128)(2,1)S(1)}, bf16[128,512]{1,0:T(8,128)(2,1)S(1)}, u32[]{:S(2)}, u32[]{:S(2)}) collective-permute-start(bf16[128,512]{1,0:T(8,128)(2,1)S(1)} %get-tuple-element.19), channel_id=1, source_target_pairs={{0,12},{4,8},{8,4},{12,0},{1,13},{5,9},{9,5},{13,1},{2,14},{6,10},... | collective-permute-start | bytes 393224 | tf_op jit(solution)/shard_map/ppermute | solution.py:343

commit v8 on v7

--- a/solution.py
+++ b/solution.py
@@ -114,59 +114,8 @@
     return run(pack_kernel, "pack", [out], pieces, after=after)[0]
 
 
-def ring_place(c, cols):
-    return jnp.where(c % 2 == 0, c // 2, cols - 1 - c // 2)
-
-
-def ring_column(p, cols):
-    return jnp.where(p < cols // 2, 2 * p, 2 * (cols - 1 - p) + 1)
-
-
-def inner(c):
-    return (c == 1) | (c == 2)
-
-
 def slot_column(c, s, cols):
-    if cols == 4:
-        near, far = jnp.where(inner(c), c ^ 3, c ^ 2), jnp.where(inner(c), c ^ 2, c ^ 3)
-        return (c, c ^ 1, near, far)[s]
-    return ring_column(mod(ring_place(c, cols) - s, cols), cols)
-
-
-def pick_kernel(inside, outside, out):
-    c = lax.axis_index("col")
-
-    @pl.when(inner(c))
-    def _():
-        out[...] = inside[...]
-
-    @pl.when(jnp.logical_not(inner(c)))
-    def _():
-        out[...] = outside[...]
-
-
-def pick(inside, outside):
-    return run(pick_kernel, "pick", [shape(*inside.shape)], [inside, outside])[0]
-
-
-def send(piece, *pairs):
-    return lax.ppermute(piece, "col", pairs)
-
-
-def gather_columns(own, cols):
-    if cols == 4:
-        first = send(own, (0, 1), (1, 0), (2, 3), (3, 2))
-        middle = send(own, (1, 2), (2, 1))
-        across = send(first, (1, 2), (2, 1))
-        outer = send(middle, (1, 0), (2, 3))
-        last = send(across, (1, 0), (2, 3))
-        return [own, first, pick(middle, outer), pick(across, last)], [middle], [across, outer]
-    trip = list(range(0, cols, 2)) + list(range(cols - 1, 0, -2))
-    ring = [(trip[i], trip[(i + 1) % cols]) for i in range(cols)]
-    slots = [own]
-    for _ in range(1, cols):
-        slots.append(lax.ppermute(slots[-1], "col", ring))
-    return slots, [slots[1]], [slots[-2]]
+    return mod(c - s, cols)
 
 
 def first_kernel(sizes, h_table, n_h, hp, zp, *refs):
@@ -214,21 +163,17 @@
 
 
 def route_kernel(sizes, row_offsets, *refs):
-    n = len(row_offsets)
-    pieces, outs, table = refs[:n], refs[n:-1], refs[-1]
-    r, c, _ = place()
-    q = sizes.quarter
-    for dr, piece in zip(row_offsets, pieces):
+    table, (r, _, _), q = refs[-1], place(), sizes.quarter
+    for dr, piece in zip(row_offsets, refs[:-1]):
         for half in range(sizes.per):
             start = pl.multiple_of(((r ^ dr) * sizes.per + half) * q, q)
             table[pl.ds(start, q), :] = piece[half * q : (half + 1) * q, :]
+
+
+def cut_kernel(sizes, table, *outs):
+    c, q = lax.axis_index("col"), sizes.quarter
     for d, out in enumerate(outs):
         out[...] = table[pl.ds(pl.multiple_of((c ^ d) * q, q), q), :]
-
-
-def bring_kernel(hp, zp, h, piece, h_out, piece_out):
-    h_out[...] = h[...]
-    piece_out[...] = piece[...]
 
 
 def layers_kernel(sizes, z_table, zp, *refs):
@@ -275,7 +220,10 @@
     striped = inv_root.reshape(per, layers, q, cols_here)
     l = lax.axis_index("layer")
     own = lax.dynamic_index_in_dim(striped, l, 1, keepdims=False).reshape(height, cols_here)
-    slots, step_one, step_two = gather_columns(own, cols)
+    ring = [(i, (i + 1) % cols) for i in range(cols)]
+    slots = [own]
+    for _ in range(1, cols):
+        slots.append(lax.ppermute(slots[-1], "col", ring))
 
     def offsets(arrays):
         starts = [0]
@@ -283,32 +231,28 @@
             starts.append(starts[-1] + array.shape[0])
         return starts
 
+    def cross(piece):
+        return lax.ppermute(piece, "layer", flip(layers, layer_bits[0]))
+
     top, low = layer_bits
-    crossed = [lax.ppermute(slots[s], "layer", flip(layers, top)) for s in range(1, cols)]
-
     h_arrays, h_table = [hamiltonian], [(0, 0, 0, 0)]
     for axis, bit in [("layer", top)] + [("row", b) for b in row_bits]:
+        perm = flip(rows if axis == "row" else layers, bit)
         for index, _, dr, dl in list(h_table):
             there = (dr ^ bit, dl) if axis == "row" else (dr, dl ^ bit)
             source = h_arrays[index]
-            if index == 1:
-                h_arrays[0], source = run(
-                    bring_kernel,
-                    "bring",
-                    [shape(*hamiltonian.shape)] * 2,
-                    [hamiltonian, source],
-                    smem=[h_pattern, z_pattern],
-                    after=[slots[1], *step_one],
-                )
+            if index and False:
+                source = pack([source], [slots[1]])
             h_table.append((len(h_arrays), 0) + there)
-            h_arrays.append(
-                lax.ppermute(source, axis, flip(rows if axis == "row" else layers, bit))
-            )
-    packed, starts = pack(h_arrays, [*step_two, crossed[0]]), offsets(h_arrays)
-    h_table += [
-        (len(h_arrays), starts[index] + row, dr, dl ^ low) for index, row, dr, dl in h_table
+            h_arrays.append(lax.ppermute(source, axis, perm))
+    across = lax.ppermute(hamiltonian, "layer", flip(layers, low))
+    crossed = [cross(slots[1])] + [cross(slots[s]) for s in range(2, cols - 1)]
+    packed, starts = pack(h_arrays[1:], [slots[-2], crossed[0]]), offsets(h_arrays[1:])
+    n = len(h_arrays)
+    h_table += [(n, 0, 0, low)] + [
+        (n + 1, starts[index - 1], dr, dl ^ low) for index, _, dr, dl in h_table[1:]
     ]
-    h_arrays = h_arrays + [lax.ppermute(packed, "layer", flip(layers, low))]
+    h_arrays = h_arrays + [across, lax.ppermute(packed, "layer", flip(layers, low))]
 
     hm, total = run(
         functools.partial(first_kernel, sizes, h_table, len(h_arrays)),
@@ -331,33 +275,34 @@
         for dr, piece in list(gathered.items()):
             gathered[dr ^ bit] = lax.ppermute(piece, "row", flip(rows, bit))
     row_offsets = list(gathered)
-    outgoing = run(
+    held, z_table = [inv_root], {}
+
+    crossed.append(cross(pack([slots[-1]], [product])))
+    table = run(
         functools.partial(route_kernel, sizes, row_offsets),
         "route",
+        [shape(cols * q, cols_here)],
+        [gathered[o] for o in row_offsets],
+    )[0]
+    outgoing = run(
+        functools.partial(cut_kernel, sizes),
+        "cut",
         [shape(q, cols_here)] * cols,
-        [gathered[o] for o in row_offsets],
+        [table],
         after=[crossed[-1]],
-        scratch=[pltpu.VMEM((cols * q, cols_here), jnp.bfloat16)],
     )
     messages = [outgoing[0]] + [
         lax.ppermute(outgoing[d], "col", flip(cols, d)) for d in range(1, cols)
     ]
 
-    held, z_table = [inv_root], {}
-
-    def share(group, gate):
-        arrays, table = [], []
-        for s in group:
-            table += [(len(arrays), 0, 0, s), (len(arrays) + 1, 0, top, s)]
-            arrays += [slots[s], crossed[s - 1]]
-        starts = offsets(arrays)
-        table += [(len(arrays), starts[index] + row, dl ^ low, s) for index, row, dl, s in table]
-        for index, row, dl, s in table:
-            z_table[dl, s] = (index + len(held), row)
-        return arrays + [lax.ppermute(pack(arrays, gate), "layer", flip(layers, low))]
-
-    held += share(range(1, cols - 1), [product])
-    held += share([cols - 1], [outgoing[0]])
+    for group, gate in ((range(1, cols - 1), [product]), ([cols - 1], [outgoing[0]])):
+        arrays = [a for s in group for a in (slots[s], crossed[s - 1])]
+        base = len(held)
+        held += arrays + [lax.ppermute(pack(arrays, gate), "layer", flip(layers, low))]
+        for n, s in enumerate(group):
+            z_table[0, s], z_table[top, s] = (base + 2 * n, 0), (base + 2 * n + 1, 0)
+            z_table[low, s] = (base + len(arrays), 2 * n * height)
+            z_table[low ^ top, s] = (base + len(arrays), (2 * n + 1) * height)
     z_full = run(
         functools.partial(layers_kernel, sizes, z_table),
         "layers",

time: 63.6 us -> 58.1 us (0.914)
  starting transfers between devices: 20.8 us -> 18.4 us
  waiting for transfers between devices: 31.6 us -> 29.4 us
  Pallas kernels: 7.4 us -> 6.62 us
    ppermute x14 -> x13, waiting for transfers between devices: 24.9 us -> 17.1 us  [the longest x3 15 us: local(): slots.append(lax.ppermute(slots[-1], 'col', ring))]
    ppermute x1, waiting for transfers between devices: 0.23 us -> 5.81 us  [local(): gathered[dr ^ bit] = lax.ppermute(piece, 'row', flip(rows, bit))]
    ppermute x14 -> x13, starting transfers between devices: 14.9 us -> 12.7 us  [the longest x3 4.5 us: local(): h_arrays.append(lax.ppermute(source, axis, perm))]
    pallas_call x12 -> x11, Pallas kernels: 7.4 us -> 6.62 us  [run(): pl.pallas_call(body, out_shape=list(outs), in_specs=[pl.BlockSpec(memory_...]
  transfers between devices with their start and end apart: 18 -> 17, of which waited for: 8 -> 8; matrix products, arithmetic and copies ran while one was open for 0% -> 0% of each run, Pallas kernels for 9% -> 9%
where the time goes in v8:
time: 58.1 us; the launch traced here: 57.9 us
  waiting for transfers between devices  29.4 us (51%)
  starting transfers between devices  18.4 us (32%)
  Pallas kernels  6.62 us (11%)
  local copies, waits for them, and re-layouts  3.3 us (6%)
    ppermute x3, waiting for transfers between devices, local(): slots.append(lax.ppermute(slots[-1], 'col', ring))  15 us
    pallas_call x11, Pallas kernels, run(): pl.pallas_call(body, out_shape=list(outs), in_specs=[pl.BlockSpec(memory_...  6.62 us
    ppermute x3, waiting for transfers between devices, local(): lax.ppermute(outgoing[d], 'col', flip(cols, d))  6.43 us
    ppermute x1, waiting for transfers between devices, local(): gathered[dr ^ bit] = lax.ppermute(piece, 'row', flip(rows, bit))  5.81 us
    ppermute x3, starting transfers between devices, local(): h_arrays.append(lax.ppermute(source, axis, perm))  4.5 us
    ppermute x3, starting transfers between devices, local(): lax.ppermute(outgoing[d], 'col', flip(cols, d))  4.44 us
    ppermute x3, starting transfers between devices, cross(): return lax.ppermute(piece, 'layer', flip(layers, layer_bits[0]))  4.25 us
    ppermute x3, starting transfers between devices, local(): slots.append(lax.ppermute(slots[-1], 'col', ring))  3.21 us
  transfers between devices with their start and end apart: 17, of which 8 were waited for; matrix products, arithmetic and copies ran while one was open for 0% of the time, Pallas kernels for 9%

profile of v8, /device:TPU:0, one launch (start us, length us, event | category | flops | bytes accessed | tf_op | source)
XLA Modules:
  0.0 57.9 jit_solution(12306440525173456073)
XLA Ops:
  0.0 1.0 %constant_dynamic-slice_fusion = bf16[2,1,128,512]{3,2,1,0:T(8,128)(2,1)S(1)} fusion(bf16[2,4,128,512]{3,2,1,0:T(8,128)(2,1)} %bitcast.4, s32[]{:T(128)S(6)} %select_n.4), kind=kLoop, calls=%fused_computation | loop fusion | bytes 524292 | tf_op jit(solution)/shard_map/jit(dynamic_index_in_dim)/dynamic_slice | solution.py:222
  1.0 3.1 %collective-permute-start = (bf16[256,512]{1,0:T(8,128)(2,1)S(1)}, bf16[256,512]{1,0:T(8,128)(2,1)S(1)}, u32[]{:S(2)}, u32[]{:S(2)}) collective-permute-start(bf16[256,512]{1,0:T(8,128)(2,1)S(1)} %bitcast.5), channel_id=1, source_target_pairs={{0,4},{4,8},{8,12},{12,0},{1,5},{5,9},{9,13},{13,1},{2,6},{6,10},{... | collective-permute-start | bytes 786440 | tf_op jit(solution)/shard_map/ppermute | solution.py:226
  4.0 1.5 %collective-permute-start.4 = (bf16[1024,128]{1,0:T(8,128)(2,1)}, bf16[1024,128]{1,0:T(8,128)(2,1)S(1)}, u32[]{:S(2)}, u32[]{:S(2)}) collective-permute-start(bf16[1024,128]{1,0:T(8,128)(2,1)} %refs_5_.1), channel_id=1, source_target_pairs={{0,2},{1,3},{2,0},{3,1},{4,6},{5,7},{6,4},{7,5},{8,10},{9,11},{10,... | collective-permute-start | bytes 786440 | tf_op jit(solution)/shard_map/ppermute | solution.py:247
  5.6 1.5 %collective-permute-start.5 = (bf16[1024,128]{1,0:T(8,128)(2,1)}, bf16[1024,128]{1,0:T(8,128)(2,1)S(1)}, u32[]{:S(2)}, u32[]{:S(2)}) collective-permute-start(bf16[1024,128]{1,0:T(8,128)(2,1)} %refs_5_.1), channel_id=1, source_target_pairs={{0,16},{16,0},{1,17},{17,1},{2,18},{18,2},{3,19},{19,3},{4,20},{20... | collective-permute-start | bytes 786440 | tf_op jit(solution)/shard_map/ppermute | solution.py:247
  7.1 5.3 %collective-permute-done.refs_3_.refs_0_.refs_2_ = bf16[256,512]{1,0:T(8,128)(2,1)S(1)} collective-permute-done((bf16[256,512]{1,0:T(8,128)(2,1)S(1)}, bf16[256,512]{1,0:T(8,128)(2,1)S(1)}, u32[]{:S(2)}, u32[]{:S(2)}) %collective-permute-start) | collective-permute-done | bytes 262176 | tf_op jit(solution)/shard_map/ppermute | solution.py:226
  12.4 1.5 %collective-permute-start.1 = (bf16[256,512]{1,0:T(8,128)(2,1)S(1)}, bf16[256,512]{1,0:T(8,128)(2,1)S(1)}, u32[]{:S(2)}, u32[]{:S(2)}) collective-permute-start(bf16[256,512]{1,0:T(8,128)(2,1)S(1)} %collective-permute-done.refs_3_.refs_0_.refs_2_), channel_id=1, source_target_pairs={{0,2},{1,3},{2,0},{3,1},{4,6},{5,7},{6,4},{7,5},{8,10},{9,11},{10,... | collective-permute-start | bytes 786440 | tf_op jit(solution)/shard_map/ppermute | solution.py:235
  13.9 1.5 %collective-permute-start.6 = (bf16[1024,128]{1,0:T(8,128)(2,1)S(1)}, bf16[1024,128]{1,0:T(8,128)(2,1)S(1)}, u32[]{:S(2)}, u32[]{:S(2)}) collective-permute-start(bf16[1024,128]{1,0:T(8,128)(2,1)S(1)} %collective-permute-done.4.refs_0_.refs_6_), channel_id=1, source_target_pairs={{0,16},{16,0},{1,17},{17,1},{2,18},{18,2},{3,19},{19,3},{4,20},{20... | collective-permute-start | bytes 786440 | tf_op jit(solution)/shard_map/ppermute | solution.py:247
  15.4 6.3 %collective-permute-done.2.refs_3_.refs_4_.refs_2_ = bf16[256,512]{1,0:T(8,128)(2,1)S(1)} collective-permute-done((bf16[256,512]{1,0:T(8,128)(2,1)S(1)}, bf16[256,512]{1,0:T(8,128)(2,1)S(1)}, u32[]{:S(2)}, u32[]{:S(2)}) %collective-permute-start.2) | collective-permute-done | bytes 262176 | tf_op jit(solution)/shard_map/ppermute | solution.py:226
  22.4 1.1 %collective-permute-start.3 = (bf16[256,512]{1,0:T(8,128)(2,1)S(1)}, bf16[256,512]{1,0:T(8,128)(2,1)S(1)}, u32[]{:S(2)}, u32[]{:S(2)}) collective-permute-start(bf16[256,512]{1,0:T(8,128)(2,1)S(1)} %collective-permute-done.2.refs_3_.refs_4_.refs_2_), channel_id=1, source_target_pairs={{0,2},{1,3},{2,0},{3,1},{4,6},{5,7},{6,4},{7,5},{8,10},{9,11},{10,... | collective-permute-start | bytes 786440 | tf_op jit(solution)/shard_map/ppermute | solution.py:235
  23.6 1.1 %collective-permute-done.7.refs_9_ = bf16[1024,128]{1,0:T(8,128)(2,1)S(1)} collective-permute-done((bf16[1024,128]{1,0:T(8,128)(2,1)}, bf16[1024,128]{1,0:T(8,128)(2,1)S(1)}, u32[]{:S(2)}, u32[]{:S(2)}) %collective-permute-start.7) | collective-permute-done | bytes 262176 | tf_op jit(solution)/shard_map/ppermute | solution.py:248
  24.7 0.9 %copy-done.1 = bf16[1024,128]{1,0:T(8,128)(2,1)S(1)} copy-done((bf16[1024,128]{1,0:T(8,128)(2,1)S(1)}, bf16[1024,128]{1,0:T(8,128)(2,1)}, u32[]{:S(2)}) %copy-start.1) | copy-done | bytes 262168
  27.0 1.9 %first_product.1 = (bf16[2048,512]{1,0:T(8,128)(2,1)S(1)}, f32[256,512]{1,0:T(8,128)S(1)}) custom-call(s32[8,8]{1,0:T(8,128)S(1)} %copy-done.4, s32[8,8]{1,0:T(8,128)S(1)} %copy-done.2, bf16[256,512]{1,0:T(8,128)(2,1)S(1)} %bitcast.6, bf16[256,512]{1,0:T(8,128)(2,1)S(1)} %collective-permute-done.refs_3_.refs_0_.refs_2_, ...), custom_call_target="tpu_custom_call" | custom-call | bytes 6553600 | tf_op jit(solution)/shard_map/first_product/pallas_call | solution.py:51
  28.9 3.5 %collective-permute-done.9.refs_3_.refs_0_.refs_7_ = bf16[256,512]{1,0:T(8,128)(2,1)S(1)} collective-permute-done((bf16[256,512]{1,0:T(8,128)(2,1)S(1)}, bf16[256,512]{1,0:T(8,128)(2,1)S(1)}, u32[]{:S(2)}, u32[]{:S(2)}) %collective-permute-start.9) | collective-permute-done | bytes 262176 | tf_op jit(solution)/shard_map/ppermute | solution.py:226
  32.4 0.9 %finish_product.1.refs_4_.refs_1_.refs_0_ = bf16[256,512]{1,0:T(8,128)(2,1)S(1)} custom-call(s32[8,8]{1,0:T(8,128)S(1)} %copy-done.2, bf16[2048,512]{1,0:T(8,128)(2,1)S(1)} %get-tuple-element.11.refs_1_, f32[256,512]{1,0:T(8,128)S(1)} %get-tuple-element.12.refs_2_, bf16[256,512]{1,0:T(8,128)(2,1)S(1)} %collective-permute-done.9.refs_3_.refs_0_.refs_7_), custom_call_target="tpu_custom_call" | custom-call | bytes 3145728 | tf_op jit(solution)/shard_map/finish_product/pallas_call | solution.py:51
  33.5 1.3 %collective-permute-start.12 = (bf16[256,512]{1,0:T(8,128)(2,1)S(1)}, bf16[256,512]{1,0:T(8,128)(2,1)S(1)}, u32[]{:S(2)}, u32[]{:S(2)}) collective-permute-start(bf16[256,512]{1,0:T(8,128)(2,1)S(1)} %finish_product.1.refs_4_.refs_1_.refs_0_), channel_id=1, source_target_pairs={{0,16},{16,0},{1,17},{17,1},{2,18},{18,2},{3,19},{19,3},{4,20},{20... | collective-permute-start | bytes 786440 | tf_op jit(solution)/shard_map/ppermute | solution.py:276
  34.8 1.6 %collective-permute-start.11 = (bf16[256,512]{1,0:T(8,128)(2,1)S(1)}, bf16[256,512]{1,0:T(8,128)(2,1)S(1)}, u32[]{:S(2)}, u32[]{:S(2)}) collective-permute-start(bf16[256,512]{1,0:T(8,128)(2,1)S(1)} %pack.6), channel_id=1, source_target_pairs={{0,2},{1,3},{2,0},{3,1},{4,6},{5,7},{6,4},{7,5},{8,10},{9,11},{10,... | collective-permute-start | bytes 786440 | tf_op jit(solution)/shard_map/ppermute | solution.py:235
  36.4 5.8 %collective-permute-done.12.refs_1_ = bf16[256,512]{1,0:T(8,128)(2,1)S(1)} collective-permute-done((bf16[256,512]{1,0:T(8,128)(2,1)S(1)}, bf16[256,512]{1,0:T(8,128)(2,1)S(1)}, u32[]{:S(2)}, u32[]{:S(2)}) %collective-permute-start.12) | collective-permute-done | bytes 262176 | tf_op jit(solution)/shard_map/ppermute | solution.py:276
  42.3 1.0 %collective-permute-done.11.refs_1_.refs_8_ = bf16[256,512]{1,0:T(8,128)(2,1)S(1)} collective-permute-done((bf16[256,512]{1,0:T(8,128)(2,1)S(1)}, bf16[256,512]{1,0:T(8,128)(2,1)S(1)}, u32[]{:S(2)}, u32[]{:S(2)}) %collective-permute-start.11) | collective-permute-done | bytes 262176 | tf_op jit(solution)/shard_map/ppermute | solution.py:235
  43.5 1.7 %collective-permute-start.14 = (bf16[128,512]{1,0:T(8,128)(2,1)S(1)}, bf16[128,512]{1,0:T(8,128)(2,1)S(1)}, u32[]{:S(2)}, u32[]{:S(2)}) collective-permute-start(bf16[128,512]{1,0:T(8,128)(2,1)S(1)} %get-tuple-element.14), channel_id=1, source_target_pairs={{0,8},{4,12},{8,0},{12,4},{1,9},{5,13},{9,1},{13,5},{2,10},{6,14},... | collective-permute-start | bytes 393224 | tf_op jit(solution)/shard_map/ppermute | solution.py:295
  45.2 2.6 %collective-permute-start.15 = (bf16[128,512]{1,0:T(8,128)(2,1)S(1)}, bf16[128,512]{1,0:T(8,128)(2,1)S(1)}, u32[]{:S(2)}, u32[]{:S(2)}) collective-permute-start(bf16[128,512]{1,0:T(8,128)(2,1)S(1)} %get-tuple-element.15), channel_id=1, source_target_pairs={{0,12},{4,8},{8,4},{12,0},{1,13},{5,9},{9,5},{13,1},{2,14},{6,10},... | collective-permute-start | bytes 393224 | tf_op jit(solution)/shard_map/ppermute | solution.py:295
  47.9 1.4 %layers.1.refs_0_ = bf16[1024,2048]{1,0:T(8,128)(2,1)S(1)} custom-call(s32[8,8]{1,0:T(8,128)S(1)} %copy-done.3, bf16[1024,512]{1,0:T(8,128)(2,1)S(1)} %copy-done, bf16[256,512]{1,0:T(8,128)(2,1)S(1)} %collective-permute-done.refs_3_.refs_0_.refs_2_, bf16[256,512]{1,0:T(8,128)(2,1)S(1)} %collective-permute-done.1.refs_4_.refs_1_.refs_3_, ...), custom_call_target="tpu_custom_call" | custom-call | bytes 8388608 | tf_op jit(solution)/shard_map/layers/pallas_call | solution.py:51
  49.3 2.0 %collective-permute-done.16.refs_2_ = bf16[128,512]{1,0:T(8,128)(2,1)S(1)} collective-permute-done((bf16[128,512]{1,0:T(8,128)(2,1)S(1)}, bf16[128,512]{1,0:T(8,128)(2,1)S(1)}, u32[]{:S(2)}, u32[]{:S(2)}) %collective-permute-start.16) | collective-permute-done | bytes 131104 | tf_op jit(solution)/shard_map/ppermute | solution.py:295
  52.0 4.5 %collective-permute-done.14.refs_1_ = bf16[128,512]{1,0:T(8,128)(2,1)S(1)} collective-permute-done((bf16[128,512]{1,0:T(8,128)(2,1)S(1)}, bf16[128,512]{1,0:T(8,128)(2,1)S(1)}, u32[]{:S(2)}, u32[]{:S(2)}) %collective-permute-start.14) | collective-permute-done | bytes 131104 | tf_op jit(solution)/shard_map/ppermute | solution.py:295
  56.4 1.4 %second_product.3 = bf16[1024,128]{1,0:T(8,128)(2,1)} custom-call(bf16[1024,2048]{1,0:T(8,128)(2,1)S(1)} %layers.1.refs_0_, bf16[128,512]{1,0:T(8,128)(2,1)S(1)} %collective-permute-done.14.refs_1_, bf16[128,512]{1,0:T(8,128)(2,1)S(1)} %collective-permute-done.15.refs_2_, f32[1024,128]{1,0:T(8,128)S(1)} %second_product.2.refs_3_), custom_call_target="tpu_custom_call" | custom-call | bytes 5242880 | tf_op jit(solution)/shard_map/second_product/pallas_call | solution.py:51
  (32 shorter events, 3.3 us)
Async XLA Ops:
  1.0 11.4 %collective-permute-start = (bf16[256,512]{1,0:T(8,128)(2,1)S(1)}, bf16[256,512]{1,0:T(8,128)(2,1)S(1)}, u32[]{:S(2)}, u32[]{:S(2)}) collective-permute-start(bf16[256,512]{1,0:T(8,128)(2,1)S(1)} %bitcast.5), channel_id=1, source_target_pairs={{0,4},{4,8},{8,12},{12,0},{1,5},{5,9},{9,13},{13,1},{2,6},{6,10},{... | collective-permute-start | bytes 786440 | tf_op jit(solution)/shard_map/ppermute | solution.py:226
  4.0 9.9 %collective-permute-start.4 = (bf16[1024,128]{1,0:T(8,128)(2,1)}, bf16[1024,128]{1,0:T(8,128)(2,1)S(1)}, u32[]{:S(2)}, u32[]{:S(2)}) collective-permute-start(bf16[1024,128]{1,0:T(8,128)(2,1)} %refs_5_.1), channel_id=1, source_target_pairs={{0,2},{1,3},{2,0},{3,1},{4,6},{5,7},{6,4},{7,5},{8,10},{9,11},{10,... | collective-permute-start | bytes 786440 | tf_op jit(solution)/shard_map/ppermute | solution.py:247
  5.6 9.8 %collective-permute-start.5 = (bf16[1024,128]{1,0:T(8,128)(2,1)}, bf16[1024,128]{1,0:T(8,128)(2,1)S(1)}, u32[]{:S(2)}, u32[]{:S(2)}) collective-permute-start(bf16[1024,128]{1,0:T(8,128)(2,1)} %refs_5_.1), channel_id=1, source_target_pairs={{0,16},{16,0},{1,17},{17,1},{2,18},{18,2},{3,19},{19,3},{4,20},{20... | collective-permute-start | bytes 786440 | tf_op jit(solution)/shard_map/ppermute | solution.py:247
  12.4 9.3 %collective-permute-start.2 = (bf16[256,512]{1,0:T(8,128)(2,1)S(1)}, bf16[256,512]{1,0:T(8,128)(2,1)S(1)}, u32[]{:S(2)}, u32[]{:S(2)}) collective-permute-start(bf16[256,512]{1,0:T(8,128)(2,1)S(1)} %collective-permute-done.refs_3_.refs_0_.refs_2_), channel_id=1, source_target_pairs={{0,4},{4,8},{8,12},{12,0},{1,5},{5,9},{9,13},{13,1},{2,6},{6,10},{... | collective-permute-start | bytes 786440 | tf_op jit(solution)/shard_map/ppermute | solution.py:226
  12.4 9.3 %collective-permute-start.1 = (bf16[256,512]{1,0:T(8,128)(2,1)S(1)}, bf16[256,512]{1,0:T(8,128)(2,1)S(1)}, u32[]{:S(2)}, u32[]{:S(2)}) collective-permute-start(bf16[256,512]{1,0:T(8,128)(2,1)S(1)} %collective-permute-done.refs_3_.refs_0_.refs_2_), channel_id=1, source_target_pairs={{0,2},{1,3},{2,0},{3,1},{4,6},{5,7},{6,4},{7,5},{8,10},{9,11},{10,... | collective-permute-start | bytes 786440 | tf_op jit(solution)/shard_map/ppermute | solution.py:235
  13.9 7.8 %collective-permute-start.6 = (bf16[1024,128]{1,0:T(8,128)(2,1)S(1)}, bf16[1024,128]{1,0:T(8,128)(2,1)S(1)}, u32[]{:S(2)}, u32[]{:S(2)}) collective-permute-start(bf16[1024,128]{1,0:T(8,128)(2,1)S(1)} %collective-permute-done.4.refs_0_.refs_6_), channel_id=1, source_target_pairs={{0,16},{16,0},{1,17},{17,1},{2,18},{18,2},{3,19},{19,3},{4,20},{20... | collective-permute-start | bytes 786440 | tf_op jit(solution)/shard_map/ppermute | solution.py:247
  21.7 2.9 %collective-permute-start.8 = (bf16[3072,128]{1,0:T(8,128)(2,1)S(1)}, bf16[3072,128]{1,0:T(8,128)(2,1)S(1)}, u32[]{:S(2)}, u32[]{:S(2)}) collective-permute-start(bf16[3072,128]{1,0:T(8,128)(2,1)S(1)} %pack.4), channel_id=1, source_target_pairs={{0,1},{1,0},{2,3},{3,2},{4,5},{5,4},{6,7},{7,6},{8,9},{9,8},{10,11... | collective-permute-start | bytes 2359304 | tf_op jit(solution)/shard_map/ppermute | solution.py:255
  21.8 2.9 %collective-permute-start.7 = (bf16[1024,128]{1,0:T(8,128)(2,1)}, bf16[1024,128]{1,0:T(8,128)(2,1)S(1)}, u32[]{:S(2)}, u32[]{:S(2)}) collective-permute-start(bf16[1024,128]{1,0:T(8,128)(2,1)} %refs_5_.1), channel_id=1, source_target_pairs={{0,1},{1,0},{2,3},{3,2},{4,5},{5,4},{6,7},{7,6},{8,9},{9,8},{10,11... | collective-permute-start | bytes 786440 | tf_op jit(solution)/shard_map/ppermute | solution.py:248
  22.3 10.1 %collective-permute-start.9 = (bf16[256,512]{1,0:T(8,128)(2,1)S(1)}, bf16[256,512]{1,0:T(8,128)(2,1)S(1)}, u32[]{:S(2)}, u32[]{:S(2)}) collective-permute-start(bf16[256,512]{1,0:T(8,128)(2,1)S(1)} %collective-permute-done.2.refs_3_.refs_4_.refs_2_), channel_id=1, source_target_pairs={{0,4},{4,8},{8,12},{12,0},{1,5},{5,9},{9,13},{13,1},{2,6},{6,10},{... | collective-permute-start | bytes 786440 | tf_op jit(solution)/shard_map/ppermute | solution.py:226
  22.4 10.9 %collective-permute-start.3 = (bf16[256,512]{1,0:T(8,128)(2,1)S(1)}, bf16[256,512]{1,0:T(8,128)(2,1)S(1)}, u32[]{:S(2)}, u32[]{:S(2)}) collective-permute-start(bf16[256,512]{1,0:T(8,128)(2,1)S(1)} %collective-permute-done.2.refs_3_.refs_4_.refs_2_), channel_id=1, source_target_pairs={{0,2},{1,3},{2,0},{3,1},{4,6},{5,7},{6,4},{7,5},{8,10},{9,11},{10,... | collective-permute-start | bytes 786440 | tf_op jit(solution)/shard_map/ppermute | solution.py:235
  24.7 1.0 %copy-start.1 = (bf16[1024,128]{1,0:T(8,128)(2,1)S(1)}, bf16[1024,128]{1,0:T(8,128)(2,1)}, u32[]{:S(2)}) copy-start(bf16[1024,128]{1,0:T(8,128)(2,1)} %refs_5_.1) | copy-start | bytes 786436
  25.6 0.7 %copy-start.2 = (s32[8,8]{1,0:T(8,128)S(1)}, s32[8,8]{1,0:T(8,128)}, u32[]{:S(2)}) copy-start(s32[8,8]{1,0:T(8,128)} %refs_0_.5) | copy-start | bytes 772
  26.3 0.7 %copy-start.4 = (s32[8,8]{1,0:T(8,128)S(1)}, s32[8,8]{1,0:T(8,128)}, u32[]{:S(2)}) copy-start(s32[8,8]{1,0:T(8,128)} %refs_0_.3) | copy-start | bytes 772
  32.4 15.5 %copy-start = (bf16[1024,512]{1,0:T(8,128)(2,1)S(1)}, bf16[1024,512]{1,0:T(8,128)(2,1)}, u32[]{:S(2)}) copy-start(bf16[1024,512]{1,0:T(8,128)(2,1)} %refs_1_.3) | copy-start | bytes 3145732
  32.4 15.5 %copy-start.3 = (s32[8,8]{1,0:T(8,128)S(1)}, s32[8,8]{1,0:T(8,128)}, u32[]{:S(2)}) copy-start(s32[8,8]{1,0:T(8,128)} %refs_0_.5) | copy-start | bytes 772
  33.4 14.5 %collective-permute-start.10 = (bf16[1024,512]{1,0:T(8,128)(2,1)S(1)}, bf16[1024,512]{1,0:T(8,128)(2,1)S(1)}, u32[]{:S(2)}, u32[]{:S(2)}) collective-permute-start(bf16[1024,512]{1,0:T(8,128)(2,1)S(1)} %pack.5), channel_id=1, source_target_pairs={{0,1},{1,0},{2,3},{3,2},{4,5},{5,4},{6,7},{7,6},{8,9},{9,8},{10,11... | collective-permute-start | bytes 3145736 | tf_op jit(solution)/shard_map/ppermute | solution.py:301
  33.5 8.7 %collective-permute-start.12 = (bf16[256,512]{1,0:T(8,128)(2,1)S(1)}, bf16[256,512]{1,0:T(8,128)(2,1)S(1)}, u32[]{:S(2)}, u32[]{:S(2)}) collective-permute-start(bf16[256,512]{1,0:T(8,128)(2,1)S(1)} %finish_product.1.refs_4_.refs_1_.refs_0_), channel_id=1, source_target_pairs={{0,16},{16,0},{1,17},{17,1},{2,18},{18,2},{3,19},{19,3},{4,20},{20... | collective-permute-start | bytes 786440 | tf_op jit(solution)/shard_map/ppermute | solution.py:276
  34.8 8.4 %collective-permute-start.11 = (bf16[256,512]{1,0:T(8,128)(2,1)S(1)}, bf16[256,512]{1,0:T(8,128)(2,1)S(1)}, u32[]{:S(2)}, u32[]{:S(2)}) collective-permute-start(bf16[256,512]{1,0:T(8,128)(2,1)S(1)} %pack.6), channel_id=1, source_target_pairs={{0,2},{1,3},{2,0},{3,1},{4,6},{5,7},{6,4},{7,5},{8,10},{9,11},{10,... | collective-permute-start | bytes 786440 | tf_op jit(solution)/shard_map/ppermute | solution.py:235
  43.3 4.5 %collective-permute-start.13 = (bf16[512,512]{1,0:T(8,128)(2,1)S(1)}, bf16[512,512]{1,0:T(8,128)(2,1)S(1)}, u32[]{:S(2)}, u32[]{:S(2)}) collective-permute-start(bf16[512,512]{1,0:T(8,128)(2,1)S(1)} %pack.7), channel_id=1, source_target_pairs={{0,1},{1,0},{2,3},{3,2},{4,5},{5,4},{6,7},{7,6},{8,9},{9,8},{10,11... | collective-permute-start | bytes 1572872 | tf_op jit(solution)/shard_map/ppermute | solution.py:301
  43.4 7.9 %collective-permute-start.16 = (bf16[128,512]{1,0:T(8,128)(2,1)S(1)}, bf16[128,512]{1,0:T(8,128)(2,1)S(1)}, u32[]{:S(2)}, u32[]{:S(2)}) collective-permute-start(bf16[128,512]{1,0:T(8,128)(2,1)S(1)} %get-tuple-element.16), channel_id=1, source_target_pairs={{0,4},{4,0},{8,12},{12,8},{1,5},{5,1},{9,13},{13,9},{2,6},{6,2},{1... | collective-permute-start | bytes 393224 | tf_op jit(solution)/shard_map/ppermute | solution.py:295
  43.5 12.9 %collective-permute-start.14 = (bf16[128,512]{1,0:T(8,128)(2,1)S(1)}, bf16[128,512]{1,0:T(8,128)(2,1)S(1)}, u32[]{:S(2)}, u32[]{:S(2)}) collective-permute-start(bf16[128,512]{1,0:T(8,128)(2,1)S(1)} %get-tuple-element.14), channel_id=1, source_target_pairs={{0,8},{4,12},{8,0},{12,4},{1,9},{5,13},{9,1},{13,5},{2,10},{6,14},... | collective-permute-start | bytes 393224 | tf_op jit(solution)/shard_map/ppermute | solution.py:295
  45.2 11.2 %collective-permute-start.15 = (bf16[128,512]{1,0:T(8,128)(2,1)S(1)}, bf16[128,512]{1,0:T(8,128)(2,1)S(1)}, u32[]{:S(2)}, u32[]{:S(2)}) collective-permute-start(bf16[128,512]{1,0:T(8,128)(2,1)S(1)} %get-tuple-element.15), channel_id=1, source_target_pairs={{0,12},{4,8},{8,4},{12,0},{1,13},{5,9},{9,5},{13,1},{2,14},{6,10},... | collective-permute-start | bytes 393224 | tf_op jit(solution)/shard_map/ppermute | solution.py:295

commit v9 on v8

--- a/solution.py
+++ b/solution.py
@@ -291,9 +291,10 @@
         [table],
         after=[crossed[-1]],
     )
-    messages = [outgoing[0]] + [
-        lax.ppermute(outgoing[d], "col", flip(cols, d)) for d in range(1, cols)
+    messages = [
+        lax.ppermute(outgoing[d], "col", flip(cols, d)) for d in range(cols - 1, 0, -1)
     ]
+    messages = [outgoing[0]] + messages[::-1]
 
     for group, gate in ((range(1, cols - 1), [product]), ([cols - 1], [outgoing[0]])):
         arrays = [a for s in group for a in (slots[s], crossed[s - 1])]
@@ -311,8 +312,9 @@
         smem=[z_pattern],
     )[0]
     total = []
-    for part in (range(cols // 2), range(cols // 2, cols)):
-        last_part = part[-1] == cols - 1
+    far = list(range(cols - 1, cols // 2, -1))
+    for part in ([0, *far], [d for d in range(cols - 1, 0, -1) if d not in far]):
+        last_part = 0 not in part
         total = run(
             functools.partial(second_kernel, sizes, part),
             "second_product",

time: 58.1 us -> 58.4 us (level)
  no operation moved by 1% of the time
where the time goes in v9:
time: 58.4 us; the launch traced here: 58.2 us
  waiting for transfers between devices  29.7 us (51%)
  starting transfers between devices  18.4 us (32%)
  Pallas kernels  6.62 us (11%)
  local copies, waits for them, and re-layouts  3.3 us (6%)
    ppermute x3, waiting for transfers between devices, local(): slots.append(lax.ppermute(slots[-1], 'col', ring))  15 us
    ppermute x3, waiting for transfers between devices, local(): lax.ppermute(outgoing[d], 'col', flip(cols, d))  6.79 us
    pallas_call x11, Pallas kernels, run(): pl.pallas_call(body, out_shape=list(outs), in_specs=[pl.BlockSpec(memory_...  6.62 us
    ppermute x1, waiting for transfers between devices, local(): gathered[dr ^ bit] = lax.ppermute(piece, 'row', flip(rows, bit))  5.81 us
    ppermute x3, starting transfers between devices, local(): h_arrays.append(lax.ppermute(source, axis, perm))  4.5 us
    ppermute x3, starting transfers between devices, local(): lax.ppermute(outgoing[d], 'col', flip(cols, d))  4.45 us
    ppermute x3, starting transfers between devices, cross(): return lax.ppermute(piece, 'layer', flip(layers, layer_bits[0]))  4.25 us
    ppermute x3, starting transfers between devices, local(): slots.append(lax.ppermute(slots[-1], 'col', ring))  3.21 us
  transfers between devices with their start and end apart: 17, of which 8 were waited for; matrix products, arithmetic and copies ran while one was open for 0% of the time, Pallas kernels for 9%

profile of v9, /device:TPU:0, one launch (start us, length us, event | category | flops | bytes accessed | tf_op | source)
XLA Modules:
  0.0 58.2 jit_solution(7459982706937198455)
XLA Ops:
  0.0 1.0 %constant_dynamic-slice_fusion = bf16[2,1,128,512]{3,2,1,0:T(8,128)(2,1)S(1)} fusion(bf16[2,4,128,512]{3,2,1,0:T(8,128)(2,1)} %bitcast.4, s32[]{:T(128)S(6)} %select_n.4), kind=kLoop, calls=%fused_computation | loop fusion | bytes 524292 | tf_op jit(solution)/shard_map/jit(dynamic_index_in_dim)/dynamic_slice | solution.py:222
  1.0 3.1 %collective-permute-start = (bf16[256,512]{1,0:T(8,128)(2,1)S(1)}, bf16[256,512]{1,0:T(8,128)(2,1)S(1)}, u32[]{:S(2)}, u32[]{:S(2)}) collective-permute-start(bf16[256,512]{1,0:T(8,128)(2,1)S(1)} %bitcast.5), channel_id=1, source_target_pairs={{0,4},{4,8},{8,12},{12,0},{1,5},{5,9},{9,13},{13,1},{2,6},{6,10},{... | collective-permute-start | bytes 786440 | tf_op jit(solution)/shard_map/ppermute | solution.py:226
  4.0 1.5 %collective-permute-start.4 = (bf16[1024,128]{1,0:T(8,128)(2,1)}, bf16[1024,128]{1,0:T(8,128)(2,1)S(1)}, u32[]{:S(2)}, u32[]{:S(2)}) collective-permute-start(bf16[1024,128]{1,0:T(8,128)(2,1)} %refs_5_.1), channel_id=1, source_target_pairs={{0,2},{1,3},{2,0},{3,1},{4,6},{5,7},{6,4},{7,5},{8,10},{9,11},{10,... | collective-permute-start | bytes 786440 | tf_op jit(solution)/shard_map/ppermute | solution.py:247
  5.6 1.5 %collective-permute-start.5 = (bf16[1024,128]{1,0:T(8,128)(2,1)}, bf16[1024,128]{1,0:T(8,128)(2,1)S(1)}, u32[]{:S(2)}, u32[]{:S(2)}) collective-permute-start(bf16[1024,128]{1,0:T(8,128)(2,1)} %refs_5_.1), channel_id=1, source_target_pairs={{0,16},{16,0},{1,17},{17,1},{2,18},{18,2},{3,19},{19,3},{4,20},{20... | collective-permute-start | bytes 786440 | tf_op jit(solution)/shard_map/ppermute | solution.py:247
  7.1 5.3 %collective-permute-done.refs_3_.refs_0_.refs_2_ = bf16[256,512]{1,0:T(8,128)(2,1)S(1)} collective-permute-done((bf16[256,512]{1,0:T(8,128)(2,1)S(1)}, bf16[256,512]{1,0:T(8,128)(2,1)S(1)}, u32[]{:S(2)}, u32[]{:S(2)}) %collective-permute-start) | collective-permute-done | bytes 262176 | tf_op jit(solution)/shard_map/ppermute | solution.py:226
  12.4 1.5 %collective-permute-start.1 = (bf16[256,512]{1,0:T(8,128)(2,1)S(1)}, bf16[256,512]{1,0:T(8,128)(2,1)S(1)}, u32[]{:S(2)}, u32[]{:S(2)}) collective-permute-start(bf16[256,512]{1,0:T(8,128)(2,1)S(1)} %collective-permute-done.refs_3_.refs_0_.refs_2_), channel_id=1, source_target_pairs={{0,2},{1,3},{2,0},{3,1},{4,6},{5,7},{6,4},{7,5},{8,10},{9,11},{10,... | collective-permute-start | bytes 786440 | tf_op jit(solution)/shard_map/ppermute | solution.py:235
  13.9 1.5 %collective-permute-start.6 = (bf16[1024,128]{1,0:T(8,128)(2,1)S(1)}, bf16[1024,128]{1,0:T(8,128)(2,1)S(1)}, u32[]{:S(2)}, u32[]{:S(2)}) collective-permute-start(bf16[1024,128]{1,0:T(8,128)(2,1)S(1)} %collective-permute-done.4.refs_0_.refs_6_), channel_id=1, source_target_pairs={{0,16},{16,0},{1,17},{17,1},{2,18},{18,2},{3,19},{19,3},{4,20},{20... | collective-permute-start | bytes 786440 | tf_op jit(solution)/shard_map/ppermute | solution.py:247
  15.4 6.3 %collective-permute-done.2.refs_3_.refs_4_.refs_2_ = bf16[256,512]{1,0:T(8,128)(2,1)S(1)} collective-permute-done((bf16[256,512]{1,0:T(8,128)(2,1)S(1)}, bf16[256,512]{1,0:T(8,128)(2,1)S(1)}, u32[]{:S(2)}, u32[]{:S(2)}) %collective-permute-start.2) | collective-permute-done | bytes 262176 | tf_op jit(solution)/shard_map/ppermute | solution.py:226
  22.4 1.1 %collective-permute-start.3 = (bf16[256,512]{1,0:T(8,128)(2,1)S(1)}, bf16[256,512]{1,0:T(8,128)(2,1)S(1)}, u32[]{:S(2)}, u32[]{:S(2)}) collective-permute-start(bf16[256,512]{1,0:T(8,128)(2,1)S(1)} %collective-permute-done.2.refs_3_.refs_4_.refs_2_), channel_id=1, source_target_pairs={{0,2},{1,3},{2,0},{3,1},{4,6},{5,7},{6,4},{7,5},{8,10},{9,11},{10,... | collective-permute-start | bytes 786440 | tf_op jit(solution)/shard_map/ppermute | solution.py:235
  23.6 1.1 %collective-permute-done.7.refs_9_ = bf16[1024,128]{1,0:T(8,128)(2,1)S(1)} collective-permute-done((bf16[1024,128]{1,0:T(8,128)(2,1)}, bf16[1024,128]{1,0:T(8,128)(2,1)S(1)}, u32[]{:S(2)}, u32[]{:S(2)}) %collective-permute-start.7) | collective-permute-done | bytes 262176 | tf_op jit(solution)/shard_map/ppermute | solution.py:248
  24.7 0.9 %copy-done.1 = bf16[1024,128]{1,0:T(8,128)(2,1)S(1)} copy-done((bf16[1024,128]{1,0:T(8,128)(2,1)S(1)}, bf16[1024,128]{1,0:T(8,128)(2,1)}, u32[]{:S(2)}) %copy-start.1) | copy-done | bytes 262168
  27.0 1.9 %first_product.1 = (bf16[2048,512]{1,0:T(8,128)(2,1)S(1)}, f32[256,512]{1,0:T(8,128)S(1)}) custom-call(s32[8,8]{1,0:T(8,128)S(1)} %copy-done.4, s32[8,8]{1,0:T(8,128)S(1)} %copy-done.2, bf16[256,512]{1,0:T(8,128)(2,1)S(1)} %bitcast.6, bf16[256,512]{1,0:T(8,128)(2,1)S(1)} %collective-permute-done.refs_3_.refs_0_.refs_2_, ...), custom_call_target="tpu_custom_call" | custom-call | bytes 6553600 | tf_op jit(solution)/shard_map/first_product/pallas_call | solution.py:51
  29.0 3.4 %collective-permute-done.9.refs_3_.refs_0_.refs_7_ = bf16[256,512]{1,0:T(8,128)(2,1)S(1)} collective-permute-done((bf16[256,512]{1,0:T(8,128)(2,1)S(1)}, bf16[256,512]{1,0:T(8,128)(2,1)S(1)}, u32[]{:S(2)}, u32[]{:S(2)}) %collective-permute-start.9) | collective-permute-done | bytes 262176 | tf_op jit(solution)/shard_map/ppermute | solution.py:226
  32.4 0.9 %finish_product.1.refs_4_.refs_1_.refs_0_ = bf16[256,512]{1,0:T(8,128)(2,1)S(1)} custom-call(s32[8,8]{1,0:T(8,128)S(1)} %copy-done.2, bf16[2048,512]{1,0:T(8,128)(2,1)S(1)} %get-tuple-element.11.refs_1_, f32[256,512]{1,0:T(8,128)S(1)} %get-tuple-element.12.refs_2_, bf16[256,512]{1,0:T(8,128)(2,1)S(1)} %collective-permute-done.9.refs_3_.refs_0_.refs_7_), custom_call_target="tpu_custom_call" | custom-call | bytes 3145728 | tf_op jit(solution)/shard_map/finish_product/pallas_call | solution.py:51
  33.5 1.3 %collective-permute-start.12 = (bf16[256,512]{1,0:T(8,128)(2,1)S(1)}, bf16[256,512]{1,0:T(8,128)(2,1)S(1)}, u32[]{:S(2)}, u32[]{:S(2)}) collective-permute-start(bf16[256,512]{1,0:T(8,128)(2,1)S(1)} %finish_product.1.refs_4_.refs_1_.refs_0_), channel_id=1, source_target_pairs={{0,16},{16,0},{1,17},{17,1},{2,18},{18,2},{3,19},{19,3},{4,20},{20... | collective-permute-start | bytes 786440 | tf_op jit(solution)/shard_map/ppermute | solution.py:276
  34.8 1.6 %collective-permute-start.11 = (bf16[256,512]{1,0:T(8,128)(2,1)S(1)}, bf16[256,512]{1,0:T(8,128)(2,1)S(1)}, u32[]{:S(2)}, u32[]{:S(2)}) collective-permute-start(bf16[256,512]{1,0:T(8,128)(2,1)S(1)} %pack.6), channel_id=1, source_target_pairs={{0,2},{1,3},{2,0},{3,1},{4,6},{5,7},{6,4},{7,5},{8,10},{9,11},{10,... | collective-permute-start | bytes 786440 | tf_op jit(solution)/shard_map/ppermute | solution.py:235
  36.4 5.8 %collective-permute-done.12.refs_1_ = bf16[256,512]{1,0:T(8,128)(2,1)S(1)} collective-permute-done((bf16[256,512]{1,0:T(8,128)(2,1)S(1)}, bf16[256,512]{1,0:T(8,128)(2,1)S(1)}, u32[]{:S(2)}, u32[]{:S(2)}) %collective-permute-start.12) | collective-permute-done | bytes 262176 | tf_op jit(solution)/shard_map/ppermute | solution.py:276
  42.3 1.0 %collective-permute-done.11.refs_1_.refs_8_ = bf16[256,512]{1,0:T(8,128)(2,1)S(1)} collective-permute-done((bf16[256,512]{1,0:T(8,128)(2,1)S(1)}, bf16[256,512]{1,0:T(8,128)(2,1)S(1)}, u32[]{:S(2)}, u32[]{:S(2)}) %collective-permute-start.11) | collective-permute-done | bytes 262176 | tf_op jit(solution)/shard_map/ppermute | solution.py:235
  43.4 1.2 %collective-permute-start.16 = (bf16[128,512]{1,0:T(8,128)(2,1)S(1)}, bf16[128,512]{1,0:T(8,128)(2,1)S(1)}, u32[]{:S(2)}, u32[]{:S(2)}) collective-permute-start(bf16[128,512]{1,0:T(8,128)(2,1)S(1)} %get-tuple-element.16), channel_id=1, source_target_pairs={{0,12},{4,8},{8,4},{12,0},{1,13},{5,9},{9,5},{13,1},{2,14},{6,10},... | collective-permute-start | bytes 393224 | tf_op jit(solution)/shard_map/ppermute | solution.py:295
  44.7 3.2 %collective-permute-start.15 = (bf16[128,512]{1,0:T(8,128)(2,1)S(1)}, bf16[128,512]{1,0:T(8,128)(2,1)S(1)}, u32[]{:S(2)}, u32[]{:S(2)}) collective-permute-start(bf16[128,512]{1,0:T(8,128)(2,1)S(1)} %get-tuple-element.15), channel_id=1, source_target_pairs={{0,4},{4,0},{8,12},{12,8},{1,5},{5,1},{9,13},{13,9},{2,6},{6,2},{1... | collective-permute-start | bytes 393224 | tf_op jit(solution)/shard_map/ppermute | solution.py:295
  47.9 1.4 %layers.1.refs_0_ = bf16[1024,2048]{1,0:T(8,128)(2,1)S(1)} custom-call(s32[8,8]{1,0:T(8,128)S(1)} %copy-done.3, bf16[1024,512]{1,0:T(8,128)(2,1)S(1)} %copy-done, bf16[256,512]{1,0:T(8,128)(2,1)S(1)} %collective-permute-done.refs_3_.refs_0_.refs_2_, bf16[256,512]{1,0:T(8,128)(2,1)S(1)} %collective-permute-done.1.refs_4_.refs_1_.refs_3_, ...), custom_call_target="tpu_custom_call" | custom-call | bytes 8388608 | tf_op jit(solution)/shard_map/layers/pallas_call | solution.py:51
  49.3 2.4 %collective-permute-done.16.refs_2_ = bf16[128,512]{1,0:T(8,128)(2,1)S(1)} collective-permute-done((bf16[128,512]{1,0:T(8,128)(2,1)S(1)}, bf16[128,512]{1,0:T(8,128)(2,1)S(1)}, u32[]{:S(2)}, u32[]{:S(2)}) %collective-permute-start.16) | collective-permute-done | bytes 131104 | tf_op jit(solution)/shard_map/ppermute | solution.py:295
  52.4 4.4 %collective-permute-done.14.refs_1_ = bf16[128,512]{1,0:T(8,128)(2,1)S(1)} collective-permute-done((bf16[128,512]{1,0:T(8,128)(2,1)S(1)}, bf16[128,512]{1,0:T(8,128)(2,1)S(1)}, u32[]{:S(2)}, u32[]{:S(2)}) %collective-permute-start.14) | collective-permute-done | bytes 131104 | tf_op jit(solution)/shard_map/ppermute | solution.py:295
  56.8 1.4 %second_product.3 = bf16[1024,128]{1,0:T(8,128)(2,1)} custom-call(bf16[1024,2048]{1,0:T(8,128)(2,1)S(1)} %layers.1.refs_0_, bf16[128,512]{1,0:T(8,128)(2,1)S(1)} %collective-permute-done.14.refs_1_, bf16[128,512]{1,0:T(8,128)(2,1)S(1)} %collective-permute-done.15.refs_2_, f32[1024,128]{1,0:T(8,128)S(1)} %second_product.2.refs_3_), custom_call_target="tpu_custom_call" | custom-call | bytes 5242880 | tf_op jit(solution)/shard_map/second_product/pallas_call | solution.py:51
  (32 shorter events, 3.2 us)
Async XLA Ops:
  1.0 11.4 %collective-permute-start = (bf16[256,512]{1,0:T(8,128)(2,1)S(1)}, bf16[256,512]{1,0:T(8,128)(2,1)S(1)}, u32[]{:S(2)}, u32[]{:S(2)}) collective-permute-start(bf16[256,512]{1,0:T(8,128)(2,1)S(1)} %bitcast.5), channel_id=1, source_target_pairs={{0,4},{4,8},{8,12},{12,0},{1,5},{5,9},{9,13},{13,1},{2,6},{6,10},{... | collective-permute-start | bytes 786440 | tf_op jit(solution)/shard_map/ppermute | solution.py:226
  4.0 9.9 %collective-permute-start.4 = (bf16[1024,128]{1,0:T(8,128)(2,1)}, bf16[1024,128]{1,0:T(8,128)(2,1)S(1)}, u32[]{:S(2)}, u32[]{:S(2)}) collective-permute-start(bf16[1024,128]{1,0:T(8,128)(2,1)} %refs_5_.1), channel_id=1, source_target_pairs={{0,2},{1,3},{2,0},{3,1},{4,6},{5,7},{6,4},{7,5},{8,10},{9,11},{10,... | collective-permute-start | bytes 786440 | tf_op jit(solution)/shard_map/ppermute | solution.py:247
  5.6 9.8 %collective-permute-start.5 = (bf16[1024,128]{1,0:T(8,128)(2,1)}, bf16[1024,128]{1,0:T(8,128)(2,1)S(1)}, u32[]{:S(2)}, u32[]{:S(2)}) collective-permute-start(bf16[1024,128]{1,0:T(8,128)(2,1)} %refs_5_.1), channel_id=1, source_target_pairs={{0,16},{16,0},{1,17},{17,1},{2,18},{18,2},{3,19},{19,3},{4,20},{20... | collective-permute-start | bytes 786440 | tf_op jit(solution)/shard_map/ppermute | solution.py:247
  12.4 9.3 %collective-permute-start.2 = (bf16[256,512]{1,0:T(8,128)(2,1)S(1)}, bf16[256,512]{1,0:T(8,128)(2,1)S(1)}, u32[]{:S(2)}, u32[]{:S(2)}) collective-permute-start(bf16[256,512]{1,0:T(8,128)(2,1)S(1)} %collective-permute-done.refs_3_.refs_0_.refs_2_), channel_id=1, source_target_pairs={{0,4},{4,8},{8,12},{12,0},{1,5},{5,9},{9,13},{13,1},{2,6},{6,10},{... | collective-permute-start | bytes 786440 | tf_op jit(solution)/shard_map/ppermute | solution.py:226
  12.4 9.3 %collective-permute-start.1 = (bf16[256,512]{1,0:T(8,128)(2,1)S(1)}, bf16[256,512]{1,0:T(8,128)(2,1)S(1)}, u32[]{:S(2)}, u32[]{:S(2)}) collective-permute-start(bf16[256,512]{1,0:T(8,128)(2,1)S(1)} %collective-permute-done.refs_3_.refs_0_.refs_2_), channel_id=1, source_target_pairs={{0,2},{1,3},{2,0},{3,1},{4,6},{5,7},{6,4},{7,5},{8,10},{9,11},{10,... | collective-permute-start | bytes 786440 | tf_op jit(solution)/shard_map/ppermute | solution.py:235
  13.9 7.8 %collective-permute-start.6 = (bf16[1024,128]{1,0:T(8,128)(2,1)S(1)}, bf16[1024,128]{1,0:T(8,128)(2,1)S(1)}, u32[]{:S(2)}, u32[]{:S(2)}) collective-permute-start(bf16[1024,128]{1,0:T(8,128)(2,1)S(1)} %collective-permute-done.4.refs_0_.refs_6_), channel_id=1, source_target_pairs={{0,16},{16,0},{1,17},{17,1},{2,18},{18,2},{3,19},{19,3},{4,20},{20... | collective-permute-start | bytes 786440 | tf_op jit(solution)/shard_map/ppermute | solution.py:247
  21.7 2.9 %collective-permute-start.8 = (bf16[3072,128]{1,0:T(8,128)(2,1)S(1)}, bf16[3072,128]{1,0:T(8,128)(2,1)S(1)}, u32[]{:S(2)}, u32[]{:S(2)}) collective-permute-start(bf16[3072,128]{1,0:T(8,128)(2,1)S(1)} %pack.4), channel_id=1, source_target_pairs={{0,1},{1,0},{2,3},{3,2},{4,5},{5,4},{6,7},{7,6},{8,9},{9,8},{10,11... | collective-permute-start | bytes 2359304 | tf_op jit(solution)/shard_map/ppermute | solution.py:255
  21.8 2.9 %collective-permute-start.7 = (bf16[1024,128]{1,0:T(8,128)(2,1)}, bf16[1024,128]{1,0:T(8,128)(2,1)S(1)}, u32[]{:S(2)}, u32[]{:S(2)}) collective-permute-start(bf16[1024,128]{1,0:T(8,128)(2,1)} %refs_5_.1), channel_id=1, source_target_pairs={{0,1},{1,0},{2,3},{3,2},{4,5},{5,4},{6,7},{7,6},{8,9},{9,8},{10,11... | collective-permute-start | bytes 786440 | tf_op jit(solution)/shard_map/ppermute | solution.py:248
  22.3 10.1 %collective-permute-start.9 = (bf16[256,512]{1,0:T(8,128)(2,1)S(1)}, bf16[256,512]{1,0:T(8,128)(2,1)S(1)}, u32[]{:S(2)}, u32[]{:S(2)}) collective-permute-start(bf16[256,512]{1,0:T(8,128)(2,1)S(1)} %collective-permute-done.2.refs_3_.refs_4_.refs_2_), channel_id=1, source_target_pairs={{0,4},{4,8},{8,12},{12,0},{1,5},{5,9},{9,13},{13,1},{2,6},{6,10},{... | collective-permute-start | bytes 786440 | tf_op jit(solution)/shard_map/ppermute | solution.py:226
  22.4 10.9 %collective-permute-start.3 = (bf16[256,512]{1,0:T(8,128)(2,1)S(1)}, bf16[256,512]{1,0:T(8,128)(2,1)S(1)}, u32[]{:S(2)}, u32[]{:S(2)}) collective-permute-start(bf16[256,512]{1,0:T(8,128)(2,1)S(1)} %collective-permute-done.2.refs_3_.refs_4_.refs_2_), channel_id=1, source_target_pairs={{0,2},{1,3},{2,0},{3,1},{4,6},{5,7},{6,4},{7,5},{8,10},{9,11},{10,... | collective-permute-start | bytes 786440 | tf_op jit(solution)/shard_map/ppermute | solution.py:235
  24.7 1.0 %copy-start.1 = (bf16[1024,128]{1,0:T(8,128)(2,1)S(1)}, bf16[1024,128]{1,0:T(8,128)(2,1)}, u32[]{:S(2)}) copy-start(bf16[1024,128]{1,0:T(8,128)(2,1)} %refs_5_.1) | copy-start | bytes 786436
  25.6 0.7 %copy-start.2 = (s32[8,8]{1,0:T(8,128)S(1)}, s32[8,8]{1,0:T(8,128)}, u32[]{:S(2)}) copy-start(s32[8,8]{1,0:T(8,128)} %refs_0_.5) | copy-start | bytes 772
  26.3 0.7 %copy-start.4 = (s32[8,8]{1,0:T(8,128)S(1)}, s32[8,8]{1,0:T(8,128)}, u32[]{:S(2)}) copy-start(s32[8,8]{1,0:T(8,128)} %refs_0_.3) | copy-start | bytes 772
  32.4 15.5 %copy-start = (bf16[1024,512]{1,0:T(8,128)(2,1)S(1)}, bf16[1024,512]{1,0:T(8,128)(2,1)}, u32[]{:S(2)}) copy-start(bf16[1024,512]{1,0:T(8,128)(2,1)} %refs_1_.3) | copy-start | bytes 3145732
  32.4 15.5 %copy-start.3 = (s32[8,8]{1,0:T(8,128)S(1)}, s32[8,8]{1,0:T(8,128)}, u32[]{:S(2)}) copy-start(s32[8,8]{1,0:T(8,128)} %refs_0_.5) | copy-start | bytes 772
  33.4 14.5 %collective-permute-start.10 = (bf16[1024,512]{1,0:T(8,128)(2,1)S(1)}, bf16[1024,512]{1,0:T(8,128)(2,1)S(1)}, u32[]{:S(2)}, u32[]{:S(2)}) collective-permute-start(bf16[1024,512]{1,0:T(8,128)(2,1)S(1)} %pack.5), channel_id=1, source_target_pairs={{0,1},{1,0},{2,3},{3,2},{4,5},{5,4},{6,7},{7,6},{8,9},{9,8},{10,11... | collective-permute-start | bytes 3145736 | tf_op jit(solution)/shard_map/ppermute | solution.py:302
  33.5 8.7 %collective-permute-start.12 = (bf16[256,512]{1,0:T(8,128)(2,1)S(1)}, bf16[256,512]{1,0:T(8,128)(2,1)S(1)}, u32[]{:S(2)}, u32[]{:S(2)}) collective-permute-start(bf16[256,512]{1,0:T(8,128)(2,1)S(1)} %finish_product.1.refs_4_.refs_1_.refs_0_), channel_id=1, source_target_pairs={{0,16},{16,0},{1,17},{17,1},{2,18},{18,2},{3,19},{19,3},{4,20},{20... | collective-permute-start | bytes 786440 | tf_op jit(solution)/shard_map/ppermute | solution.py:276
  34.8 8.4 %collective-permute-start.11 = (bf16[256,512]{1,0:T(8,128)(2,1)S(1)}, bf16[256,512]{1,0:T(8,128)(2,1)S(1)}, u32[]{:S(2)}, u32[]{:S(2)}) collective-permute-start(bf16[256,512]{1,0:T(8,128)(2,1)S(1)} %pack.6), channel_id=1, source_target_pairs={{0,2},{1,3},{2,0},{3,1},{4,6},{5,7},{6,4},{7,5},{8,10},{9,11},{10,... | collective-permute-start | bytes 786440 | tf_op jit(solution)/shard_map/ppermute | solution.py:235
  43.3 4.5 %collective-permute-start.13 = (bf16[512,512]{1,0:T(8,128)(2,1)S(1)}, bf16[512,512]{1,0:T(8,128)(2,1)S(1)}, u32[]{:S(2)}, u32[]{:S(2)}) collective-permute-start(bf16[512,512]{1,0:T(8,128)(2,1)S(1)} %pack.7), channel_id=1, source_target_pairs={{0,1},{1,0},{2,3},{3,2},{4,5},{5,4},{6,7},{7,6},{8,9},{9,8},{10,11... | collective-permute-start | bytes 1572872 | tf_op jit(solution)/shard_map/ppermute | solution.py:302
  43.4 8.3 %collective-permute-start.16 = (bf16[128,512]{1,0:T(8,128)(2,1)S(1)}, bf16[128,512]{1,0:T(8,128)(2,1)S(1)}, u32[]{:S(2)}, u32[]{:S(2)}) collective-permute-start(bf16[128,512]{1,0:T(8,128)(2,1)S(1)} %get-tuple-element.16), channel_id=1, source_target_pairs={{0,12},{4,8},{8,4},{12,0},{1,13},{5,9},{9,5},{13,1},{2,14},{6,10},... | collective-permute-start | bytes 393224 | tf_op jit(solution)/shard_map/ppermute | solution.py:295
  44.7 12.1 %collective-permute-start.14 = (bf16[128,512]{1,0:T(8,128)(2,1)S(1)}, bf16[128,512]{1,0:T(8,128)(2,1)S(1)}, u32[]{:S(2)}, u32[]{:S(2)}) collective-permute-start(bf16[128,512]{1,0:T(8,128)(2,1)S(1)} %get-tuple-element.14), channel_id=1, source_target_pairs={{0,8},{4,12},{8,0},{12,4},{1,9},{5,13},{9,1},{13,5},{2,10},{6,14},... | collective-permute-start | bytes 393224 | tf_op jit(solution)/shard_map/ppermute | solution.py:295
  44.7 12.1 %collective-permute-start.15 = (bf16[128,512]{1,0:T(8,128)(2,1)S(1)}, bf16[128,512]{1,0:T(8,128)(2,1)S(1)}, u32[]{:S(2)}, u32[]{:S(2)}) collective-permute-start(bf16[128,512]{1,0:T(8,128)(2,1)S(1)} %get-tuple-element.15), channel_id=1, source_target_pairs={{0,4},{4,0},{8,12},{12,8},{1,5},{5,1},{9,13},{13,9},{2,6},{6,2},{1... | collective-permute-start | bytes 393224 | tf_op jit(solution)/shard_map/ppermute | solution.py:295

commit v10 on v8

v10 whole, which is shorter than its diff:
```python
import functools
from typing import NamedTuple

import jax
import jax.numpy as jnp
from jax import lax
from jax.experimental import pallas as pl
from jax.experimental.pallas import tpu as pltpu
from jax.sharding import PartitionSpec as P

BS = 256
MARGIN = 4 * 1024 * 1024


class Sizes(NamedTuple):
    rows: int
    cols: int
    layers: int
    rows_here: int
    cols_here: int
    quarter: int
    per: int


def bits_of(size):
    return [1 << b for b in reversed(range(size.bit_length() - 1))]


def flip(size, bit):
    return [(i, i ^ bit) for i in range(size)]


def mod(a, n):
    return lax.rem(a + n, n)


def place():
    return lax.axis_index("row"), lax.axis_index("col"), lax.axis_index("layer")


def run(kernel, name, outs, arrays, smem=(), after=(), scratch=(), flops=0):
    size = sum(a.size * a.dtype.itemsize for a in arrays)
    size += sum(o.size * o.dtype.itemsize for o in outs)
    for kept in scratch:
        size += kept.shape[0] * kept.shape[1] * jnp.dtype(kept.dtype).itemsize
    skip = len(smem) + len(arrays)

    def body(*refs):
        kernel(*refs[:skip], *refs[skip + len(after) :])

    return pl.pallas_call(
        body,
        out_shape=list(outs),
        in_specs=[pl.BlockSpec(memory_space=pltpu.SMEM)] * len(smem)
        + [pl.BlockSpec(memory_space=pltpu.VMEM)] * len(arrays)
        + [pl.BlockSpec(memory_space=pl.ANY)] * len(after),
        out_specs=[pl.BlockSpec(memory_space=pltpu.VMEM)] * len(outs),
        scratch_shapes=list(scratch),
        compiler_params=pltpu.CompilerParams(vmem_limit_bytes=size + MARGIN),
        cost_estimate=pl.CostEstimate(flops=flops, bytes_accessed=size, transcendentals=0),
        name=name,
    )(*smem, *arrays, *after)


def shape(rows, columns, dtype=jnp.bfloat16):
    return jax.ShapeDtypeStruct((rows, columns), dtype)


def keep_block(pattern, i, j, block):
    return jnp.where(pattern[i, j] > 0, block, jnp.zeros_like(block))


def strip_start(l, half, sizes):
    return pl.multiple_of(half * sizes.cols_here + l * sizes.quarter, sizes.quarter)


def columns_of(cc, sizes):
    return pl.ds(pl.multiple_of(cc * sizes.cols_here, sizes.cols_here), sizes.cols_here)


def mask_strip(zp, r, l, half, cc, strip, sizes):
    block_row = (r * sizes.rows_here + half * sizes.cols_here + l * sizes.quarter) // BS
    first = cc * (sizes.cols_here // BS)
    return jnp.concatenate(
        [
            keep_block(zp, block_row, first + t, strip[:, t * BS : (t + 1) * BS])
            for t in range(sizes.cols_here // BS)
        ],
        axis=1,
    )


def mask_piece(zp, r, l, cc, piece, sizes):
    q = sizes.quarter
    return jnp.concatenate(
        [
            mask_strip(zp, r, l, half, cc, piece[half * q : (half + 1) * q, :], sizes)
            for half in range(sizes.per)
        ],
        axis=0,
    )


def pack_kernel(*refs):
    out, row = refs[-1], 0
    for ref in refs[:-1]:
        out[row : row + ref.shape[0], :] = ref[...]
        row += ref.shape[0]


def pack(pieces, after=()):
    height = sum(p.shape[0] for p in pieces)
    out = shape(height, pieces[0].shape[1])
    return run(pack_kernel, "pack", [out], pieces, after=after)[0]


def slot_column(c, s, cols):
    return mod(c - (s + 1) // 2 if s % 2 else c + s // 2, cols)


def mask_kernel(sizes, zp, *refs):
    slots, out = refs[:-1], refs[-1]
    r, c, l = place()
    out[...] = jnp.zeros_like(out)
    for s, slot in enumerate(slots):
        cc = slot_column(c, s, sizes.cols)
        out[:, columns_of(cc, sizes)] = mask_piece(zp, r, l, cc, slot[...], sizes)


def bring_kernel(sizes, dr, with_z, hp, zp, near, far, *refs):
    slots, blocks = (refs[: sizes.cols - 1], refs[sizes.cols :]) if with_z else ((), refs)
    r, c, l = place()
    q, wide = sizes.quarter, sizes.cols_here
    for n, (h, dl) in enumerate(((near, 0), (far, sizes.layers // 2))):
        block_col = (c * wide + (l ^ dl) * q) // BS
        for part in range(sizes.per):
            for first in range(0, wide, BS):
                row = part * wide + first
                j = ((r ^ dr) * sizes.rows_here + row) // BS
                blocks[part][first : first + BS, n * q : (n + 1) * q] = keep_block(
                    hp, j, block_col, h[row : row + BS, :]
                )
    if with_z:
        mask_kernel(sizes, zp, *slots, refs[sizes.cols - 1])


def first_kernel(sizes, zp, zm, last, *refs):
    cols, q, width, per = sizes.cols, sizes.quarter, sizes.cols_here, sizes.per
    sides, (out, zs) = (refs[:cols], refs[cols : 2 * cols]), refs[-2:]
    r, c, l = place()
    cc = slot_column(c, cols - 1, cols)
    zs[...] = zm[...]
    zs[:, columns_of(cc, sizes)] = mask_piece(zp, r, l, cc, last[...], sizes)
    for side, blocks in zip((l, l ^ 1), sides):
        acc = None
        for n, block in enumerate(blocks):
            at = (r ^ (n // per)) * per + n % per
            part = jnp.dot(
                zs[:, columns_of(at, sizes)], block[...], preferred_element_type=jnp.float32
            )
            acc = part if acc is None else acc + part
        for n, ll in enumerate((side, side ^ (sizes.layers // 2))):
            out[:, pl.ds(pl.multiple_of(ll * q, q), q)] = acc[:, n * q : (n + 1) * q].astype(
                out.dtype
            )


def route_kernel(sizes, row_offsets, *refs):
    n = len(row_offsets)
    pieces, outs, table = refs[:n], refs[n:-1], refs[-1]
    r, c, _ = place()
    q = sizes.quarter
    for dr, piece in zip(row_offsets, pieces):
        for half in range(sizes.per):
            start = pl.multiple_of(((r ^ dr) * sizes.per + half) * q, q)
            table[pl.ds(start, q), :] = piece[half * q : (half + 1) * q, :]
    for d, out in enumerate(outs):
        out[...] = table[pl.ds(pl.multiple_of((c ^ d) * q, q), q), :]


def split_kernel(*refs):
    pieces, outs = [], []
    for ref in refs:
        (pieces if ref.shape[0] > refs[-1].shape[0] else outs).append(ref)
    per, height = len(outs) // len(pieces), outs[0].shape[0]
    for n, out in enumerate(outs):
        first = n % per * height
        out[...] = pieces[n // per][first : first + height, :]


def layers_kernel(sizes, z_table, zp, *refs):
    cols, q = sizes.cols, sizes.quarter
    out, held = refs[-1], refs[:-1]
    r, c, l = place()
    for dl in range(sizes.layers):
        ll = l ^ dl
        for half in range(sizes.per):
            rows = pl.ds(strip_start(ll, half, sizes), q)
            for s in range(cols):
                cc = slot_column(c, s, cols)
                columns = columns_of(cc, sizes)
                if s and (dl, s) not in z_table:
                    out[rows, columns] = jnp.zeros((q, sizes.cols_here), out.dtype)
                    continue
                if s == 0:
                    strip = held[0][rows, :]
                else:
                    index, row = z_table[dl, s]
                    strip = held[index][row + half * q : row + (half + 1) * q, :]
                out[rows, columns] = mask_strip(zp, r, ll, half, cc, strip, sizes)


def turned_dot(left, right):
    return lax.dot_general(
        left, right, (((1,), (1,)), ((), ())), preferred_element_type=jnp.float32
    )


def second_kernel(sizes, part, z_full, *refs):
    messages, before, out = refs[: len(part)], refs[len(part) : -1], refs[-1]
    c = lax.axis_index("col")
    total = before[0][...] if before else None
    for d, message in zip(part, messages):
        added = turned_dot(z_full[:, columns_of(c ^ d, sizes)], message[...])
        total = added if total is None else total + added
    out[...] = total


def last_kernel(sizes, offsets, zp, total, *refs):
    cols, q, per = sizes.cols, sizes.quarter, sizes.per
    messages, strips, out, xm, acc = refs[:cols], refs[cols:-3], refs[-3], refs[-2], refs[-1]
    r, c, l = place()
    for d, message in enumerate(messages):
        xm[:, columns_of(c ^ d, sizes)] = message[...]
    acc[...] = total[...]
    cc = slot_column(c, cols - 1, cols)
    for n, dl in enumerate(offsets):
        for half in range(per):
            rows = pl.ds(strip_start(l ^ dl, half, sizes), q)
            strip = strips[n * per + half][...]
            acc[rows, :] += turned_dot(
                mask_strip(zp, r, l ^ dl, half, cc, strip, sizes), xm[:, columns_of(cc, sizes)]
            )
    out[...] = acc[...].astype(out.dtype)


def local(sizes, hamiltonian, inv_root, h_pattern, z_pattern):
    rows, cols, layers, per = sizes.rows, sizes.cols, sizes.layers, sizes.per
    q, cols_here, rows_here = sizes.quarter, sizes.cols_here, sizes.rows_here
    order = rows * rows_here
    height = per * q
    row_bits, layer_bits = bits_of(rows), bits_of(layers)
    f32 = jnp.float32
    strip_shape = shape(q, cols_here)

    striped = inv_root.reshape(per, layers, q, cols_here)
    l = lax.axis_index("layer")
    own = lax.dynamic_index_in_dim(striped, l, 1, keepdims=False).reshape(height, cols_here)
    slots = [own]
    right = left = own
    for s in range(1, cols):
        if s % 2:
            right = lax.ppermute(right, "col", [(i, (i + 1) % cols) for i in range(cols)])
        else:
            left = lax.ppermute(left, "col", [(i, (i - 1) % cols) for i in range(cols)])
        slots.append(right if s % 2 else left)

    def cross(piece):
        return lax.ppermute(piece, "layer", flip(layers, layer_bits[0]))

    top, low = layer_bits
    h_pieces, h_table = [hamiltonian], [(0, 0)]
    for axis, bit in [("layer", top)] + [("row", b) for b in row_bits]:
        perm = flip(rows if axis == "row" else layers, bit)
        for piece, (dr, dl) in list(zip(h_pieces, h_table)):
            h_table.append((dr ^ bit, dl) if axis == "row" else (dr, dl ^ bit))
            if dl and axis == 'row':
                piece = pack([piece], [slots[1]])
            h_pieces.append(lax.ppermute(piece, axis, perm))
    h_own, h_other, zm = [], [], []
    for dr in range(rows):
        with_z = dr == rows - 1
        blocks = run(
            functools.partial(bring_kernel, sizes, dr, with_z),
            "bring",
            ([shape(height, order)] if with_z else []) + [shape(cols_here, 2 * q)] * per,
            [h_pieces[h_table.index((dr, 0))], h_pieces[h_table.index((dr, top))]]
            + (slots[:-1] if with_z else []),
            smem=[h_pattern, z_pattern],
            after=h_other[-per:] or slots[2:3],
        )
        zm, h_own = blocks[:-per], [*h_own, *blocks[-per:]]
        h_other += [lax.ppermute(block, "layer", flip(layers, low)) for block in blocks[-per:]]
    product = run(
        functools.partial(first_kernel, sizes),
        "first_product",
        [shape(height, cols_here)],
        [*zm, slots[-1], *h_own, *h_other],
        smem=[z_pattern],
        scratch=[pltpu.VMEM((height, order), jnp.bfloat16)],
    )[0]

    gathered = {0: product}
    for bit in row_bits:
        for dr, piece in list(gathered.items()):
            gathered[dr ^ bit] = lax.ppermute(piece, "row", flip(rows, bit))
    row_offsets = list(gathered)
    held, z_table = [inv_root], {}

    last = pack([slots[-1]], [product])
    last_top = cross(last)
    outgoing = run(
        functools.partial(route_kernel, sizes, row_offsets),
        "route",
        [shape(q, cols_here)] * cols,
        [gathered[o] for o in row_offsets],
        scratch=[pltpu.VMEM((cols * q, cols_here), jnp.bfloat16)],
    )
    messages = [outgoing[0]] + [
        lax.ppermute(outgoing[d], "col", flip(cols, d)) for d in range(1, cols)
    ]
    group = range(1, cols - 1)
    mine = pack([slots[s] for s in group])
    other = cross(mine)
    both = lax.ppermute(pack([mine, other], [outgoing[0]]), "layer", flip(layers, low))
    held, z_table = [inv_root, mine, other, both, last, last_top], {}
    for n, s in enumerate(group):
        row = n * height
        z_table[0, s], z_table[top, s], z_table[low, s] = (1, row), (2, row), (3, row)
        z_table[low ^ top, s] = (3, len(group) * height + row)
    z_table[0, cols - 1], z_table[top, cols - 1] = (4, 0), (5, 0)
    parts = run(split_kernel, "split", [strip_shape] * (2 * per), [last, last_top])
    parts = [lax.ppermute(part, "layer", flip(layers, low)) for part in parts]
    z_full = run(
        functools.partial(layers_kernel, sizes, z_table),
        "layers",
        [shape(rows_here, order)],
        held,
        smem=[z_pattern],
    )[0]
    total = []
    for part in (range(cols // 2), range(cols // 2, cols)):
        total = run(
            functools.partial(second_kernel, sizes, part),
            "second_product",
            [shape(*hamiltonian.shape, f32)],
            [z_full, *[messages[d] for d in part], *total],
        )
    return run(
        functools.partial(last_kernel, sizes, (low, low ^ top)),
        "last_product",
        [shape(*hamiltonian.shape)],
        [*total, *messages, *parts],
        smem=[z_pattern],
        scratch=[pltpu.VMEM((q, order), jnp.bfloat16), pltpu.VMEM(hamiltonian.shape, f32)],
    )[0]


def solution(mesh):
    rows, cols, layers = (mesh.shape[a] for a in ("row", "col", "layer"))

    def whole(hamiltonian, inv_root, h_pattern, z_pattern):
        order = hamiltonian.shape[0]
        cols_here = order // cols
        sizes = Sizes(
            rows, cols, layers, order // rows, cols_here, cols_here // layers, cols // rows
        )
        return jax.shard_map(
            functools.partial(local, sizes),
            mesh=mesh,
            in_specs=(P("row", ("col", "layer")), P("row", "col"), P(), P()),
            out_specs=P("row", ("col", "layer")),
            check_vma=False,
        )(hamiltonian, inv_root, h_pattern, z_pattern)

    return whole
```

time: 58.1 us -> 59.9 us (1.031)
  waiting for transfers between devices: 29.4 us -> 26.4 us
  starting transfers between devices: 18.4 us -> 21.2 us
  Pallas kernels: 6.62 us -> 7.89 us
  local copies, waits for them, and re-layouts: 3.3 us -> 4 us
    ppermute x10 -> x15, starting transfers between devices: 8.42 us -> 12.5 us  [the longest x3 4.81 us: local(): h_pieces.append(lax.ppermute(piece, axis, perm))]
    ppermute x10 -> x15, waiting for transfers between devices: 16.1 us -> 12.9 us  [the longest x2 9.15 us: local(): lax.ppermute(right, 'col', [(i, (i + 1) % cols) for i in range(cols)])]
    ppermute x3 -> x2, waiting for transfers between devices: 1.01 us -> 2.87 us  [cross(): return lax.ppermute(piece, 'layer', flip(layers, layer_bits[0]))]
    ppermute x3, waiting for transfers between devices: 6.43 us -> 4.64 us  [local(): lax.ppermute(outgoing[d], 'col', flip(cols, d))]
    ppermute x3 -> x2, starting transfers between devices: 4.25 us -> 2.75 us  [cross(): return lax.ppermute(piece, 'layer', flip(layers, layer_bits[0]))]
    pallas_call x11 -> x13, Pallas kernels: 6.62 us -> 7.89 us  [run(): pl.pallas_call(body, out_shape=list(outs), in_specs=[pl.BlockSpec(memory_...]
    unnamed x10 -> x12, local copies, waits for them, and re-layouts: 2.33 us -> 3.02 us
  transfers between devices with their start and end apart: 17 -> 21, of which waited for: 8 -> 9; matrix products, arithmetic and copies ran while one was open for 0% -> 0% of each run, Pallas kernels for 9% -> 10%
where the time goes in v10:
time: 59.9 us; the launch traced here: 59.7 us
  waiting for transfers between devices  26.4 us (44%)
  starting transfers between devices  21.2 us (35%)
  Pallas kernels  7.89 us (13%)
  local copies, waits for them, and re-layouts  4 us (7%)
    ppermute x2, waiting for transfers between devices, local(): lax.ppermute(right, 'col', [(i, (i + 1) % cols) for i in range(cols)])  9.15 us
    pallas_call x13, Pallas kernels, run(): pl.pallas_call(body, out_shape=list(outs), in_specs=[pl.BlockSpec(memory_...  7.89 us
    ppermute x1, waiting for transfers between devices, local(): gathered[dr ^ bit] = lax.ppermute(piece, 'row', flip(rows, bit))  5.96 us
    ppermute x3, starting transfers between devices, local(): h_pieces.append(lax.ppermute(piece, axis, perm))  4.81 us
    ppermute x3, waiting for transfers between devices, local(): lax.ppermute(outgoing[d], 'col', flip(cols, d))  4.64 us
    ppermute x3, starting transfers between devices, local(): lax.ppermute(outgoing[d], 'col', flip(cols, d))  4.39 us
    ppermute x2, starting transfers between devices, local(): lax.ppermute(right, 'col', [(i, (i + 1) % cols) for i in range(cols)])  3.64 us
    unnamed x12, local copies, waits for them, and re-layouts  3.02 us
  transfers between devices with their start and end apart: 21, of which 9 were waited for; matrix products, arithmetic and copies ran while one was open for 0% of the time, Pallas kernels for 10%

profile of v10, /device:TPU:0, one launch (start us, length us, event | category | flops | bytes accessed | tf_op | source)
XLA Modules:
  0.0 59.7 jit_solution(11272721096231929144)
XLA Ops:
  0.0 1.0 %constant_dynamic-slice_fusion = bf16[2,1,128,512]{3,2,1,0:T(8,128)(2,1)S(1)} fusion(bf16[2,4,128,512]{3,2,1,0:T(8,128)(2,1)} %bitcast.4, s32[]{:T(128)S(6)} %select_n.4), kind=kLoop, calls=%fused_computation | loop fusion | bytes 524292 | tf_op jit(solution)/shard_map/jit(dynamic_index_in_dim)/dynamic_slice | solution.py:258
  1.0 3.1 %collective-permute-start = (bf16[256,512]{1,0:T(8,128)(2,1)S(1)}, bf16[256,512]{1,0:T(8,128)(2,1)S(1)}, u32[]{:S(2)}, u32[]{:S(2)}) collective-permute-start(bf16[256,512]{1,0:T(8,128)(2,1)S(1)} %bitcast.5), channel_id=1, source_target_pairs={{0,4},{4,8},{8,12},{12,0},{1,5},{5,9},{9,13},{13,1},{2,6},{6,10},{... | collective-permute-start | bytes 786440 | tf_op jit(solution)/shard_map/ppermute | solution.py:263
  4.1 1.5 %collective-permute-start.4 = (bf16[1024,128]{1,0:T(8,128)(2,1)}, bf16[1024,128]{1,0:T(8,128)(2,1)S(1)}, u32[]{:S(2)}, u32[]{:S(2)}) collective-permute-start(bf16[1024,128]{1,0:T(8,128)(2,1)} %refs_2_.1), channel_id=1, source_target_pairs={{0,2},{1,3},{2,0},{3,1},{4,6},{5,7},{6,4},{7,5},{8,10},{9,11},{10,... | collective-permute-start | bytes 786440 | tf_op jit(solution)/shard_map/ppermute | solution.py:279
  5.6 2.2 %collective-permute-start.1 = (bf16[256,512]{1,0:T(8,128)(2,1)S(1)}, bf16[256,512]{1,0:T(8,128)(2,1)S(1)}, u32[]{:S(2)}, u32[]{:S(2)}) collective-permute-start(bf16[256,512]{1,0:T(8,128)(2,1)S(1)} %bitcast.6), channel_id=1, source_target_pairs={{0,12},{4,0},{8,4},{12,8},{1,13},{5,1},{9,5},{13,9},{2,14},{6,2},{... | collective-permute-start | bytes 786440 | tf_op jit(solution)/shard_map/ppermute | solution.py:265
  7.8 1.5 %collective-permute-start.3 = (bf16[1024,128]{1,0:T(8,128)(2,1)}, bf16[1024,128]{1,0:T(8,128)(2,1)S(1)}, u32[]{:S(2)}, u32[]{:S(2)}) collective-permute-start(bf16[1024,128]{1,0:T(8,128)(2,1)} %refs_2_.1), channel_id=1, source_target_pairs={{0,16},{16,0},{1,17},{17,1},{2,18},{18,2},{3,19},{19,3},{4,20},{20... | collective-permute-start | bytes 786440 | tf_op jit(solution)/shard_map/ppermute | solution.py:279
  9.3 3.9 %collective-permute-done.refs_0_.refs_1_.refs_5_ = bf16[256,512]{1,0:T(8,128)(2,1)S(1)} collective-permute-done((bf16[256,512]{1,0:T(8,128)(2,1)S(1)}, bf16[256,512]{1,0:T(8,128)(2,1)S(1)}, u32[]{:S(2)}, u32[]{:S(2)}) %collective-permute-start) | collective-permute-done | bytes 262176 | tf_op jit(solution)/shard_map/ppermute | solution.py:263
  13.3 1.8 %collective-permute-start.5 = (bf16[1024,128]{1,0:T(8,128)(2,1)S(1)}, bf16[1024,128]{1,0:T(8,128)(2,1)S(1)}, u32[]{:S(2)}, u32[]{:S(2)}) collective-permute-start(bf16[1024,128]{1,0:T(8,128)(2,1)S(1)} %pack.5), channel_id=1, source_target_pairs={{0,16},{16,0},{1,17},{17,1},{2,18},{18,2},{3,19},{19,3},{4,20},{20... | collective-permute-start | bytes 786440 | tf_op jit(solution)/shard_map/ppermute | solution.py:279
  15.1 2.9 %collective-permute-done.1.refs_1_.refs_4_.refs_6_ = bf16[256,512]{1,0:T(8,128)(2,1)S(1)} collective-permute-done((bf16[256,512]{1,0:T(8,128)(2,1)S(1)}, bf16[256,512]{1,0:T(8,128)(2,1)S(1)}, u32[]{:S(2)}, u32[]{:S(2)}) %collective-permute-start.1) | collective-permute-done | bytes 262176 | tf_op jit(solution)/shard_map/ppermute | solution.py:265
  18.0 0.9 %copy-done.1 = bf16[1024,128]{1,0:T(8,128)(2,1)S(1)} copy-done((bf16[1024,128]{1,0:T(8,128)(2,1)S(1)}, bf16[1024,128]{1,0:T(8,128)(2,1)}, u32[]{:S(2)}) %copy-start.1) | copy-done | bytes 262168
  23.8 0.9 %bring.3 = (bf16[256,2048]{1,0:T(8,128)(2,1)S(1)}, bf16[512,256]{1,0:T(8,128)(2,1)S(1)}, bf16[512,256]{1,0:T(8,128)(2,1)S(1)}) custom-call(s32[8,8]{1,0:T(8,128)S(1)} %copy-done.5, s32[8,8]{1,0:T(8,128)S(1)} %copy-done.3, bf16[1024,128]{1,0:T(8,128)(2,1)S(1)} %collective-permute-done.3.refs_2_, bf16[1024,128]{1,0:T(8,128)(2,1)S(1)} %collective-permute-done.5.refs_3_, ...), custom_call_target="tpu_custom_call" | custom-call | bytes 2883584 | tf_op jit(solution)/shard_map/bring/pallas_call | solution.py:51
  25.4 1.2 %collective-permute-start.2 = (bf16[512,512]{1,0:T(8,128)(2,1)S(1)}, bf16[512,512]{1,0:T(8,128)(2,1)S(1)}, u32[]{:S(2)}, u32[]{:S(2)}) collective-permute-start(bf16[512,512]{1,0:T(8,128)(2,1)S(1)} %pack.4.refs_0_.refs_2_), channel_id=1, source_target_pairs={{0,2},{1,3},{2,0},{3,1},{4,6},{5,7},{6,4},{7,5},{8,10},{9,11},{10,... | collective-permute-start | bytes 1572872 | tf_op jit(solution)/shard_map/ppermute | solution.py:269
  26.6 5.2 %collective-permute-done.8.refs_2_.refs_0_ = bf16[256,512]{1,0:T(8,128)(2,1)S(1)} collective-permute-done((bf16[256,512]{1,0:T(8,128)(2,1)S(1)}, bf16[256,512]{1,0:T(8,128)(2,1)S(1)}, u32[]{:S(2)}, u32[]{:S(2)}) %collective-permute-start.8) | collective-permute-done | bytes 262176 | tf_op jit(solution)/shard_map/ppermute | solution.py:263
  31.8 1.4 %first_product.1.refs_0_.refs_1_ = bf16[256,512]{1,0:T(8,128)(2,1)S(1)} custom-call(s32[8,8]{1,0:T(8,128)S(1)} %copy-done.4, bf16[256,2048]{1,0:T(8,128)(2,1)S(1)} %get-tuple-element.20.refs_1_, bf16[256,512]{1,0:T(8,128)(2,1)S(1)} %collective-permute-done.8.refs_2_.refs_0_, bf16[512,256]{1,0:T(8,128)(2,1)S(1)} %get-tuple-element.18.refs_3_, ...), custom_call_target="tpu_custom_call" | custom-call | bytes 4718592 | tf_op jit(solution)/shard_map/first_product/pallas_call | solution.py:51
  33.3 1.6 %collective-permute-start.11 = (bf16[256,512]{1,0:T(8,128)(2,1)S(1)}, bf16[256,512]{1,0:T(8,128)(2,1)S(1)}, u32[]{:S(2)}, u32[]{:S(2)}) collective-permute-start(bf16[256,512]{1,0:T(8,128)(2,1)S(1)} %first_product.1.refs_0_.refs_1_), channel_id=1, source_target_pairs={{0,16},{16,0},{1,17},{17,1},{2,18},{18,2},{3,19},{19,3},{4,20},{20... | collective-permute-start | bytes 786440 | tf_op jit(solution)/shard_map/ppermute | solution.py:306
  34.8 6.0 %collective-permute-done.11.refs_1_ = bf16[256,512]{1,0:T(8,128)(2,1)S(1)} collective-permute-done((bf16[256,512]{1,0:T(8,128)(2,1)S(1)}, bf16[256,512]{1,0:T(8,128)(2,1)S(1)}, u32[]{:S(2)}, u32[]{:S(2)}) %collective-permute-start.11) | collective-permute-done | bytes 262176 | tf_op jit(solution)/shard_map/ppermute | solution.py:306
  41.0 1.5 %collective-permute-start.13 = (bf16[256,512]{1,0:T(8,128)(2,1)S(1)}, bf16[256,512]{1,0:T(8,128)(2,1)S(1)}, u32[]{:S(2)}, u32[]{:S(2)}) collective-permute-start(bf16[256,512]{1,0:T(8,128)(2,1)S(1)} %pack.7.refs_5_.refs_0_), channel_id=1, source_target_pairs={{0,2},{1,3},{2,0},{3,1},{4,6},{5,7},{6,4},{7,5},{8,10},{9,11},{10,... | collective-permute-start | bytes 786440 | tf_op jit(solution)/shard_map/ppermute | solution.py:269
  42.6 1.1 %collective-permute-start.14 = (bf16[128,512]{1,0:T(8,128)(2,1)S(1)}, bf16[128,512]{1,0:T(8,128)(2,1)S(1)}, u32[]{:S(2)}, u32[]{:S(2)}) collective-permute-start(bf16[128,512]{1,0:T(8,128)(2,1)S(1)} %get-tuple-element.24), channel_id=1, source_target_pairs={{0,8},{4,12},{8,0},{12,4},{1,9},{5,13},{9,1},{13,5},{2,10},{6,14},... | collective-permute-start | bytes 393224 | tf_op jit(solution)/shard_map/ppermute | solution.py:320
  43.6 1.4 %collective-permute-start.16 = (bf16[128,512]{1,0:T(8,128)(2,1)S(1)}, bf16[128,512]{1,0:T(8,128)(2,1)S(1)}, u32[]{:S(2)}, u32[]{:S(2)}) collective-permute-start(bf16[128,512]{1,0:T(8,128)(2,1)S(1)} %get-tuple-element.26), channel_id=1, source_target_pairs={{0,4},{4,0},{8,12},{12,8},{1,5},{5,1},{9,13},{13,9},{2,6},{6,2},{1... | collective-permute-start | bytes 393224 | tf_op jit(solution)/shard_map/ppermute | solution.py:320
  45.0 1.9 %collective-permute-start.15 = (bf16[128,512]{1,0:T(8,128)(2,1)S(1)}, bf16[128,512]{1,0:T(8,128)(2,1)S(1)}, u32[]{:S(2)}, u32[]{:S(2)}) collective-permute-start(bf16[128,512]{1,0:T(8,128)(2,1)S(1)} %get-tuple-element.25), channel_id=1, source_target_pairs={{0,12},{4,8},{8,4},{12,0},{1,13},{5,9},{9,5},{13,1},{2,14},{6,10},... | collective-permute-start | bytes 393224 | tf_op jit(solution)/shard_map/ppermute | solution.py:320
  46.9 2.9 %collective-permute-done.13.refs_6_.refs_1_ = bf16[256,512]{1,0:T(8,128)(2,1)S(1)} collective-permute-done((bf16[256,512]{1,0:T(8,128)(2,1)S(1)}, bf16[256,512]{1,0:T(8,128)(2,1)S(1)}, u32[]{:S(2)}, u32[]{:S(2)}) %collective-permute-start.13) | collective-permute-done | bytes 262176 | tf_op jit(solution)/shard_map/ppermute | solution.py:269
  49.9 2.3 %collective-permute-done.14.refs_1_.refs_4_ = bf16[128,512]{1,0:T(8,128)(2,1)S(1)} collective-permute-done((bf16[128,512]{1,0:T(8,128)(2,1)S(1)}, bf16[128,512]{1,0:T(8,128)(2,1)S(1)}, u32[]{:S(2)}, u32[]{:S(2)}) %collective-permute-start.14) | collective-permute-done | bytes 131104 | tf_op jit(solution)/shard_map/ppermute | solution.py:320
  52.2 2.4 %collective-permute-done.16.refs_2_.refs_3_ = bf16[128,512]{1,0:T(8,128)(2,1)S(1)} collective-permute-done((bf16[128,512]{1,0:T(8,128)(2,1)S(1)}, bf16[128,512]{1,0:T(8,128)(2,1)S(1)}, u32[]{:S(2)}, u32[]{:S(2)}) %collective-permute-start.16) | collective-permute-done | bytes 131104 | tf_op jit(solution)/shard_map/ppermute | solution.py:320
  55.1 1.3 %layers.1.refs_0_ = bf16[1024,2048]{1,0:T(8,128)(2,1)S(1)} custom-call(s32[8,8]{1,0:T(8,128)S(1)} %copy-done.4, bf16[1024,512]{1,0:T(8,128)(2,1)S(1)} %copy-done, bf16[512,512]{1,0:T(8,128)(2,1)S(1)} %pack.4.refs_0_.refs_2_, bf16[512,512]{1,0:T(8,128)(2,1)S(1)} %collective-permute-done.2.refs_1_.refs_3_, ...), custom_call_target="tpu_custom_call" | custom-call | bytes 7864320 | tf_op jit(solution)/shard_map/layers/pallas_call | solution.py:51
  57.9 1.7 %last_product.1 = bf16[1024,128]{1,0:T(8,128)(2,1)} custom-call(s32[8,8]{1,0:T(8,128)S(1)} %copy-done.4, f32[1024,128]{1,0:T(8,128)S(1)} %second_product.3.refs_1_, bf16[128,512]{1,0:T(8,128)(2,1)S(1)} %get-tuple-element.23.refs_2_.refs_1_, bf16[128,512]{1,0:T(8,128)(2,1)S(1)} %collective-permute-done.16.refs_2_.refs_3_, ...), custom_call_target="tpu_custom_call" | custom-call | bytes 2883584 | tf_op jit(solution)/shard_map/last_product/pallas_call | solution.py:51
  (44 shorter events, 7.8 us)
Async XLA Ops:
  0.0 31.8 %copy-start.4 = (s32[8,8]{1,0:T(8,128)S(1)}, s32[8,8]{1,0:T(8,128)}, u32[]{:S(2)}) copy-start(s32[8,8]{1,0:T(8,128)} %refs_0_.9) | copy-start | bytes 772
  1.0 12.3 %collective-permute-start = (bf16[256,512]{1,0:T(8,128)(2,1)S(1)}, bf16[256,512]{1,0:T(8,128)(2,1)S(1)}, u32[]{:S(2)}, u32[]{:S(2)}) collective-permute-start(bf16[256,512]{1,0:T(8,128)(2,1)S(1)} %bitcast.5), channel_id=1, source_target_pairs={{0,4},{4,8},{8,12},{12,0},{1,5},{5,9},{9,13},{13,1},{2,6},{6,10},{... | collective-permute-start | bytes 786440 | tf_op jit(solution)/shard_map/ppermute | solution.py:263
  4.1 9.2 %collective-permute-start.4 = (bf16[1024,128]{1,0:T(8,128)(2,1)}, bf16[1024,128]{1,0:T(8,128)(2,1)S(1)}, u32[]{:S(2)}, u32[]{:S(2)}) collective-permute-start(bf16[1024,128]{1,0:T(8,128)(2,1)} %refs_2_.1), channel_id=1, source_target_pairs={{0,2},{1,3},{2,0},{3,1},{4,6},{5,7},{6,4},{7,5},{8,10},{9,11},{10,... | collective-permute-start | bytes 786440 | tf_op jit(solution)/shard_map/ppermute | solution.py:279
  5.6 12.4 %collective-permute-start.1 = (bf16[256,512]{1,0:T(8,128)(2,1)S(1)}, bf16[256,512]{1,0:T(8,128)(2,1)S(1)}, u32[]{:S(2)}, u32[]{:S(2)}) collective-permute-start(bf16[256,512]{1,0:T(8,128)(2,1)S(1)} %bitcast.6), channel_id=1, source_target_pairs={{0,12},{4,0},{8,4},{12,8},{1,13},{5,1},{9,5},{13,9},{2,14},{6,2},{... | collective-permute-start | bytes 786440 | tf_op jit(solution)/shard_map/ppermute | solution.py:265
  7.8 14.5 %collective-permute-start.3 = (bf16[1024,128]{1,0:T(8,128)(2,1)}, bf16[1024,128]{1,0:T(8,128)(2,1)S(1)}, u32[]{:S(2)}, u32[]{:S(2)}) collective-permute-start(bf16[1024,128]{1,0:T(8,128)(2,1)} %refs_2_.1), channel_id=1, source_target_pairs={{0,16},{16,0},{1,17},{17,1},{2,18},{18,2},{3,19},{19,3},{4,20},{20... | collective-permute-start | bytes 786440 | tf_op jit(solution)/shard_map/ppermute | solution.py:279
  13.3 9.0 %collective-permute-start.5 = (bf16[1024,128]{1,0:T(8,128)(2,1)S(1)}, bf16[1024,128]{1,0:T(8,128)(2,1)S(1)}, u32[]{:S(2)}, u32[]{:S(2)}) collective-permute-start(bf16[1024,128]{1,0:T(8,128)(2,1)S(1)} %pack.5), channel_id=1, source_target_pairs={{0,16},{16,0},{1,17},{17,1},{2,18},{18,2},{3,19},{19,3},{4,20},{20... | collective-permute-start | bytes 786440 | tf_op jit(solution)/shard_map/ppermute | solution.py:279
  18.0 1.0 %copy-start.1 = (bf16[1024,128]{1,0:T(8,128)(2,1)S(1)}, bf16[1024,128]{1,0:T(8,128)(2,1)}, u32[]{:S(2)}) copy-start(bf16[1024,128]{1,0:T(8,128)(2,1)} %refs_2_.1) | copy-start | bytes 786436
  21.1 1.6 %collective-permute-start.6 = (bf16[512,256]{1,0:T(8,128)(2,1)S(1)}, bf16[512,256]{1,0:T(8,128)(2,1)S(1)}, u32[]{:S(2)}, u32[]{:S(2)}) collective-permute-start(bf16[512,256]{1,0:T(8,128)(2,1)S(1)} %get-tuple-element.18.refs_3_), channel_id=1, source_target_pairs={{0,1},{1,0},{2,3},{3,2},{4,5},{5,4},{6,7},{7,6},{8,9},{9,8},{10,11... | collective-permute-start | bytes 786440 | tf_op jit(solution)/shard_map/ppermute | solution.py:293
  21.2 1.9 %collective-permute-start.7 = (bf16[512,256]{1,0:T(8,128)(2,1)S(1)}, bf16[512,256]{1,0:T(8,128)(2,1)S(1)}, u32[]{:S(2)}, u32[]{:S(2)}) collective-permute-start(bf16[512,256]{1,0:T(8,128)(2,1)S(1)} %get-tuple-element.19.refs_4_), channel_id=1, source_target_pairs={{0,1},{1,0},{2,3},{3,2},{4,5},{5,4},{6,7},{7,6},{8,9},{9,8},{10,11... | collective-permute-start | bytes 786440 | tf_op jit(solution)/shard_map/ppermute | solution.py:293
  21.7 10.1 %collective-permute-start.8 = (bf16[256,512]{1,0:T(8,128)(2,1)S(1)}, bf16[256,512]{1,0:T(8,128)(2,1)S(1)}, u32[]{:S(2)}, u32[]{:S(2)}) collective-permute-start(bf16[256,512]{1,0:T(8,128)(2,1)S(1)} %collective-permute-done.refs_0_.refs_1_.refs_5_), channel_id=1, source_target_pairs={{0,4},{4,8},{8,12},{12,0},{1,5},{5,9},{9,13},{13,1},{2,6},{6,10},{... | collective-permute-start | bytes 786440 | tf_op jit(solution)/shard_map/ppermute | solution.py:263
  24.7 7.1 %collective-permute-start.9 = (bf16[512,256]{1,0:T(8,128)(2,1)S(1)}, bf16[512,256]{1,0:T(8,128)(2,1)S(1)}, u32[]{:S(2)}, u32[]{:S(2)}) collective-permute-start(bf16[512,256]{1,0:T(8,128)(2,1)S(1)} %get-tuple-element.21.refs_5_), channel_id=1, source_target_pairs={{0,1},{1,0},{2,3},{3,2},{4,5},{5,4},{6,7},{7,6},{8,9},{9,8},{10,11... | collective-permute-start | bytes 786440 | tf_op jit(solution)/shard_map/ppermute | solution.py:293
  24.9 30.1 %copy-start = (bf16[1024,512]{1,0:T(8,128)(2,1)S(1)}, bf16[1024,512]{1,0:T(8,128)(2,1)}, u32[]{:S(2)}) copy-start(bf16[1024,512]{1,0:T(8,128)(2,1)} %refs_1_.5) | copy-start | bytes 3145732
  24.9 6.9 %collective-permute-start.10 = (bf16[512,256]{1,0:T(8,128)(2,1)S(1)}, bf16[512,256]{1,0:T(8,128)(2,1)S(1)}, u32[]{:S(2)}, u32[]{:S(2)}) collective-permute-start(bf16[512,256]{1,0:T(8,128)(2,1)S(1)} %get-tuple-element.22.refs_6_), channel_id=1, source_target_pairs={{0,1},{1,0},{2,3},{3,2},{4,5},{5,4},{6,7},{7,6},{8,9},{9,8},{10,11... | collective-permute-start | bytes 786440 | tf_op jit(solution)/shard_map/ppermute | solution.py:293
  25.4 15.5 %collective-permute-start.2 = (bf16[512,512]{1,0:T(8,128)(2,1)S(1)}, bf16[512,512]{1,0:T(8,128)(2,1)S(1)}, u32[]{:S(2)}, u32[]{:S(2)}) collective-permute-start(bf16[512,512]{1,0:T(8,128)(2,1)S(1)} %pack.4.refs_0_.refs_2_), channel_id=1, source_target_pairs={{0,2},{1,3},{2,0},{3,1},{4,6},{5,7},{6,4},{7,5},{8,10},{9,11},{10,... | collective-permute-start | bytes 1572872 | tf_op jit(solution)/shard_map/ppermute | solution.py:269
  33.3 7.5 %collective-permute-start.11 = (bf16[256,512]{1,0:T(8,128)(2,1)S(1)}, bf16[256,512]{1,0:T(8,128)(2,1)S(1)}, u32[]{:S(2)}, u32[]{:S(2)}) collective-permute-start(bf16[256,512]{1,0:T(8,128)(2,1)S(1)} %first_product.1.refs_0_.refs_1_), channel_id=1, source_target_pairs={{0,16},{16,0},{1,17},{17,1},{2,18},{18,2},{3,19},{19,3},{4,20},{20... | collective-permute-start | bytes 786440 | tf_op jit(solution)/shard_map/ppermute | solution.py:306
  40.9 13.6 %collective-permute-start.12 = (bf16[1024,512]{1,0:T(8,128)(2,1)S(1)}, bf16[1024,512]{1,0:T(8,128)(2,1)S(1)}, u32[]{:S(2)}, u32[]{:S(2)}) collective-permute-start(bf16[1024,512]{1,0:T(8,128)(2,1)S(1)} %pack.6), channel_id=1, source_target_pairs={{0,1},{1,0},{2,3},{3,2},{4,5},{5,4},{6,7},{7,6},{8,9},{9,8},{10,11... | collective-permute-start | bytes 3145736 | tf_op jit(solution)/shard_map/ppermute | solution.py:325
  41.0 8.8 %collective-permute-start.13 = (bf16[256,512]{1,0:T(8,128)(2,1)S(1)}, bf16[256,512]{1,0:T(8,128)(2,1)S(1)}, u32[]{:S(2)}, u32[]{:S(2)}) collective-permute-start(bf16[256,512]{1,0:T(8,128)(2,1)S(1)} %pack.7.refs_5_.refs_0_), channel_id=1, source_target_pairs={{0,2},{1,3},{2,0},{3,1},{4,6},{5,7},{6,4},{7,5},{8,10},{9,11},{10,... | collective-permute-start | bytes 786440 | tf_op jit(solution)/shard_map/ppermute | solution.py:269
  42.6 9.7 %collective-permute-start.14 = (bf16[128,512]{1,0:T(8,128)(2,1)S(1)}, bf16[128,512]{1,0:T(8,128)(2,1)S(1)}, u32[]{:S(2)}, u32[]{:S(2)}) collective-permute-start(bf16[128,512]{1,0:T(8,128)(2,1)S(1)} %get-tuple-element.24), channel_id=1, source_target_pairs={{0,8},{4,12},{8,0},{12,4},{1,9},{5,13},{9,1},{13,5},{2,10},{6,14},... | collective-permute-start | bytes 393224 | tf_op jit(solution)/shard_map/ppermute | solution.py:320
  43.6 11.0 %collective-permute-start.16 = (bf16[128,512]{1,0:T(8,128)(2,1)S(1)}, bf16[128,512]{1,0:T(8,128)(2,1)S(1)}, u32[]{:S(2)}, u32[]{:S(2)}) collective-permute-start(bf16[128,512]{1,0:T(8,128)(2,1)S(1)} %get-tuple-element.26), channel_id=1, source_target_pairs={{0,4},{4,0},{8,12},{12,8},{1,5},{5,1},{9,13},{13,9},{2,6},{6,2},{1... | collective-permute-start | bytes 393224 | tf_op jit(solution)/shard_map/ppermute | solution.py:320
  45.0 12.1 %collective-permute-start.15 = (bf16[128,512]{1,0:T(8,128)(2,1)S(1)}, bf16[128,512]{1,0:T(8,128)(2,1)S(1)}, u32[]{:S(2)}, u32[]{:S(2)}) collective-permute-start(bf16[128,512]{1,0:T(8,128)(2,1)S(1)} %get-tuple-element.25), channel_id=1, source_target_pairs={{0,12},{4,8},{8,4},{12,0},{1,13},{5,9},{9,5},{13,1},{2,14},{6,10},... | collective-permute-start | bytes 393224 | tf_op jit(solution)/shard_map/ppermute | solution.py:320
  49.9 8.0 %collective-permute-start.17 = (bf16[128,512]{1,0:T(8,128)(2,1)S(1)}, bf16[128,512]{1,0:T(8,128)(2,1)S(1)}, u32[]{:S(2)}, u32[]{:S(2)}) collective-permute-start(bf16[128,512]{1,0:T(8,128)(2,1)S(1)} %get-tuple-element.27), channel_id=1, source_target_pairs={{0,1},{1,0},{2,3},{3,2},{4,5},{5,4},{6,7},{7,6},{8,9},{9,8},{10,11... | collective-permute-start | bytes 393224 | tf_op jit(solution)/shard_map/ppermute | solution.py:333
  52.2 5.7 %collective-permute-start.18 = (bf16[128,512]{1,0:T(8,128)(2,1)S(1)}, bf16[128,512]{1,0:T(8,128)(2,1)S(1)}, u32[]{:S(2)}, u32[]{:S(2)}) collective-permute-start(bf16[128,512]{1,0:T(8,128)(2,1)S(1)} %get-tuple-element.28), channel_id=1, source_target_pairs={{0,1},{1,0},{2,3},{3,2},{4,5},{5,4},{6,7},{7,6},{8,9},{9,8},{10,11... | collective-permute-start | bytes 393224 | tf_op jit(solution)/shard_map/ppermute | solution.py:333
  54.6 3.3 %collective-permute-start.19 = (bf16[128,512]{1,0:T(8,128)(2,1)S(1)}, bf16[128,512]{1,0:T(8,128)(2,1)S(1)}, u32[]{:S(2)}, u32[]{:S(2)}) collective-permute-start(bf16[128,512]{1,0:T(8,128)(2,1)S(1)} %get-tuple-element.29), channel_id=1, source_target_pairs={{0,1},{1,0},{2,3},{3,2},{4,5},{5,4},{6,7},{7,6},{8,9},{9,8},{10,11... | collective-permute-start | bytes 393224 | tf_op jit(solution)/shard_map/ppermute | solution.py:333
  54.6 3.3 %collective-permute-start.20 = (bf16[128,512]{1,0:T(8,128)(2,1)S(1)}, bf16[128,512]{1,0:T(8,128)(2,1)S(1)}, u32[]{:S(2)}, u32[]{:S(2)}) collective-permute-start(bf16[128,512]{1,0:T(8,128)(2,1)S(1)} %get-tuple-element.30), channel_id=1, source_target_pairs={{0,1},{1,0},{2,3},{3,2},{4,5},{5,4},{6,7},{7,6},{8,9},{9,8},{10,11... | collective-permute-start | bytes 393224 | tf_op jit(solution)/shard_map/ppermute | solution.py:333
  (3 other events, 2.1 us)

commit v11 on v10

--- a/solution.py
+++ b/solution.py
@@ -54,7 +54,10 @@
         in_specs=[pl.BlockSpec(memory_space=pltpu.SMEM)] * len(smem)
         + [pl.BlockSpec(memory_space=pltpu.VMEM)] * len(arrays)
         + [pl.BlockSpec(memory_space=pl.ANY)] * len(after),
-        out_specs=[pl.BlockSpec(memory_space=pltpu.VMEM)] * len(outs),
+        out_specs=[
+            pl.BlockSpec(memory_space=pltpu.SMEM if o.dtype == jnp.int32 else pltpu.VMEM)
+            for o in outs
+        ],
         scratch_shapes=list(scratch),
         compiler_params=pltpu.CompilerParams(vmem_limit_bytes=size + MARGIN),
         cost_estimate=pl.CostEstimate(flops=flops, bytes_accessed=size, transcendentals=0),
@@ -127,26 +130,41 @@
         out[:, columns_of(cc, sizes)] = mask_piece(zp, r, l, cc, slot[...], sizes)
 
 
-def bring_kernel(sizes, dr, with_z, hp, zp, near, far, *refs):
-    slots, blocks = (refs[: sizes.cols - 1], refs[sizes.cols :]) if with_z else ((), refs)
+def fetch_kernel(hp, zp, h, hp_out, zp_out, h_out):
+    h_out[...] = h[...]
+    for i in range(hp.shape[0]):
+        for j in range(hp.shape[1]):
+            hp_out[i, j] = hp[i, j]
+            zp_out[i, j] = zp[i, j]
+
+
+def bring_kernel(sizes, h_table, hp, zp, *refs):
+    n = len(h_table)
+    pieces, slots = refs[:n], refs[n : n + sizes.cols - 1]
+    zm, blocks = refs[n + sizes.cols - 1], refs[n + sizes.cols :]
     r, c, l = place()
-    q, wide = sizes.quarter, sizes.cols_here
-    for n, (h, dl) in enumerate(((near, 0), (far, sizes.layers // 2))):
-        block_col = (c * wide + (l ^ dl) * q) // BS
-        for part in range(sizes.per):
-            for first in range(0, wide, BS):
-                row = part * wide + first
-                j = ((r ^ dr) * sizes.rows_here + row) // BS
-                blocks[part][first : first + BS, n * q : (n + 1) * q] = keep_block(
-                    hp, j, block_col, h[row : row + BS, :]
-                )
-    if with_z:
-        mask_kernel(sizes, zp, *slots, refs[sizes.cols - 1])
-
-
-def first_kernel(sizes, zp, zm, last, *refs):
-    cols, q, width, per = sizes.cols, sizes.quarter, sizes.cols_here, sizes.per
-    sides, (out, zs) = (refs[:cols], refs[cols : 2 * cols]), refs[-2:]
+    q, wide = sizes.quarter, blocks[0].shape[0]
+    for h, (dr, dl) in zip(pieces, h_table):
+        columns = slice(q, 2 * q) if dl else slice(0, q)
+        block_col = (c * sizes.cols_here + (l ^ dl) * q) // BS
+        for rr in range(sizes.rows):
+
+            @pl.when((r ^ dr) == rr)
+            def _(h=h, rr=rr, columns=columns, block_col=block_col):
+                for first in range(0, sizes.rows_here, BS):
+                    row = rr * sizes.rows_here + first
+                    at = row % wide
+                    blocks[row // wide][at : at + BS, columns] = keep_block(
+                        hp, row // BS, block_col, h[first : first + BS, :]
+                    )
+
+    mask_kernel(sizes, zp, *slots, zm)
+
+
+def first_kernel(sizes, top, zp, zm, last, *refs):
+    cols, q = sizes.cols, sizes.quarter
+    n, (out, zs) = len(refs) // 2 - 1, refs[-2:]
+    sides, width = (refs[:n], refs[n : 2 * n]), refs[0].shape[0]
     r, c, l = place()
     cc = slot_column(c, cols - 1, cols)
     zs[...] = zm[...]
@@ -154,12 +172,11 @@
     for side, blocks in zip((l, l ^ 1), sides):
         acc = None
         for n, block in enumerate(blocks):
-            at = (r ^ (n // per)) * per + n % per
             part = jnp.dot(
-                zs[:, columns_of(at, sizes)], block[...], preferred_element_type=jnp.float32
+                zs[:, n * width : (n + 1) * width], block[...], preferred_element_type=jnp.float32
             )
             acc = part if acc is None else acc + part
-        for n, ll in enumerate((side, side ^ (sizes.layers // 2))):
+        for n, ll in enumerate((side, side ^ top)):
             out[:, pl.ds(pl.multiple_of(ll * q, q), q)] = acc[:, n * q : (n + 1) * q].astype(
                 out.dtype
             )
@@ -226,21 +243,27 @@
     out[...] = total
 
 
-def last_kernel(sizes, offsets, zp, total, *refs):
+def last_kernel(sizes, part, offsets, zp, z_full, before, *refs):
     cols, q, per = sizes.cols, sizes.quarter, sizes.per
-    messages, strips, out, xm, acc = refs[:cols], refs[cols:-3], refs[-3], refs[-2], refs[-1]
+    messages, piece, strips = refs[:cols], refs[cols], refs[cols + 1 : -3]
+    out, acc, xm = refs[-3:]
     r, c, l = place()
-    for d, message in enumerate(messages):
-        xm[:, columns_of(c ^ d, sizes)] = message[...]
-    acc[...] = total[...]
+    total = before[...]
+    for d in part:
+        total += turned_dot(z_full[:, columns_of(c ^ d, sizes)], messages[d][...])
+    acc[...] = total
     cc = slot_column(c, cols - 1, cols)
+    for d in range(cols):
+
+        @pl.when((c ^ d) == cc)
+        def _(d=d):
+            xm[...] = messages[d][...]
+
     for n, dl in enumerate(offsets):
         for half in range(per):
             rows = pl.ds(strip_start(l ^ dl, half, sizes), q)
-            strip = strips[n * per + half][...]
-            acc[rows, :] += turned_dot(
-                mask_strip(zp, r, l ^ dl, half, cc, strip, sizes), xm[:, columns_of(cc, sizes)]
-            )
+            strip = strips[half][...] if n else piece[half * q : (half + 1) * q, :]
+            acc[rows, :] += turned_dot(mask_strip(zp, r, l ^ dl, half, cc, strip, sizes), xm[...])
     out[...] = acc[...].astype(out.dtype)
 
 
@@ -269,33 +292,36 @@
         return lax.ppermute(piece, "layer", flip(layers, layer_bits[0]))
 
     top, low = layer_bits
+    h_pattern, z_pattern, fetched = run(
+        fetch_kernel,
+        "fetch",
+        [shape(*h_pattern.shape, jnp.int32)] * 2 + [shape(*hamiltonian.shape)],
+        [hamiltonian],
+        smem=[h_pattern, z_pattern],
+    )
     h_pieces, h_table = [hamiltonian], [(0, 0)]
     for axis, bit in [("layer", top)] + [("row", b) for b in row_bits]:
         perm = flip(rows if axis == "row" else layers, bit)
         for piece, (dr, dl) in list(zip(h_pieces, h_table)):
             h_table.append((dr ^ bit, dl) if axis == "row" else (dr, dl ^ bit))
+            if axis == "row" and not dr and not dl:
+                piece = fetched
             if dl and axis == 'row':
                 piece = pack([piece], [slots[1]])
             h_pieces.append(lax.ppermute(piece, axis, perm))
-    h_own, h_other, zm = [], [], []
-    for dr in range(rows):
-        with_z = dr == rows - 1
-        blocks = run(
-            functools.partial(bring_kernel, sizes, dr, with_z),
-            "bring",
-            ([shape(height, order)] if with_z else []) + [shape(cols_here, 2 * q)] * per,
-            [h_pieces[h_table.index((dr, 0))], h_pieces[h_table.index((dr, top))]]
-            + (slots[:-1] if with_z else []),
-            smem=[h_pattern, z_pattern],
-            after=h_other[-per:] or slots[2:3],
-        )
-        zm, h_own = blocks[:-per], [*h_own, *blocks[-per:]]
-        h_other += [lax.ppermute(block, "layer", flip(layers, low)) for block in blocks[-per:]]
+    zm, *h_own = run(
+        functools.partial(bring_kernel, sizes, h_table),
+        "bring",
+        [shape(height, order)] + [shape(cols_here, 2 * q)] * cols,
+        [fetched, *h_pieces[1:], *slots[:-1]],
+        smem=[h_pattern, z_pattern],
+    )
+    h_other = [lax.ppermute(block, "layer", flip(layers, low)) for block in h_own]
     product = run(
-        functools.partial(first_kernel, sizes),
+        functools.partial(first_kernel, sizes, top),
         "first_product",
         [shape(height, cols_here)],
-        [*zm, slots[-1], *h_own, *h_other],
+        [zm, slots[-1], *h_own, *h_other],
         smem=[z_pattern],
         scratch=[pltpu.VMEM((height, order), jnp.bfloat16)],
     )[0]
@@ -309,11 +335,13 @@
 
     last = pack([slots[-1]], [product])
     last_top = cross(last)
+    last_low = lax.ppermute(last, "layer", flip(layers, low))
     outgoing = run(
         functools.partial(route_kernel, sizes, row_offsets),
         "route",
         [shape(q, cols_here)] * cols,
         [gathered[o] for o in row_offsets],
+        after=[last_low],
         scratch=[pltpu.VMEM((cols * q, cols_here), jnp.bfloat16)],
     )
     messages = [outgoing[0]] + [
@@ -323,13 +351,13 @@
     mine = pack([slots[s] for s in group])
     other = cross(mine)
     both = lax.ppermute(pack([mine, other], [outgoing[0]]), "layer", flip(layers, low))
-    held, z_table = [inv_root, mine, other, both, last, last_top], {}
+    held, z_table = [inv_root, mine, other, both, last, last_low], {}
     for n, s in enumerate(group):
         row = n * height
         z_table[0, s], z_table[top, s], z_table[low, s] = (1, row), (2, row), (3, row)
         z_table[low ^ top, s] = (3, len(group) * height + row)
-    z_table[0, cols - 1], z_table[top, cols - 1] = (4, 0), (5, 0)
-    parts = run(split_kernel, "split", [strip_shape] * (2 * per), [last, last_top])
+    z_table[0, cols - 1], z_table[low, cols - 1] = (4, 0), (5, 0)
+    parts = run(split_kernel, "split", [strip_shape] * per, [last_top])
     parts = [lax.ppermute(part, "layer", flip(layers, low)) for part in parts]
     z_full = run(
         functools.partial(layers_kernel, sizes, z_table),
@@ -338,21 +366,20 @@
         held,
         smem=[z_pattern],
     )[0]
-    total = []
-    for part in (range(cols // 2), range(cols // 2, cols)):
-        total = run(
-            functools.partial(second_kernel, sizes, part),
-            "second_product",
-            [shape(*hamiltonian.shape, f32)],
-            [z_full, *[messages[d] for d in part], *total],
-        )
+    early, late = range(cols // 2), range(cols // 2, cols)
+    total = run(
+        functools.partial(second_kernel, sizes, early),
+        "second_product",
+        [shape(*hamiltonian.shape, f32)],
+        [z_full, *[messages[d] for d in early]],
+    )[0]
     return run(
-        functools.partial(last_kernel, sizes, (low, low ^ top)),
+        functools.partial(last_kernel, sizes, late, (top, low ^ top)),
         "last_product",
         [shape(*hamiltonian.shape)],
-        [*total, *messages, *parts],
+        [z_full, total, *messages, last_top, *parts],
         smem=[z_pattern],
-        scratch=[pltpu.VMEM((q, order), jnp.bfloat16), pltpu.VMEM(hamiltonian.shape, f32)],
+        scratch=[pltpu.VMEM(hamiltonian.shape, f32), pltpu.VMEM((q, cols_here), jnp.bfloat16)],
     )[0]
 
 

time: 59.9 us -> 57.3 us (0.957)
  starting transfers between devices: 21.2 us -> 19.2 us
  Pallas kernels: 7.89 us -> 8.78 us
  waiting for transfers between devices: 26.4 us -> 25.6 us
  local copies, waits for them, and re-layouts: 4 us -> 3.29 us
    ppermute x2, waiting for transfers between devices: 9.15 us -> 0.13 us  [local(): lax.ppermute(right, 'col', [(i, (i + 1) % cols) for i in range(cols)])]
    ppermute x3, waiting for transfers between devices: 0.01 us -> 5.81 us  [local(): h_pieces.append(lax.ppermute(piece, axis, perm))]
    ppermute x2, waiting for transfers between devices: 2.87 us -> 5.82 us  [cross(): return lax.ppermute(piece, 'layer', flip(layers, layer_bits[0]))]
    ppermute x3, waiting for transfers between devices: 4.64 us -> 2.1 us  [local(): lax.ppermute(outgoing[d], 'col', flip(cols, d))]
    ppermute x2, starting transfers between devices: 2.75 us -> 1.14 us  [cross(): return lax.ppermute(piece, 'layer', flip(layers, layer_bits[0]))]
    ppermute x1, waiting for transfers between devices: 5.96 us -> 7.08 us  [local(): gathered[dr ^ bit] = lax.ppermute(piece, 'row', flip(rows, bit))]
    pallas_call x13 -> x12, Pallas kernels: 7.89 us -> 8.78 us  [run(): pl.pallas_call(body, out_shape=list(outs), in_specs=[pl.BlockSpec(memory_...]
    unnamed x12 -> x8, local copies, waits for them, and re-layouts: 3.02 us -> 2.33 us
  transfers between devices with their start and end apart: 21 -> 20, of which waited for: 9 -> 11; matrix products, arithmetic and copies ran while one was open for 0% -> 0% of each run, Pallas kernels for 10% -> 11%
where the time goes in v11:
time: 57.3 us; the launch traced here: 57 us
  waiting for transfers between devices  25.6 us (45%)
  starting transfers between devices  19.2 us (34%)
  Pallas kernels  8.78 us (15%)
  local copies, waits for them, and re-layouts  3.29 us (6%)
    pallas_call x12, Pallas kernels, run(): pl.pallas_call(body, out_shape=list(outs), in_specs=[pl.BlockSpec(memory_...  8.78 us
    ppermute x1, waiting for transfers between devices, local(): gathered[dr ^ bit] = lax.ppermute(piece, 'row', flip(rows, bit))  7.08 us
    ppermute x2, waiting for transfers between devices, cross(): return lax.ppermute(piece, 'layer', flip(layers, layer_bits[0]))  5.82 us
    ppermute x3, waiting for transfers between devices, local(): h_pieces.append(lax.ppermute(piece, axis, perm))  5.81 us
    ppermute x3, starting transfers between devices, local(): h_pieces.append(lax.ppermute(piece, axis, perm))  4.88 us
    ppermute x3, starting transfers between devices, local(): lax.ppermute(outgoing[d], 'col', flip(cols, d))  4.39 us
    ppermute x1, waiting for transfers between devices, local(): left = lax.ppermute(left, 'col', [(i, (i - 1) % cols) for i in range(cols)])  3.6 us
    ppermute x2, starting transfers between devices, local(): lax.ppermute(right, 'col', [(i, (i + 1) % cols) for i in range(cols)])  3.17 us
  transfers between devices with their start and end apart: 20, of which 11 were waited for; matrix products, arithmetic and copies ran while one was open for 0% of the time, Pallas kernels for 11%

profile of v11, /device:TPU:0, one launch (start us, length us, event | category | flops | bytes accessed | tf_op | source)
XLA Modules:
  0.0 57.0 jit_solution(11656075857506163350)
XLA Ops:
  0.0 1.0 %constant_dynamic-slice_fusion = bf16[2,1,128,512]{3,2,1,0:T(8,128)(2,1)S(1)} fusion(bf16[2,4,128,512]{3,2,1,0:T(8,128)(2,1)} %bitcast.4, s32[]{:T(128)S(6)} %select_n.4), kind=kLoop, calls=%fused_computation | loop fusion | bytes 524292 | tf_op jit(solution)/shard_map/jit(dynamic_index_in_dim)/dynamic_slice | solution.py:281
  1.0 3.1 %collective-permute-start = (bf16[256,512]{1,0:T(8,128)(2,1)S(1)}, bf16[256,512]{1,0:T(8,128)(2,1)S(1)}, u32[]{:S(2)}, u32[]{:S(2)}) collective-permute-start(bf16[256,512]{1,0:T(8,128)(2,1)S(1)} %bitcast.5), channel_id=1, source_target_pairs={{0,4},{4,8},{8,12},{12,0},{1,5},{5,9},{9,13},{13,1},{2,6},{6,10},{... | collective-permute-start | bytes 786440 | tf_op jit(solution)/shard_map/ppermute | solution.py:286
  4.0 1.5 %collective-permute-start.3 = (bf16[1024,128]{1,0:T(8,128)(2,1)}, bf16[1024,128]{1,0:T(8,128)(2,1)S(1)}, u32[]{:S(2)}, u32[]{:S(2)}) collective-permute-start(bf16[1024,128]{1,0:T(8,128)(2,1)} %refs_2_.1), channel_id=1, source_target_pairs={{0,2},{1,3},{2,0},{3,1},{4,6},{5,7},{6,4},{7,5},{8,10},{9,11},{10,... | collective-permute-start | bytes 786440 | tf_op jit(solution)/shard_map/ppermute | solution.py:311
  5.6 2.2 %collective-permute-start.1 = (bf16[256,512]{1,0:T(8,128)(2,1)S(1)}, bf16[256,512]{1,0:T(8,128)(2,1)S(1)}, u32[]{:S(2)}, u32[]{:S(2)}) collective-permute-start(bf16[256,512]{1,0:T(8,128)(2,1)S(1)} %bitcast.6), channel_id=1, source_target_pairs={{0,12},{4,0},{8,4},{12,8},{1,13},{5,1},{9,5},{13,9},{2,14},{6,2},{... | collective-permute-start | bytes 786440 | tf_op jit(solution)/shard_map/ppermute | solution.py:288
  7.8 0.9 %copy-done.1 = bf16[1024,128]{1,0:T(8,128)(2,1)S(1)} copy-done((bf16[1024,128]{1,0:T(8,128)(2,1)S(1)}, bf16[1024,128]{1,0:T(8,128)(2,1)}, u32[]{:S(2)}) %copy-start.1) | copy-done | bytes 262168
  8.8 0.7 %copy-done.2 = s32[8,8]{1,0:T(8,128)S(1)} copy-done((s32[8,8]{1,0:T(8,128)S(1)}, s32[8,8]{1,0:T(8,128)}, u32[]{:S(2)}) %copy-start.2) | copy-done | bytes 280
  10.1 1.4 %fetch.1 = (s32[8,8]{1,0:T(8,128)S(1)}, s32[8,8]{1,0:T(8,128)S(1)}, bf16[1024,128]{1,0:T(8,128)(2,1)S(1)}) custom-call(s32[8,8]{1,0:T(8,128)S(1)} %copy-done.2, s32[8,8]{1,0:T(8,128)S(1)} %copy-done.3, bf16[1024,128]{1,0:T(8,128)(2,1)S(1)} %copy-done.1), custom_call_target="tpu_custom_call" | custom-call | bytes 524800 | tf_op jit(solution)/shard_map/fetch/pallas_call | solution.py:51
  11.6 1.6 %collective-permute-start.4 = (bf16[1024,128]{1,0:T(8,128)(2,1)S(1)}, bf16[1024,128]{1,0:T(8,128)(2,1)S(1)}, u32[]{:S(2)}, u32[]{:S(2)}) collective-permute-start(bf16[1024,128]{1,0:T(8,128)(2,1)S(1)} %get-tuple-element.21.refs_2_), channel_id=1, source_target_pairs={{0,16},{16,0},{1,17},{17,1},{2,18},{18,2},{3,19},{19,3},{4,20},{20... | collective-permute-start | bytes 786440 | tf_op jit(solution)/shard_map/ppermute | solution.py:311
  13.3 1.8 %collective-permute-start.5 = (bf16[1024,128]{1,0:T(8,128)(2,1)S(1)}, bf16[1024,128]{1,0:T(8,128)(2,1)S(1)}, u32[]{:S(2)}, u32[]{:S(2)}) collective-permute-start(bf16[1024,128]{1,0:T(8,128)(2,1)S(1)} %pack.5), channel_id=1, source_target_pairs={{0,16},{16,0},{1,17},{17,1},{2,18},{18,2},{3,19},{19,3},{4,20},{20... | collective-permute-start | bytes 786440 | tf_op jit(solution)/shard_map/ppermute | solution.py:311
  15.2 3.6 %collective-permute-done.1.refs_1_.refs_8_ = bf16[256,512]{1,0:T(8,128)(2,1)S(1)} collective-permute-done((bf16[256,512]{1,0:T(8,128)(2,1)S(1)}, bf16[256,512]{1,0:T(8,128)(2,1)S(1)}, u32[]{:S(2)}, u32[]{:S(2)}) %collective-permute-start.1) | collective-permute-done | bytes 262176 | tf_op jit(solution)/shard_map/ppermute | solution.py:288
  18.8 2.1 %collective-permute-done.4.refs_4_ = bf16[1024,128]{1,0:T(8,128)(2,1)S(1)} collective-permute-done((bf16[1024,128]{1,0:T(8,128)(2,1)S(1)}, bf16[1024,128]{1,0:T(8,128)(2,1)S(1)}, u32[]{:S(2)}, u32[]{:S(2)}) %collective-permute-start.4) | collective-permute-done | bytes 262176 | tf_op jit(solution)/shard_map/ppermute | solution.py:311
  20.9 3.7 %collective-permute-done.5.refs_5_ = bf16[1024,128]{1,0:T(8,128)(2,1)S(1)} collective-permute-done((bf16[1024,128]{1,0:T(8,128)(2,1)S(1)}, bf16[1024,128]{1,0:T(8,128)(2,1)S(1)}, u32[]{:S(2)}, u32[]{:S(2)}) %collective-permute-start.5) | collective-permute-done | bytes 262176 | tf_op jit(solution)/shard_map/ppermute | solution.py:311
  24.6 1.1 %bring.1 = (bf16[256,2048]{1,0:T(8,128)(2,1)S(1)}, bf16[512,256]{1,0:T(8,128)(2,1)S(1)}, bf16[512,256]{1,0:T(8,128)(2,1)S(1)}, bf16[512,256]{1,0:T(8,128)(2,1)S(1)}, bf16[512,256]{1,0:T(8,128)(2,1)S(1)}) custom-call(s32[8,8]{1,0:T(8,128)S(1)} %get-tuple-element.20.refs_0_, s32[8,8]{1,0:T(8,128)S(1)} %get-tuple-element.19.refs_1_.refs_0_, ...), custom_call_target="tpu_custom_call" | custom-call | bytes 3932160 | tf_op jit(solution)/shard_map/bring/pallas_call | solution.py:51
  28.4 1.4 %first_product.1.refs_1_.refs_0_ = bf16[256,512]{1,0:T(8,128)(2,1)S(1)} custom-call(s32[8,8]{1,0:T(8,128)S(1)} %get-tuple-element.19.refs_1_.refs_0_, bf16[256,2048]{1,0:T(8,128)(2,1)S(1)} %get-tuple-element.22.refs_1_, bf16[256,512]{1,0:T(8,128)(2,1)S(1)} %collective-permute-done.6.refs_2_.refs_0_, bf16[512,256]{1,0:T(8,128)(2,1)S(1)} %get-tuple-element.23.refs_3_, ...), custom_call_target="tpu_custom_call" | custom-call | bytes 4718592 | tf_op jit(solution)/shard_map/first_product/pallas_call | solution.py:51
  30.1 1.5 %collective-permute-start.11 = (bf16[256,512]{1,0:T(8,128)(2,1)S(1)}, bf16[256,512]{1,0:T(8,128)(2,1)S(1)}, u32[]{:S(2)}, u32[]{:S(2)}) collective-permute-start(bf16[256,512]{1,0:T(8,128)(2,1)S(1)} %first_product.1.refs_1_.refs_0_), channel_id=1, source_target_pairs={{0,16},{16,0},{1,17},{17,1},{2,18},{18,2},{3,19},{19,3},{4,20},{20... | collective-permute-start | bytes 786440 | tf_op jit(solution)/shard_map/ppermute | solution.py:332
  31.6 7.1 %collective-permute-done.11.refs_1_ = bf16[256,512]{1,0:T(8,128)(2,1)S(1)} collective-permute-done((bf16[256,512]{1,0:T(8,128)(2,1)S(1)}, bf16[256,512]{1,0:T(8,128)(2,1)S(1)}, u32[]{:S(2)}, u32[]{:S(2)}) %collective-permute-start.11) | collective-permute-done | bytes 262176 | tf_op jit(solution)/shard_map/ppermute | solution.py:332
  38.7 2.1 %collective-permute-done.2.refs_1_.refs_3_ = bf16[512,512]{1,0:T(8,128)(2,1)S(1)} collective-permute-done((bf16[512,512]{1,0:T(8,128)(2,1)S(1)}, bf16[512,512]{1,0:T(8,128)(2,1)S(1)}, u32[]{:S(2)}, u32[]{:S(2)}) %collective-permute-start.2) | collective-permute-done | bytes 524320 | tf_op jit(solution)/shard_map/ppermute | solution.py:292
  41.5 2.2 %collective-permute-start.15 = (bf16[128,512]{1,0:T(8,128)(2,1)S(1)}, bf16[128,512]{1,0:T(8,128)(2,1)S(1)}, u32[]{:S(2)}, u32[]{:S(2)}) collective-permute-start(bf16[128,512]{1,0:T(8,128)(2,1)S(1)} %get-tuple-element.29), channel_id=1, source_target_pairs={{0,8},{4,12},{8,0},{12,4},{1,9},{5,13},{9,1},{13,5},{2,10},{6,14},... | collective-permute-start | bytes 393224 | tf_op jit(solution)/shard_map/ppermute | solution.py:348
  43.7 2.2 %collective-permute-start.16 = (bf16[128,512]{1,0:T(8,128)(2,1)S(1)}, bf16[128,512]{1,0:T(8,128)(2,1)S(1)}, u32[]{:S(2)}, u32[]{:S(2)}) collective-permute-start(bf16[128,512]{1,0:T(8,128)(2,1)S(1)} %get-tuple-element.30), channel_id=1, source_target_pairs={{0,12},{4,8},{8,4},{12,0},{1,13},{5,9},{9,5},{13,1},{2,14},{6,10},... | collective-permute-start | bytes 393224 | tf_op jit(solution)/shard_map/ppermute | solution.py:348
  45.9 3.8 %collective-permute-done.17.refs_0_.refs_7_ = bf16[256,512]{1,0:T(8,128)(2,1)S(1)} collective-permute-done((bf16[256,512]{1,0:T(8,128)(2,1)S(1)}, bf16[256,512]{1,0:T(8,128)(2,1)S(1)}, u32[]{:S(2)}, u32[]{:S(2)}) %collective-permute-start.17) | collective-permute-done | bytes 262176 | tf_op jit(solution)/shard_map/ppermute | solution.py:292
  50.3 1.3 %layers.1.refs_0_.refs_1_ = bf16[1024,2048]{1,0:T(8,128)(2,1)S(1)} custom-call(s32[8,8]{1,0:T(8,128)S(1)} %get-tuple-element.19.refs_1_.refs_0_, bf16[1024,512]{1,0:T(8,128)(2,1)S(1)} %copy-done, bf16[512,512]{1,0:T(8,128)(2,1)S(1)} %pack.4.refs_0_.refs_2_, bf16[512,512]{1,0:T(8,128)(2,1)S(1)} %collective-permute-done.2.refs_1_.refs_3_, ...), custom_call_target="tpu_custom_call" | custom-call | bytes 7864320 | tf_op jit(solution)/shard_map/layers/pallas_call | solution.py:51
  51.6 0.7 %second_product.1.refs_2_ = f32[1024,128]{1,0:T(8,128)S(1)} custom-call(bf16[1024,2048]{1,0:T(8,128)(2,1)S(1)} %layers.1.refs_0_.refs_1_, bf16[128,512]{1,0:T(8,128)(2,1)S(1)} %get-tuple-element.27.refs_2_.refs_1_.refs_3_, bf16[128,512]{1,0:T(8,128)(2,1)S(1)} %collective-permute-done.14.refs_2_.refs_4_), custom_call_target="tpu_custom_call" | custom-call | bytes 4980736 | tf_op jit(solution)/shard_map/second_product/pallas_call | solution.py:51
  52.3 2.1 %collective-permute-done.15.refs_5_ = bf16[128,512]{1,0:T(8,128)(2,1)S(1)} collective-permute-done((bf16[128,512]{1,0:T(8,128)(2,1)S(1)}, bf16[128,512]{1,0:T(8,128)(2,1)S(1)}, u32[]{:S(2)}, u32[]{:S(2)}) %collective-permute-start.15) | collective-permute-done | bytes 131104 | tf_op jit(solution)/shard_map/ppermute | solution.py:348
  54.4 2.6 %last_product.1 = bf16[1024,128]{1,0:T(8,128)(2,1)} custom-call(s32[8,8]{1,0:T(8,128)S(1)} %get-tuple-element.19.refs_1_.refs_0_, bf16[1024,2048]{1,0:T(8,128)(2,1)S(1)} %layers.1.refs_0_.refs_1_, f32[1024,128]{1,0:T(8,128)S(1)} %second_product.1.refs_2_, bf16[128,512]{1,0:T(8,128)(2,1)S(1)} %get-tuple-element.27.refs_2_.refs_1_.refs_3_, ...), custom_call_target="tpu_custom_call" | custom-call | bytes 6684672 | tf_op jit(solution)/shard_map/last_product/pallas_call | solution.py:51
  (37 shorter events, 5.2 us)
Async XLA Ops:
  1.0 12.3 %collective-permute-start = (bf16[256,512]{1,0:T(8,128)(2,1)S(1)}, bf16[256,512]{1,0:T(8,128)(2,1)S(1)}, u32[]{:S(2)}, u32[]{:S(2)}) collective-permute-start(bf16[256,512]{1,0:T(8,128)(2,1)S(1)} %bitcast.5), channel_id=1, source_target_pairs={{0,4},{4,8},{8,12},{12,0},{1,5},{5,9},{9,13},{13,1},{2,6},{6,10},{... | collective-permute-start | bytes 786440 | tf_op jit(solution)/shard_map/ppermute | solution.py:286
  4.0 9.2 %collective-permute-start.3 = (bf16[1024,128]{1,0:T(8,128)(2,1)}, bf16[1024,128]{1,0:T(8,128)(2,1)S(1)}, u32[]{:S(2)}, u32[]{:S(2)}) collective-permute-start(bf16[1024,128]{1,0:T(8,128)(2,1)} %refs_2_.1), channel_id=1, source_target_pairs={{0,2},{1,3},{2,0},{3,1},{4,6},{5,7},{6,4},{7,5},{8,10},{9,11},{10,... | collective-permute-start | bytes 786440 | tf_op jit(solution)/shard_map/ppermute | solution.py:311
  5.6 13.2 %collective-permute-start.1 = (bf16[256,512]{1,0:T(8,128)(2,1)S(1)}, bf16[256,512]{1,0:T(8,128)(2,1)S(1)}, u32[]{:S(2)}, u32[]{:S(2)}) collective-permute-start(bf16[256,512]{1,0:T(8,128)(2,1)S(1)} %bitcast.6), channel_id=1, source_target_pairs={{0,12},{4,0},{8,4},{12,8},{1,13},{5,1},{9,5},{13,9},{2,14},{6,2},{... | collective-permute-start | bytes 786440 | tf_op jit(solution)/shard_map/ppermute | solution.py:288
  7.8 0.9 %copy-start.1 = (bf16[1024,128]{1,0:T(8,128)(2,1)S(1)}, bf16[1024,128]{1,0:T(8,128)(2,1)}, u32[]{:S(2)}) copy-start(bf16[1024,128]{1,0:T(8,128)(2,1)} %refs_2_.1) | copy-start | bytes 786436
  8.8 0.7 %copy-start.2 = (s32[8,8]{1,0:T(8,128)S(1)}, s32[8,8]{1,0:T(8,128)}, u32[]{:S(2)}) copy-start(s32[8,8]{1,0:T(8,128)} %refs_0_.1) | copy-start | bytes 772
  9.5 0.7 %copy-start.3 = (s32[8,8]{1,0:T(8,128)S(1)}, s32[8,8]{1,0:T(8,128)}, u32[]{:S(2)}) copy-start(s32[8,8]{1,0:T(8,128)} %refs_1_.2) | copy-start | bytes 772
  11.6 9.3 %collective-permute-start.4 = (bf16[1024,128]{1,0:T(8,128)(2,1)S(1)}, bf16[1024,128]{1,0:T(8,128)(2,1)S(1)}, u32[]{:S(2)}, u32[]{:S(2)}) collective-permute-start(bf16[1024,128]{1,0:T(8,128)(2,1)S(1)} %get-tuple-element.21.refs_2_), channel_id=1, source_target_pairs={{0,16},{16,0},{1,17},{17,1},{2,18},{18,2},{3,19},{19,3},{4,20},{20... | collective-permute-start | bytes 786440 | tf_op jit(solution)/shard_map/ppermute | solution.py:311
  13.3 11.3 %collective-permute-start.5 = (bf16[1024,128]{1,0:T(8,128)(2,1)S(1)}, bf16[1024,128]{1,0:T(8,128)(2,1)S(1)}, u32[]{:S(2)}, u32[]{:S(2)}) collective-permute-start(bf16[1024,128]{1,0:T(8,128)(2,1)S(1)} %pack.5), channel_id=1, source_target_pairs={{0,16},{16,0},{1,17},{17,1},{2,18},{18,2},{3,19},{19,3},{4,20},{20... | collective-permute-start | bytes 786440 | tf_op jit(solution)/shard_map/ppermute | solution.py:311
  15.1 11.7 %collective-permute-start.6 = (bf16[256,512]{1,0:T(8,128)(2,1)S(1)}, bf16[256,512]{1,0:T(8,128)(2,1)S(1)}, u32[]{:S(2)}, u32[]{:S(2)}) collective-permute-start(bf16[256,512]{1,0:T(8,128)(2,1)S(1)} %collective-permute-done.refs_0_.refs_1_.refs_7_), channel_id=1, source_target_pairs={{0,4},{4,8},{8,12},{12,0},{1,5},{5,9},{9,13},{13,1},{2,6},{6,10},{... | collective-permute-start | bytes 786440 | tf_op jit(solution)/shard_map/ppermute | solution.py:286
  25.7 1.7 %collective-permute-start.10 = (bf16[512,256]{1,0:T(8,128)(2,1)S(1)}, bf16[512,256]{1,0:T(8,128)(2,1)S(1)}, u32[]{:S(2)}, u32[]{:S(2)}) collective-permute-start(bf16[512,256]{1,0:T(8,128)(2,1)S(1)} %get-tuple-element.26.refs_6_), channel_id=1, source_target_pairs={{0,1},{1,0},{2,3},{3,2},{4,5},{5,4},{6,7},{7,6},{8,9},{9,8},{10,11... | collective-permute-start | bytes 786440 | tf_op jit(solution)/shard_map/ppermute | solution.py:319
  25.8 1.9 %collective-permute-start.7 = (bf16[512,256]{1,0:T(8,128)(2,1)S(1)}, bf16[512,256]{1,0:T(8,128)(2,1)S(1)}, u32[]{:S(2)}, u32[]{:S(2)}) collective-permute-start(bf16[512,256]{1,0:T(8,128)(2,1)S(1)} %get-tuple-element.23.refs_3_), channel_id=1, source_target_pairs={{0,1},{1,0},{2,3},{3,2},{4,5},{5,4},{6,7},{7,6},{8,9},{9,8},{10,11... | collective-permute-start | bytes 786440 | tf_op jit(solution)/shard_map/ppermute | solution.py:319
  26.3 1.8 %collective-permute-start.8 = (bf16[512,256]{1,0:T(8,128)(2,1)S(1)}, bf16[512,256]{1,0:T(8,128)(2,1)S(1)}, u32[]{:S(2)}, u32[]{:S(2)}) collective-permute-start(bf16[512,256]{1,0:T(8,128)(2,1)S(1)} %get-tuple-element.24.refs_4_), channel_id=1, source_target_pairs={{0,1},{1,0},{2,3},{3,2},{4,5},{5,4},{6,7},{7,6},{8,9},{9,8},{10,11... | collective-permute-start | bytes 786440 | tf_op jit(solution)/shard_map/ppermute | solution.py:319
  26.3 23.9 %copy-start = (bf16[1024,512]{1,0:T(8,128)(2,1)S(1)}, bf16[1024,512]{1,0:T(8,128)(2,1)}, u32[]{:S(2)}) copy-start(bf16[1024,512]{1,0:T(8,128)(2,1)} %refs_1_.3) | copy-start | bytes 3145732
  26.3 2.1 %collective-permute-start.9 = (bf16[512,256]{1,0:T(8,128)(2,1)S(1)}, bf16[512,256]{1,0:T(8,128)(2,1)S(1)}, u32[]{:S(2)}, u32[]{:S(2)}) collective-permute-start(bf16[512,256]{1,0:T(8,128)(2,1)S(1)} %get-tuple-element.25.refs_5_), channel_id=1, source_target_pairs={{0,1},{1,0},{2,3},{3,2},{4,5},{5,4},{6,7},{7,6},{8,9},{9,8},{10,11... | collective-permute-start | bytes 786440 | tf_op jit(solution)/shard_map/ppermute | solution.py:319
  26.8 14.0 %collective-permute-start.2 = (bf16[512,512]{1,0:T(8,128)(2,1)S(1)}, bf16[512,512]{1,0:T(8,128)(2,1)S(1)}, u32[]{:S(2)}, u32[]{:S(2)}) collective-permute-start(bf16[512,512]{1,0:T(8,128)(2,1)S(1)} %pack.4.refs_0_.refs_2_), channel_id=1, source_target_pairs={{0,2},{1,3},{2,0},{3,1},{4,6},{5,7},{6,4},{7,5},{8,10},{9,11},{10,... | collective-permute-start | bytes 1572872 | tf_op jit(solution)/shard_map/ppermute | solution.py:292
  29.9 1.7 %collective-permute-start.12 = (bf16[256,512]{1,0:T(8,128)(2,1)S(1)}, bf16[256,512]{1,0:T(8,128)(2,1)S(1)}, u32[]{:S(2)}, u32[]{:S(2)}) collective-permute-start(bf16[256,512]{1,0:T(8,128)(2,1)S(1)} %pack.6.refs_5_), channel_id=1, source_target_pairs={{0,1},{1,0},{2,3},{3,2},{4,5},{5,4},{6,7},{7,6},{8,9},{9,8},{10,11... | collective-permute-start | bytes 786440 | tf_op jit(solution)/shard_map/ppermute | solution.py:338
  30.1 8.6 %collective-permute-start.11 = (bf16[256,512]{1,0:T(8,128)(2,1)S(1)}, bf16[256,512]{1,0:T(8,128)(2,1)S(1)}, u32[]{:S(2)}, u32[]{:S(2)}) collective-permute-start(bf16[256,512]{1,0:T(8,128)(2,1)S(1)} %first_product.1.refs_1_.refs_0_), channel_id=1, source_target_pairs={{0,16},{16,0},{1,17},{17,1},{2,18},{18,2},{3,19},{19,3},{4,20},{20... | collective-permute-start | bytes 786440 | tf_op jit(solution)/shard_map/ppermute | solution.py:332
  40.9 8.9 %collective-permute-start.13 = (bf16[1024,512]{1,0:T(8,128)(2,1)S(1)}, bf16[1024,512]{1,0:T(8,128)(2,1)S(1)}, u32[]{:S(2)}, u32[]{:S(2)}) collective-permute-start(bf16[1024,512]{1,0:T(8,128)(2,1)S(1)} %pack.7), channel_id=1, source_target_pairs={{0,1},{1,0},{2,3},{3,2},{4,5},{5,4},{6,7},{7,6},{8,9},{9,8},{10,11... | collective-permute-start | bytes 3145736 | tf_op jit(solution)/shard_map/ppermute | solution.py:353
  40.9 8.7 %collective-permute-start.17 = (bf16[256,512]{1,0:T(8,128)(2,1)S(1)}, bf16[256,512]{1,0:T(8,128)(2,1)S(1)}, u32[]{:S(2)}, u32[]{:S(2)}) collective-permute-start(bf16[256,512]{1,0:T(8,128)(2,1)S(1)} %pack.6.refs_5_), channel_id=1, source_target_pairs={{0,2},{1,3},{2,0},{3,1},{4,6},{5,7},{6,4},{7,5},{8,10},{9,11},{10,... | collective-permute-start | bytes 786440 | tf_op jit(solution)/shard_map/ppermute | solution.py:292
  41.5 10.1 %collective-permute-start.14 = (bf16[128,512]{1,0:T(8,128)(2,1)S(1)}, bf16[128,512]{1,0:T(8,128)(2,1)S(1)}, u32[]{:S(2)}, u32[]{:S(2)}) collective-permute-start(bf16[128,512]{1,0:T(8,128)(2,1)S(1)} %get-tuple-element.28), channel_id=1, source_target_pairs={{0,4},{4,0},{8,12},{12,8},{1,5},{5,1},{9,13},{13,9},{2,6},{6,2},{1... | collective-permute-start | bytes 393224 | tf_op jit(solution)/shard_map/ppermute | solution.py:348
  41.5 12.9 %collective-permute-start.15 = (bf16[128,512]{1,0:T(8,128)(2,1)S(1)}, bf16[128,512]{1,0:T(8,128)(2,1)S(1)}, u32[]{:S(2)}, u32[]{:S(2)}) collective-permute-start(bf16[128,512]{1,0:T(8,128)(2,1)S(1)} %get-tuple-element.29), channel_id=1, source_target_pairs={{0,8},{4,12},{8,0},{12,4},{1,9},{5,13},{9,1},{13,5},{2,10},{6,14},... | collective-permute-start | bytes 393224 | tf_op jit(solution)/shard_map/ppermute | solution.py:348
  43.7 10.7 %collective-permute-start.16 = (bf16[128,512]{1,0:T(8,128)(2,1)S(1)}, bf16[128,512]{1,0:T(8,128)(2,1)S(1)}, u32[]{:S(2)}, u32[]{:S(2)}) collective-permute-start(bf16[128,512]{1,0:T(8,128)(2,1)S(1)} %get-tuple-element.30), channel_id=1, source_target_pairs={{0,12},{4,8},{8,4},{12,0},{1,13},{5,9},{9,5},{13,1},{2,14},{6,10},... | collective-permute-start | bytes 393224 | tf_op jit(solution)/shard_map/ppermute | solution.py:348
  49.7 4.7 %collective-permute-start.18 = (bf16[128,512]{1,0:T(8,128)(2,1)S(1)}, bf16[128,512]{1,0:T(8,128)(2,1)S(1)}, u32[]{:S(2)}, u32[]{:S(2)}) collective-permute-start(bf16[128,512]{1,0:T(8,128)(2,1)S(1)} %get-tuple-element.31), channel_id=1, source_target_pairs={{0,1},{1,0},{2,3},{3,2},{4,5},{5,4},{6,7},{7,6},{8,9},{9,8},{10,11... | collective-permute-start | bytes 393224 | tf_op jit(solution)/shard_map/ppermute | solution.py:361
  49.8 4.7 %collective-permute-start.19 = (bf16[128,512]{1,0:T(8,128)(2,1)S(1)}, bf16[128,512]{1,0:T(8,128)(2,1)S(1)}, u32[]{:S(2)}, u32[]{:S(2)}) collective-permute-start(bf16[128,512]{1,0:T(8,128)(2,1)S(1)} %get-tuple-element.32), channel_id=1, source_target_pairs={{0,1},{1,0},{2,3},{3,2},{4,5},{5,4},{6,7},{7,6},{8,9},{9,8},{10,11... | collective-permute-start | bytes 393224 | tf_op jit(solution)/shard_map/ppermute | solution.py:361

commit v12 on v11

--- a/solution.py
+++ b/solution.py
@@ -183,26 +183,11 @@
 
 
 def route_kernel(sizes, row_offsets, *refs):
-    n = len(row_offsets)
-    pieces, outs, table = refs[:n], refs[n:-1], refs[-1]
-    r, c, _ = place()
-    q = sizes.quarter
-    for dr, piece in zip(row_offsets, pieces):
+    table, (r, _, _), q = refs[-1], place(), sizes.quarter
+    for dr, piece in zip(row_offsets, refs[:-1]):
         for half in range(sizes.per):
             start = pl.multiple_of(((r ^ dr) * sizes.per + half) * q, q)
             table[pl.ds(start, q), :] = piece[half * q : (half + 1) * q, :]
-    for d, out in enumerate(outs):
-        out[...] = table[pl.ds(pl.multiple_of((c ^ d) * q, q), q), :]
-
-
-def split_kernel(*refs):
-    pieces, outs = [], []
-    for ref in refs:
-        (pieces if ref.shape[0] > refs[-1].shape[0] else outs).append(ref)
-    per, height = len(outs) // len(pieces), outs[0].shape[0]
-    for n, out in enumerate(outs):
-        first = n % per * height
-        out[...] = pieces[n // per][first : first + height, :]
 
 
 def layers_kernel(sizes, z_table, zp, *refs):
@@ -215,56 +200,28 @@
             rows = pl.ds(strip_start(ll, half, sizes), q)
             for s in range(cols):
                 cc = slot_column(c, s, cols)
-                columns = columns_of(cc, sizes)
-                if s and (dl, s) not in z_table:
-                    out[rows, columns] = jnp.zeros((q, sizes.cols_here), out.dtype)
-                    continue
                 if s == 0:
                     strip = held[0][rows, :]
                 else:
                     index, row = z_table[dl, s]
                     strip = held[index][row + half * q : row + (half + 1) * q, :]
-                out[rows, columns] = mask_strip(zp, r, ll, half, cc, strip, sizes)
-
-
-def turned_dot(left, right):
-    return lax.dot_general(
-        left, right, (((1,), (1,)), ((), ())), preferred_element_type=jnp.float32
-    )
-
-
-def second_kernel(sizes, part, z_full, *refs):
-    messages, before, out = refs[: len(part)], refs[len(part) : -1], refs[-1]
-    c = lax.axis_index("col")
+                out[rows, columns_of(cc, sizes)] = mask_strip(zp, r, ll, half, cc, strip, sizes)
+
+
+def second_kernel(sizes, part, z_full, messages, *refs):
+    before, out = refs[:-1], refs[-1]
+    q, c = sizes.quarter, lax.axis_index("col")
     total = before[0][...] if before else None
-    for d, message in zip(part, messages):
-        added = turned_dot(z_full[:, columns_of(c ^ d, sizes)], message[...])
+    for d in part:
+        cc = c ^ d
+        added = lax.dot_general(
+            z_full[:, columns_of(cc, sizes)],
+            messages[pl.ds(pl.multiple_of(cc * q, q), q), :],
+            (((1,), (1,)), ((), ())),
+            preferred_element_type=jnp.float32,
+        )
         total = added if total is None else total + added
-    out[...] = total
-
-
-def last_kernel(sizes, part, offsets, zp, z_full, before, *refs):
-    cols, q, per = sizes.cols, sizes.quarter, sizes.per
-    messages, piece, strips = refs[:cols], refs[cols], refs[cols + 1 : -3]
-    out, acc, xm = refs[-3:]
-    r, c, l = place()
-    total = before[...]
-    for d in part:
-        total += turned_dot(z_full[:, columns_of(c ^ d, sizes)], messages[d][...])
-    acc[...] = total
-    cc = slot_column(c, cols - 1, cols)
-    for d in range(cols):
-
-        @pl.when((c ^ d) == cc)
-        def _(d=d):
-            xm[...] = messages[d][...]
-
-    for n, dl in enumerate(offsets):
-        for half in range(per):
-            rows = pl.ds(strip_start(l ^ dl, half, sizes), q)
-            strip = strips[half][...] if n else piece[half * q : (half + 1) * q, :]
-            acc[rows, :] += turned_dot(mask_strip(zp, r, l ^ dl, half, cc, strip, sizes), xm[...])
-    out[...] = acc[...].astype(out.dtype)
+    out[...] = total.astype(out.dtype)
 
 
 def local(sizes, hamiltonian, inv_root, h_pattern, z_pattern):
@@ -304,8 +261,6 @@
         perm = flip(rows if axis == "row" else layers, bit)
         for piece, (dr, dl) in list(zip(h_pieces, h_table)):
             h_table.append((dr ^ bit, dl) if axis == "row" else (dr, dl ^ bit))
-            if axis == "row" and not dr and not dl:
-                piece = fetched
             if dl and axis == 'row':
                 piece = pack([piece], [slots[1]])
             h_pieces.append(lax.ppermute(piece, axis, perm))
@@ -331,34 +286,26 @@
         for dr, piece in list(gathered.items()):
             gathered[dr ^ bit] = lax.ppermute(piece, "row", flip(rows, bit))
     row_offsets = list(gathered)
-    held, z_table = [inv_root], {}
-
-    last = pack([slots[-1]], [product])
-    last_top = cross(last)
-    last_low = lax.ppermute(last, "layer", flip(layers, low))
-    outgoing = run(
+    table = run(
         functools.partial(route_kernel, sizes, row_offsets),
         "route",
-        [shape(q, cols_here)] * cols,
+        [shape(cols * q, cols_here)],
         [gathered[o] for o in row_offsets],
-        after=[last_low],
-        scratch=[pltpu.VMEM((cols * q, cols_here), jnp.bfloat16)],
-    )
-    messages = [outgoing[0]] + [
-        lax.ppermute(outgoing[d], "col", flip(cols, d)) for d in range(1, cols)
-    ]
-    group = range(1, cols - 1)
-    mine = pack([slots[s] for s in group])
-    other = cross(mine)
-    both = lax.ppermute(pack([mine, other], [outgoing[0]]), "layer", flip(layers, low))
-    held, z_table = [inv_root, mine, other, both, last, last_low], {}
-    for n, s in enumerate(group):
-        row = n * height
-        z_table[0, s], z_table[top, s], z_table[low, s] = (1, row), (2, row), (3, row)
-        z_table[low ^ top, s] = (3, len(group) * height + row)
-    z_table[0, cols - 1], z_table[low, cols - 1] = (4, 0), (5, 0)
-    parts = run(split_kernel, "split", [strip_shape] * per, [last_top])
-    parts = [lax.ppermute(part, "layer", flip(layers, low)) for part in parts]
+    )[0]
+    messages = lax.all_to_all(table, "col", 0, 0, tiled=True)
+
+    held, z_table = [inv_root], {}
+    for group, gates in ((range(1, cols - 1), [[], [table]]), ([cols - 1], [[product], []])):
+        mine = pack([slots[s] for s in group], gates[0])
+        other = cross(mine)
+        both = lax.ppermute(pack([mine, other], gates[1]), "layer", flip(layers, low))
+        base = len(held)
+        held += [mine, other, both]
+        for n, s in enumerate(group):
+            row = n * height
+            z_table[0, s], z_table[top, s] = (base, row), (base + 1, row)
+            z_table[low, s] = (base + 2, row)
+            z_table[low ^ top, s] = (base + 2, len(group) * height + row)
     z_full = run(
         functools.partial(layers_kernel, sizes, z_table),
         "layers",
@@ -366,20 +313,17 @@
         held,
         smem=[z_pattern],
     )[0]
-    early, late = range(cols // 2), range(cols // 2, cols)
     total = run(
-        functools.partial(second_kernel, sizes, early),
+        functools.partial(second_kernel, sizes, (0,)),
         "second_product",
         [shape(*hamiltonian.shape, f32)],
-        [z_full, *[messages[d] for d in early]],
-    )[0]
+        [z_full, table],
+    )
     return run(
-        functools.partial(last_kernel, sizes, late, (top, low ^ top)),
-        "last_product",
+        functools.partial(second_kernel, sizes, range(1, cols)),
+        "second_product",
         [shape(*hamiltonian.shape)],
-        [z_full, total, *messages, last_top, *parts],
-        smem=[z_pattern],
-        scratch=[pltpu.VMEM(hamiltonian.shape, f32), pltpu.VMEM((q, cols_here), jnp.bfloat16)],
+        [z_full, messages, *total],
     )[0]
 
 

time: 57.3 us -> 64.5 us (1.13)
  local copies, waits for them, and re-layouts: 3.29 us -> 7.43 us
  Pallas kernels: 8.78 us -> 11.1 us
  starting transfers between devices: 19.2 us -> 20.6 us
  waiting for transfers between devices: 25.6 us -> 24.9 us
    all_to_all x0 -> x1, starting transfers between devices: none -> 6.53 us  [local(): messages = lax.all_to_all(table, 'col', 0, 0, tiled=True)]
    all_to_all x0 -> x1, waiting for transfers between devices: none -> 5.74 us  [local(): messages = lax.all_to_all(table, 'col', 0, 0, tiled=True)]
    ppermute x2, waiting for transfers between devices: 0.13 us -> 5.44 us  [local(): lax.ppermute(right, 'col', [(i, (i + 1) % cols) for i in range(cols)])]
    ppermute x7 -> x2, starting transfers between devices: 5.22 us -> 0.07 us  [local(): lax.ppermute(pack([mine, other], gates[1]), 'layer', flip(layers, low))]
    unnamed x8 -> x12, local copies, waits for them, and re-layouts: 2.33 us -> 6.46 us
    ppermute x3, waiting for transfers between devices: 5.81 us -> 2.04 us  [local(): h_pieces.append(lax.ppermute(piece, axis, perm))]
    ppermute x1, waiting for transfers between devices: 3.6 us -> 0.01 us  [local(): left = lax.ppermute(left, 'col', [(i, (i - 1) % cols) for i in range(cols)])]
    ppermute x2, waiting for transfers between devices: 5.82 us -> 3.37 us  [cross(): return lax.ppermute(piece, 'layer', flip(layers, layer_bits[0]))]
  transfers between devices with their start and end apart: 20 -> 16, of which waited for: 11 -> 8; matrix products, arithmetic and copies ran while one was open for 0% -> 0% of each run, Pallas kernels for 11% -> 13%
where the time goes in v12:
time: 64.5 us; the launch traced here: 64.1 us
  waiting for transfers between devices  24.9 us (39%)
  starting transfers between devices  20.6 us (32%)
  Pallas kernels  11.1 us (17%)
  local copies, waits for them, and re-layouts  7.43 us (12%)
    pallas_call x12, Pallas kernels, run(): pl.pallas_call(body, out_shape=list(outs), in_specs=[pl.BlockSpec(memory_...  11.1 us
    all_to_all x1, starting transfers between devices, local(): messages = lax.all_to_all(table, 'col', 0, 0, tiled=True)  6.53 us
    unnamed x12, local copies, waits for them, and re-layouts  6.46 us
    ppermute x1, waiting for transfers between devices, local(): gathered[dr ^ bit] = lax.ppermute(piece, 'row', flip(rows, bit))  6.36 us
    all_to_all x1, waiting for transfers between devices, local(): messages = lax.all_to_all(table, 'col', 0, 0, tiled=True)  5.74 us
    ppermute x2, waiting for transfers between devices, local(): lax.ppermute(right, 'col', [(i, (i + 1) % cols) for i in range(cols)])  5.44 us
    ppermute x3, starting transfers between devices, local(): h_pieces.append(lax.ppermute(piece, axis, perm))  4.81 us
    ppermute x2, waiting for transfers between devices, cross(): return lax.ppermute(piece, 'layer', flip(layers, layer_bits[0]))  3.37 us
  transfers between devices with their start and end apart: 16, of which 8 were waited for; matrix products, arithmetic and copies ran while one was open for 0% of the time, Pallas kernels for 13%

profile of v12, /device:TPU:0, one launch (start us, length us, event | category | flops | bytes accessed | tf_op | source)
XLA Modules:
  0.0 64.1 jit_solution(17841000063322844362)
XLA Ops:
  1.0 3.1 %collective-permute-start = (bf16[256,512]{1,0:T(8,128)(2,1)S(1)}, bf16[256,512]{1,0:T(8,128)(2,1)S(1)}, u32[]{:S(2)}, u32[]{:S(2)}) collective-permute-start(bf16[256,512]{1,0:T(8,128)(2,1)S(1)} %bitcast.8), channel_id=1, source_target_pairs={{0,4},{4,8},{8,12},{12,0},{1,5},{5,9},{9,13},{13,1},{2,6},{6,10},{... | collective-permute-start | bytes 786440 | tf_op jit(solution)/shard_map/ppermute | solution.py:243
  4.0 1.5 %collective-permute-start.3 = (bf16[1024,128]{1,0:T(8,128)(2,1)}, bf16[1024,128]{1,0:T(8,128)(2,1)S(1)}, u32[]{:S(2)}, u32[]{:S(2)}) collective-permute-start(bf16[1024,128]{1,0:T(8,128)(2,1)} %refs_2_.1), channel_id=1, source_target_pairs={{0,2},{1,3},{2,0},{3,1},{4,6},{5,7},{6,4},{7,5},{8,10},{9,11},{10,... | collective-permute-start | bytes 786440 | tf_op jit(solution)/shard_map/ppermute | solution.py:266
  5.6 2.2 %collective-permute-start.1 = (bf16[256,512]{1,0:T(8,128)(2,1)S(1)}, bf16[256,512]{1,0:T(8,128)(2,1)S(1)}, u32[]{:S(2)}, u32[]{:S(2)}) collective-permute-start(bf16[256,512]{1,0:T(8,128)(2,1)S(1)} %bitcast.9), channel_id=1, source_target_pairs={{0,12},{4,0},{8,4},{12,8},{1,13},{5,1},{9,5},{13,9},{2,14},{6,2},{... | collective-permute-start | bytes 786440 | tf_op jit(solution)/shard_map/ppermute | solution.py:245
  7.8 1.5 %collective-permute-start.4 = (bf16[1024,128]{1,0:T(8,128)(2,1)}, bf16[1024,128]{1,0:T(8,128)(2,1)S(1)}, u32[]{:S(2)}, u32[]{:S(2)}) collective-permute-start(bf16[1024,128]{1,0:T(8,128)(2,1)} %refs_2_.1), channel_id=1, source_target_pairs={{0,16},{16,0},{1,17},{17,1},{2,18},{18,2},{3,19},{19,3},{4,20},{20... | collective-permute-start | bytes 786440 | tf_op jit(solution)/shard_map/ppermute | solution.py:266
  9.3 3.9 %collective-permute-done.refs_0_.refs_1_.refs_7_ = bf16[256,512]{1,0:T(8,128)(2,1)S(1)} collective-permute-done((bf16[256,512]{1,0:T(8,128)(2,1)S(1)}, bf16[256,512]{1,0:T(8,128)(2,1)S(1)}, u32[]{:S(2)}, u32[]{:S(2)}) %collective-permute-start) | collective-permute-done | bytes 262176 | tf_op jit(solution)/shard_map/ppermute | solution.py:243
  13.3 1.8 %collective-permute-start.5 = (bf16[1024,128]{1,0:T(8,128)(2,1)S(1)}, bf16[1024,128]{1,0:T(8,128)(2,1)S(1)}, u32[]{:S(2)}, u32[]{:S(2)}) collective-permute-start(bf16[1024,128]{1,0:T(8,128)(2,1)S(1)} %pack.6), channel_id=1, source_target_pairs={{0,16},{16,0},{1,17},{17,1},{2,18},{18,2},{3,19},{19,3},{4,20},{20... | collective-permute-start | bytes 786440 | tf_op jit(solution)/shard_map/ppermute | solution.py:266
  17.5 1.4 %fetch.1 = (s32[8,8]{1,0:T(8,128)S(1)}, s32[8,8]{1,0:T(8,128)S(1)}, bf16[1024,128]{1,0:T(8,128)(2,1)S(1)}) custom-call(s32[8,8]{1,0:T(8,128)S(1)} %copy-done.4, s32[8,8]{1,0:T(8,128)S(1)} %copy-done.5, bf16[1024,128]{1,0:T(8,128)(2,1)S(1)} %copy-done.3), custom_call_target="tpu_custom_call" | custom-call | bytes 524800 | tf_op jit(solution)/shard_map/fetch/pallas_call | solution.py:51
  18.9 2.0 %collective-permute-done.5.refs_5_ = bf16[1024,128]{1,0:T(8,128)(2,1)S(1)} collective-permute-done((bf16[1024,128]{1,0:T(8,128)(2,1)S(1)}, bf16[1024,128]{1,0:T(8,128)(2,1)S(1)}, u32[]{:S(2)}, u32[]{:S(2)}) %collective-permute-start.5) | collective-permute-done | bytes 262176 | tf_op jit(solution)/shard_map/ppermute | solution.py:266
  21.0 1.1 %bring.1 = (bf16[256,2048]{1,0:T(8,128)(2,1)S(1)}, bf16[512,256]{1,0:T(8,128)(2,1)S(1)}, bf16[512,256]{1,0:T(8,128)(2,1)S(1)}, bf16[512,256]{1,0:T(8,128)(2,1)S(1)}, bf16[512,256]{1,0:T(8,128)(2,1)S(1)}) custom-call(s32[8,8]{1,0:T(8,128)S(1)} %get-tuple-element.14.refs_0_, s32[8,8]{1,0:T(8,128)S(1)} %get-tuple-element.13.refs_1_.refs_0_, ...), custom_call_target="tpu_custom_call" | custom-call | bytes 3932160 | tf_op jit(solution)/shard_map/bring/pallas_call | solution.py:51
  23.2 1.5 %collective-permute-done.6.refs_2_.refs_0_ = bf16[256,512]{1,0:T(8,128)(2,1)S(1)} collective-permute-done((bf16[256,512]{1,0:T(8,128)(2,1)S(1)}, bf16[256,512]{1,0:T(8,128)(2,1)S(1)}, u32[]{:S(2)}, u32[]{:S(2)}) %collective-permute-start.6) | collective-permute-done | bytes 262176 | tf_op jit(solution)/shard_map/ppermute | solution.py:243
  24.7 1.5 %collective-permute-start.2 = (bf16[512,512]{1,0:T(8,128)(2,1)S(1)}, bf16[512,512]{1,0:T(8,128)(2,1)S(1)}, u32[]{:S(2)}, u32[]{:S(2)}) collective-permute-start(bf16[512,512]{1,0:T(8,128)(2,1)S(1)} %pack.5.refs_0_.refs_2_), channel_id=1, source_target_pairs={{0,2},{1,3},{2,0},{3,1},{4,6},{5,7},{6,4},{7,5},{8,10},{9,11},{10,... | collective-permute-start | bytes 1572872 | tf_op jit(solution)/shard_map/ppermute | solution.py:249
  26.2 1.4 %first_product.1.refs_0_.refs_1_ = bf16[256,512]{1,0:T(8,128)(2,1)S(1)} custom-call(s32[8,8]{1,0:T(8,128)S(1)} %get-tuple-element.13.refs_1_.refs_0_, bf16[256,2048]{1,0:T(8,128)(2,1)S(1)} %get-tuple-element.16.refs_1_, bf16[256,512]{1,0:T(8,128)(2,1)S(1)} %collective-permute-done.6.refs_2_.refs_0_, bf16[512,256]{1,0:T(8,128)(2,1)S(1)} %get-tuple-element.17.refs_3_, ...), custom_call_target="tpu_custom_call" | custom-call | bytes 4718592 | tf_op jit(solution)/shard_map/first_product/pallas_call | solution.py:51
  28.3 6.4 %collective-permute-done.11.refs_1_ = bf16[256,512]{1,0:T(8,128)(2,1)S(1)} collective-permute-done((bf16[256,512]{1,0:T(8,128)(2,1)S(1)}, bf16[256,512]{1,0:T(8,128)(2,1)S(1)}, u32[]{:S(2)}, u32[]{:S(2)}) %collective-permute-start.11) | collective-permute-done | bytes 262176 | tf_op jit(solution)/shard_map/ppermute | solution.py:287
  35.5 1.7 %collective-permute-done.2.refs_1_.refs_3_ = bf16[512,512]{1,0:T(8,128)(2,1)S(1)} collective-permute-done((bf16[512,512]{1,0:T(8,128)(2,1)S(1)}, bf16[512,512]{1,0:T(8,128)(2,1)S(1)}, u32[]{:S(2)}, u32[]{:S(2)}) %collective-permute-start.2) | collective-permute-done | bytes 524320 | tf_op jit(solution)/shard_map/ppermute | solution.py:249
  37.2 1.1 %pack.7 = bf16[1024,512]{1,0:T(8,128)(2,1)} custom-call(bf16[512,512]{1,0:T(8,128)(2,1)S(1)} %pack.5.refs_0_.refs_2_, bf16[512,512]{1,0:T(8,128)(2,1)S(1)} %collective-permute-done.2.refs_1_.refs_3_, bf16[512,512]{1,0:T(8,128)(2,1)} %route.1.refs_2_.refs_1_), custom_call_target="tpu_custom_call" | custom-call | bytes 2097152 | tf_op jit(solution)/shard_map/pack/pallas_call | solution.py:51
  38.8 6.5 %all-to-all-start = ((bf16[4,128,512]{2,1,0:T(8,128)(2,1)}), bf16[4,128,512]{2,1,0:T(8,128)(2,1)S(1)}, u32[]{:S(2)}, u32[]{:S(2)}) async-start(bf16[4,128,512]{2,1,0:T(8,128)(2,1)} %bitcast.2), calls=%async_computation | async-start | bytes 1048576 | tf_op jit(solution)/shard_map/all_to_all | solution.py:295
  45.4 1.7 %collective-permute-done.13.refs_1_.refs_6_ = bf16[256,512]{1,0:T(8,128)(2,1)S(1)} collective-permute-done((bf16[256,512]{1,0:T(8,128)(2,1)S(1)}, bf16[256,512]{1,0:T(8,128)(2,1)S(1)}, u32[]{:S(2)}, u32[]{:S(2)}) %collective-permute-start.13) | collective-permute-done | bytes 262176 | tf_op jit(solution)/shard_map/ppermute | solution.py:249
  47.2 1.9 %collective-permute-done.14.refs_7_ = bf16[512,512]{1,0:T(8,128)(2,1)S(1)} collective-permute-done((bf16[512,512]{1,0:T(8,128)(2,1)S(1)}, bf16[512,512]{1,0:T(8,128)(2,1)S(1)}, u32[]{:S(2)}, u32[]{:S(2)}) %collective-permute-start.14) | collective-permute-done | bytes 524320 | tf_op jit(solution)/shard_map/ppermute | solution.py:301
  49.1 2.0 %layers.1.refs_0_ = bf16[1024,2048]{1,0:T(8,128)(2,1)S(1)} custom-call(s32[8,8]{1,0:T(8,128)S(1)} %get-tuple-element.13.refs_1_.refs_0_, bf16[1024,512]{1,0:T(8,128)(2,1)S(1)} %copy-done.2, bf16[512,512]{1,0:T(8,128)(2,1)S(1)} %pack.5.refs_0_.refs_2_, bf16[512,512]{1,0:T(8,128)(2,1)S(1)} %collective-permute-done.2.refs_1_.refs_3_, ...), custom_call_target="tpu_custom_call" | custom-call | bytes 8388608 | tf_op jit(solution)/shard_map/layers/pallas_call | solution.py:51
  51.1 1.5 %second_product.2.refs_2_ = f32[1024,128]{1,0:T(8,128)S(1)} custom-call(bf16[1024,2048]{1,0:T(8,128)(2,1)S(1)} %layers.1.refs_0_, bf16[512,512]{1,0:T(8,128)(2,1)} %route.1.refs_2_.refs_1_), custom_call_target="tpu_custom_call" | custom-call | bytes 5242880 | tf_op jit(solution)/shard_map/second_product/pallas_call | solution.py:51
  52.6 1.9 %copy-done = bf16[1024,2048]{1,0:T(8,128)(2,1)} copy-done((bf16[1024,2048]{1,0:T(8,128)(2,1)}, bf16[1024,2048]{1,0:T(8,128)(2,1)S(1)}, u32[]{:S(2)}) %copy-start) | copy-done | bytes 4194328
  54.5 5.7 %all-to-all-done = bf16[4,128,512]{2,1,0:T(8,128)(2,1)S(1)} async-done(((bf16[4,128,512]{2,1,0:T(8,128)(2,1)}), bf16[4,128,512]{2,1,0:T(8,128)(2,1)S(1)}, u32[]{:S(2)}, u32[]{:S(2)}) %all-to-all-start) | async-done | bytes 524320 | tf_op jit(solution)/shard_map/all_to_all | solution.py:295
  60.3 2.2 %copy-done.1 = bf16[1024,2048]{1,0:T(8,128)(2,1)S(1)} copy-done((bf16[1024,2048]{1,0:T(8,128)(2,1)S(1)}, bf16[1024,2048]{1,0:T(8,128)(2,1)}, u32[]{:S(2)}) %copy-start.1) | copy-done | bytes 4194328
  62.4 1.7 %second_product.3 = bf16[1024,128]{1,0:T(8,128)(2,1)} custom-call(bf16[1024,2048]{1,0:T(8,128)(2,1)S(1)} %copy-done.1, bf16[512,512]{1,0:T(8,128)(2,1)S(1)} %bitcast.6, f32[1024,128]{1,0:T(8,128)S(1)} %second_product.2.refs_2_), custom_call_target="tpu_custom_call" | custom-call | bytes 5505024 | tf_op jit(solution)/shard_map/second_product/pallas_call | solution.py:51
  (33 shorter events, 6.7 us)
Async XLA Ops:
  1.0 12.3 %collective-permute-start = (bf16[256,512]{1,0:T(8,128)(2,1)S(1)}, bf16[256,512]{1,0:T(8,128)(2,1)S(1)}, u32[]{:S(2)}, u32[]{:S(2)}) collective-permute-start(bf16[256,512]{1,0:T(8,128)(2,1)S(1)} %bitcast.8), channel_id=1, source_target_pairs={{0,4},{4,8},{8,12},{12,0},{1,5},{5,9},{9,13},{13,1},{2,6},{6,10},{... | collective-permute-start | bytes 786440 | tf_op jit(solution)/shard_map/ppermute | solution.py:243
  4.0 9.2 %collective-permute-start.3 = (bf16[1024,128]{1,0:T(8,128)(2,1)}, bf16[1024,128]{1,0:T(8,128)(2,1)S(1)}, u32[]{:S(2)}, u32[]{:S(2)}) collective-permute-start(bf16[1024,128]{1,0:T(8,128)(2,1)} %refs_2_.1), channel_id=1, source_target_pairs={{0,2},{1,3},{2,0},{3,1},{4,6},{5,7},{6,4},{7,5},{8,10},{9,11},{10,... | collective-permute-start | bytes 786440 | tf_op jit(solution)/shard_map/ppermute | solution.py:266
  5.6 13.4 %collective-permute-start.1 = (bf16[256,512]{1,0:T(8,128)(2,1)S(1)}, bf16[256,512]{1,0:T(8,128)(2,1)S(1)}, u32[]{:S(2)}, u32[]{:S(2)}) collective-permute-start(bf16[256,512]{1,0:T(8,128)(2,1)S(1)} %bitcast.9), channel_id=1, source_target_pairs={{0,12},{4,0},{8,4},{12,8},{1,13},{5,1},{9,5},{13,9},{2,14},{6,2},{... | collective-permute-start | bytes 786440 | tf_op jit(solution)/shard_map/ppermute | solution.py:245
  7.8 11.1 %collective-permute-start.4 = (bf16[1024,128]{1,0:T(8,128)(2,1)}, bf16[1024,128]{1,0:T(8,128)(2,1)S(1)}, u32[]{:S(2)}, u32[]{:S(2)}) collective-permute-start(bf16[1024,128]{1,0:T(8,128)(2,1)} %refs_2_.1), channel_id=1, source_target_pairs={{0,16},{16,0},{1,17},{17,1},{2,18},{18,2},{3,19},{19,3},{4,20},{20... | collective-permute-start | bytes 786440 | tf_op jit(solution)/shard_map/ppermute | solution.py:266
  13.3 7.7 %collective-permute-start.5 = (bf16[1024,128]{1,0:T(8,128)(2,1)S(1)}, bf16[1024,128]{1,0:T(8,128)(2,1)S(1)}, u32[]{:S(2)}, u32[]{:S(2)}) collective-permute-start(bf16[1024,128]{1,0:T(8,128)(2,1)S(1)} %pack.6), channel_id=1, source_target_pairs={{0,16},{16,0},{1,17},{17,1},{2,18},{18,2},{3,19},{19,3},{4,20},{20... | collective-permute-start | bytes 786440 | tf_op jit(solution)/shard_map/ppermute | solution.py:266
  15.1 9.6 %collective-permute-start.6 = (bf16[256,512]{1,0:T(8,128)(2,1)S(1)}, bf16[256,512]{1,0:T(8,128)(2,1)S(1)}, u32[]{:S(2)}, u32[]{:S(2)}) collective-permute-start(bf16[256,512]{1,0:T(8,128)(2,1)S(1)} %collective-permute-done.refs_0_.refs_1_.refs_7_), channel_id=1, source_target_pairs={{0,4},{4,8},{8,12},{12,0},{1,5},{5,9},{9,13},{13,1},{2,6},{6,10},{... | collective-permute-start | bytes 786440 | tf_op jit(solution)/shard_map/ppermute | solution.py:243
  15.2 0.9 %copy-start.3 = (bf16[1024,128]{1,0:T(8,128)(2,1)S(1)}, bf16[1024,128]{1,0:T(8,128)(2,1)}, u32[]{:S(2)}) copy-start(bf16[1024,128]{1,0:T(8,128)(2,1)} %refs_2_.1) | copy-start | bytes 786436
  16.1 0.7 %copy-start.4 = (s32[8,8]{1,0:T(8,128)S(1)}, s32[8,8]{1,0:T(8,128)}, u32[]{:S(2)}) copy-start(s32[8,8]{1,0:T(8,128)} %refs_0_.1) | copy-start | bytes 772
  16.8 0.7 %copy-start.5 = (s32[8,8]{1,0:T(8,128)S(1)}, s32[8,8]{1,0:T(8,128)}, u32[]{:S(2)}) copy-start(s32[8,8]{1,0:T(8,128)} %refs_1_.2) | copy-start | bytes 772
  22.1 4.1 %collective-permute-start.10 = (bf16[512,256]{1,0:T(8,128)(2,1)S(1)}, bf16[512,256]{1,0:T(8,128)(2,1)S(1)}, u32[]{:S(2)}, u32[]{:S(2)}) collective-permute-start(bf16[512,256]{1,0:T(8,128)(2,1)S(1)} %get-tuple-element.20.refs_6_), channel_id=1, source_target_pairs={{0,1},{1,0},{2,3},{3,2},{4,5},{5,4},{6,7},{7,6},{8,9},{9,8},{10,11... | collective-permute-start | bytes 786440 | tf_op jit(solution)/shard_map/ppermute | solution.py:274
  22.2 4.1 %collective-permute-start.7 = (bf16[512,256]{1,0:T(8,128)(2,1)S(1)}, bf16[512,256]{1,0:T(8,128)(2,1)S(1)}, u32[]{:S(2)}, u32[]{:S(2)}) collective-permute-start(bf16[512,256]{1,0:T(8,128)(2,1)S(1)} %get-tuple-element.17.refs_3_), channel_id=1, source_target_pairs={{0,1},{1,0},{2,3},{3,2},{4,5},{5,4},{6,7},{7,6},{8,9},{9,8},{10,11... | collective-permute-start | bytes 786440 | tf_op jit(solution)/shard_map/ppermute | solution.py:274
  22.7 3.6 %collective-permute-start.8 = (bf16[512,256]{1,0:T(8,128)(2,1)S(1)}, bf16[512,256]{1,0:T(8,128)(2,1)S(1)}, u32[]{:S(2)}, u32[]{:S(2)}) collective-permute-start(bf16[512,256]{1,0:T(8,128)(2,1)S(1)} %get-tuple-element.18.refs_4_), channel_id=1, source_target_pairs={{0,1},{1,0},{2,3},{3,2},{4,5},{5,4},{6,7},{7,6},{8,9},{9,8},{10,11... | collective-permute-start | bytes 786440 | tf_op jit(solution)/shard_map/ppermute | solution.py:274
  22.7 3.5 %collective-permute-start.9 = (bf16[512,256]{1,0:T(8,128)(2,1)S(1)}, bf16[512,256]{1,0:T(8,128)(2,1)S(1)}, u32[]{:S(2)}, u32[]{:S(2)}) collective-permute-start(bf16[512,256]{1,0:T(8,128)(2,1)S(1)} %get-tuple-element.19.refs_5_), channel_id=1, source_target_pairs={{0,1},{1,0},{2,3},{3,2},{4,5},{5,4},{6,7},{7,6},{8,9},{9,8},{10,11... | collective-permute-start | bytes 786440 | tf_op jit(solution)/shard_map/ppermute | solution.py:274
  24.7 12.5 %collective-permute-start.2 = (bf16[512,512]{1,0:T(8,128)(2,1)S(1)}, bf16[512,512]{1,0:T(8,128)(2,1)S(1)}, u32[]{:S(2)}, u32[]{:S(2)}) collective-permute-start(bf16[512,512]{1,0:T(8,128)(2,1)S(1)} %pack.5.refs_0_.refs_2_), channel_id=1, source_target_pairs={{0,2},{1,3},{2,0},{3,1},{4,6},{5,7},{6,4},{7,5},{8,10},{9,11},{10,... | collective-permute-start | bytes 1572872 | tf_op jit(solution)/shard_map/ppermute | solution.py:249
  27.7 21.4 %copy-start.2 = (bf16[1024,512]{1,0:T(8,128)(2,1)S(1)}, bf16[1024,512]{1,0:T(8,128)(2,1)}, u32[]{:S(2)}) copy-start(bf16[1024,512]{1,0:T(8,128)(2,1)} %refs_1_.3) | copy-start | bytes 3145732
  27.7 7.0 %collective-permute-start.11 = (bf16[256,512]{1,0:T(8,128)(2,1)S(1)}, bf16[256,512]{1,0:T(8,128)(2,1)S(1)}, u32[]{:S(2)}, u32[]{:S(2)}) collective-permute-start(bf16[256,512]{1,0:T(8,128)(2,1)S(1)} %first_product.1.refs_0_.refs_1_), channel_id=1, source_target_pairs={{0,16},{16,0},{1,17},{17,1},{2,18},{18,2},{3,19},{19,3},{4,20},{20... | collective-permute-start | bytes 786440 | tf_op jit(solution)/shard_map/ppermute | solution.py:287
  38.2 10.8 %collective-permute-start.12 = (bf16[1024,512]{1,0:T(8,128)(2,1)}, bf16[1024,512]{1,0:T(8,128)(2,1)}, u32[]{:S(2)}, u32[]{:S(2)}) collective-permute-start(bf16[1024,512]{1,0:T(8,128)(2,1)} %pack.7), channel_id=1, source_target_pairs={{0,1},{1,0},{2,3},{3,2},{4,5},{5,4},{6,7},{7,6},{8,9},{9,8},{10,11... | collective-permute-start | bytes 3145736 | tf_op jit(solution)/shard_map/ppermute | solution.py:301
  38.3 8.8 %collective-permute-start.13 = (bf16[256,512]{1,0:T(8,128)(2,1)S(1)}, bf16[256,512]{1,0:T(8,128)(2,1)S(1)}, u32[]{:S(2)}, u32[]{:S(2)}) collective-permute-start(bf16[256,512]{1,0:T(8,128)(2,1)S(1)} %pack.8.refs_0_.refs_5_), channel_id=1, source_target_pairs={{0,2},{1,3},{2,0},{3,1},{4,6},{5,7},{6,4},{7,5},{8,10},{9,11},{10,... | collective-permute-start | bytes 786440 | tf_op jit(solution)/shard_map/ppermute | solution.py:249
  38.8 21.4 %all-to-all-start = ((bf16[4,128,512]{2,1,0:T(8,128)(2,1)}), bf16[4,128,512]{2,1,0:T(8,128)(2,1)S(1)}, u32[]{:S(2)}, u32[]{:S(2)}) async-start(bf16[4,128,512]{2,1,0:T(8,128)(2,1)} %bitcast.2), calls=%async_computation | async-start | bytes 1048576 | tf_op jit(solution)/shard_map/all_to_all | solution.py:295
  47.1 2.0 %collective-permute-start.14 = (bf16[512,512]{1,0:T(8,128)(2,1)S(1)}, bf16[512,512]{1,0:T(8,128)(2,1)S(1)}, u32[]{:S(2)}, u32[]{:S(2)}) collective-permute-start(bf16[512,512]{1,0:T(8,128)(2,1)S(1)} %pack.9), channel_id=1, source_target_pairs={{0,1},{1,0},{2,3},{3,2},{4,5},{5,4},{6,7},{7,6},{8,9},{9,8},{10,11... | collective-permute-start | bytes 1572872 | tf_op jit(solution)/shard_map/ppermute | solution.py:301
  52.6 2.0 %copy-start = (bf16[1024,2048]{1,0:T(8,128)(2,1)}, bf16[1024,2048]{1,0:T(8,128)(2,1)S(1)}, u32[]{:S(2)}) copy-start(bf16[1024,2048]{1,0:T(8,128)(2,1)S(1)} %layers.1.refs_0_) | copy-start | bytes 12582916
  60.3 2.2 %copy-start.1 = (bf16[1024,2048]{1,0:T(8,128)(2,1)S(1)}, bf16[1024,2048]{1,0:T(8,128)(2,1)}, u32[]{:S(2)}) copy-start(bf16[1024,2048]{1,0:T(8,128)(2,1)} %copy-done) | copy-start | bytes 12582916

commit v13 on v11

--- a/solution.py
+++ b/solution.py
@@ -243,15 +243,16 @@
     out[...] = total
 
 
-def last_kernel(sizes, part, offsets, zp, z_full, before, *refs):
-    cols, q, per = sizes.cols, sizes.quarter, sizes.per
-    messages, piece, strips = refs[:cols], refs[cols], refs[cols + 1 : -3]
+def last_kernel(sizes, part, dl, zp, z_full, before, *refs):
+    cols, q = sizes.cols, sizes.quarter
+    messages, strips = refs[:cols], refs[cols:-3]
     out, acc, xm = refs[-3:]
     r, c, l = place()
     total = before[...]
     for d in part:
         total += turned_dot(z_full[:, columns_of(c ^ d, sizes)], messages[d][...])
     acc[...] = total
+    out[...] = total.astype(out.dtype)
     cc = slot_column(c, cols - 1, cols)
     for d in range(cols):
 
@@ -259,12 +260,11 @@
         def _(d=d):
             xm[...] = messages[d][...]
 
-    for n, dl in enumerate(offsets):
-        for half in range(per):
-            rows = pl.ds(strip_start(l ^ dl, half, sizes), q)
-            strip = strips[half][...] if n else piece[half * q : (half + 1) * q, :]
-            acc[rows, :] += turned_dot(mask_strip(zp, r, l ^ dl, half, cc, strip, sizes), xm[...])
-    out[...] = acc[...].astype(out.dtype)
+    masked = [mask_strip(zp, r, l ^ dl, n, cc, strip[...], sizes) for n, strip in enumerate(strips)]
+    added = turned_dot(jnp.concatenate(masked, axis=0), xm[...])
+    for n in range(len(strips)):
+        rows = pl.ds(strip_start(l ^ dl, n, sizes), q)
+        out[rows, :] = (acc[rows, :] + added[n * q : (n + 1) * q, :]).astype(out.dtype)
 
 
 def local(sizes, hamiltonian, inv_root, h_pattern, z_pattern):
@@ -304,8 +304,6 @@
         perm = flip(rows if axis == "row" else layers, bit)
         for piece, (dr, dl) in list(zip(h_pieces, h_table)):
             h_table.append((dr ^ bit, dl) if axis == "row" else (dr, dl ^ bit))
-            if axis == "row" and not dr and not dl:
-                piece = fetched
             if dl and axis == 'row':
                 piece = pack([piece], [slots[1]])
             h_pieces.append(lax.ppermute(piece, axis, perm))
@@ -351,12 +349,13 @@
     mine = pack([slots[s] for s in group])
     other = cross(mine)
     both = lax.ppermute(pack([mine, other], [outgoing[0]]), "layer", flip(layers, low))
-    held, z_table = [inv_root, mine, other, both, last, last_low], {}
+    held, z_table = [inv_root, mine, other, both, last, last_low, last_top], {}
     for n, s in enumerate(group):
         row = n * height
         z_table[0, s], z_table[top, s], z_table[low, s] = (1, row), (2, row), (3, row)
         z_table[low ^ top, s] = (3, len(group) * height + row)
-    z_table[0, cols - 1], z_table[low, cols - 1] = (4, 0), (5, 0)
+    for n, dl in enumerate((0, low, top)):
+        z_table[dl, cols - 1] = (4 + n, 0)
     parts = run(split_kernel, "split", [strip_shape] * per, [last_top])
     parts = [lax.ppermute(part, "layer", flip(layers, low)) for part in parts]
     z_full = run(
@@ -374,10 +373,10 @@
         [z_full, *[messages[d] for d in early]],
     )[0]
     return run(
-        functools.partial(last_kernel, sizes, late, (top, low ^ top)),
+        functools.partial(last_kernel, sizes, late, low ^ top),
         "last_product",
         [shape(*hamiltonian.shape)],
-        [z_full, total, *messages, last_top, *parts],
+        [z_full, total, *messages, *parts],
         smem=[z_pattern],
         scratch=[pltpu.VMEM(hamiltonian.shape, f32), pltpu.VMEM((q, cols_here), jnp.bfloat16)],
     )[0]

time: 57.3 us -> 57 us (level)
  waiting for transfers between devices: 25.6 us -> 23.8 us
  starting transfers between devices: 19.2 us -> 20.9 us
    ppermute x2, waiting for transfers between devices: 0.13 us -> 5.44 us  [local(): lax.ppermute(right, 'col', [(i, (i + 1) % cols) for i in range(cols)])]
    ppermute x3, waiting for transfers between devices: 5.81 us -> 2.04 us  [local(): h_pieces.append(lax.ppermute(piece, axis, perm))]
    ppermute x1, waiting for transfers between devices: 3.6 us -> 0.01 us  [local(): left = lax.ppermute(left, 'col', [(i, (i - 1) % cols) for i in range(cols)])]
    ppermute x3, waiting for transfers between devices: 2.1 us -> 5.65 us  [local(): lax.ppermute(outgoing[d], 'col', flip(cols, d))]
    ppermute x2, waiting for transfers between devices: 5.82 us -> 2.55 us  [cross(): return lax.ppermute(piece, 'layer', flip(layers, layer_bits[0]))]
    ppermute x3, starting transfers between devices: 4.39 us -> 6.19 us  [local(): lax.ppermute(outgoing[d], 'col', flip(cols, d))]
    ppermute x4, waiting for transfers between devices: 1.01 us -> 0.01 us  [local(): lax.ppermute(block, 'layer', flip(layers, low))]
    ppermute x2, starting transfers between devices: 1.14 us -> 2.09 us  [cross(): return lax.ppermute(piece, 'layer', flip(layers, layer_bits[0]))]
  transfers between devices with their start and end apart: 20 -> 20, of which waited for: 11 -> 8; matrix products, arithmetic and copies ran while one was open for 0% -> 0% of each run, Pallas kernels for 11% -> 11%
where the time goes in v13:
time: 57 us; the launch traced here: 56.8 us
  waiting for transfers between devices  23.8 us (42%)
  starting transfers between devices  20.9 us (37%)
  Pallas kernels  8.59 us (15%)
  local copies, waits for them, and re-layouts  3.29 us (6%)
    pallas_call x12, Pallas kernels, run(): pl.pallas_call(body, out_shape=list(outs), in_specs=[pl.BlockSpec(memory_...  8.59 us
    ppermute x1, waiting for transfers between devices, local(): gathered[dr ^ bit] = lax.ppermute(piece, 'row', flip(rows, bit))  7.2 us
    ppermute x3, starting transfers between devices, local(): lax.ppermute(outgoing[d], 'col', flip(cols, d))  6.19 us
    ppermute x3, waiting for transfers between devices, local(): lax.ppermute(outgoing[d], 'col', flip(cols, d))  5.65 us
    ppermute x2, waiting for transfers between devices, local(): lax.ppermute(right, 'col', [(i, (i + 1) % cols) for i in range(cols)])  5.44 us
    ppermute x3, starting transfers between devices, local(): h_pieces.append(lax.ppermute(piece, axis, perm))  4.81 us
    ppermute x2, starting transfers between devices, local(): lax.ppermute(right, 'col', [(i, (i + 1) % cols) for i in range(cols)])  3.17 us
    ppermute x2, waiting for transfers between devices, cross(): return lax.ppermute(piece, 'layer', flip(layers, layer_bits[0]))  2.55 us
  transfers between devices with their start and end apart: 20, of which 8 were waited for; matrix products, arithmetic and copies ran while one was open for 0% of the time, Pallas kernels for 11%

profile of v13, /device:TPU:0, one launch (start us, length us, event | category | flops | bytes accessed | tf_op | source)
XLA Modules:
  0.0 56.8 jit_solution(4015569460446883769)
XLA Ops:
  0.0 1.0 %constant_dynamic-slice_fusion = bf16[2,1,128,512]{3,2,1,0:T(8,128)(2,1)S(1)} fusion(bf16[2,4,128,512]{3,2,1,0:T(8,128)(2,1)} %bitcast.4, s32[]{:T(128)S(6)} %select_n.4), kind=kLoop, calls=%fused_computation | loop fusion | bytes 524292 | tf_op jit(solution)/shard_map/jit(dynamic_index_in_dim)/dynamic_slice | solution.py:281
  1.0 3.1 %collective-permute-start = (bf16[256,512]{1,0:T(8,128)(2,1)S(1)}, bf16[256,512]{1,0:T(8,128)(2,1)S(1)}, u32[]{:S(2)}, u32[]{:S(2)}) collective-permute-start(bf16[256,512]{1,0:T(8,128)(2,1)S(1)} %bitcast.5), channel_id=1, source_target_pairs={{0,4},{4,8},{8,12},{12,0},{1,5},{5,9},{9,13},{13,1},{2,6},{6,10},{... | collective-permute-start | bytes 786440 | tf_op jit(solution)/shard_map/ppermute | solution.py:286
  4.0 1.5 %collective-permute-start.3 = (bf16[1024,128]{1,0:T(8,128)(2,1)}, bf16[1024,128]{1,0:T(8,128)(2,1)S(1)}, u32[]{:S(2)}, u32[]{:S(2)}) collective-permute-start(bf16[1024,128]{1,0:T(8,128)(2,1)} %refs_2_.1), channel_id=1, source_target_pairs={{0,2},{1,3},{2,0},{3,1},{4,6},{5,7},{6,4},{7,5},{8,10},{9,11},{10,... | collective-permute-start | bytes 786440 | tf_op jit(solution)/shard_map/ppermute | solution.py:309
  5.6 2.2 %collective-permute-start.1 = (bf16[256,512]{1,0:T(8,128)(2,1)S(1)}, bf16[256,512]{1,0:T(8,128)(2,1)S(1)}, u32[]{:S(2)}, u32[]{:S(2)}) collective-permute-start(bf16[256,512]{1,0:T(8,128)(2,1)S(1)} %bitcast.6), channel_id=1, source_target_pairs={{0,12},{4,0},{8,4},{12,8},{1,13},{5,1},{9,5},{13,9},{2,14},{6,2},{... | collective-permute-start | bytes 786440 | tf_op jit(solution)/shard_map/ppermute | solution.py:288
  7.8 1.5 %collective-permute-start.4 = (bf16[1024,128]{1,0:T(8,128)(2,1)}, bf16[1024,128]{1,0:T(8,128)(2,1)S(1)}, u32[]{:S(2)}, u32[]{:S(2)}) collective-permute-start(bf16[1024,128]{1,0:T(8,128)(2,1)} %refs_2_.1), channel_id=1, source_target_pairs={{0,16},{16,0},{1,17},{17,1},{2,18},{18,2},{3,19},{19,3},{4,20},{20... | collective-permute-start | bytes 786440 | tf_op jit(solution)/shard_map/ppermute | solution.py:309
  9.3 3.9 %collective-permute-done.refs_0_.refs_1_.refs_7_ = bf16[256,512]{1,0:T(8,128)(2,1)S(1)} collective-permute-done((bf16[256,512]{1,0:T(8,128)(2,1)S(1)}, bf16[256,512]{1,0:T(8,128)(2,1)S(1)}, u32[]{:S(2)}, u32[]{:S(2)}) %collective-permute-start) | collective-permute-done | bytes 262176 | tf_op jit(solution)/shard_map/ppermute | solution.py:286
  13.3 1.8 %collective-permute-start.5 = (bf16[1024,128]{1,0:T(8,128)(2,1)S(1)}, bf16[1024,128]{1,0:T(8,128)(2,1)S(1)}, u32[]{:S(2)}, u32[]{:S(2)}) collective-permute-start(bf16[1024,128]{1,0:T(8,128)(2,1)S(1)} %pack.5), channel_id=1, source_target_pairs={{0,16},{16,0},{1,17},{17,1},{2,18},{18,2},{3,19},{19,3},{4,20},{20... | collective-permute-start | bytes 786440 | tf_op jit(solution)/shard_map/ppermute | solution.py:309
  15.2 0.9 %copy-done.1 = bf16[1024,128]{1,0:T(8,128)(2,1)S(1)} copy-done((bf16[1024,128]{1,0:T(8,128)(2,1)S(1)}, bf16[1024,128]{1,0:T(8,128)(2,1)}, u32[]{:S(2)}) %copy-start.1) | copy-done | bytes 262168
  16.1 0.7 %copy-done.2 = s32[8,8]{1,0:T(8,128)S(1)} copy-done((s32[8,8]{1,0:T(8,128)S(1)}, s32[8,8]{1,0:T(8,128)}, u32[]{:S(2)}) %copy-start.2) | copy-done | bytes 280
  17.5 1.4 %fetch.1 = (s32[8,8]{1,0:T(8,128)S(1)}, s32[8,8]{1,0:T(8,128)S(1)}, bf16[1024,128]{1,0:T(8,128)(2,1)S(1)}) custom-call(s32[8,8]{1,0:T(8,128)S(1)} %copy-done.2, s32[8,8]{1,0:T(8,128)S(1)} %copy-done.3, bf16[1024,128]{1,0:T(8,128)(2,1)S(1)} %copy-done.1), custom_call_target="tpu_custom_call" | custom-call | bytes 524800 | tf_op jit(solution)/shard_map/fetch/pallas_call | solution.py:51
  18.9 2.0 %collective-permute-done.5.refs_5_ = bf16[1024,128]{1,0:T(8,128)(2,1)S(1)} collective-permute-done((bf16[1024,128]{1,0:T(8,128)(2,1)S(1)}, bf16[1024,128]{1,0:T(8,128)(2,1)S(1)}, u32[]{:S(2)}, u32[]{:S(2)}) %collective-permute-start.5) | collective-permute-done | bytes 262176 | tf_op jit(solution)/shard_map/ppermute | solution.py:309
  21.0 1.1 %bring.1 = (bf16[256,2048]{1,0:T(8,128)(2,1)S(1)}, bf16[512,256]{1,0:T(8,128)(2,1)S(1)}, bf16[512,256]{1,0:T(8,128)(2,1)S(1)}, bf16[512,256]{1,0:T(8,128)(2,1)S(1)}, bf16[512,256]{1,0:T(8,128)(2,1)S(1)}) custom-call(s32[8,8]{1,0:T(8,128)S(1)} %get-tuple-element.20.refs_0_, s32[8,8]{1,0:T(8,128)S(1)} %get-tuple-element.19.refs_1_.refs_0_, ...), custom_call_target="tpu_custom_call" | custom-call | bytes 3932160 | tf_op jit(solution)/shard_map/bring/pallas_call | solution.py:51
  23.2 1.5 %collective-permute-done.6.refs_2_.refs_0_ = bf16[256,512]{1,0:T(8,128)(2,1)S(1)} collective-permute-done((bf16[256,512]{1,0:T(8,128)(2,1)S(1)}, bf16[256,512]{1,0:T(8,128)(2,1)S(1)}, u32[]{:S(2)}, u32[]{:S(2)}) %collective-permute-start.6) | collective-permute-done | bytes 262176 | tf_op jit(solution)/shard_map/ppermute | solution.py:286
  24.7 1.5 %collective-permute-start.2 = (bf16[512,512]{1,0:T(8,128)(2,1)S(1)}, bf16[512,512]{1,0:T(8,128)(2,1)S(1)}, u32[]{:S(2)}, u32[]{:S(2)}) collective-permute-start(bf16[512,512]{1,0:T(8,128)(2,1)S(1)} %pack.4.refs_0_.refs_2_), channel_id=1, source_target_pairs={{0,2},{1,3},{2,0},{3,1},{4,6},{5,7},{6,4},{7,5},{8,10},{9,11},{10,... | collective-permute-start | bytes 1572872 | tf_op jit(solution)/shard_map/ppermute | solution.py:292
  26.2 1.4 %first_product.1.refs_1_.refs_0_ = bf16[256,512]{1,0:T(8,128)(2,1)S(1)} custom-call(s32[8,8]{1,0:T(8,128)S(1)} %get-tuple-element.19.refs_1_.refs_0_, bf16[256,2048]{1,0:T(8,128)(2,1)S(1)} %get-tuple-element.22.refs_1_, bf16[256,512]{1,0:T(8,128)(2,1)S(1)} %collective-permute-done.6.refs_2_.refs_0_, bf16[512,256]{1,0:T(8,128)(2,1)S(1)} %get-tuple-element.23.refs_3_, ...), custom_call_target="tpu_custom_call" | custom-call | bytes 4718592 | tf_op jit(solution)/shard_map/first_product/pallas_call | solution.py:51
  28.4 0.9 %collective-permute-done.12.refs_2_.refs_6_ = bf16[256,512]{1,0:T(8,128)(2,1)S(1)} collective-permute-done((bf16[256,512]{1,0:T(8,128)(2,1)S(1)}, bf16[256,512]{1,0:T(8,128)(2,1)S(1)}, u32[]{:S(2)}, u32[]{:S(2)}) %collective-permute-start.12) | collective-permute-done | bytes 262176 | tf_op jit(solution)/shard_map/ppermute | solution.py:336
  29.3 7.2 %collective-permute-done.11.refs_1_ = bf16[256,512]{1,0:T(8,128)(2,1)S(1)} collective-permute-done((bf16[256,512]{1,0:T(8,128)(2,1)S(1)}, bf16[256,512]{1,0:T(8,128)(2,1)S(1)}, u32[]{:S(2)}, u32[]{:S(2)}) %collective-permute-start.11) | collective-permute-done | bytes 262176 | tf_op jit(solution)/shard_map/ppermute | solution.py:330
  37.9 3.6 %collective-permute-start.15 = (bf16[128,512]{1,0:T(8,128)(2,1)S(1)}, bf16[128,512]{1,0:T(8,128)(2,1)S(1)}, u32[]{:S(2)}, u32[]{:S(2)}) collective-permute-start(bf16[128,512]{1,0:T(8,128)(2,1)S(1)} %get-tuple-element.28), channel_id=1, source_target_pairs={{0,4},{4,0},{8,12},{12,8},{1,5},{5,1},{9,13},{13,9},{2,6},{6,2},{1... | collective-permute-start | bytes 393224 | tf_op jit(solution)/shard_map/ppermute | solution.py:346
  41.5 2.2 %collective-permute-start.16 = (bf16[128,512]{1,0:T(8,128)(2,1)S(1)}, bf16[128,512]{1,0:T(8,128)(2,1)S(1)}, u32[]{:S(2)}, u32[]{:S(2)}) collective-permute-start(bf16[128,512]{1,0:T(8,128)(2,1)S(1)} %get-tuple-element.29), channel_id=1, source_target_pairs={{0,8},{4,12},{8,0},{12,4},{1,9},{5,13},{9,1},{13,5},{2,10},{6,14},... | collective-permute-start | bytes 393224 | tf_op jit(solution)/shard_map/ppermute | solution.py:346
  44.1 2.0 %collective-permute-done.14.refs_7_.refs_0_ = bf16[256,512]{1,0:T(8,128)(2,1)S(1)} collective-permute-done((bf16[256,512]{1,0:T(8,128)(2,1)S(1)}, bf16[256,512]{1,0:T(8,128)(2,1)S(1)}, u32[]{:S(2)}, u32[]{:S(2)}) %collective-permute-start.14) | collective-permute-done | bytes 262176 | tf_op jit(solution)/shard_map/ppermute | solution.py:292
  46.7 1.4 %layers.1.refs_0_.refs_1_ = bf16[1024,2048]{1,0:T(8,128)(2,1)S(1)} custom-call(s32[8,8]{1,0:T(8,128)S(1)} %get-tuple-element.19.refs_1_.refs_0_, bf16[1024,512]{1,0:T(8,128)(2,1)S(1)} %copy-done, bf16[512,512]{1,0:T(8,128)(2,1)S(1)} %pack.4.refs_0_.refs_2_, bf16[512,512]{1,0:T(8,128)(2,1)S(1)} %collective-permute-done.2.refs_1_.refs_3_, ...), custom_call_target="tpu_custom_call" | custom-call | bytes 8126464 | tf_op jit(solution)/shard_map/layers/pallas_call | solution.py:51
  48.0 0.7 %second_product.1.refs_2_ = f32[1024,128]{1,0:T(8,128)S(1)} custom-call(bf16[1024,2048]{1,0:T(8,128)(2,1)S(1)} %layers.1.refs_0_.refs_1_, bf16[128,512]{1,0:T(8,128)(2,1)S(1)} %get-tuple-element.27.refs_2_.refs_1_.refs_3_, bf16[128,512]{1,0:T(8,128)(2,1)S(1)} %collective-permute-done.15.refs_2_.refs_4_), custom_call_target="tpu_custom_call" | custom-call | bytes 4980736 | tf_op jit(solution)/shard_map/second_product/pallas_call | solution.py:51
  48.8 5.6 %collective-permute-done.16.refs_5_ = bf16[128,512]{1,0:T(8,128)(2,1)S(1)} collective-permute-done((bf16[128,512]{1,0:T(8,128)(2,1)S(1)}, bf16[128,512]{1,0:T(8,128)(2,1)S(1)}, u32[]{:S(2)}, u32[]{:S(2)}) %collective-permute-start.16) | collective-permute-done | bytes 131104 | tf_op jit(solution)/shard_map/ppermute | solution.py:346
  54.4 2.4 %last_product.1 = bf16[1024,128]{1,0:T(8,128)(2,1)} custom-call(s32[8,8]{1,0:T(8,128)S(1)} %get-tuple-element.19.refs_1_.refs_0_, bf16[1024,2048]{1,0:T(8,128)(2,1)S(1)} %layers.1.refs_0_.refs_1_, f32[1024,128]{1,0:T(8,128)S(1)} %second_product.1.refs_2_, bf16[128,512]{1,0:T(8,128)(2,1)S(1)} %get-tuple-element.27.refs_2_.refs_1_.refs_3_, ...), custom_call_target="tpu_custom_call" | custom-call | bytes 6422528 | tf_op jit(solution)/shard_map/last_product/pallas_call | solution.py:51
  (37 shorter events, 5.0 us)
Async XLA Ops:
  1.0 12.3 %collective-permute-start = (bf16[256,512]{1,0:T(8,128)(2,1)S(1)}, bf16[256,512]{1,0:T(8,128)(2,1)S(1)}, u32[]{:S(2)}, u32[]{:S(2)}) collective-permute-start(bf16[256,512]{1,0:T(8,128)(2,1)S(1)} %bitcast.5), channel_id=1, source_target_pairs={{0,4},{4,8},{8,12},{12,0},{1,5},{5,9},{9,13},{13,1},{2,6},{6,10},{... | collective-permute-start | bytes 786440 | tf_op jit(solution)/shard_map/ppermute | solution.py:286
  4.0 9.2 %collective-permute-start.3 = (bf16[1024,128]{1,0:T(8,128)(2,1)}, bf16[1024,128]{1,0:T(8,128)(2,1)S(1)}, u32[]{:S(2)}, u32[]{:S(2)}) collective-permute-start(bf16[1024,128]{1,0:T(8,128)(2,1)} %refs_2_.1), channel_id=1, source_target_pairs={{0,2},{1,3},{2,0},{3,1},{4,6},{5,7},{6,4},{7,5},{8,10},{9,11},{10,... | collective-permute-start | bytes 786440 | tf_op jit(solution)/shard_map/ppermute | solution.py:309
  5.6 13.4 %collective-permute-start.1 = (bf16[256,512]{1,0:T(8,128)(2,1)S(1)}, bf16[256,512]{1,0:T(8,128)(2,1)S(1)}, u32[]{:S(2)}, u32[]{:S(2)}) collective-permute-start(bf16[256,512]{1,0:T(8,128)(2,1)S(1)} %bitcast.6), channel_id=1, source_target_pairs={{0,12},{4,0},{8,4},{12,8},{1,13},{5,1},{9,5},{13,9},{2,14},{6,2},{... | collective-permute-start | bytes 786440 | tf_op jit(solution)/shard_map/ppermute | solution.py:288
  7.8 11.1 %collective-permute-start.4 = (bf16[1024,128]{1,0:T(8,128)(2,1)}, bf16[1024,128]{1,0:T(8,128)(2,1)S(1)}, u32[]{:S(2)}, u32[]{:S(2)}) collective-permute-start(bf16[1024,128]{1,0:T(8,128)(2,1)} %refs_2_.1), channel_id=1, source_target_pairs={{0,16},{16,0},{1,17},{17,1},{2,18},{18,2},{3,19},{19,3},{4,20},{20... | collective-permute-start | bytes 786440 | tf_op jit(solution)/shard_map/ppermute | solution.py:309
  13.3 7.7 %collective-permute-start.5 = (bf16[1024,128]{1,0:T(8,128)(2,1)S(1)}, bf16[1024,128]{1,0:T(8,128)(2,1)S(1)}, u32[]{:S(2)}, u32[]{:S(2)}) collective-permute-start(bf16[1024,128]{1,0:T(8,128)(2,1)S(1)} %pack.5), channel_id=1, source_target_pairs={{0,16},{16,0},{1,17},{17,1},{2,18},{18,2},{3,19},{19,3},{4,20},{20... | collective-permute-start | bytes 786440 | tf_op jit(solution)/shard_map/ppermute | solution.py:309
  15.1 9.6 %collective-permute-start.6 = (bf16[256,512]{1,0:T(8,128)(2,1)S(1)}, bf16[256,512]{1,0:T(8,128)(2,1)S(1)}, u32[]{:S(2)}, u32[]{:S(2)}) collective-permute-start(bf16[256,512]{1,0:T(8,128)(2,1)S(1)} %collective-permute-done.refs_0_.refs_1_.refs_7_), channel_id=1, source_target_pairs={{0,4},{4,8},{8,12},{12,0},{1,5},{5,9},{9,13},{13,1},{2,6},{6,10},{... | collective-permute-start | bytes 786440 | tf_op jit(solution)/shard_map/ppermute | solution.py:286
  15.2 0.9 %copy-start.1 = (bf16[1024,128]{1,0:T(8,128)(2,1)S(1)}, bf16[1024,128]{1,0:T(8,128)(2,1)}, u32[]{:S(2)}) copy-start(bf16[1024,128]{1,0:T(8,128)(2,1)} %refs_2_.1) | copy-start | bytes 786436
  16.1 0.7 %copy-start.2 = (s32[8,8]{1,0:T(8,128)S(1)}, s32[8,8]{1,0:T(8,128)}, u32[]{:S(2)}) copy-start(s32[8,8]{1,0:T(8,128)} %refs_0_.1) | copy-start | bytes 772
  16.8 0.7 %copy-start.3 = (s32[8,8]{1,0:T(8,128)S(1)}, s32[8,8]{1,0:T(8,128)}, u32[]{:S(2)}) copy-start(s32[8,8]{1,0:T(8,128)} %refs_1_.2) | copy-start | bytes 772
  22.1 4.1 %collective-permute-start.10 = (bf16[512,256]{1,0:T(8,128)(2,1)S(1)}, bf16[512,256]{1,0:T(8,128)(2,1)S(1)}, u32[]{:S(2)}, u32[]{:S(2)}) collective-permute-start(bf16[512,256]{1,0:T(8,128)(2,1)S(1)} %get-tuple-element.26.refs_6_), channel_id=1, source_target_pairs={{0,1},{1,0},{2,3},{3,2},{4,5},{5,4},{6,7},{7,6},{8,9},{9,8},{10,11... | collective-permute-start | bytes 786440 | tf_op jit(solution)/shard_map/ppermute | solution.py:317
  22.2 4.1 %collective-permute-start.7 = (bf16[512,256]{1,0:T(8,128)(2,1)S(1)}, bf16[512,256]{1,0:T(8,128)(2,1)S(1)}, u32[]{:S(2)}, u32[]{:S(2)}) collective-permute-start(bf16[512,256]{1,0:T(8,128)(2,1)S(1)} %get-tuple-element.23.refs_3_), channel_id=1, source_target_pairs={{0,1},{1,0},{2,3},{3,2},{4,5},{5,4},{6,7},{7,6},{8,9},{9,8},{10,11... | collective-permute-start | bytes 786440 | tf_op jit(solution)/shard_map/ppermute | solution.py:317
  22.7 3.6 %collective-permute-start.8 = (bf16[512,256]{1,0:T(8,128)(2,1)S(1)}, bf16[512,256]{1,0:T(8,128)(2,1)S(1)}, u32[]{:S(2)}, u32[]{:S(2)}) collective-permute-start(bf16[512,256]{1,0:T(8,128)(2,1)S(1)} %get-tuple-element.24.refs_4_), channel_id=1, source_target_pairs={{0,1},{1,0},{2,3},{3,2},{4,5},{5,4},{6,7},{7,6},{8,9},{9,8},{10,11... | collective-permute-start | bytes 786440 | tf_op jit(solution)/shard_map/ppermute | solution.py:317
  22.7 23.9 %copy-start = (bf16[1024,512]{1,0:T(8,128)(2,1)S(1)}, bf16[1024,512]{1,0:T(8,128)(2,1)}, u32[]{:S(2)}) copy-start(bf16[1024,512]{1,0:T(8,128)(2,1)} %refs_1_.3) | copy-start | bytes 3145732
  22.7 3.5 %collective-permute-start.9 = (bf16[512,256]{1,0:T(8,128)(2,1)S(1)}, bf16[512,256]{1,0:T(8,128)(2,1)S(1)}, u32[]{:S(2)}, u32[]{:S(2)}) collective-permute-start(bf16[512,256]{1,0:T(8,128)(2,1)S(1)} %get-tuple-element.25.refs_5_), channel_id=1, source_target_pairs={{0,1},{1,0},{2,3},{3,2},{4,5},{5,4},{6,7},{7,6},{8,9},{9,8},{10,11... | collective-permute-start | bytes 786440 | tf_op jit(solution)/shard_map/ppermute | solution.py:317
  24.7 12.5 %collective-permute-start.2 = (bf16[512,512]{1,0:T(8,128)(2,1)S(1)}, bf16[512,512]{1,0:T(8,128)(2,1)S(1)}, u32[]{:S(2)}, u32[]{:S(2)}) collective-permute-start(bf16[512,512]{1,0:T(8,128)(2,1)S(1)} %pack.4.refs_0_.refs_2_), channel_id=1, source_target_pairs={{0,2},{1,3},{2,0},{3,1},{4,6},{5,7},{6,4},{7,5},{8,10},{9,11},{10,... | collective-permute-start | bytes 1572872 | tf_op jit(solution)/shard_map/ppermute | solution.py:292
  27.7 1.6 %collective-permute-start.12 = (bf16[256,512]{1,0:T(8,128)(2,1)S(1)}, bf16[256,512]{1,0:T(8,128)(2,1)S(1)}, u32[]{:S(2)}, u32[]{:S(2)}) collective-permute-start(bf16[256,512]{1,0:T(8,128)(2,1)S(1)} %pack.6.refs_5_), channel_id=1, source_target_pairs={{0,1},{1,0},{2,3},{3,2},{4,5},{5,4},{6,7},{7,6},{8,9},{9,8},{10,11... | collective-permute-start | bytes 786440 | tf_op jit(solution)/shard_map/ppermute | solution.py:336
  27.8 8.7 %collective-permute-start.11 = (bf16[256,512]{1,0:T(8,128)(2,1)S(1)}, bf16[256,512]{1,0:T(8,128)(2,1)S(1)}, u32[]{:S(2)}, u32[]{:S(2)}) collective-permute-start(bf16[256,512]{1,0:T(8,128)(2,1)S(1)} %first_product.1.refs_1_.refs_0_), channel_id=1, source_target_pairs={{0,16},{16,0},{1,17},{17,1},{2,18},{18,2},{3,19},{19,3},{4,20},{20... | collective-permute-start | bytes 786440 | tf_op jit(solution)/shard_map/ppermute | solution.py:330
  37.3 8.9 %collective-permute-start.13 = (bf16[1024,512]{1,0:T(8,128)(2,1)S(1)}, bf16[1024,512]{1,0:T(8,128)(2,1)S(1)}, u32[]{:S(2)}, u32[]{:S(2)}) collective-permute-start(bf16[1024,512]{1,0:T(8,128)(2,1)S(1)} %pack.7), channel_id=1, source_target_pairs={{0,1},{1,0},{2,3},{3,2},{4,5},{5,4},{6,7},{7,6},{8,9},{9,8},{10,11... | collective-permute-start | bytes 3145736 | tf_op jit(solution)/shard_map/ppermute | solution.py:351
  37.3 8.7 %collective-permute-start.14 = (bf16[256,512]{1,0:T(8,128)(2,1)S(1)}, bf16[256,512]{1,0:T(8,128)(2,1)S(1)}, u32[]{:S(2)}, u32[]{:S(2)}) collective-permute-start(bf16[256,512]{1,0:T(8,128)(2,1)S(1)} %pack.6.refs_5_), channel_id=1, source_target_pairs={{0,2},{1,3},{2,0},{3,1},{4,6},{5,7},{6,4},{7,5},{8,10},{9,11},{10,... | collective-permute-start | bytes 786440 | tf_op jit(solution)/shard_map/ppermute | solution.py:292
  37.9 10.1 %collective-permute-start.15 = (bf16[128,512]{1,0:T(8,128)(2,1)S(1)}, bf16[128,512]{1,0:T(8,128)(2,1)S(1)}, u32[]{:S(2)}, u32[]{:S(2)}) collective-permute-start(bf16[128,512]{1,0:T(8,128)(2,1)S(1)} %get-tuple-element.28), channel_id=1, source_target_pairs={{0,4},{4,0},{8,12},{12,8},{1,5},{5,1},{9,13},{13,9},{2,6},{6,2},{1... | collective-permute-start | bytes 393224 | tf_op jit(solution)/shard_map/ppermute | solution.py:346
  41.5 12.9 %collective-permute-start.16 = (bf16[128,512]{1,0:T(8,128)(2,1)S(1)}, bf16[128,512]{1,0:T(8,128)(2,1)S(1)}, u32[]{:S(2)}, u32[]{:S(2)}) collective-permute-start(bf16[128,512]{1,0:T(8,128)(2,1)S(1)} %get-tuple-element.29), channel_id=1, source_target_pairs={{0,8},{4,12},{8,0},{12,4},{1,9},{5,13},{9,1},{13,5},{2,10},{6,14},... | collective-permute-start | bytes 393224 | tf_op jit(solution)/shard_map/ppermute | solution.py:346
  43.7 10.7 %collective-permute-start.17 = (bf16[128,512]{1,0:T(8,128)(2,1)S(1)}, bf16[128,512]{1,0:T(8,128)(2,1)S(1)}, u32[]{:S(2)}, u32[]{:S(2)}) collective-permute-start(bf16[128,512]{1,0:T(8,128)(2,1)S(1)} %get-tuple-element.30), channel_id=1, source_target_pairs={{0,12},{4,8},{8,4},{12,0},{1,13},{5,9},{9,5},{13,1},{2,14},{6,10},... | collective-permute-start | bytes 393224 | tf_op jit(solution)/shard_map/ppermute | solution.py:346
  46.1 8.3 %collective-permute-start.18 = (bf16[128,512]{1,0:T(8,128)(2,1)S(1)}, bf16[128,512]{1,0:T(8,128)(2,1)S(1)}, u32[]{:S(2)}, u32[]{:S(2)}) collective-permute-start(bf16[128,512]{1,0:T(8,128)(2,1)S(1)} %get-tuple-element.31), channel_id=1, source_target_pairs={{0,1},{1,0},{2,3},{3,2},{4,5},{5,4},{6,7},{7,6},{8,9},{9,8},{10,11... | collective-permute-start | bytes 393224 | tf_op jit(solution)/shard_map/ppermute | solution.py:360
  46.2 8.2 %collective-permute-start.19 = (bf16[128,512]{1,0:T(8,128)(2,1)S(1)}, bf16[128,512]{1,0:T(8,128)(2,1)S(1)}, u32[]{:S(2)}, u32[]{:S(2)}) collective-permute-start(bf16[128,512]{1,0:T(8,128)(2,1)S(1)} %get-tuple-element.32), channel_id=1, source_target_pairs={{0,1},{1,0},{2,3},{3,2},{4,5},{5,4},{6,7},{7,6},{8,9},{9,8},{10,11... | collective-permute-start | bytes 393224 | tf_op jit(solution)/shard_map/ppermute | solution.py:360

commit v14 on v13

--- a/solution.py
+++ b/solution.py
@@ -245,26 +245,20 @@
 
 def last_kernel(sizes, part, dl, zp, z_full, before, *refs):
     cols, q = sizes.cols, sizes.quarter
-    messages, strips = refs[:cols], refs[cols:-3]
-    out, acc, xm = refs[-3:]
-    r, c, l = place()
+    messages, strips = refs[: len(part)], refs[len(part) : -2]
+    out, zs = refs[-2:]
+    r, c, l = place()
+    far = c ^ (cols // 2)
+    zs[...] = z_full[:, columns_of(far, sizes)]
+    for n, strip in enumerate(strips):
+        zs[pl.ds(strip_start(l ^ dl, n, sizes), q), :] = mask_strip(
+            zp, r, l ^ dl, n, far, strip[...], sizes
+        )
     total = before[...]
-    for d in part:
-        total += turned_dot(z_full[:, columns_of(c ^ d, sizes)], messages[d][...])
-    acc[...] = total
+    for d, message in zip(part, messages):
+        piece = zs[...] if d == cols // 2 else z_full[:, columns_of(c ^ d, sizes)]
+        total += turned_dot(piece, message[...])
     out[...] = total.astype(out.dtype)
-    cc = slot_column(c, cols - 1, cols)
-    for d in range(cols):
-
-        @pl.when((c ^ d) == cc)
-        def _(d=d):
-            xm[...] = messages[d][...]
-
-    masked = [mask_strip(zp, r, l ^ dl, n, cc, strip[...], sizes) for n, strip in enumerate(strips)]
-    added = turned_dot(jnp.concatenate(masked, axis=0), xm[...])
-    for n in range(len(strips)):
-        rows = pl.ds(strip_start(l ^ dl, n, sizes), q)
-        out[rows, :] = (acc[rows, :] + added[n * q : (n + 1) * q, :]).astype(out.dtype)
 
 
 def local(sizes, hamiltonian, inv_root, h_pattern, z_pattern):
@@ -342,9 +336,10 @@
         after=[last_low],
         scratch=[pltpu.VMEM((cols * q, cols_here), jnp.bfloat16)],
     )
-    messages = [outgoing[0]] + [
-        lax.ppermute(outgoing[d], "col", flip(cols, d)) for d in range(1, cols)
+    messages = [
+        lax.ppermute(outgoing[d], "col", flip(cols, d)) for d in range(cols - 1, 0, -1)
     ]
+    messages = [outgoing[0]] + messages[::-1]
     group = range(1, cols - 1)
     mine = pack([slots[s] for s in group])
     other = cross(mine)
@@ -365,7 +360,8 @@
         held,
         smem=[z_pattern],
     )[0]
-    early, late = range(cols // 2), range(cols // 2, cols)
+    early = [0, *range(cols - 1, cols // 2, -1)]
+    late = range(cols // 2, 0, -1)
     total = run(
         functools.partial(second_kernel, sizes, early),
         "second_product",
@@ -376,9 +372,9 @@
         functools.partial(last_kernel, sizes, late, low ^ top),
         "last_product",
         [shape(*hamiltonian.shape)],
-        [z_full, total, *messages, *parts],
+        [z_full, total, *[messages[d] for d in late], *parts],
         smem=[z_pattern],
-        scratch=[pltpu.VMEM(hamiltonian.shape, f32), pltpu.VMEM((q, cols_here), jnp.bfloat16)],
+        scratch=[pltpu.VMEM((rows_here, cols_here), jnp.bfloat16)],
     )[0]
 
 

time: 57 us -> 57.3 us (level)
  waiting for transfers between devices: 23.8 us -> 24.7 us
where the time goes in v14:
time: 57.3 us; the launch traced here: 57 us
  waiting for transfers between devices  24.7 us (43%)
  starting transfers between devices  20.5 us (36%)
  Pallas kernels  8.32 us (15%)
  local copies, waits for them, and re-layouts  3.29 us (6%)
    pallas_call x12, Pallas kernels, run(): pl.pallas_call(body, out_shape=list(outs), in_specs=[pl.BlockSpec(memory_...  8.32 us
    ppermute x1, waiting for transfers between devices, local(): gathered[dr ^ bit] = lax.ppermute(piece, 'row', flip(rows, bit))  7.2 us
    ppermute x3, waiting for transfers between devices, local(): lax.ppermute(outgoing[d], 'col', flip(cols, d))  6.18 us
    ppermute x3, starting transfers between devices, local(): lax.ppermute(outgoing[d], 'col', flip(cols, d))  5.83 us
    ppermute x2, waiting for transfers between devices, local(): lax.ppermute(right, 'col', [(i, (i + 1) % cols) for i in range(cols)])  5.44 us
    ppermute x3, starting transfers between devices, local(): h_pieces.append(lax.ppermute(piece, axis, perm))  4.81 us
    ppermute x2, starting transfers between devices, local(): lax.ppermute(right, 'col', [(i, (i + 1) % cols) for i in range(cols)])  3.17 us
    ppermute x2, waiting for transfers between devices, cross(): return lax.ppermute(piece, 'layer', flip(layers, layer_bits[0]))  2.92 us
  transfers between devices with their start and end apart: 20, of which 8 were waited for; matrix products, arithmetic and copies ran while one was open for 0% of the time, Pallas kernels for 11%

profile of v14, /device:TPU:0, one launch (start us, length us, event | category | flops | bytes accessed | tf_op | source)
XLA Modules:
  0.0 57.0 jit_solution(13285579090133920603)
XLA Ops:
  0.0 1.0 %constant_dynamic-slice_fusion = bf16[2,1,128,512]{3,2,1,0:T(8,128)(2,1)S(1)} fusion(bf16[2,4,128,512]{3,2,1,0:T(8,128)(2,1)} %bitcast.4, s32[]{:T(128)S(6)} %select_n.4), kind=kLoop, calls=%fused_computation | loop fusion | bytes 524292 | tf_op jit(solution)/shard_map/jit(dynamic_index_in_dim)/dynamic_slice | solution.py:275
  1.0 3.1 %collective-permute-start = (bf16[256,512]{1,0:T(8,128)(2,1)S(1)}, bf16[256,512]{1,0:T(8,128)(2,1)S(1)}, u32[]{:S(2)}, u32[]{:S(2)}) collective-permute-start(bf16[256,512]{1,0:T(8,128)(2,1)S(1)} %bitcast.5), channel_id=1, source_target_pairs={{0,4},{4,8},{8,12},{12,0},{1,5},{5,9},{9,13},{13,1},{2,6},{6,10},{... | collective-permute-start | bytes 786440 | tf_op jit(solution)/shard_map/ppermute | solution.py:280
  4.0 1.5 %collective-permute-start.3 = (bf16[1024,128]{1,0:T(8,128)(2,1)}, bf16[1024,128]{1,0:T(8,128)(2,1)S(1)}, u32[]{:S(2)}, u32[]{:S(2)}) collective-permute-start(bf16[1024,128]{1,0:T(8,128)(2,1)} %refs_2_.1), channel_id=1, source_target_pairs={{0,2},{1,3},{2,0},{3,1},{4,6},{5,7},{6,4},{7,5},{8,10},{9,11},{10,... | collective-permute-start | bytes 786440 | tf_op jit(solution)/shard_map/ppermute | solution.py:303
  5.6 2.2 %collective-permute-start.1 = (bf16[256,512]{1,0:T(8,128)(2,1)S(1)}, bf16[256,512]{1,0:T(8,128)(2,1)S(1)}, u32[]{:S(2)}, u32[]{:S(2)}) collective-permute-start(bf16[256,512]{1,0:T(8,128)(2,1)S(1)} %bitcast.6), channel_id=1, source_target_pairs={{0,12},{4,0},{8,4},{12,8},{1,13},{5,1},{9,5},{13,9},{2,14},{6,2},{... | collective-permute-start | bytes 786440 | tf_op jit(solution)/shard_map/ppermute | solution.py:282
  7.8 1.5 %collective-permute-start.4 = (bf16[1024,128]{1,0:T(8,128)(2,1)}, bf16[1024,128]{1,0:T(8,128)(2,1)S(1)}, u32[]{:S(2)}, u32[]{:S(2)}) collective-permute-start(bf16[1024,128]{1,0:T(8,128)(2,1)} %refs_2_.1), channel_id=1, source_target_pairs={{0,16},{16,0},{1,17},{17,1},{2,18},{18,2},{3,19},{19,3},{4,20},{20... | collective-permute-start | bytes 786440 | tf_op jit(solution)/shard_map/ppermute | solution.py:303
  9.3 3.9 %collective-permute-done.refs_0_.refs_1_.refs_7_ = bf16[256,512]{1,0:T(8,128)(2,1)S(1)} collective-permute-done((bf16[256,512]{1,0:T(8,128)(2,1)S(1)}, bf16[256,512]{1,0:T(8,128)(2,1)S(1)}, u32[]{:S(2)}, u32[]{:S(2)}) %collective-permute-start) | collective-permute-done | bytes 262176 | tf_op jit(solution)/shard_map/ppermute | solution.py:280
  13.3 1.8 %collective-permute-start.5 = (bf16[1024,128]{1,0:T(8,128)(2,1)S(1)}, bf16[1024,128]{1,0:T(8,128)(2,1)S(1)}, u32[]{:S(2)}, u32[]{:S(2)}) collective-permute-start(bf16[1024,128]{1,0:T(8,128)(2,1)S(1)} %pack.5), channel_id=1, source_target_pairs={{0,16},{16,0},{1,17},{17,1},{2,18},{18,2},{3,19},{19,3},{4,20},{20... | collective-permute-start | bytes 786440 | tf_op jit(solution)/shard_map/ppermute | solution.py:303
  15.2 0.9 %copy-done.1 = bf16[1024,128]{1,0:T(8,128)(2,1)S(1)} copy-done((bf16[1024,128]{1,0:T(8,128)(2,1)S(1)}, bf16[1024,128]{1,0:T(8,128)(2,1)}, u32[]{:S(2)}) %copy-start.1) | copy-done | bytes 262168
  16.1 0.7 %copy-done.2 = s32[8,8]{1,0:T(8,128)S(1)} copy-done((s32[8,8]{1,0:T(8,128)S(1)}, s32[8,8]{1,0:T(8,128)}, u32[]{:S(2)}) %copy-start.2) | copy-done | bytes 280
  16.8 0.7 %copy-done.3 = s32[8,8]{1,0:T(8,128)S(1)} copy-done((s32[8,8]{1,0:T(8,128)S(1)}, s32[8,8]{1,0:T(8,128)}, u32[]{:S(2)}) %copy-start.3) | copy-done | bytes 280
  17.5 1.4 %fetch.1 = (s32[8,8]{1,0:T(8,128)S(1)}, s32[8,8]{1,0:T(8,128)S(1)}, bf16[1024,128]{1,0:T(8,128)(2,1)S(1)}) custom-call(s32[8,8]{1,0:T(8,128)S(1)} %copy-done.2, s32[8,8]{1,0:T(8,128)S(1)} %copy-done.3, bf16[1024,128]{1,0:T(8,128)(2,1)S(1)} %copy-done.1), custom_call_target="tpu_custom_call" | custom-call | bytes 524800 | tf_op jit(solution)/shard_map/fetch/pallas_call | solution.py:51
  18.9 2.0 %collective-permute-done.5.refs_5_ = bf16[1024,128]{1,0:T(8,128)(2,1)S(1)} collective-permute-done((bf16[1024,128]{1,0:T(8,128)(2,1)S(1)}, bf16[1024,128]{1,0:T(8,128)(2,1)S(1)}, u32[]{:S(2)}, u32[]{:S(2)}) %collective-permute-start.5) | collective-permute-done | bytes 262176 | tf_op jit(solution)/shard_map/ppermute | solution.py:303
  21.0 1.1 %bring.1 = (bf16[256,2048]{1,0:T(8,128)(2,1)S(1)}, bf16[512,256]{1,0:T(8,128)(2,1)S(1)}, bf16[512,256]{1,0:T(8,128)(2,1)S(1)}, bf16[512,256]{1,0:T(8,128)(2,1)S(1)}, bf16[512,256]{1,0:T(8,128)(2,1)S(1)}) custom-call(s32[8,8]{1,0:T(8,128)S(1)} %get-tuple-element.20.refs_0_, s32[8,8]{1,0:T(8,128)S(1)} %get-tuple-element.19.refs_1_.refs_0_, ...), custom_call_target="tpu_custom_call" | custom-call | bytes 3932160 | tf_op jit(solution)/shard_map/bring/pallas_call | solution.py:51
  23.2 1.5 %collective-permute-done.6.refs_2_.refs_0_ = bf16[256,512]{1,0:T(8,128)(2,1)S(1)} collective-permute-done((bf16[256,512]{1,0:T(8,128)(2,1)S(1)}, bf16[256,512]{1,0:T(8,128)(2,1)S(1)}, u32[]{:S(2)}, u32[]{:S(2)}) %collective-permute-start.6) | collective-permute-done | bytes 262176 | tf_op jit(solution)/shard_map/ppermute | solution.py:280
  24.7 1.5 %collective-permute-start.2 = (bf16[512,512]{1,0:T(8,128)(2,1)S(1)}, bf16[512,512]{1,0:T(8,128)(2,1)S(1)}, u32[]{:S(2)}, u32[]{:S(2)}) collective-permute-start(bf16[512,512]{1,0:T(8,128)(2,1)S(1)} %pack.4.refs_0_.refs_2_), channel_id=1, source_target_pairs={{0,2},{1,3},{2,0},{3,1},{4,6},{5,7},{6,4},{7,5},{8,10},{9,11},{10,... | collective-permute-start | bytes 1572872 | tf_op jit(solution)/shard_map/ppermute | solution.py:286
  26.2 1.4 %first_product.1.refs_1_.refs_0_ = bf16[256,512]{1,0:T(8,128)(2,1)S(1)} custom-call(s32[8,8]{1,0:T(8,128)S(1)} %get-tuple-element.19.refs_1_.refs_0_, bf16[256,2048]{1,0:T(8,128)(2,1)S(1)} %get-tuple-element.22.refs_1_, bf16[256,512]{1,0:T(8,128)(2,1)S(1)} %collective-permute-done.6.refs_2_.refs_0_, bf16[512,256]{1,0:T(8,128)(2,1)S(1)} %get-tuple-element.23.refs_3_, ...), custom_call_target="tpu_custom_call" | custom-call | bytes 4718592 | tf_op jit(solution)/shard_map/first_product/pallas_call | solution.py:51
  28.4 0.9 %collective-permute-done.12.refs_2_.refs_6_ = bf16[256,512]{1,0:T(8,128)(2,1)S(1)} collective-permute-done((bf16[256,512]{1,0:T(8,128)(2,1)S(1)}, bf16[256,512]{1,0:T(8,128)(2,1)S(1)}, u32[]{:S(2)}, u32[]{:S(2)}) %collective-permute-start.12) | collective-permute-done | bytes 262176 | tf_op jit(solution)/shard_map/ppermute | solution.py:330
  29.3 7.2 %collective-permute-done.11.refs_1_ = bf16[256,512]{1,0:T(8,128)(2,1)S(1)} collective-permute-done((bf16[256,512]{1,0:T(8,128)(2,1)S(1)}, bf16[256,512]{1,0:T(8,128)(2,1)S(1)}, u32[]{:S(2)}, u32[]{:S(2)}) %collective-permute-start.11) | collective-permute-done | bytes 262176 | tf_op jit(solution)/shard_map/ppermute | solution.py:324
  37.9 5.3 %collective-permute-start.15 = (bf16[128,512]{1,0:T(8,128)(2,1)S(1)}, bf16[128,512]{1,0:T(8,128)(2,1)S(1)}, u32[]{:S(2)}, u32[]{:S(2)}) collective-permute-start(bf16[128,512]{1,0:T(8,128)(2,1)S(1)} %get-tuple-element.28), channel_id=1, source_target_pairs={{0,12},{4,8},{8,4},{12,0},{1,13},{5,9},{9,5},{13,1},{2,14},{6,10},... | collective-permute-start | bytes 393224 | tf_op jit(solution)/shard_map/ppermute | solution.py:340
  43.7 2.3 %collective-permute-done.14.refs_7_.refs_0_ = bf16[256,512]{1,0:T(8,128)(2,1)S(1)} collective-permute-done((bf16[256,512]{1,0:T(8,128)(2,1)S(1)}, bf16[256,512]{1,0:T(8,128)(2,1)S(1)}, u32[]{:S(2)}, u32[]{:S(2)}) %collective-permute-start.14) | collective-permute-done | bytes 262176 | tf_op jit(solution)/shard_map/ppermute | solution.py:286
  46.7 1.4 %layers.1.refs_0_.refs_1_ = bf16[1024,2048]{1,0:T(8,128)(2,1)S(1)} custom-call(s32[8,8]{1,0:T(8,128)S(1)} %get-tuple-element.19.refs_1_.refs_0_, bf16[1024,512]{1,0:T(8,128)(2,1)S(1)} %copy-done, bf16[512,512]{1,0:T(8,128)(2,1)S(1)} %pack.4.refs_0_.refs_2_, bf16[512,512]{1,0:T(8,128)(2,1)S(1)} %collective-permute-done.2.refs_1_.refs_3_, ...), custom_call_target="tpu_custom_call" | custom-call | bytes 8126464 | tf_op jit(solution)/shard_map/layers/pallas_call | solution.py:51
  48.0 0.7 %second_product.1.refs_2_ = f32[1024,128]{1,0:T(8,128)S(1)} custom-call(bf16[1024,2048]{1,0:T(8,128)(2,1)S(1)} %layers.1.refs_0_.refs_1_, bf16[128,512]{1,0:T(8,128)(2,1)S(1)} %get-tuple-element.27.refs_2_.refs_1_, bf16[128,512]{1,0:T(8,128)(2,1)S(1)} %collective-permute-done.15.refs_2_), custom_call_target="tpu_custom_call" | custom-call | bytes 4980736 | tf_op jit(solution)/shard_map/second_product/pallas_call | solution.py:51
  48.7 6.2 %collective-permute-done.16.refs_3_ = bf16[128,512]{1,0:T(8,128)(2,1)S(1)} collective-permute-done((bf16[128,512]{1,0:T(8,128)(2,1)S(1)}, bf16[128,512]{1,0:T(8,128)(2,1)S(1)}, u32[]{:S(2)}, u32[]{:S(2)}) %collective-permute-start.16) | collective-permute-done | bytes 131104 | tf_op jit(solution)/shard_map/ppermute | solution.py:340
  54.9 2.1 %last_product.1 = bf16[1024,128]{1,0:T(8,128)(2,1)} custom-call(s32[8,8]{1,0:T(8,128)S(1)} %get-tuple-element.19.refs_1_.refs_0_, bf16[1024,2048]{1,0:T(8,128)(2,1)S(1)} %layers.1.refs_0_.refs_1_, f32[1024,128]{1,0:T(8,128)S(1)} %second_product.1.refs_2_, bf16[128,512]{1,0:T(8,128)(2,1)S(1)} %collective-permute-done.16.refs_3_, ...), custom_call_target="tpu_custom_call" | custom-call | bytes 6553600 | tf_op jit(solution)/shard_map/last_product/pallas_call | solution.py:51
  (37 shorter events, 4.5 us)
Async XLA Ops:
  1.0 12.3 %collective-permute-start = (bf16[256,512]{1,0:T(8,128)(2,1)S(1)}, bf16[256,512]{1,0:T(8,128)(2,1)S(1)}, u32[]{:S(2)}, u32[]{:S(2)}) collective-permute-start(bf16[256,512]{1,0:T(8,128)(2,1)S(1)} %bitcast.5), channel_id=1, source_target_pairs={{0,4},{4,8},{8,12},{12,0},{1,5},{5,9},{9,13},{13,1},{2,6},{6,10},{... | collective-permute-start | bytes 786440 | tf_op jit(solution)/shard_map/ppermute | solution.py:280
  4.0 9.2 %collective-permute-start.3 = (bf16[1024,128]{1,0:T(8,128)(2,1)}, bf16[1024,128]{1,0:T(8,128)(2,1)S(1)}, u32[]{:S(2)}, u32[]{:S(2)}) collective-permute-start(bf16[1024,128]{1,0:T(8,128)(2,1)} %refs_2_.1), channel_id=1, source_target_pairs={{0,2},{1,3},{2,0},{3,1},{4,6},{5,7},{6,4},{7,5},{8,10},{9,11},{10,... | collective-permute-start | bytes 786440 | tf_op jit(solution)/shard_map/ppermute | solution.py:303
  5.6 13.4 %collective-permute-start.1 = (bf16[256,512]{1,0:T(8,128)(2,1)S(1)}, bf16[256,512]{1,0:T(8,128)(2,1)S(1)}, u32[]{:S(2)}, u32[]{:S(2)}) collective-permute-start(bf16[256,512]{1,0:T(8,128)(2,1)S(1)} %bitcast.6), channel_id=1, source_target_pairs={{0,12},{4,0},{8,4},{12,8},{1,13},{5,1},{9,5},{13,9},{2,14},{6,2},{... | collective-permute-start | bytes 786440 | tf_op jit(solution)/shard_map/ppermute | solution.py:282
  7.8 11.1 %collective-permute-start.4 = (bf16[1024,128]{1,0:T(8,128)(2,1)}, bf16[1024,128]{1,0:T(8,128)(2,1)S(1)}, u32[]{:S(2)}, u32[]{:S(2)}) collective-permute-start(bf16[1024,128]{1,0:T(8,128)(2,1)} %refs_2_.1), channel_id=1, source_target_pairs={{0,16},{16,0},{1,17},{17,1},{2,18},{18,2},{3,19},{19,3},{4,20},{20... | collective-permute-start | bytes 786440 | tf_op jit(solution)/shard_map/ppermute | solution.py:303
  13.3 7.7 %collective-permute-start.5 = (bf16[1024,128]{1,0:T(8,128)(2,1)S(1)}, bf16[1024,128]{1,0:T(8,128)(2,1)S(1)}, u32[]{:S(2)}, u32[]{:S(2)}) collective-permute-start(bf16[1024,128]{1,0:T(8,128)(2,1)S(1)} %pack.5), channel_id=1, source_target_pairs={{0,16},{16,0},{1,17},{17,1},{2,18},{18,2},{3,19},{19,3},{4,20},{20... | collective-permute-start | bytes 786440 | tf_op jit(solution)/shard_map/ppermute | solution.py:303
  15.1 9.6 %collective-permute-start.6 = (bf16[256,512]{1,0:T(8,128)(2,1)S(1)}, bf16[256,512]{1,0:T(8,128)(2,1)S(1)}, u32[]{:S(2)}, u32[]{:S(2)}) collective-permute-start(bf16[256,512]{1,0:T(8,128)(2,1)S(1)} %collective-permute-done.refs_0_.refs_1_.refs_7_), channel_id=1, source_target_pairs={{0,4},{4,8},{8,12},{12,0},{1,5},{5,9},{9,13},{13,1},{2,6},{6,10},{... | collective-permute-start | bytes 786440 | tf_op jit(solution)/shard_map/ppermute | solution.py:280
  15.2 0.9 %copy-start.1 = (bf16[1024,128]{1,0:T(8,128)(2,1)S(1)}, bf16[1024,128]{1,0:T(8,128)(2,1)}, u32[]{:S(2)}) copy-start(bf16[1024,128]{1,0:T(8,128)(2,1)} %refs_2_.1) | copy-start | bytes 786436
  16.1 0.7 %copy-start.2 = (s32[8,8]{1,0:T(8,128)S(1)}, s32[8,8]{1,0:T(8,128)}, u32[]{:S(2)}) copy-start(s32[8,8]{1,0:T(8,128)} %refs_0_.1) | copy-start | bytes 772
  16.8 0.7 %copy-start.3 = (s32[8,8]{1,0:T(8,128)S(1)}, s32[8,8]{1,0:T(8,128)}, u32[]{:S(2)}) copy-start(s32[8,8]{1,0:T(8,128)} %refs_1_.2) | copy-start | bytes 772
  22.1 4.1 %collective-permute-start.10 = (bf16[512,256]{1,0:T(8,128)(2,1)S(1)}, bf16[512,256]{1,0:T(8,128)(2,1)S(1)}, u32[]{:S(2)}, u32[]{:S(2)}) collective-permute-start(bf16[512,256]{1,0:T(8,128)(2,1)S(1)} %get-tuple-element.26.refs_6_), channel_id=1, source_target_pairs={{0,1},{1,0},{2,3},{3,2},{4,5},{5,4},{6,7},{7,6},{8,9},{9,8},{10,11... | collective-permute-start | bytes 786440 | tf_op jit(solution)/shard_map/ppermute | solution.py:311
  22.2 4.1 %collective-permute-start.7 = (bf16[512,256]{1,0:T(8,128)(2,1)S(1)}, bf16[512,256]{1,0:T(8,128)(2,1)S(1)}, u32[]{:S(2)}, u32[]{:S(2)}) collective-permute-start(bf16[512,256]{1,0:T(8,128)(2,1)S(1)} %get-tuple-element.23.refs_3_), channel_id=1, source_target_pairs={{0,1},{1,0},{2,3},{3,2},{4,5},{5,4},{6,7},{7,6},{8,9},{9,8},{10,11... | collective-permute-start | bytes 786440 | tf_op jit(solution)/shard_map/ppermute | solution.py:311
  22.7 3.6 %collective-permute-start.8 = (bf16[512,256]{1,0:T(8,128)(2,1)S(1)}, bf16[512,256]{1,0:T(8,128)(2,1)S(1)}, u32[]{:S(2)}, u32[]{:S(2)}) collective-permute-start(bf16[512,256]{1,0:T(8,128)(2,1)S(1)} %get-tuple-element.24.refs_4_), channel_id=1, source_target_pairs={{0,1},{1,0},{2,3},{3,2},{4,5},{5,4},{6,7},{7,6},{8,9},{9,8},{10,11... | collective-permute-start | bytes 786440 | tf_op jit(solution)/shard_map/ppermute | solution.py:311
  22.7 23.9 %copy-start = (bf16[1024,512]{1,0:T(8,128)(2,1)S(1)}, bf16[1024,512]{1,0:T(8,128)(2,1)}, u32[]{:S(2)}) copy-start(bf16[1024,512]{1,0:T(8,128)(2,1)} %refs_1_.3) | copy-start | bytes 3145732
  22.7 3.5 %collective-permute-start.9 = (bf16[512,256]{1,0:T(8,128)(2,1)S(1)}, bf16[512,256]{1,0:T(8,128)(2,1)S(1)}, u32[]{:S(2)}, u32[]{:S(2)}) collective-permute-start(bf16[512,256]{1,0:T(8,128)(2,1)S(1)} %get-tuple-element.25.refs_5_), channel_id=1, source_target_pairs={{0,1},{1,0},{2,3},{3,2},{4,5},{5,4},{6,7},{7,6},{8,9},{9,8},{10,11... | collective-permute-start | bytes 786440 | tf_op jit(solution)/shard_map/ppermute | solution.py:311
  24.7 12.5 %collective-permute-start.2 = (bf16[512,512]{1,0:T(8,128)(2,1)S(1)}, bf16[512,512]{1,0:T(8,128)(2,1)S(1)}, u32[]{:S(2)}, u32[]{:S(2)}) collective-permute-start(bf16[512,512]{1,0:T(8,128)(2,1)S(1)} %pack.4.refs_0_.refs_2_), channel_id=1, source_target_pairs={{0,2},{1,3},{2,0},{3,1},{4,6},{5,7},{6,4},{7,5},{8,10},{9,11},{10,... | collective-permute-start | bytes 1572872 | tf_op jit(solution)/shard_map/ppermute | solution.py:286
  27.7 1.6 %collective-permute-start.12 = (bf16[256,512]{1,0:T(8,128)(2,1)S(1)}, bf16[256,512]{1,0:T(8,128)(2,1)S(1)}, u32[]{:S(2)}, u32[]{:S(2)}) collective-permute-start(bf16[256,512]{1,0:T(8,128)(2,1)S(1)} %pack.6.refs_5_), channel_id=1, source_target_pairs={{0,1},{1,0},{2,3},{3,2},{4,5},{5,4},{6,7},{7,6},{8,9},{9,8},{10,11... | collective-permute-start | bytes 786440 | tf_op jit(solution)/shard_map/ppermute | solution.py:330
  27.8 8.7 %collective-permute-start.11 = (bf16[256,512]{1,0:T(8,128)(2,1)S(1)}, bf16[256,512]{1,0:T(8,128)(2,1)S(1)}, u32[]{:S(2)}, u32[]{:S(2)}) collective-permute-start(bf16[256,512]{1,0:T(8,128)(2,1)S(1)} %first_product.1.refs_1_.refs_0_), channel_id=1, source_target_pairs={{0,16},{16,0},{1,17},{17,1},{2,18},{18,2},{3,19},{19,3},{4,20},{20... | collective-permute-start | bytes 786440 | tf_op jit(solution)/shard_map/ppermute | solution.py:324
  37.3 8.9 %collective-permute-start.13 = (bf16[1024,512]{1,0:T(8,128)(2,1)S(1)}, bf16[1024,512]{1,0:T(8,128)(2,1)S(1)}, u32[]{:S(2)}, u32[]{:S(2)}) collective-permute-start(bf16[1024,512]{1,0:T(8,128)(2,1)S(1)} %pack.7), channel_id=1, source_target_pairs={{0,1},{1,0},{2,3},{3,2},{4,5},{5,4},{6,7},{7,6},{8,9},{9,8},{10,11... | collective-permute-start | bytes 3145736 | tf_op jit(solution)/shard_map/ppermute | solution.py:346
  37.3 8.7 %collective-permute-start.14 = (bf16[256,512]{1,0:T(8,128)(2,1)S(1)}, bf16[256,512]{1,0:T(8,128)(2,1)S(1)}, u32[]{:S(2)}, u32[]{:S(2)}) collective-permute-start(bf16[256,512]{1,0:T(8,128)(2,1)S(1)} %pack.6.refs_5_), channel_id=1, source_target_pairs={{0,2},{1,3},{2,0},{3,1},{4,6},{5,7},{6,4},{7,5},{8,10},{9,11},{10,... | collective-permute-start | bytes 786440 | tf_op jit(solution)/shard_map/ppermute | solution.py:286
  37.9 10.1 %collective-permute-start.15 = (bf16[128,512]{1,0:T(8,128)(2,1)S(1)}, bf16[128,512]{1,0:T(8,128)(2,1)S(1)}, u32[]{:S(2)}, u32[]{:S(2)}) collective-permute-start(bf16[128,512]{1,0:T(8,128)(2,1)S(1)} %get-tuple-element.28), channel_id=1, source_target_pairs={{0,12},{4,8},{8,4},{12,0},{1,13},{5,9},{9,5},{13,1},{2,14},{6,10},... | collective-permute-start | bytes 393224 | tf_op jit(solution)/shard_map/ppermute | solution.py:340
  43.2 11.8 %collective-permute-start.16 = (bf16[128,512]{1,0:T(8,128)(2,1)S(1)}, bf16[128,512]{1,0:T(8,128)(2,1)S(1)}, u32[]{:S(2)}, u32[]{:S(2)}) collective-permute-start(bf16[128,512]{1,0:T(8,128)(2,1)S(1)} %get-tuple-element.29), channel_id=1, source_target_pairs={{0,8},{4,12},{8,0},{12,4},{1,9},{5,13},{9,1},{13,5},{2,10},{6,14},... | collective-permute-start | bytes 393224 | tf_op jit(solution)/shard_map/ppermute | solution.py:340
  43.2 11.8 %collective-permute-start.17 = (bf16[128,512]{1,0:T(8,128)(2,1)S(1)}, bf16[128,512]{1,0:T(8,128)(2,1)S(1)}, u32[]{:S(2)}, u32[]{:S(2)}) collective-permute-start(bf16[128,512]{1,0:T(8,128)(2,1)S(1)} %get-tuple-element.30), channel_id=1, source_target_pairs={{0,4},{4,0},{8,12},{12,8},{1,5},{5,1},{9,13},{13,9},{2,6},{6,2},{1... | collective-permute-start | bytes 393224 | tf_op jit(solution)/shard_map/ppermute | solution.py:340
  46.1 8.9 %collective-permute-start.18 = (bf16[128,512]{1,0:T(8,128)(2,1)S(1)}, bf16[128,512]{1,0:T(8,128)(2,1)S(1)}, u32[]{:S(2)}, u32[]{:S(2)}) collective-permute-start(bf16[128,512]{1,0:T(8,128)(2,1)S(1)} %get-tuple-element.31), channel_id=1, source_target_pairs={{0,1},{1,0},{2,3},{3,2},{4,5},{5,4},{6,7},{7,6},{8,9},{9,8},{10,11... | collective-permute-start | bytes 393224 | tf_op jit(solution)/shard_map/ppermute | solution.py:355
  46.2 8.8 %collective-permute-start.19 = (bf16[128,512]{1,0:T(8,128)(2,1)S(1)}, bf16[128,512]{1,0:T(8,128)(2,1)S(1)}, u32[]{:S(2)}, u32[]{:S(2)}) collective-permute-start(bf16[128,512]{1,0:T(8,128)(2,1)S(1)} %get-tuple-element.32), channel_id=1, source_target_pairs={{0,1},{1,0},{2,3},{3,2},{4,5},{5,4},{6,7},{7,6},{8,9},{9,8},{10,11... | collective-permute-start | bytes 393224 | tf_op jit(solution)/shard_map/ppermute | solution.py:355

commit v15 on v14

--- a/solution.py
+++ b/solution.py
@@ -141,7 +141,9 @@
 def bring_kernel(sizes, h_table, hp, zp, *refs):
     n = len(h_table)
     pieces, slots = refs[:n], refs[n : n + sizes.cols - 1]
-    zm, blocks = refs[n + sizes.cols - 1], refs[n + sizes.cols :]
+    zm, sent, blocks = refs[n + sizes.cols - 1], refs[n + sizes.cols : 2 * n + sizes.cols - 1], refs[
+        2 * n + sizes.cols - 1 :
+    ]
     r, c, l = place()
     q, wide = sizes.quarter, blocks[0].shape[0]
     for h, (dr, dl) in zip(pieces, h_table):
@@ -158,28 +160,44 @@
                         hp, row // BS, block_col, h[first : first + BS, :]
                     )
 
+    for (dr, dl), h, out in zip(h_table[1:], pieces[1:], sent):
+        block_col = (c * sizes.cols_here + (l ^ dl) * q) // BS
+        for first in range(0, sizes.rows_here, BS):
+            j = ((r ^ dr) * sizes.rows_here + first) // BS
+            out[first : first + BS, :] = keep_block(hp, j, block_col, h[first : first + BS, :])
     mask_kernel(sizes, zp, *slots, zm)
 
 
-def first_kernel(sizes, top, zp, zm, last, *refs):
-    cols, q = sizes.cols, sizes.quarter
-    n, (out, zs) = len(refs) // 2 - 1, refs[-2:]
-    sides, width = (refs[:n], refs[n : 2 * n]), refs[0].shape[0]
+def first_kernel(sizes, top, h_table, hp, zp, zm, last, raw, *refs):
+    cols, q, n = sizes.cols, sizes.quarter, len(h_table) - 1
+    others, blocks, (out, zs, hs) = refs[:n], refs[n:-3], refs[-3:]
     r, c, l = place()
     cc = slot_column(c, cols - 1, cols)
     zs[...] = zm[...]
     zs[:, columns_of(cc, sizes)] = mask_piece(zp, r, l, cc, last[...], sizes)
-    for side, blocks in zip((l, l ^ 1), sides):
+    block_col = (c * sizes.cols_here + (l ^ 1) * q) // BS
+    for first in range(0, sizes.rows_here, BS):
+        j = (r * sizes.rows_here + first) // BS
+        hs[first : first + BS, :] = keep_block(hp, j, block_col, raw[first : first + BS, :])
+    width, acc = blocks[0].shape[0], None
+    for n, block in enumerate(blocks):
+        part = jnp.dot(
+            zs[:, n * width : (n + 1) * width], block[...], preferred_element_type=jnp.float32
+        )
+        acc = part if acc is None else acc + part
+    for n, ll in enumerate((l, l ^ top)):
+        out[:, pl.ds(pl.multiple_of(ll * q, q), q)] = acc[:, n * q : (n + 1) * q].astype(out.dtype)
+    for dl in (0, top):
         acc = None
-        for n, block in enumerate(blocks):
-            part = jnp.dot(
-                zs[:, n * width : (n + 1) * width], block[...], preferred_element_type=jnp.float32
-            )
-            acc = part if acc is None else acc + part
-        for n, ll in enumerate((side, side ^ top)):
-            out[:, pl.ds(pl.multiple_of(ll * q, q), q)] = acc[:, n * q : (n + 1) * q].astype(
-                out.dtype
-            )
+        for (dr, there), h in zip(h_table, [hs, *others]):
+            if there == dl:
+                rows = pl.ds(
+                    pl.multiple_of((r ^ dr) * sizes.rows_here, sizes.rows_here), sizes.rows_here
+                )
+                part = jnp.dot(zs[:, rows], h[...], preferred_element_type=jnp.float32)
+                acc = part if acc is None else acc + part
+        ll = l ^ 1 ^ dl
+        out[:, pl.ds(pl.multiple_of(ll * q, q), q)] = acc.astype(out.dtype)
 
 
 def route_kernel(sizes, row_offsets, *refs):
@@ -301,21 +319,34 @@
             if dl and axis == 'row':
                 piece = pack([piece], [slots[1]])
             h_pieces.append(lax.ppermute(piece, axis, perm))
+    raw = lax.ppermute(hamiltonian, "layer", flip(layers, low))
+    group = range(1, cols - 1)
+    mine = pack([slots[s] for s in group])
+    other = cross(mine)
+    n_sent = len(h_table) - 1
     zm, *h_own = run(
         functools.partial(bring_kernel, sizes, h_table),
         "bring",
-        [shape(height, order)] + [shape(cols_here, 2 * q)] * cols,
+        [shape(height, order)]
+        + [shape(*hamiltonian.shape)] * n_sent
+        + [shape(cols_here, 2 * q)] * cols,
         [fetched, *h_pieces[1:], *slots[:-1]],
         smem=[h_pattern, z_pattern],
-    )
-    h_other = [lax.ppermute(block, "layer", flip(layers, low)) for block in h_own]
+        after=[raw, mine],
+    )
+    sent, h_own = h_own[:n_sent], h_own[n_sent:]
+    h_other = [lax.ppermute(piece, "layer", flip(layers, low)) for piece in sent]
+    crossed = []
     product = run(
-        functools.partial(first_kernel, sizes, top),
+        functools.partial(first_kernel, sizes, top, h_table),
         "first_product",
         [shape(height, cols_here)],
-        [zm, slots[-1], *h_own, *h_other],
-        smem=[z_pattern],
-        scratch=[pltpu.VMEM((height, order), jnp.bfloat16)],
+        [zm, slots[-1], raw, *h_other, *h_own],
+        smem=[h_pattern, z_pattern],
+        scratch=[
+            pltpu.VMEM((height, order), jnp.bfloat16),
+            pltpu.VMEM(hamiltonian.shape, jnp.bfloat16),
+        ],
     )[0]
 
     gathered = {0: product}
@@ -340,9 +371,6 @@
         lax.ppermute(outgoing[d], "col", flip(cols, d)) for d in range(cols - 1, 0, -1)
     ]
     messages = [outgoing[0]] + messages[::-1]
-    group = range(1, cols - 1)
-    mine = pack([slots[s] for s in group])
-    other = cross(mine)
     both = lax.ppermute(pack([mine, other], [outgoing[0]]), "layer", flip(layers, low))
     held, z_table = [inv_root, mine, other, both, last, last_low, last_top], {}
     for n, s in enumerate(group):

time: 57.3 us -> 58.5 us (1.021)
  waiting for transfers between devices: 24.7 us -> 27.3 us
  starting transfers between devices: 20.5 us -> 18.6 us
    ppermute x2, waiting for transfers between devices: 5.44 us -> 8.75 us  [local(): lax.ppermute(right, 'col', [(i, (i + 1) % cols) for i in range(cols)])]
    ppermute x3, waiting for transfers between devices: 6.18 us -> 4.36 us  [local(): lax.ppermute(outgoing[d], 'col', flip(cols, d))]
    ppermute x3, starting transfers between devices: 5.83 us -> 4.39 us  [local(): lax.ppermute(outgoing[d], 'col', flip(cols, d))]
    ppermute x3, waiting for transfers between devices: 2.04 us -> 3.33 us  [local(): h_pieces.append(lax.ppermute(piece, axis, perm))]
  transfers between devices with their start and end apart: 20 -> 20, of which waited for: 8 -> 7; matrix products, arithmetic and copies ran while one was open for 0% -> 0% of each run, Pallas kernels for 11% -> 12%
where the time goes in v15:
time: 58.5 us; the launch traced here: 58.3 us
  waiting for transfers between devices  27.3 us (47%)
  starting transfers between devices  18.6 us (32%)
  Pallas kernels  8.88 us (15%)
  local copies, waits for them, and re-layouts  3.3 us (6%)
    pallas_call x12, Pallas kernels, run(): pl.pallas_call(body, out_shape=list(outs), in_specs=[pl.BlockSpec(memory_...  8.88 us
    ppermute x2, waiting for transfers between devices, local(): lax.ppermute(right, 'col', [(i, (i + 1) % cols) for i in range(cols)])  8.75 us
    ppermute x1, waiting for transfers between devices, local(): gathered[dr ^ bit] = lax.ppermute(piece, 'row', flip(rows, bit))  7.2 us
    ppermute x3, starting transfers between devices, local(): h_pieces.append(lax.ppermute(piece, axis, perm))  4.81 us
    ppermute x3, starting transfers between devices, local(): lax.ppermute(outgoing[d], 'col', flip(cols, d))  4.39 us
    ppermute x3, waiting for transfers between devices, local(): lax.ppermute(outgoing[d], 'col', flip(cols, d))  4.36 us
    ppermute x3, waiting for transfers between devices, local(): h_pieces.append(lax.ppermute(piece, axis, perm))  3.33 us
    ppermute x2, starting transfers between devices, local(): lax.ppermute(right, 'col', [(i, (i + 1) % cols) for i in range(cols)])  3.23 us
  transfers between devices with their start and end apart: 20, of which 7 were waited for; matrix products, arithmetic and copies ran while one was open for 0% of the time, Pallas kernels for 12%

profile of v15, /device:TPU:0, one launch (start us, length us, event | category | flops | bytes accessed | tf_op | source)
XLA Modules:
  0.0 58.3 jit_solution(11271415774352439474)
XLA Ops:
  0.0 1.0 %constant_dynamic-slice_fusion = bf16[2,1,128,512]{3,2,1,0:T(8,128)(2,1)S(1)} fusion(bf16[2,4,128,512]{3,2,1,0:T(8,128)(2,1)} %bitcast.4, s32[]{:T(128)S(6)} %select_n.4), kind=kLoop, calls=%fused_computation | loop fusion | bytes 524292 | tf_op jit(solution)/shard_map/jit(dynamic_index_in_dim)/dynamic_slice | solution.py:293
  1.0 3.1 %collective-permute-start = (bf16[256,512]{1,0:T(8,128)(2,1)S(1)}, bf16[256,512]{1,0:T(8,128)(2,1)S(1)}, u32[]{:S(2)}, u32[]{:S(2)}) collective-permute-start(bf16[256,512]{1,0:T(8,128)(2,1)S(1)} %bitcast.5), channel_id=1, source_target_pairs={{0,4},{4,8},{8,12},{12,0},{1,5},{5,9},{9,13},{13,1},{2,6},{6,10},{... | collective-permute-start | bytes 786440 | tf_op jit(solution)/shard_map/ppermute | solution.py:298
  4.0 1.5 %collective-permute-start.3 = (bf16[1024,128]{1,0:T(8,128)(2,1)}, bf16[1024,128]{1,0:T(8,128)(2,1)S(1)}, u32[]{:S(2)}, u32[]{:S(2)}) collective-permute-start(bf16[1024,128]{1,0:T(8,128)(2,1)} %refs_2_.1), channel_id=1, source_target_pairs={{0,2},{1,3},{2,0},{3,1},{4,6},{5,7},{6,4},{7,5},{8,10},{9,11},{10,... | collective-permute-start | bytes 786440 | tf_op jit(solution)/shard_map/ppermute | solution.py:321
  5.6 2.2 %collective-permute-start.1 = (bf16[256,512]{1,0:T(8,128)(2,1)S(1)}, bf16[256,512]{1,0:T(8,128)(2,1)S(1)}, u32[]{:S(2)}, u32[]{:S(2)}) collective-permute-start(bf16[256,512]{1,0:T(8,128)(2,1)S(1)} %bitcast.6), channel_id=1, source_target_pairs={{0,12},{4,0},{8,4},{12,8},{1,13},{5,1},{9,5},{13,9},{2,14},{6,2},{... | collective-permute-start | bytes 786440 | tf_op jit(solution)/shard_map/ppermute | solution.py:300
  7.8 1.5 %collective-permute-start.4 = (bf16[1024,128]{1,0:T(8,128)(2,1)}, bf16[1024,128]{1,0:T(8,128)(2,1)S(1)}, u32[]{:S(2)}, u32[]{:S(2)}) collective-permute-start(bf16[1024,128]{1,0:T(8,128)(2,1)} %refs_2_.1), channel_id=1, source_target_pairs={{0,16},{16,0},{1,17},{17,1},{2,18},{18,2},{3,19},{19,3},{4,20},{20... | collective-permute-start | bytes 786440 | tf_op jit(solution)/shard_map/ppermute | solution.py:321
  9.3 3.9 %collective-permute-done.refs_0_.refs_1_.refs_7_ = bf16[256,512]{1,0:T(8,128)(2,1)S(1)} collective-permute-done((bf16[256,512]{1,0:T(8,128)(2,1)S(1)}, bf16[256,512]{1,0:T(8,128)(2,1)S(1)}, u32[]{:S(2)}, u32[]{:S(2)}) %collective-permute-start) | collective-permute-done | bytes 262176 | tf_op jit(solution)/shard_map/ppermute | solution.py:298
  13.3 1.8 %collective-permute-start.5 = (bf16[1024,128]{1,0:T(8,128)(2,1)S(1)}, bf16[1024,128]{1,0:T(8,128)(2,1)S(1)}, u32[]{:S(2)}, u32[]{:S(2)}) collective-permute-start(bf16[1024,128]{1,0:T(8,128)(2,1)S(1)} %pack.5), channel_id=1, source_target_pairs={{0,16},{16,0},{1,17},{17,1},{2,18},{18,2},{3,19},{19,3},{4,20},{20... | collective-permute-start | bytes 786440 | tf_op jit(solution)/shard_map/ppermute | solution.py:321
  15.1 0.9 %copy-done.1 = bf16[1024,128]{1,0:T(8,128)(2,1)S(1)} copy-done((bf16[1024,128]{1,0:T(8,128)(2,1)S(1)}, bf16[1024,128]{1,0:T(8,128)(2,1)}, u32[]{:S(2)}) %copy-start.1) | copy-done | bytes 262168
  16.0 0.7 %copy-done.2 = s32[8,8]{1,0:T(8,128)S(1)} copy-done((s32[8,8]{1,0:T(8,128)S(1)}, s32[8,8]{1,0:T(8,128)}, u32[]{:S(2)}) %copy-start.2) | copy-done | bytes 280
  17.4 1.4 %fetch.1 = (s32[8,8]{1,0:T(8,128)S(1)}, s32[8,8]{1,0:T(8,128)S(1)}, bf16[1024,128]{1,0:T(8,128)(2,1)S(1)}) custom-call(s32[8,8]{1,0:T(8,128)S(1)} %copy-done.2, s32[8,8]{1,0:T(8,128)S(1)} %copy-done.3, bf16[1024,128]{1,0:T(8,128)(2,1)S(1)} %copy-done.1), custom_call_target="tpu_custom_call" | custom-call | bytes 524800 | tf_op jit(solution)/shard_map/fetch/pallas_call | solution.py:51
  19.0 3.3 %collective-permute-done.5.refs_5_ = bf16[1024,128]{1,0:T(8,128)(2,1)S(1)} collective-permute-done((bf16[1024,128]{1,0:T(8,128)(2,1)S(1)}, bf16[1024,128]{1,0:T(8,128)(2,1)S(1)}, u32[]{:S(2)}, u32[]{:S(2)}) %collective-permute-start.5) | collective-permute-done | bytes 262176 | tf_op jit(solution)/shard_map/ppermute | solution.py:321
  22.4 1.3 %bring.1 = (bf16[256,2048]{1,0:T(8,128)(2,1)S(1)}, bf16[1024,128]{1,0:T(8,128)(2,1)S(1)}, bf16[1024,128]{1,0:T(8,128)(2,1)S(1)}, bf16[1024,128]{1,0:T(8,128)(2,1...) custom-call(s32[8,8]{1,0:T(8,128)S(1)} %get-tuple-element.23.refs_0_, ...), custom_call_target="tpu_custom_call" | custom-call | bytes 4718592 | tf_op jit(solution)/shard_map/bring/pallas_call | solution.py:51
  24.7 4.8 %collective-permute-done.7.refs_3_.refs_0_ = bf16[256,512]{1,0:T(8,128)(2,1)S(1)} collective-permute-done((bf16[256,512]{1,0:T(8,128)(2,1)S(1)}, bf16[256,512]{1,0:T(8,128)(2,1)S(1)}, u32[]{:S(2)}, u32[]{:S(2)}) %collective-permute-start.7) | collective-permute-done | bytes 262176 | tf_op jit(solution)/shard_map/ppermute | solution.py:298
  29.5 1.8 %first_product.1.refs_1_.refs_0_ = bf16[256,512]{1,0:T(8,128)(2,1)S(1)} custom-call(s32[8,8]{1,0:T(8,128)S(1)} %get-tuple-element.23.refs_0_, s32[8,8]{1,0:T(8,128)S(1)} %get-tuple-element.22.refs_1_.refs_0_, bf16[256,2048]{1,0:T(8,128)(2,1)S(1)} %get-tuple-element.25.refs_2_, bf16[256,512]{1,0:T(8,128)(2,1)S(1)} %collective-permute-done.7.refs_3_.refs_0_, ...), custom_call_target="tpu_custom_call" | custom-call | bytes 4980736 | tf_op jit(solution)/shard_map/first_product/pallas_call | solution.py:51
  32.0 0.9 %collective-permute-done.12.refs_2_.refs_6_ = bf16[256,512]{1,0:T(8,128)(2,1)S(1)} collective-permute-done((bf16[256,512]{1,0:T(8,128)(2,1)S(1)}, bf16[256,512]{1,0:T(8,128)(2,1)S(1)}, u32[]{:S(2)}, u32[]{:S(2)}) %collective-permute-start.12) | collective-permute-done | bytes 262176 | tf_op jit(solution)/shard_map/ppermute | solution.py:361
  32.9 7.2 %collective-permute-done.11.refs_1_ = bf16[256,512]{1,0:T(8,128)(2,1)S(1)} collective-permute-done((bf16[256,512]{1,0:T(8,128)(2,1)S(1)}, bf16[256,512]{1,0:T(8,128)(2,1)S(1)}, u32[]{:S(2)}, u32[]{:S(2)}) %collective-permute-start.11) | collective-permute-done | bytes 262176 | tf_op jit(solution)/shard_map/ppermute | solution.py:355
  40.4 1.6 %collective-permute-start.14 = (bf16[256,512]{1,0:T(8,128)(2,1)S(1)}, bf16[256,512]{1,0:T(8,128)(2,1)S(1)}, u32[]{:S(2)}, u32[]{:S(2)}) collective-permute-start(bf16[256,512]{1,0:T(8,128)(2,1)S(1)} %pack.6.refs_5_), channel_id=1, source_target_pairs={{0,2},{1,3},{2,0},{3,1},{4,6},{5,7},{6,4},{7,5},{8,10},{9,11},{10,... | collective-permute-start | bytes 786440 | tf_op jit(solution)/shard_map/ppermute | solution.py:304
  42.0 2.2 %collective-permute-start.15 = (bf16[128,512]{1,0:T(8,128)(2,1)S(1)}, bf16[128,512]{1,0:T(8,128)(2,1)S(1)}, u32[]{:S(2)}, u32[]{:S(2)}) collective-permute-start(bf16[128,512]{1,0:T(8,128)(2,1)S(1)} %get-tuple-element.34), channel_id=1, source_target_pairs={{0,12},{4,8},{8,4},{12,0},{1,13},{5,9},{9,5},{13,1},{2,14},{6,10},... | collective-permute-start | bytes 393224 | tf_op jit(solution)/shard_map/ppermute | solution.py:371
  44.2 2.2 %collective-permute-start.17 = (bf16[128,512]{1,0:T(8,128)(2,1)S(1)}, bf16[128,512]{1,0:T(8,128)(2,1)S(1)}, u32[]{:S(2)}, u32[]{:S(2)}) collective-permute-start(bf16[128,512]{1,0:T(8,128)(2,1)S(1)} %get-tuple-element.36), channel_id=1, source_target_pairs={{0,4},{4,0},{8,12},{12,8},{1,5},{5,1},{9,13},{13,9},{2,6},{6,2},{1... | collective-permute-start | bytes 393224 | tf_op jit(solution)/shard_map/ppermute | solution.py:371
  46.3 2.7 %collective-permute-done.14.refs_7_.refs_0_ = bf16[256,512]{1,0:T(8,128)(2,1)S(1)} collective-permute-done((bf16[256,512]{1,0:T(8,128)(2,1)S(1)}, bf16[256,512]{1,0:T(8,128)(2,1)S(1)}, u32[]{:S(2)}, u32[]{:S(2)}) %collective-permute-start.14) | collective-permute-done | bytes 262176 | tf_op jit(solution)/shard_map/ppermute | solution.py:304
  49.7 1.4 %layers.1.refs_0_.refs_1_ = bf16[1024,2048]{1,0:T(8,128)(2,1)S(1)} custom-call(s32[8,8]{1,0:T(8,128)S(1)} %get-tuple-element.22.refs_1_.refs_0_, bf16[1024,512]{1,0:T(8,128)(2,1)S(1)} %copy-done, bf16[512,512]{1,0:T(8,128)(2,1)S(1)} %pack.4.refs_10_.refs_0_.refs_2_, bf16[512,512]{1,0:T(8,128)(2,1)S(1)} %collective-permute-done.2.refs_1_.refs_3_, ...), custom_call_target="tpu_custom_call" | custom-call | bytes 8126464 | tf_op jit(solution)/shard_map/layers/pallas_call | solution.py:51
  51.1 0.7 %second_product.1.refs_2_ = f32[1024,128]{1,0:T(8,128)S(1)} custom-call(bf16[1024,2048]{1,0:T(8,128)(2,1)S(1)} %layers.1.refs_0_.refs_1_, bf16[128,512]{1,0:T(8,128)(2,1)S(1)} %get-tuple-element.33.refs_2_.refs_1_, bf16[128,512]{1,0:T(8,128)(2,1)S(1)} %collective-permute-done.15.refs_2_), custom_call_target="tpu_custom_call" | custom-call | bytes 4980736 | tf_op jit(solution)/shard_map/second_product/pallas_call | solution.py:51
  51.8 4.4 %collective-permute-done.16.refs_3_ = bf16[128,512]{1,0:T(8,128)(2,1)S(1)} collective-permute-done((bf16[128,512]{1,0:T(8,128)(2,1)S(1)}, bf16[128,512]{1,0:T(8,128)(2,1)S(1)}, u32[]{:S(2)}, u32[]{:S(2)}) %collective-permute-start.16) | collective-permute-done | bytes 131104 | tf_op jit(solution)/shard_map/ppermute | solution.py:371
  56.2 2.1 %last_product.1 = bf16[1024,128]{1,0:T(8,128)(2,1)} custom-call(s32[8,8]{1,0:T(8,128)S(1)} %get-tuple-element.22.refs_1_.refs_0_, bf16[1024,2048]{1,0:T(8,128)(2,1)S(1)} %layers.1.refs_0_.refs_1_, f32[1024,128]{1,0:T(8,128)S(1)} %second_product.1.refs_2_, bf16[128,512]{1,0:T(8,128)(2,1)S(1)} %collective-permute-done.16.refs_3_, ...), custom_call_target="tpu_custom_call" | custom-call | bytes 6553600 | tf_op jit(solution)/shard_map/last_product/pallas_call | solution.py:51
  (37 shorter events, 3.5 us)
Async XLA Ops:
  1.0 12.3 %collective-permute-start = (bf16[256,512]{1,0:T(8,128)(2,1)S(1)}, bf16[256,512]{1,0:T(8,128)(2,1)S(1)}, u32[]{:S(2)}, u32[]{:S(2)}) collective-permute-start(bf16[256,512]{1,0:T(8,128)(2,1)S(1)} %bitcast.5), channel_id=1, source_target_pairs={{0,4},{4,8},{8,12},{12,0},{1,5},{5,9},{9,13},{13,1},{2,6},{6,10},{... | collective-permute-start | bytes 786440 | tf_op jit(solution)/shard_map/ppermute | solution.py:298
  4.0 9.2 %collective-permute-start.3 = (bf16[1024,128]{1,0:T(8,128)(2,1)}, bf16[1024,128]{1,0:T(8,128)(2,1)S(1)}, u32[]{:S(2)}, u32[]{:S(2)}) collective-permute-start(bf16[1024,128]{1,0:T(8,128)(2,1)} %refs_2_.1), channel_id=1, source_target_pairs={{0,2},{1,3},{2,0},{3,1},{4,6},{5,7},{6,4},{7,5},{8,10},{9,11},{10,... | collective-permute-start | bytes 786440 | tf_op jit(solution)/shard_map/ppermute | solution.py:321
  5.6 13.4 %collective-permute-start.1 = (bf16[256,512]{1,0:T(8,128)(2,1)S(1)}, bf16[256,512]{1,0:T(8,128)(2,1)S(1)}, u32[]{:S(2)}, u32[]{:S(2)}) collective-permute-start(bf16[256,512]{1,0:T(8,128)(2,1)S(1)} %bitcast.6), channel_id=1, source_target_pairs={{0,12},{4,0},{8,4},{12,8},{1,13},{5,1},{9,5},{13,9},{2,14},{6,2},{... | collective-permute-start | bytes 786440 | tf_op jit(solution)/shard_map/ppermute | solution.py:300
  7.8 11.2 %collective-permute-start.6 = (bf16[1024,128]{1,0:T(8,128)(2,1)}, bf16[1024,128]{1,0:T(8,128)(2,1)S(1)}, u32[]{:S(2)}, u32[]{:S(2)}) collective-permute-start(bf16[1024,128]{1,0:T(8,128)(2,1)} %refs_2_.1), channel_id=1, source_target_pairs={{0,1},{1,0},{2,3},{3,2},{4,5},{5,4},{6,7},{7,6},{8,9},{9,8},{10,11... | collective-permute-start | bytes 786440 | tf_op jit(solution)/shard_map/ppermute | solution.py:322
  7.8 11.2 %collective-permute-start.4 = (bf16[1024,128]{1,0:T(8,128)(2,1)}, bf16[1024,128]{1,0:T(8,128)(2,1)S(1)}, u32[]{:S(2)}, u32[]{:S(2)}) collective-permute-start(bf16[1024,128]{1,0:T(8,128)(2,1)} %refs_2_.1), channel_id=1, source_target_pairs={{0,16},{16,0},{1,17},{17,1},{2,18},{18,2},{3,19},{19,3},{4,20},{20... | collective-permute-start | bytes 786440 | tf_op jit(solution)/shard_map/ppermute | solution.py:321
  13.3 9.1 %collective-permute-start.5 = (bf16[1024,128]{1,0:T(8,128)(2,1)S(1)}, bf16[1024,128]{1,0:T(8,128)(2,1)S(1)}, u32[]{:S(2)}, u32[]{:S(2)}) collective-permute-start(bf16[1024,128]{1,0:T(8,128)(2,1)S(1)} %pack.5), channel_id=1, source_target_pairs={{0,16},{16,0},{1,17},{17,1},{2,18},{18,2},{3,19},{19,3},{4,20},{20... | collective-permute-start | bytes 786440 | tf_op jit(solution)/shard_map/ppermute | solution.py:321
  15.1 0.9 %copy-start.1 = (bf16[1024,128]{1,0:T(8,128)(2,1)S(1)}, bf16[1024,128]{1,0:T(8,128)(2,1)}, u32[]{:S(2)}) copy-start(bf16[1024,128]{1,0:T(8,128)(2,1)} %refs_2_.1) | copy-start | bytes 786436
  16.0 0.7 %copy-start.2 = (s32[8,8]{1,0:T(8,128)S(1)}, s32[8,8]{1,0:T(8,128)}, u32[]{:S(2)}) copy-start(s32[8,8]{1,0:T(8,128)} %refs_0_.1) | copy-start | bytes 772
  16.7 0.7 %copy-start.3 = (s32[8,8]{1,0:T(8,128)S(1)}, s32[8,8]{1,0:T(8,128)}, u32[]{:S(2)}) copy-start(s32[8,8]{1,0:T(8,128)} %refs_1_.2) | copy-start | bytes 772
  18.8 10.6 %collective-permute-start.7 = (bf16[256,512]{1,0:T(8,128)(2,1)S(1)}, bf16[256,512]{1,0:T(8,128)(2,1)S(1)}, u32[]{:S(2)}, u32[]{:S(2)}) collective-permute-start(bf16[256,512]{1,0:T(8,128)(2,1)S(1)} %collective-permute-done.refs_0_.refs_1_.refs_7_), channel_id=1, source_target_pairs={{0,4},{4,8},{8,12},{12,0},{1,5},{5,9},{9,13},{13,1},{2,6},{6,10},{... | collective-permute-start | bytes 786440 | tf_op jit(solution)/shard_map/ppermute | solution.py:298
  23.6 26.1 %copy-start = (bf16[1024,512]{1,0:T(8,128)(2,1)S(1)}, bf16[1024,512]{1,0:T(8,128)(2,1)}, u32[]{:S(2)}) copy-start(bf16[1024,512]{1,0:T(8,128)(2,1)} %refs_1_.3) | copy-start | bytes 3145732
  23.6 5.8 %collective-permute-start.10 = (bf16[1024,128]{1,0:T(8,128)(2,1)S(1)}, bf16[1024,128]{1,0:T(8,128)(2,1)S(1)}, u32[]{:S(2)}, u32[]{:S(2)}) collective-permute-start(bf16[1024,128]{1,0:T(8,128)(2,1)S(1)} %get-tuple-element.28), channel_id=1, source_target_pairs={{0,1},{1,0},{2,3},{3,2},{4,5},{5,4},{6,7},{7,6},{8,9},{9,8},{10,11... | collective-permute-start | bytes 786440 | tf_op jit(solution)/shard_map/ppermute | solution.py:338
  23.7 5.8 %collective-permute-start.8 = (bf16[1024,128]{1,0:T(8,128)(2,1)S(1)}, bf16[1024,128]{1,0:T(8,128)(2,1)S(1)}, u32[]{:S(2)}, u32[]{:S(2)}) collective-permute-start(bf16[1024,128]{1,0:T(8,128)(2,1)S(1)} %get-tuple-element.26), channel_id=1, source_target_pairs={{0,1},{1,0},{2,3},{3,2},{4,5},{5,4},{6,7},{7,6},{8,9},{9,8},{10,11... | collective-permute-start | bytes 786440 | tf_op jit(solution)/shard_map/ppermute | solution.py:338
  24.2 5.3 %collective-permute-start.9 = (bf16[1024,128]{1,0:T(8,128)(2,1)S(1)}, bf16[1024,128]{1,0:T(8,128)(2,1)S(1)}, u32[]{:S(2)}, u32[]{:S(2)}) collective-permute-start(bf16[1024,128]{1,0:T(8,128)(2,1)S(1)} %get-tuple-element.27), channel_id=1, source_target_pairs={{0,1},{1,0},{2,3},{3,2},{4,5},{5,4},{6,7},{7,6},{8,9},{9,8},{10,11... | collective-permute-start | bytes 786440 | tf_op jit(solution)/shard_map/ppermute | solution.py:338
  24.3 15.9 %collective-permute-start.2 = (bf16[512,512]{1,0:T(8,128)(2,1)S(1)}, bf16[512,512]{1,0:T(8,128)(2,1)S(1)}, u32[]{:S(2)}, u32[]{:S(2)}) collective-permute-start(bf16[512,512]{1,0:T(8,128)(2,1)S(1)} %pack.4.refs_10_.refs_0_.refs_2_), channel_id=1, source_target_pairs={{0,2},{1,3},{2,0},{3,1},{4,6},{5,7},{6,4},{7,5},{8,10},{9,11},{10,... | collective-permute-start | bytes 1572872 | tf_op jit(solution)/shard_map/ppermute | solution.py:304
  31.3 1.6 %collective-permute-start.12 = (bf16[256,512]{1,0:T(8,128)(2,1)S(1)}, bf16[256,512]{1,0:T(8,128)(2,1)S(1)}, u32[]{:S(2)}, u32[]{:S(2)}) collective-permute-start(bf16[256,512]{1,0:T(8,128)(2,1)S(1)} %pack.6.refs_5_), channel_id=1, source_target_pairs={{0,1},{1,0},{2,3},{3,2},{4,5},{5,4},{6,7},{7,6},{8,9},{9,8},{10,11... | collective-permute-start | bytes 786440 | tf_op jit(solution)/shard_map/ppermute | solution.py:361
  31.4 8.7 %collective-permute-start.11 = (bf16[256,512]{1,0:T(8,128)(2,1)S(1)}, bf16[256,512]{1,0:T(8,128)(2,1)S(1)}, u32[]{:S(2)}, u32[]{:S(2)}) collective-permute-start(bf16[256,512]{1,0:T(8,128)(2,1)S(1)} %first_product.1.refs_1_.refs_0_), channel_id=1, source_target_pairs={{0,16},{16,0},{1,17},{17,1},{2,18},{18,2},{3,19},{19,3},{4,20},{20... | collective-permute-start | bytes 786440 | tf_op jit(solution)/shard_map/ppermute | solution.py:355
  40.3 8.9 %collective-permute-start.13 = (bf16[1024,512]{1,0:T(8,128)(2,1)S(1)}, bf16[1024,512]{1,0:T(8,128)(2,1)S(1)}, u32[]{:S(2)}, u32[]{:S(2)}) collective-permute-start(bf16[1024,512]{1,0:T(8,128)(2,1)S(1)} %pack.7), channel_id=1, source_target_pairs={{0,1},{1,0},{2,3},{3,2},{4,5},{5,4},{6,7},{7,6},{8,9},{9,8},{10,11... | collective-permute-start | bytes 3145736 | tf_op jit(solution)/shard_map/ppermute | solution.py:374
  40.4 8.7 %collective-permute-start.14 = (bf16[256,512]{1,0:T(8,128)(2,1)S(1)}, bf16[256,512]{1,0:T(8,128)(2,1)S(1)}, u32[]{:S(2)}, u32[]{:S(2)}) collective-permute-start(bf16[256,512]{1,0:T(8,128)(2,1)S(1)} %pack.6.refs_5_), channel_id=1, source_target_pairs={{0,2},{1,3},{2,0},{3,1},{4,6},{5,7},{6,4},{7,5},{8,10},{9,11},{10,... | collective-permute-start | bytes 786440 | tf_op jit(solution)/shard_map/ppermute | solution.py:304
  42.0 9.1 %collective-permute-start.15 = (bf16[128,512]{1,0:T(8,128)(2,1)S(1)}, bf16[128,512]{1,0:T(8,128)(2,1)S(1)}, u32[]{:S(2)}, u32[]{:S(2)}) collective-permute-start(bf16[128,512]{1,0:T(8,128)(2,1)S(1)} %get-tuple-element.34), channel_id=1, source_target_pairs={{0,12},{4,8},{8,4},{12,0},{1,13},{5,9},{9,5},{13,1},{2,14},{6,10},... | collective-permute-start | bytes 393224 | tf_op jit(solution)/shard_map/ppermute | solution.py:371
  44.1 12.0 %collective-permute-start.16 = (bf16[128,512]{1,0:T(8,128)(2,1)S(1)}, bf16[128,512]{1,0:T(8,128)(2,1)S(1)}, u32[]{:S(2)}, u32[]{:S(2)}) collective-permute-start(bf16[128,512]{1,0:T(8,128)(2,1)S(1)} %get-tuple-element.35), channel_id=1, source_target_pairs={{0,8},{4,12},{8,0},{12,4},{1,9},{5,13},{9,1},{13,5},{2,10},{6,14},... | collective-permute-start | bytes 393224 | tf_op jit(solution)/shard_map/ppermute | solution.py:371
  44.2 12.0 %collective-permute-start.17 = (bf16[128,512]{1,0:T(8,128)(2,1)S(1)}, bf16[128,512]{1,0:T(8,128)(2,1)S(1)}, u32[]{:S(2)}, u32[]{:S(2)}) collective-permute-start(bf16[128,512]{1,0:T(8,128)(2,1)S(1)} %get-tuple-element.36), channel_id=1, source_target_pairs={{0,4},{4,0},{8,12},{12,8},{1,5},{5,1},{9,13},{13,9},{2,6},{6,2},{1... | collective-permute-start | bytes 393224 | tf_op jit(solution)/shard_map/ppermute | solution.py:371
  49.1 7.0 %collective-permute-start.18 = (bf16[128,512]{1,0:T(8,128)(2,1)S(1)}, bf16[128,512]{1,0:T(8,128)(2,1)S(1)}, u32[]{:S(2)}, u32[]{:S(2)}) collective-permute-start(bf16[128,512]{1,0:T(8,128)(2,1)S(1)} %get-tuple-element.37), channel_id=1, source_target_pairs={{0,1},{1,0},{2,3},{3,2},{4,5},{5,4},{6,7},{7,6},{8,9},{9,8},{10,11... | collective-permute-start | bytes 393224 | tf_op jit(solution)/shard_map/ppermute | solution.py:383
  49.2 6.9 %collective-permute-start.19 = (bf16[128,512]{1,0:T(8,128)(2,1)S(1)}, bf16[128,512]{1,0:T(8,128)(2,1)S(1)}, u32[]{:S(2)}, u32[]{:S(2)}) collective-permute-start(bf16[128,512]{1,0:T(8,128)(2,1)S(1)} %get-tuple-element.38), channel_id=1, source_target_pairs={{0,1},{1,0},{2,3},{3,2},{4,5},{5,4},{6,7},{7,6},{8,9},{9,8},{10,11... | collective-permute-start | bytes 393224 | tf_op jit(solution)/shard_map/ppermute | solution.py:383

commit v16 on v14

--- a/solution.py
+++ b/solution.py
@@ -298,8 +298,8 @@
         perm = flip(rows if axis == "row" else layers, bit)
         for piece, (dr, dl) in list(zip(h_pieces, h_table)):
             h_table.append((dr ^ bit, dl) if axis == "row" else (dr, dl ^ bit))
-            if dl and axis == 'row':
-                piece = pack([piece], [slots[1]])
+            if False:
+                piece = pack([piece], [])
             h_pieces.append(lax.ppermute(piece, axis, perm))
     zm, *h_own = run(
         functools.partial(bring_kernel, sizes, h_table),

time: 57.3 us -> 55.6 us (0.970)
  starting transfers between devices: 20.5 us -> 18.8 us
    ppermute x2, waiting for transfers between devices: 2.92 us -> 5.18 us  [cross(): return lax.ppermute(piece, 'layer', flip(layers, layer_bits[0]))]
    ppermute x3, waiting for transfers between devices: 6.18 us -> 4.52 us  [local(): lax.ppermute(outgoing[d], 'col', flip(cols, d))]
    ppermute x2, starting transfers between devices: 3.17 us -> 1.63 us  [local(): lax.ppermute(right, 'col', [(i, (i + 1) % cols) for i in range(cols)])]
    ppermute x3, starting transfers between devices: 5.83 us -> 4.39 us  [local(): lax.ppermute(outgoing[d], 'col', flip(cols, d))]
    ppermute x3, starting transfers between devices: 4.81 us -> 6.17 us  [local(): h_pieces.append(lax.ppermute(piece, axis, perm))]
    ppermute x2, starting transfers between devices: 2.09 us -> 1.08 us  [cross(): return lax.ppermute(piece, 'layer', flip(layers, layer_bits[0]))]
    ppermute x1, starting transfers between devices: 0.59 us -> 1.54 us  [local(): gathered[dr ^ bit] = lax.ppermute(piece, 'row', flip(rows, bit))]
    ppermute x1, waiting for transfers between devices: 0.93 us -> 0.01 us  [local(): last_low = lax.ppermute(last, 'layer', flip(layers, low))]
  transfers between devices with their start and end apart: 20 -> 20, of which waited for: 8 -> 9; matrix products, arithmetic and copies ran while one was open for 0% -> 2% of each run, Pallas kernels for 11% -> 11%
where the time goes in v16:
time: 55.6 us; the launch traced here: 55.4 us
  waiting for transfers between devices  24.8 us (45%)
  starting transfers between devices  18.8 us (34%)
  Pallas kernels  8.29 us (15%)
  local copies, waits for them, and re-layouts  3.29 us (6%)
    pallas_call x11, Pallas kernels, run(): pl.pallas_call(body, out_shape=list(outs), in_specs=[pl.BlockSpec(memory_...  8.29 us
    ppermute x1, waiting for transfers between devices, local(): gathered[dr ^ bit] = lax.ppermute(piece, 'row', flip(rows, bit))  7.18 us
    ppermute x3, starting transfers between devices, local(): h_pieces.append(lax.ppermute(piece, axis, perm))  6.17 us
    ppermute x2, waiting for transfers between devices, local(): lax.ppermute(right, 'col', [(i, (i + 1) % cols) for i in range(cols)])  5.57 us
    ppermute x2, waiting for transfers between devices, cross(): return lax.ppermute(piece, 'layer', flip(layers, layer_bits[0]))  5.18 us
    ppermute x3, waiting for transfers between devices, local(): lax.ppermute(outgoing[d], 'col', flip(cols, d))  4.52 us
    ppermute x3, starting transfers between devices, local(): lax.ppermute(outgoing[d], 'col', flip(cols, d))  4.39 us
    unnamed x8, local copies, waits for them, and re-layouts  2.33 us
  transfers between devices with their start and end apart: 20, of which 9 were waited for; matrix products, arithmetic and copies ran while one was open for 2% of the time, Pallas kernels for 11%

profile of v16, /device:TPU:0, one launch (start us, length us, event | category | flops | bytes accessed | tf_op | source)
XLA Modules:
  0.0 55.4 jit_solution(17122373711028821918)
XLA Ops:
  0.0 3.0 %collective-permute-start.3 = (bf16[1024,128]{1,0:T(8,128)(2,1)}, bf16[1024,128]{1,0:T(8,128)(2,1)S(1)}, u32[]{:S(2)}, u32[]{:S(2)}) collective-permute-start(bf16[1024,128]{1,0:T(8,128)(2,1)} %refs_2_.1), channel_id=1, source_target_pairs={{0,2},{1,3},{2,0},{3,1},{4,6},{5,7},{6,4},{7,5},{8,10},{9,11},{10,... | collective-permute-start | bytes 786440 | tf_op jit(solution)/shard_map/ppermute | solution.py:303
  3.0 1.0 %constant_dynamic-slice_fusion = bf16[2,1,128,512]{3,2,1,0:T(8,128)(2,1)S(1)} fusion(bf16[2,4,128,512]{3,2,1,0:T(8,128)(2,1)} %bitcast.4, s32[]{:T(128)S(6)} %select_n.4), kind=kLoop, calls=%fused_computation | loop fusion | bytes 524292 | tf_op jit(solution)/shard_map/jit(dynamic_index_in_dim)/dynamic_slice | solution.py:275
  3.9 1.6 %collective-permute-start = (bf16[256,512]{1,0:T(8,128)(2,1)S(1)}, bf16[256,512]{1,0:T(8,128)(2,1)S(1)}, u32[]{:S(2)}, u32[]{:S(2)}) collective-permute-start(bf16[256,512]{1,0:T(8,128)(2,1)S(1)} %bitcast.5), channel_id=1, source_target_pairs={{0,4},{4,8},{8,12},{12,0},{1,5},{5,9},{9,13},{13,1},{2,6},{6,10},{... | collective-permute-start | bytes 786440 | tf_op jit(solution)/shard_map/ppermute | solution.py:280
  5.6 2.2 %collective-permute-start.1 = (bf16[256,512]{1,0:T(8,128)(2,1)S(1)}, bf16[256,512]{1,0:T(8,128)(2,1)S(1)}, u32[]{:S(2)}, u32[]{:S(2)}) collective-permute-start(bf16[256,512]{1,0:T(8,128)(2,1)S(1)} %bitcast.6), channel_id=1, source_target_pairs={{0,12},{4,0},{8,4},{12,8},{1,13},{5,1},{9,5},{13,9},{2,14},{6,2},{... | collective-permute-start | bytes 786440 | tf_op jit(solution)/shard_map/ppermute | solution.py:282
  7.8 1.5 %collective-permute-start.4 = (bf16[1024,128]{1,0:T(8,128)(2,1)}, bf16[1024,128]{1,0:T(8,128)(2,1)S(1)}, u32[]{:S(2)}, u32[]{:S(2)}) collective-permute-start(bf16[1024,128]{1,0:T(8,128)(2,1)} %refs_2_.1), channel_id=1, source_target_pairs={{0,16},{16,0},{1,17},{17,1},{2,18},{18,2},{3,19},{19,3},{4,20},{20... | collective-permute-start | bytes 786440 | tf_op jit(solution)/shard_map/ppermute | solution.py:303
  9.5 1.7 %collective-permute-start.5 = (bf16[1024,128]{1,0:T(8,128)(2,1)S(1)}, bf16[1024,128]{1,0:T(8,128)(2,1)S(1)}, u32[]{:S(2)}, u32[]{:S(2)}) collective-permute-start(bf16[1024,128]{1,0:T(8,128)(2,1)S(1)} %collective-permute-done.3.refs_3_), channel_id=1, source_target_pairs={{0,16},{16,0},{1,17},{17,1},{2,18},{18,2},{3,19},{19,3},{4,20},{20... | collective-permute-start | bytes 786440 | tf_op jit(solution)/shard_map/ppermute | solution.py:303
  11.2 3.9 %collective-permute-done.refs_0_.refs_7_ = bf16[256,512]{1,0:T(8,128)(2,1)S(1)} collective-permute-done((bf16[256,512]{1,0:T(8,128)(2,1)S(1)}, bf16[256,512]{1,0:T(8,128)(2,1)S(1)}, u32[]{:S(2)}, u32[]{:S(2)}) %collective-permute-start) | collective-permute-done | bytes 262176 | tf_op jit(solution)/shard_map/ppermute | solution.py:280
  15.1 0.9 %copy-done.1 = bf16[1024,128]{1,0:T(8,128)(2,1)S(1)} copy-done((bf16[1024,128]{1,0:T(8,128)(2,1)S(1)}, bf16[1024,128]{1,0:T(8,128)(2,1)}, u32[]{:S(2)}) %copy-start.1) | copy-done | bytes 262168
  17.4 1.4 %fetch.1 = (s32[8,8]{1,0:T(8,128)S(1)}, s32[8,8]{1,0:T(8,128)S(1)}, bf16[1024,128]{1,0:T(8,128)(2,1)S(1)}) custom-call(s32[8,8]{1,0:T(8,128)S(1)} %copy-done.2, s32[8,8]{1,0:T(8,128)S(1)} %copy-done.3, bf16[1024,128]{1,0:T(8,128)(2,1)S(1)} %copy-done.1), custom_call_target="tpu_custom_call" | custom-call | bytes 524800 | tf_op jit(solution)/shard_map/fetch/pallas_call | solution.py:51
  19.5 1.5 %collective-permute-done.5.refs_5_ = bf16[1024,128]{1,0:T(8,128)(2,1)S(1)} collective-permute-done((bf16[1024,128]{1,0:T(8,128)(2,1)S(1)}, bf16[1024,128]{1,0:T(8,128)(2,1)S(1)}, u32[]{:S(2)}, u32[]{:S(2)}) %collective-permute-start.5) | collective-permute-done | bytes 262176 | tf_op jit(solution)/shard_map/ppermute | solution.py:303
  21.0 1.1 %bring.1 = (bf16[256,2048]{1,0:T(8,128)(2,1)S(1)}, bf16[512,256]{1,0:T(8,128)(2,1)S(1)}, bf16[512,256]{1,0:T(8,128)(2,1)S(1)}, bf16[512,256]{1,0:T(8,128)(2,1)S(1)}, bf16[512,256]{1,0:T(8,128)(2,1)S(1)}) custom-call(s32[8,8]{1,0:T(8,128)S(1)} %get-tuple-element.20.refs_0_, s32[8,8]{1,0:T(8,128)S(1)} %get-tuple-element.19.refs_1_.refs_0_, ...), custom_call_target="tpu_custom_call" | custom-call | bytes 3932160 | tf_op jit(solution)/shard_map/bring/pallas_call | solution.py:51
  23.2 1.7 %collective-permute-done.6.refs_2_.refs_0_ = bf16[256,512]{1,0:T(8,128)(2,1)S(1)} collective-permute-done((bf16[256,512]{1,0:T(8,128)(2,1)S(1)}, bf16[256,512]{1,0:T(8,128)(2,1)S(1)}, u32[]{:S(2)}, u32[]{:S(2)}) %collective-permute-start.6) | collective-permute-done | bytes 262176 | tf_op jit(solution)/shard_map/ppermute | solution.py:280
  25.4 1.4 %first_product.1.refs_1_.refs_0_ = bf16[256,512]{1,0:T(8,128)(2,1)S(1)} custom-call(s32[8,8]{1,0:T(8,128)S(1)} %get-tuple-element.19.refs_1_.refs_0_, bf16[256,2048]{1,0:T(8,128)(2,1)S(1)} %get-tuple-element.22.refs_1_, bf16[256,512]{1,0:T(8,128)(2,1)S(1)} %collective-permute-done.6.refs_2_.refs_0_, bf16[512,256]{1,0:T(8,128)(2,1)S(1)} %get-tuple-element.23.refs_3_, ...), custom_call_target="tpu_custom_call" | custom-call | bytes 4718592 | tf_op jit(solution)/shard_map/first_product/pallas_call | solution.py:51
  26.9 1.5 %collective-permute-start.11 = (bf16[256,512]{1,0:T(8,128)(2,1)S(1)}, bf16[256,512]{1,0:T(8,128)(2,1)S(1)}, u32[]{:S(2)}, u32[]{:S(2)}) collective-permute-start(bf16[256,512]{1,0:T(8,128)(2,1)S(1)} %first_product.1.refs_1_.refs_0_), channel_id=1, source_target_pairs={{0,16},{16,0},{1,17},{17,1},{2,18},{18,2},{3,19},{19,3},{4,20},{20... | collective-permute-start | bytes 786440 | tf_op jit(solution)/shard_map/ppermute | solution.py:324
  28.5 7.2 %collective-permute-done.11.refs_1_ = bf16[256,512]{1,0:T(8,128)(2,1)S(1)} collective-permute-done((bf16[256,512]{1,0:T(8,128)(2,1)S(1)}, bf16[256,512]{1,0:T(8,128)(2,1)S(1)}, u32[]{:S(2)}, u32[]{:S(2)}) %collective-permute-start.11) | collective-permute-done | bytes 262176 | tf_op jit(solution)/shard_map/ppermute | solution.py:324
  35.8 1.4 %collective-permute-done.2.refs_1_.refs_3_ = bf16[512,512]{1,0:T(8,128)(2,1)S(1)} collective-permute-done((bf16[512,512]{1,0:T(8,128)(2,1)S(1)}, bf16[512,512]{1,0:T(8,128)(2,1)S(1)}, u32[]{:S(2)}, u32[]{:S(2)}) %collective-permute-start.2) | collective-permute-done | bytes 524320 | tf_op jit(solution)/shard_map/ppermute | solution.py:286
  37.9 2.5 %collective-permute-start.15 = (bf16[128,512]{1,0:T(8,128)(2,1)S(1)}, bf16[128,512]{1,0:T(8,128)(2,1)S(1)}, u32[]{:S(2)}, u32[]{:S(2)}) collective-permute-start(bf16[128,512]{1,0:T(8,128)(2,1)S(1)} %get-tuple-element.28), channel_id=1, source_target_pairs={{0,12},{4,8},{8,4},{12,0},{1,13},{5,9},{9,5},{13,1},{2,14},{6,10},... | collective-permute-start | bytes 393224 | tf_op jit(solution)/shard_map/ppermute | solution.py:340
  40.4 0.9 %collective-permute-start.16 = (bf16[128,512]{1,0:T(8,128)(2,1)S(1)}, bf16[128,512]{1,0:T(8,128)(2,1)S(1)}, u32[]{:S(2)}, u32[]{:S(2)}) collective-permute-start(bf16[128,512]{1,0:T(8,128)(2,1)S(1)} %get-tuple-element.29), channel_id=1, source_target_pairs={{0,8},{4,12},{8,0},{12,4},{1,9},{5,13},{9,1},{13,5},{2,10},{6,14},... | collective-permute-start | bytes 393224 | tf_op jit(solution)/shard_map/ppermute | solution.py:340
  41.3 1.0 %collective-permute-start.17 = (bf16[128,512]{1,0:T(8,128)(2,1)S(1)}, bf16[128,512]{1,0:T(8,128)(2,1)S(1)}, u32[]{:S(2)}, u32[]{:S(2)}) collective-permute-start(bf16[128,512]{1,0:T(8,128)(2,1)S(1)} %get-tuple-element.30), channel_id=1, source_target_pairs={{0,4},{4,0},{8,12},{12,8},{1,5},{5,1},{9,13},{13,9},{2,6},{6,2},{1... | collective-permute-start | bytes 393224 | tf_op jit(solution)/shard_map/ppermute | solution.py:340
  42.3 3.8 %collective-permute-done.14.refs_7_.refs_0_ = bf16[256,512]{1,0:T(8,128)(2,1)S(1)} collective-permute-done((bf16[256,512]{1,0:T(8,128)(2,1)S(1)}, bf16[256,512]{1,0:T(8,128)(2,1)S(1)}, u32[]{:S(2)}, u32[]{:S(2)}) %collective-permute-start.14) | collective-permute-done | bytes 262176 | tf_op jit(solution)/shard_map/ppermute | solution.py:286
  46.7 1.4 %layers.1.refs_0_.refs_1_ = bf16[1024,2048]{1,0:T(8,128)(2,1)S(1)} custom-call(s32[8,8]{1,0:T(8,128)S(1)} %get-tuple-element.19.refs_1_.refs_0_, bf16[1024,512]{1,0:T(8,128)(2,1)S(1)} %copy-done, bf16[512,512]{1,0:T(8,128)(2,1)S(1)} %pack.3.refs_0_.refs_2_, bf16[512,512]{1,0:T(8,128)(2,1)S(1)} %collective-permute-done.2.refs_1_.refs_3_, ...), custom_call_target="tpu_custom_call" | custom-call | bytes 8126464 | tf_op jit(solution)/shard_map/layers/pallas_call | solution.py:51
  48.0 0.7 %second_product.1.refs_2_ = f32[1024,128]{1,0:T(8,128)S(1)} custom-call(bf16[1024,2048]{1,0:T(8,128)(2,1)S(1)} %layers.1.refs_0_.refs_1_, bf16[128,512]{1,0:T(8,128)(2,1)S(1)} %get-tuple-element.27.refs_2_.refs_1_, bf16[128,512]{1,0:T(8,128)(2,1)S(1)} %collective-permute-done.15.refs_2_), custom_call_target="tpu_custom_call" | custom-call | bytes 4980736 | tf_op jit(solution)/shard_map/second_product/pallas_call | solution.py:51
  48.7 4.5 %collective-permute-done.16.refs_3_ = bf16[128,512]{1,0:T(8,128)(2,1)S(1)} collective-permute-done((bf16[128,512]{1,0:T(8,128)(2,1)S(1)}, bf16[128,512]{1,0:T(8,128)(2,1)S(1)}, u32[]{:S(2)}, u32[]{:S(2)}) %collective-permute-start.16) | collective-permute-done | bytes 131104 | tf_op jit(solution)/shard_map/ppermute | solution.py:340
  53.3 2.1 %last_product.1 = bf16[1024,128]{1,0:T(8,128)(2,1)} custom-call(s32[8,8]{1,0:T(8,128)S(1)} %get-tuple-element.19.refs_1_.refs_0_, bf16[1024,2048]{1,0:T(8,128)(2,1)S(1)} %layers.1.refs_0_.refs_1_, f32[1024,128]{1,0:T(8,128)S(1)} %second_product.1.refs_2_, bf16[128,512]{1,0:T(8,128)(2,1)S(1)} %collective-permute-done.16.refs_3_, ...), custom_call_target="tpu_custom_call" | custom-call | bytes 6553600 | tf_op jit(solution)/shard_map/last_product/pallas_call | solution.py:51
  (36 shorter events, 5.3 us)
Async XLA Ops:
  0.0 9.5 %collective-permute-start.3 = (bf16[1024,128]{1,0:T(8,128)(2,1)}, bf16[1024,128]{1,0:T(8,128)(2,1)S(1)}, u32[]{:S(2)}, u32[]{:S(2)}) collective-permute-start(bf16[1024,128]{1,0:T(8,128)(2,1)} %refs_2_.1), channel_id=1, source_target_pairs={{0,2},{1,3},{2,0},{3,1},{4,6},{5,7},{6,4},{7,5},{8,10},{9,11},{10,... | collective-permute-start | bytes 786440 | tf_op jit(solution)/shard_map/ppermute | solution.py:303
  3.9 11.1 %collective-permute-start = (bf16[256,512]{1,0:T(8,128)(2,1)S(1)}, bf16[256,512]{1,0:T(8,128)(2,1)S(1)}, u32[]{:S(2)}, u32[]{:S(2)}) collective-permute-start(bf16[256,512]{1,0:T(8,128)(2,1)S(1)} %bitcast.5), channel_id=1, source_target_pairs={{0,4},{4,8},{8,12},{12,0},{1,5},{5,9},{9,13},{13,1},{2,6},{6,10},{... | collective-permute-start | bytes 786440 | tf_op jit(solution)/shard_map/ppermute | solution.py:280
  5.6 13.9 %collective-permute-start.1 = (bf16[256,512]{1,0:T(8,128)(2,1)S(1)}, bf16[256,512]{1,0:T(8,128)(2,1)S(1)}, u32[]{:S(2)}, u32[]{:S(2)}) collective-permute-start(bf16[256,512]{1,0:T(8,128)(2,1)S(1)} %bitcast.6), channel_id=1, source_target_pairs={{0,12},{4,0},{8,4},{12,8},{1,13},{5,1},{9,5},{13,9},{2,14},{6,2},{... | collective-permute-start | bytes 786440 | tf_op jit(solution)/shard_map/ppermute | solution.py:282
  7.8 11.6 %collective-permute-start.4 = (bf16[1024,128]{1,0:T(8,128)(2,1)}, bf16[1024,128]{1,0:T(8,128)(2,1)S(1)}, u32[]{:S(2)}, u32[]{:S(2)}) collective-permute-start(bf16[1024,128]{1,0:T(8,128)(2,1)} %refs_2_.1), channel_id=1, source_target_pairs={{0,16},{16,0},{1,17},{17,1},{2,18},{18,2},{3,19},{19,3},{4,20},{20... | collective-permute-start | bytes 786440 | tf_op jit(solution)/shard_map/ppermute | solution.py:303
  9.5 11.5 %collective-permute-start.5 = (bf16[1024,128]{1,0:T(8,128)(2,1)S(1)}, bf16[1024,128]{1,0:T(8,128)(2,1)S(1)}, u32[]{:S(2)}, u32[]{:S(2)}) collective-permute-start(bf16[1024,128]{1,0:T(8,128)(2,1)S(1)} %collective-permute-done.3.refs_3_), channel_id=1, source_target_pairs={{0,16},{16,0},{1,17},{17,1},{2,18},{18,2},{3,19},{19,3},{4,20},{20... | collective-permute-start | bytes 786440 | tf_op jit(solution)/shard_map/ppermute | solution.py:303
  15.1 9.8 %collective-permute-start.6 = (bf16[256,512]{1,0:T(8,128)(2,1)S(1)}, bf16[256,512]{1,0:T(8,128)(2,1)S(1)}, u32[]{:S(2)}, u32[]{:S(2)}) collective-permute-start(bf16[256,512]{1,0:T(8,128)(2,1)S(1)} %collective-permute-done.refs_0_.refs_7_), channel_id=1, source_target_pairs={{0,4},{4,8},{8,12},{12,0},{1,5},{5,9},{9,13},{13,1},{2,6},{6,10},{... | collective-permute-start | bytes 786440 | tf_op jit(solution)/shard_map/ppermute | solution.py:280
  15.1 1.0 %copy-start.1 = (bf16[1024,128]{1,0:T(8,128)(2,1)S(1)}, bf16[1024,128]{1,0:T(8,128)(2,1)}, u32[]{:S(2)}) copy-start(bf16[1024,128]{1,0:T(8,128)(2,1)} %refs_2_.1) | copy-start | bytes 786436
  16.0 0.7 %copy-start.2 = (s32[8,8]{1,0:T(8,128)S(1)}, s32[8,8]{1,0:T(8,128)}, u32[]{:S(2)}) copy-start(s32[8,8]{1,0:T(8,128)} %refs_0_.1) | copy-start | bytes 772
  16.7 0.7 %copy-start.3 = (s32[8,8]{1,0:T(8,128)S(1)}, s32[8,8]{1,0:T(8,128)}, u32[]{:S(2)}) copy-start(s32[8,8]{1,0:T(8,128)} %refs_1_.2) | copy-start | bytes 772
  22.1 3.3 %collective-permute-start.10 = (bf16[512,256]{1,0:T(8,128)(2,1)S(1)}, bf16[512,256]{1,0:T(8,128)(2,1)S(1)}, u32[]{:S(2)}, u32[]{:S(2)}) collective-permute-start(bf16[512,256]{1,0:T(8,128)(2,1)S(1)} %get-tuple-element.26.refs_6_), channel_id=1, source_target_pairs={{0,1},{1,0},{2,3},{3,2},{4,5},{5,4},{6,7},{7,6},{8,9},{9,8},{10,11... | collective-permute-start | bytes 786440 | tf_op jit(solution)/shard_map/ppermute | solution.py:311
  22.1 3.3 %collective-permute-start.7 = (bf16[512,256]{1,0:T(8,128)(2,1)S(1)}, bf16[512,256]{1,0:T(8,128)(2,1)S(1)}, u32[]{:S(2)}, u32[]{:S(2)}) collective-permute-start(bf16[512,256]{1,0:T(8,128)(2,1)S(1)} %get-tuple-element.23.refs_3_), channel_id=1, source_target_pairs={{0,1},{1,0},{2,3},{3,2},{4,5},{5,4},{6,7},{7,6},{8,9},{9,8},{10,11... | collective-permute-start | bytes 786440 | tf_op jit(solution)/shard_map/ppermute | solution.py:311
  22.6 2.8 %collective-permute-start.8 = (bf16[512,256]{1,0:T(8,128)(2,1)S(1)}, bf16[512,256]{1,0:T(8,128)(2,1)S(1)}, u32[]{:S(2)}, u32[]{:S(2)}) collective-permute-start(bf16[512,256]{1,0:T(8,128)(2,1)S(1)} %get-tuple-element.24.refs_4_), channel_id=1, source_target_pairs={{0,1},{1,0},{2,3},{3,2},{4,5},{5,4},{6,7},{7,6},{8,9},{9,8},{10,11... | collective-permute-start | bytes 786440 | tf_op jit(solution)/shard_map/ppermute | solution.py:311
  22.7 23.9 %copy-start = (bf16[1024,512]{1,0:T(8,128)(2,1)S(1)}, bf16[1024,512]{1,0:T(8,128)(2,1)}, u32[]{:S(2)}) copy-start(bf16[1024,512]{1,0:T(8,128)(2,1)} %refs_1_.3) | copy-start | bytes 3145732
  22.7 2.7 %collective-permute-start.9 = (bf16[512,256]{1,0:T(8,128)(2,1)S(1)}, bf16[512,256]{1,0:T(8,128)(2,1)S(1)}, u32[]{:S(2)}, u32[]{:S(2)}) collective-permute-start(bf16[512,256]{1,0:T(8,128)(2,1)S(1)} %get-tuple-element.25.refs_5_), channel_id=1, source_target_pairs={{0,1},{1,0},{2,3},{3,2},{4,5},{5,4},{6,7},{7,6},{8,9},{9,8},{10,11... | collective-permute-start | bytes 786440 | tf_op jit(solution)/shard_map/ppermute | solution.py:311
  24.9 12.3 %collective-permute-start.2 = (bf16[512,512]{1,0:T(8,128)(2,1)S(1)}, bf16[512,512]{1,0:T(8,128)(2,1)S(1)}, u32[]{:S(2)}, u32[]{:S(2)}) collective-permute-start(bf16[512,512]{1,0:T(8,128)(2,1)S(1)} %pack.3.refs_0_.refs_2_), channel_id=1, source_target_pairs={{0,2},{1,3},{2,0},{3,1},{4,6},{5,7},{6,4},{7,5},{8,10},{9,11},{10,... | collective-permute-start | bytes 1572872 | tf_op jit(solution)/shard_map/ppermute | solution.py:286
  26.9 1.6 %collective-permute-start.12 = (bf16[256,512]{1,0:T(8,128)(2,1)S(1)}, bf16[256,512]{1,0:T(8,128)(2,1)S(1)}, u32[]{:S(2)}, u32[]{:S(2)}) collective-permute-start(bf16[256,512]{1,0:T(8,128)(2,1)S(1)} %pack.4.refs_5_), channel_id=1, source_target_pairs={{0,1},{1,0},{2,3},{3,2},{4,5},{5,4},{6,7},{7,6},{8,9},{9,8},{10,11... | collective-permute-start | bytes 786440 | tf_op jit(solution)/shard_map/ppermute | solution.py:330
  26.9 8.7 %collective-permute-start.11 = (bf16[256,512]{1,0:T(8,128)(2,1)S(1)}, bf16[256,512]{1,0:T(8,128)(2,1)S(1)}, u32[]{:S(2)}, u32[]{:S(2)}) collective-permute-start(bf16[256,512]{1,0:T(8,128)(2,1)S(1)} %first_product.1.refs_1_.refs_0_), channel_id=1, source_target_pairs={{0,16},{16,0},{1,17},{17,1},{2,18},{18,2},{3,19},{19,3},{4,20},{20... | collective-permute-start | bytes 786440 | tf_op jit(solution)/shard_map/ppermute | solution.py:324
  37.2 8.9 %collective-permute-start.13 = (bf16[1024,512]{1,0:T(8,128)(2,1)S(1)}, bf16[1024,512]{1,0:T(8,128)(2,1)S(1)}, u32[]{:S(2)}, u32[]{:S(2)}) collective-permute-start(bf16[1024,512]{1,0:T(8,128)(2,1)S(1)} %pack.5), channel_id=1, source_target_pairs={{0,1},{1,0},{2,3},{3,2},{4,5},{5,4},{6,7},{7,6},{8,9},{9,8},{10,11... | collective-permute-start | bytes 3145736 | tf_op jit(solution)/shard_map/ppermute | solution.py:346
  37.3 8.7 %collective-permute-start.14 = (bf16[256,512]{1,0:T(8,128)(2,1)S(1)}, bf16[256,512]{1,0:T(8,128)(2,1)S(1)}, u32[]{:S(2)}, u32[]{:S(2)}) collective-permute-start(bf16[256,512]{1,0:T(8,128)(2,1)S(1)} %pack.4.refs_5_), channel_id=1, source_target_pairs={{0,2},{1,3},{2,0},{3,1},{4,6},{5,7},{6,4},{7,5},{8,10},{9,11},{10,... | collective-permute-start | bytes 786440 | tf_op jit(solution)/shard_map/ppermute | solution.py:286
  37.9 10.1 %collective-permute-start.15 = (bf16[128,512]{1,0:T(8,128)(2,1)S(1)}, bf16[128,512]{1,0:T(8,128)(2,1)S(1)}, u32[]{:S(2)}, u32[]{:S(2)}) collective-permute-start(bf16[128,512]{1,0:T(8,128)(2,1)S(1)} %get-tuple-element.28), channel_id=1, source_target_pairs={{0,12},{4,8},{8,4},{12,0},{1,13},{5,9},{9,5},{13,1},{2,14},{6,10},... | collective-permute-start | bytes 393224 | tf_op jit(solution)/shard_map/ppermute | solution.py:340
  40.4 12.8 %collective-permute-start.16 = (bf16[128,512]{1,0:T(8,128)(2,1)S(1)}, bf16[128,512]{1,0:T(8,128)(2,1)S(1)}, u32[]{:S(2)}, u32[]{:S(2)}) collective-permute-start(bf16[128,512]{1,0:T(8,128)(2,1)S(1)} %get-tuple-element.29), channel_id=1, source_target_pairs={{0,8},{4,12},{8,0},{12,4},{1,9},{5,13},{9,1},{13,5},{2,10},{6,14},... | collective-permute-start | bytes 393224 | tf_op jit(solution)/shard_map/ppermute | solution.py:340
  41.3 12.0 %collective-permute-start.17 = (bf16[128,512]{1,0:T(8,128)(2,1)S(1)}, bf16[128,512]{1,0:T(8,128)(2,1)S(1)}, u32[]{:S(2)}, u32[]{:S(2)}) collective-permute-start(bf16[128,512]{1,0:T(8,128)(2,1)S(1)} %get-tuple-element.30), channel_id=1, source_target_pairs={{0,4},{4,0},{8,12},{12,8},{1,5},{5,1},{9,13},{13,9},{2,6},{6,2},{1... | collective-permute-start | bytes 393224 | tf_op jit(solution)/shard_map/ppermute | solution.py:340
  46.1 7.2 %collective-permute-start.18 = (bf16[128,512]{1,0:T(8,128)(2,1)S(1)}, bf16[128,512]{1,0:T(8,128)(2,1)S(1)}, u32[]{:S(2)}, u32[]{:S(2)}) collective-permute-start(bf16[128,512]{1,0:T(8,128)(2,1)S(1)} %get-tuple-element.31), channel_id=1, source_target_pairs={{0,1},{1,0},{2,3},{3,2},{4,5},{5,4},{6,7},{7,6},{8,9},{9,8},{10,11... | collective-permute-start | bytes 393224 | tf_op jit(solution)/shard_map/ppermute | solution.py:355
  46.2 7.1 %collective-permute-start.19 = (bf16[128,512]{1,0:T(8,128)(2,1)S(1)}, bf16[128,512]{1,0:T(8,128)(2,1)S(1)}, u32[]{:S(2)}, u32[]{:S(2)}) collective-permute-start(bf16[128,512]{1,0:T(8,128)(2,1)S(1)} %get-tuple-element.32), channel_id=1, source_target_pairs={{0,1},{1,0},{2,3},{3,2},{4,5},{5,4},{6,7},{7,6},{8,9},{9,8},{10,11... | collective-permute-start | bytes 393224 | tf_op jit(solution)/shard_map/ppermute | solution.py:355

commit v17 on v16

--- a/solution.py
+++ b/solution.py
@@ -54,10 +54,7 @@
         in_specs=[pl.BlockSpec(memory_space=pltpu.SMEM)] * len(smem)
         + [pl.BlockSpec(memory_space=pltpu.VMEM)] * len(arrays)
         + [pl.BlockSpec(memory_space=pl.ANY)] * len(after),
-        out_specs=[
-            pl.BlockSpec(memory_space=pltpu.SMEM if o.dtype == jnp.int32 else pltpu.VMEM)
-            for o in outs
-        ],
+        out_specs=[pl.BlockSpec(memory_space=pltpu.VMEM)] * len(outs),
         scratch_shapes=list(scratch),
         compiler_params=pltpu.CompilerParams(vmem_limit_bytes=size + MARGIN),
         cost_estimate=pl.CostEstimate(flops=flops, bytes_accessed=size, transcendentals=0),
@@ -131,11 +128,8 @@
 
 
 def fetch_kernel(hp, zp, h, hp_out, zp_out, h_out):
-    h_out[...] = h[...]
-    for i in range(hp.shape[0]):
-        for j in range(hp.shape[1]):
-            hp_out[i, j] = hp[i, j]
-            zp_out[i, j] = zp[i, j]
+    for ref, out in ((hp, hp_out), (zp, zp_out), (h, h_out)):
+        out[...] = ref[...]
 
 
 def bring_kernel(sizes, h_table, hp, zp, *refs):
@@ -290,8 +284,7 @@
         fetch_kernel,
         "fetch",
         [shape(*h_pattern.shape, jnp.int32)] * 2 + [shape(*hamiltonian.shape)],
-        [hamiltonian],
-        smem=[h_pattern, z_pattern],
+        [h_pattern, z_pattern, hamiltonian],
     )
     h_pieces, h_table = [hamiltonian], [(0, 0)]
     for axis, bit in [("layer", top)] + [("row", b) for b in row_bits]:

time: 55.6 us -> 54.2 us (0.975)
  Pallas kernels: 8.29 us -> 6.89 us
    ppermute x3, waiting for transfers between devices: 4.52 us -> 3.12 us  [local(): lax.ppermute(outgoing[d], 'col', flip(cols, d))]
    ppermute x1, waiting for transfers between devices: 0.65 us -> 2.05 us  [local(): left = lax.ppermute(left, 'col', [(i, (i - 1) % cols) for i in range(cols)])]
    pallas_call x11, Pallas kernels: 8.29 us -> 6.89 us  [run(): pl.pallas_call(body, out_shape=list(outs), in_specs=[pl.BlockSpec(memory_...]
  transfers between devices with their start and end apart: 20 -> 20, of which waited for: 9 -> 9; matrix products, arithmetic and copies ran while one was open for 2% -> 2% of each run, Pallas kernels for 11% -> 9%
where the time goes in v17:
time: 54.2 us; the launch traced here: 54 us
  waiting for transfers between devices  24.8 us (46%)
  starting transfers between devices  18.8 us (35%)
  Pallas kernels  6.89 us (13%)
  local copies, waits for them, and re-layouts  3.29 us (6%)
    ppermute x1, waiting for transfers between devices, local(): gathered[dr ^ bit] = lax.ppermute(piece, 'row', flip(rows, bit))  7.18 us
    pallas_call x11, Pallas kernels, run(): pl.pallas_call(body, out_shape=list(outs), in_specs=[pl.BlockSpec(memory_...  6.89 us
    ppermute x3, starting transfers between devices, local(): h_pieces.append(lax.ppermute(piece, axis, perm))  6.17 us
    ppermute x2, waiting for transfers between devices, local(): lax.ppermute(right, 'col', [(i, (i + 1) % cols) for i in range(cols)])  5.57 us
    ppermute x2, waiting for transfers between devices, cross(): return lax.ppermute(piece, 'layer', flip(layers, layer_bits[0]))  5.18 us
    ppermute x3, starting transfers between devices, local(): lax.ppermute(outgoing[d], 'col', flip(cols, d))  4.39 us
    ppermute x3, waiting for transfers between devices, local(): lax.ppermute(outgoing[d], 'col', flip(cols, d))  3.12 us
    unnamed x8, local copies, waits for them, and re-layouts  2.33 us
  transfers between devices with their start and end apart: 20, of which 9 were waited for; matrix products, arithmetic and copies ran while one was open for 2% of the time, Pallas kernels for 9%

profile of v17, /device:TPU:0, one launch (start us, length us, event | category | flops | bytes accessed | tf_op | source)
XLA Modules:
  0.0 54.0 jit_solution(11662605266893549322)
XLA Ops:
  0.0 3.0 %collective-permute-start.3 = (bf16[1024,128]{1,0:T(8,128)(2,1)}, bf16[1024,128]{1,0:T(8,128)(2,1)S(1)}, u32[]{:S(2)}, u32[]{:S(2)}) collective-permute-start(bf16[1024,128]{1,0:T(8,128)(2,1)} %refs_2_.1), channel_id=1, source_target_pairs={{0,2},{1,3},{2,0},{3,1},{4,6},{5,7},{6,4},{7,5},{8,10},{9,11},{10,... | collective-permute-start | bytes 786440 | tf_op jit(solution)/shard_map/ppermute | solution.py:296
  3.0 1.0 %constant_dynamic-slice_fusion = bf16[2,1,128,512]{3,2,1,0:T(8,128)(2,1)S(1)} fusion(bf16[2,4,128,512]{3,2,1,0:T(8,128)(2,1)} %bitcast.4, s32[]{:T(128)S(6)} %select_n.4), kind=kLoop, calls=%fused_computation | loop fusion | bytes 524292 | tf_op jit(solution)/shard_map/jit(dynamic_index_in_dim)/dynamic_slice | solution.py:269
  3.9 1.6 %collective-permute-start = (bf16[256,512]{1,0:T(8,128)(2,1)S(1)}, bf16[256,512]{1,0:T(8,128)(2,1)S(1)}, u32[]{:S(2)}, u32[]{:S(2)}) collective-permute-start(bf16[256,512]{1,0:T(8,128)(2,1)S(1)} %bitcast.5), channel_id=1, source_target_pairs={{0,4},{4,8},{8,12},{12,0},{1,5},{5,9},{9,13},{13,1},{2,6},{6,10},{... | collective-permute-start | bytes 786440 | tf_op jit(solution)/shard_map/ppermute | solution.py:274
  5.6 2.2 %collective-permute-start.1 = (bf16[256,512]{1,0:T(8,128)(2,1)S(1)}, bf16[256,512]{1,0:T(8,128)(2,1)S(1)}, u32[]{:S(2)}, u32[]{:S(2)}) collective-permute-start(bf16[256,512]{1,0:T(8,128)(2,1)S(1)} %bitcast.6), channel_id=1, source_target_pairs={{0,12},{4,0},{8,4},{12,8},{1,13},{5,1},{9,5},{13,9},{2,14},{6,2},{... | collective-permute-start | bytes 786440 | tf_op jit(solution)/shard_map/ppermute | solution.py:276
  7.8 1.5 %collective-permute-start.4 = (bf16[1024,128]{1,0:T(8,128)(2,1)}, bf16[1024,128]{1,0:T(8,128)(2,1)S(1)}, u32[]{:S(2)}, u32[]{:S(2)}) collective-permute-start(bf16[1024,128]{1,0:T(8,128)(2,1)} %refs_2_.1), channel_id=1, source_target_pairs={{0,16},{16,0},{1,17},{17,1},{2,18},{18,2},{3,19},{19,3},{4,20},{20... | collective-permute-start | bytes 786440 | tf_op jit(solution)/shard_map/ppermute | solution.py:296
  9.5 1.7 %collective-permute-start.5 = (bf16[1024,128]{1,0:T(8,128)(2,1)S(1)}, bf16[1024,128]{1,0:T(8,128)(2,1)S(1)}, u32[]{:S(2)}, u32[]{:S(2)}) collective-permute-start(bf16[1024,128]{1,0:T(8,128)(2,1)S(1)} %collective-permute-done.3.refs_3_), channel_id=1, source_target_pairs={{0,16},{16,0},{1,17},{17,1},{2,18},{18,2},{3,19},{19,3},{4,20},{20... | collective-permute-start | bytes 786440 | tf_op jit(solution)/shard_map/ppermute | solution.py:296
  11.2 3.9 %collective-permute-done.refs_0_.refs_7_ = bf16[256,512]{1,0:T(8,128)(2,1)S(1)} collective-permute-done((bf16[256,512]{1,0:T(8,128)(2,1)S(1)}, bf16[256,512]{1,0:T(8,128)(2,1)S(1)}, u32[]{:S(2)}, u32[]{:S(2)}) %collective-permute-start) | collective-permute-done | bytes 262176 | tf_op jit(solution)/shard_map/ppermute | solution.py:274
  15.1 0.9 %copy-done.1 = bf16[1024,128]{1,0:T(8,128)(2,1)S(1)} copy-done((bf16[1024,128]{1,0:T(8,128)(2,1)S(1)}, bf16[1024,128]{1,0:T(8,128)(2,1)}, u32[]{:S(2)}) %copy-start.1) | copy-done | bytes 262168
  16.0 0.7 %copy-done.2 = s32[8,8]{1,0:T(8,128)S(1)} copy-done((s32[8,8]{1,0:T(8,128)S(1)}, s32[8,8]{1,0:T(8,128)}, u32[]{:S(2)}) %copy-start.2) | copy-done | bytes 280
  17.4 2.0 %collective-permute-done.1.refs_1_.refs_8_ = bf16[256,512]{1,0:T(8,128)(2,1)S(1)} collective-permute-done((bf16[256,512]{1,0:T(8,128)(2,1)S(1)}, bf16[256,512]{1,0:T(8,128)(2,1)S(1)}, u32[]{:S(2)}, u32[]{:S(2)}) %collective-permute-start.1) | collective-permute-done | bytes 262176 | tf_op jit(solution)/shard_map/ppermute | solution.py:276
  19.5 1.5 %collective-permute-done.5.refs_5_ = bf16[1024,128]{1,0:T(8,128)(2,1)S(1)} collective-permute-done((bf16[1024,128]{1,0:T(8,128)(2,1)S(1)}, bf16[1024,128]{1,0:T(8,128)(2,1)S(1)}, u32[]{:S(2)}, u32[]{:S(2)}) %collective-permute-start.5) | collective-permute-done | bytes 262176 | tf_op jit(solution)/shard_map/ppermute | solution.py:296
  21.0 1.1 %bring.1 = (bf16[256,2048]{1,0:T(8,128)(2,1)S(1)}, bf16[512,256]{1,0:T(8,128)(2,1)S(1)}, bf16[512,256]{1,0:T(8,128)(2,1)S(1)}, bf16[512,256]{1,0:T(8,128)(2,1)S(1)}, bf16[512,256]{1,0:T(8,128)(2,1)S(1)}) custom-call(s32[8,8]{1,0:T(8,128)S(1)} %get-tuple-element.20.refs_0_, s32[8,8]{1,0:T(8,128)S(1)} %get-tuple-element.19.refs_1_.refs_0_, ...), custom_call_target="tpu_custom_call" | custom-call | bytes 3932160 | tf_op jit(solution)/shard_map/bring/pallas_call | solution.py:51
  23.2 1.7 %collective-permute-done.6.refs_2_.refs_0_ = bf16[256,512]{1,0:T(8,128)(2,1)S(1)} collective-permute-done((bf16[256,512]{1,0:T(8,128)(2,1)S(1)}, bf16[256,512]{1,0:T(8,128)(2,1)S(1)}, u32[]{:S(2)}, u32[]{:S(2)}) %collective-permute-start.6) | collective-permute-done | bytes 262176 | tf_op jit(solution)/shard_map/ppermute | solution.py:274
  25.4 1.4 %first_product.1.refs_1_.refs_0_ = bf16[256,512]{1,0:T(8,128)(2,1)S(1)} custom-call(s32[8,8]{1,0:T(8,128)S(1)} %get-tuple-element.19.refs_1_.refs_0_, bf16[256,2048]{1,0:T(8,128)(2,1)S(1)} %get-tuple-element.22.refs_1_, bf16[256,512]{1,0:T(8,128)(2,1)S(1)} %collective-permute-done.6.refs_2_.refs_0_, bf16[512,256]{1,0:T(8,128)(2,1)S(1)} %get-tuple-element.23.refs_3_, ...), custom_call_target="tpu_custom_call" | custom-call | bytes 4718592 | tf_op jit(solution)/shard_map/first_product/pallas_call | solution.py:51
  26.9 1.5 %collective-permute-start.11 = (bf16[256,512]{1,0:T(8,128)(2,1)S(1)}, bf16[256,512]{1,0:T(8,128)(2,1)S(1)}, u32[]{:S(2)}, u32[]{:S(2)}) collective-permute-start(bf16[256,512]{1,0:T(8,128)(2,1)S(1)} %first_product.1.refs_1_.refs_0_), channel_id=1, source_target_pairs={{0,16},{16,0},{1,17},{17,1},{2,18},{18,2},{3,19},{19,3},{4,20},{20... | collective-permute-start | bytes 786440 | tf_op jit(solution)/shard_map/ppermute | solution.py:317
  28.5 7.2 %collective-permute-done.11.refs_1_ = bf16[256,512]{1,0:T(8,128)(2,1)S(1)} collective-permute-done((bf16[256,512]{1,0:T(8,128)(2,1)S(1)}, bf16[256,512]{1,0:T(8,128)(2,1)S(1)}, u32[]{:S(2)}, u32[]{:S(2)}) %collective-permute-start.11) | collective-permute-done | bytes 262176 | tf_op jit(solution)/shard_map/ppermute | solution.py:317
  35.8 1.4 %collective-permute-done.2.refs_1_.refs_3_ = bf16[512,512]{1,0:T(8,128)(2,1)S(1)} collective-permute-done((bf16[512,512]{1,0:T(8,128)(2,1)S(1)}, bf16[512,512]{1,0:T(8,128)(2,1)S(1)}, u32[]{:S(2)}, u32[]{:S(2)}) %collective-permute-start.2) | collective-permute-done | bytes 524320 | tf_op jit(solution)/shard_map/ppermute | solution.py:280
  37.9 1.7 %collective-permute-start.15 = (bf16[128,512]{1,0:T(8,128)(2,1)S(1)}, bf16[128,512]{1,0:T(8,128)(2,1)S(1)}, u32[]{:S(2)}, u32[]{:S(2)}) collective-permute-start(bf16[128,512]{1,0:T(8,128)(2,1)S(1)} %get-tuple-element.28), channel_id=1, source_target_pairs={{0,12},{4,8},{8,4},{12,0},{1,13},{5,9},{9,5},{13,1},{2,14},{6,10},... | collective-permute-start | bytes 393224 | tf_op jit(solution)/shard_map/ppermute | solution.py:333
  39.9 2.4 %collective-permute-start.17 = (bf16[128,512]{1,0:T(8,128)(2,1)S(1)}, bf16[128,512]{1,0:T(8,128)(2,1)S(1)}, u32[]{:S(2)}, u32[]{:S(2)}) collective-permute-start(bf16[128,512]{1,0:T(8,128)(2,1)S(1)} %get-tuple-element.30), channel_id=1, source_target_pairs={{0,4},{4,0},{8,12},{12,8},{1,5},{5,1},{9,13},{13,9},{2,6},{6,2},{1... | collective-permute-start | bytes 393224 | tf_op jit(solution)/shard_map/ppermute | solution.py:333
  42.3 3.8 %collective-permute-done.14.refs_7_.refs_0_ = bf16[256,512]{1,0:T(8,128)(2,1)S(1)} collective-permute-done((bf16[256,512]{1,0:T(8,128)(2,1)S(1)}, bf16[256,512]{1,0:T(8,128)(2,1)S(1)}, u32[]{:S(2)}, u32[]{:S(2)}) %collective-permute-start.14) | collective-permute-done | bytes 262176 | tf_op jit(solution)/shard_map/ppermute | solution.py:280
  46.7 1.4 %layers.1.refs_0_.refs_1_ = bf16[1024,2048]{1,0:T(8,128)(2,1)S(1)} custom-call(s32[8,8]{1,0:T(8,128)S(1)} %get-tuple-element.19.refs_1_.refs_0_, bf16[1024,512]{1,0:T(8,128)(2,1)S(1)} %copy-done, bf16[512,512]{1,0:T(8,128)(2,1)S(1)} %pack.3.refs_0_.refs_2_, bf16[512,512]{1,0:T(8,128)(2,1)S(1)} %collective-permute-done.2.refs_1_.refs_3_, ...), custom_call_target="tpu_custom_call" | custom-call | bytes 8126464 | tf_op jit(solution)/shard_map/layers/pallas_call | solution.py:51
  48.0 0.7 %second_product.1.refs_2_ = f32[1024,128]{1,0:T(8,128)S(1)} custom-call(bf16[1024,2048]{1,0:T(8,128)(2,1)S(1)} %layers.1.refs_0_.refs_1_, bf16[128,512]{1,0:T(8,128)(2,1)S(1)} %get-tuple-element.27.refs_2_.refs_1_, bf16[128,512]{1,0:T(8,128)(2,1)S(1)} %collective-permute-done.15.refs_2_), custom_call_target="tpu_custom_call" | custom-call | bytes 4980736 | tf_op jit(solution)/shard_map/second_product/pallas_call | solution.py:51
  48.7 3.1 %collective-permute-done.16.refs_3_ = bf16[128,512]{1,0:T(8,128)(2,1)S(1)} collective-permute-done((bf16[128,512]{1,0:T(8,128)(2,1)S(1)}, bf16[128,512]{1,0:T(8,128)(2,1)S(1)}, u32[]{:S(2)}, u32[]{:S(2)}) %collective-permute-start.16) | collective-permute-done | bytes 131104 | tf_op jit(solution)/shard_map/ppermute | solution.py:333
  51.9 2.1 %last_product.1 = bf16[1024,128]{1,0:T(8,128)(2,1)} custom-call(s32[8,8]{1,0:T(8,128)S(1)} %get-tuple-element.19.refs_1_.refs_0_, bf16[1024,2048]{1,0:T(8,128)(2,1)S(1)} %layers.1.refs_0_.refs_1_, f32[1024,128]{1,0:T(8,128)S(1)} %second_product.1.refs_2_, bf16[128,512]{1,0:T(8,128)(2,1)S(1)} %collective-permute-done.16.refs_3_, ...), custom_call_target="tpu_custom_call" | custom-call | bytes 6553600 | tf_op jit(solution)/shard_map/last_product/pallas_call | solution.py:51
  (36 shorter events, 4.3 us)
Async XLA Ops:
  0.0 9.5 %collective-permute-start.3 = (bf16[1024,128]{1,0:T(8,128)(2,1)}, bf16[1024,128]{1,0:T(8,128)(2,1)S(1)}, u32[]{:S(2)}, u32[]{:S(2)}) collective-permute-start(bf16[1024,128]{1,0:T(8,128)(2,1)} %refs_2_.1), channel_id=1, source_target_pairs={{0,2},{1,3},{2,0},{3,1},{4,6},{5,7},{6,4},{7,5},{8,10},{9,11},{10,... | collective-permute-start | bytes 786440 | tf_op jit(solution)/shard_map/ppermute | solution.py:296
  3.9 11.1 %collective-permute-start = (bf16[256,512]{1,0:T(8,128)(2,1)S(1)}, bf16[256,512]{1,0:T(8,128)(2,1)S(1)}, u32[]{:S(2)}, u32[]{:S(2)}) collective-permute-start(bf16[256,512]{1,0:T(8,128)(2,1)S(1)} %bitcast.5), channel_id=1, source_target_pairs={{0,4},{4,8},{8,12},{12,0},{1,5},{5,9},{9,13},{13,1},{2,6},{6,10},{... | collective-permute-start | bytes 786440 | tf_op jit(solution)/shard_map/ppermute | solution.py:274
  5.6 13.9 %collective-permute-start.1 = (bf16[256,512]{1,0:T(8,128)(2,1)S(1)}, bf16[256,512]{1,0:T(8,128)(2,1)S(1)}, u32[]{:S(2)}, u32[]{:S(2)}) collective-permute-start(bf16[256,512]{1,0:T(8,128)(2,1)S(1)} %bitcast.6), channel_id=1, source_target_pairs={{0,12},{4,0},{8,4},{12,8},{1,13},{5,1},{9,5},{13,9},{2,14},{6,2},{... | collective-permute-start | bytes 786440 | tf_op jit(solution)/shard_map/ppermute | solution.py:276
  7.8 11.6 %collective-permute-start.4 = (bf16[1024,128]{1,0:T(8,128)(2,1)}, bf16[1024,128]{1,0:T(8,128)(2,1)S(1)}, u32[]{:S(2)}, u32[]{:S(2)}) collective-permute-start(bf16[1024,128]{1,0:T(8,128)(2,1)} %refs_2_.1), channel_id=1, source_target_pairs={{0,16},{16,0},{1,17},{17,1},{2,18},{18,2},{3,19},{19,3},{4,20},{20... | collective-permute-start | bytes 786440 | tf_op jit(solution)/shard_map/ppermute | solution.py:296
  9.5 11.5 %collective-permute-start.5 = (bf16[1024,128]{1,0:T(8,128)(2,1)S(1)}, bf16[1024,128]{1,0:T(8,128)(2,1)S(1)}, u32[]{:S(2)}, u32[]{:S(2)}) collective-permute-start(bf16[1024,128]{1,0:T(8,128)(2,1)S(1)} %collective-permute-done.3.refs_3_), channel_id=1, source_target_pairs={{0,16},{16,0},{1,17},{17,1},{2,18},{18,2},{3,19},{19,3},{4,20},{20... | collective-permute-start | bytes 786440 | tf_op jit(solution)/shard_map/ppermute | solution.py:296
  15.1 9.8 %collective-permute-start.6 = (bf16[256,512]{1,0:T(8,128)(2,1)S(1)}, bf16[256,512]{1,0:T(8,128)(2,1)S(1)}, u32[]{:S(2)}, u32[]{:S(2)}) collective-permute-start(bf16[256,512]{1,0:T(8,128)(2,1)S(1)} %collective-permute-done.refs_0_.refs_7_), channel_id=1, source_target_pairs={{0,4},{4,8},{8,12},{12,0},{1,5},{5,9},{9,13},{13,1},{2,6},{6,10},{... | collective-permute-start | bytes 786440 | tf_op jit(solution)/shard_map/ppermute | solution.py:274
  15.1 1.0 %copy-start.1 = (bf16[1024,128]{1,0:T(8,128)(2,1)S(1)}, bf16[1024,128]{1,0:T(8,128)(2,1)}, u32[]{:S(2)}) copy-start(bf16[1024,128]{1,0:T(8,128)(2,1)} %refs_2_.1) | copy-start | bytes 786436
  16.0 0.7 %copy-start.2 = (s32[8,8]{1,0:T(8,128)S(1)}, s32[8,8]{1,0:T(8,128)}, u32[]{:S(2)}) copy-start(s32[8,8]{1,0:T(8,128)} %refs_0_.1) | copy-start | bytes 772
  16.7 0.7 %copy-start.3 = (s32[8,8]{1,0:T(8,128)S(1)}, s32[8,8]{1,0:T(8,128)}, u32[]{:S(2)}) copy-start(s32[8,8]{1,0:T(8,128)} %refs_1_.2) | copy-start | bytes 772
  22.1 3.3 %collective-permute-start.10 = (bf16[512,256]{1,0:T(8,128)(2,1)S(1)}, bf16[512,256]{1,0:T(8,128)(2,1)S(1)}, u32[]{:S(2)}, u32[]{:S(2)}) collective-permute-start(bf16[512,256]{1,0:T(8,128)(2,1)S(1)} %get-tuple-element.26.refs_6_), channel_id=1, source_target_pairs={{0,1},{1,0},{2,3},{3,2},{4,5},{5,4},{6,7},{7,6},{8,9},{9,8},{10,11... | collective-permute-start | bytes 786440 | tf_op jit(solution)/shard_map/ppermute | solution.py:304
  22.1 3.3 %collective-permute-start.7 = (bf16[512,256]{1,0:T(8,128)(2,1)S(1)}, bf16[512,256]{1,0:T(8,128)(2,1)S(1)}, u32[]{:S(2)}, u32[]{:S(2)}) collective-permute-start(bf16[512,256]{1,0:T(8,128)(2,1)S(1)} %get-tuple-element.23.refs_3_), channel_id=1, source_target_pairs={{0,1},{1,0},{2,3},{3,2},{4,5},{5,4},{6,7},{7,6},{8,9},{9,8},{10,11... | collective-permute-start | bytes 786440 | tf_op jit(solution)/shard_map/ppermute | solution.py:304
  22.6 2.8 %collective-permute-start.8 = (bf16[512,256]{1,0:T(8,128)(2,1)S(1)}, bf16[512,256]{1,0:T(8,128)(2,1)S(1)}, u32[]{:S(2)}, u32[]{:S(2)}) collective-permute-start(bf16[512,256]{1,0:T(8,128)(2,1)S(1)} %get-tuple-element.24.refs_4_), channel_id=1, source_target_pairs={{0,1},{1,0},{2,3},{3,2},{4,5},{5,4},{6,7},{7,6},{8,9},{9,8},{10,11... | collective-permute-start | bytes 786440 | tf_op jit(solution)/shard_map/ppermute | solution.py:304
  22.7 23.9 %copy-start = (bf16[1024,512]{1,0:T(8,128)(2,1)S(1)}, bf16[1024,512]{1,0:T(8,128)(2,1)}, u32[]{:S(2)}) copy-start(bf16[1024,512]{1,0:T(8,128)(2,1)} %refs_1_.3) | copy-start | bytes 3145732
  22.7 2.7 %collective-permute-start.9 = (bf16[512,256]{1,0:T(8,128)(2,1)S(1)}, bf16[512,256]{1,0:T(8,128)(2,1)S(1)}, u32[]{:S(2)}, u32[]{:S(2)}) collective-permute-start(bf16[512,256]{1,0:T(8,128)(2,1)S(1)} %get-tuple-element.25.refs_5_), channel_id=1, source_target_pairs={{0,1},{1,0},{2,3},{3,2},{4,5},{5,4},{6,7},{7,6},{8,9},{9,8},{10,11... | collective-permute-start | bytes 786440 | tf_op jit(solution)/shard_map/ppermute | solution.py:304
  24.9 12.3 %collective-permute-start.2 = (bf16[512,512]{1,0:T(8,128)(2,1)S(1)}, bf16[512,512]{1,0:T(8,128)(2,1)S(1)}, u32[]{:S(2)}, u32[]{:S(2)}) collective-permute-start(bf16[512,512]{1,0:T(8,128)(2,1)S(1)} %pack.3.refs_0_.refs_2_), channel_id=1, source_target_pairs={{0,2},{1,3},{2,0},{3,1},{4,6},{5,7},{6,4},{7,5},{8,10},{9,11},{10,... | collective-permute-start | bytes 1572872 | tf_op jit(solution)/shard_map/ppermute | solution.py:280
  26.9 1.6 %collective-permute-start.12 = (bf16[256,512]{1,0:T(8,128)(2,1)S(1)}, bf16[256,512]{1,0:T(8,128)(2,1)S(1)}, u32[]{:S(2)}, u32[]{:S(2)}) collective-permute-start(bf16[256,512]{1,0:T(8,128)(2,1)S(1)} %pack.4.refs_5_), channel_id=1, source_target_pairs={{0,1},{1,0},{2,3},{3,2},{4,5},{5,4},{6,7},{7,6},{8,9},{9,8},{10,11... | collective-permute-start | bytes 786440 | tf_op jit(solution)/shard_map/ppermute | solution.py:323
  26.9 8.7 %collective-permute-start.11 = (bf16[256,512]{1,0:T(8,128)(2,1)S(1)}, bf16[256,512]{1,0:T(8,128)(2,1)S(1)}, u32[]{:S(2)}, u32[]{:S(2)}) collective-permute-start(bf16[256,512]{1,0:T(8,128)(2,1)S(1)} %first_product.1.refs_1_.refs_0_), channel_id=1, source_target_pairs={{0,16},{16,0},{1,17},{17,1},{2,18},{18,2},{3,19},{19,3},{4,20},{20... | collective-permute-start | bytes 786440 | tf_op jit(solution)/shard_map/ppermute | solution.py:317
  37.2 8.9 %collective-permute-start.13 = (bf16[1024,512]{1,0:T(8,128)(2,1)S(1)}, bf16[1024,512]{1,0:T(8,128)(2,1)S(1)}, u32[]{:S(2)}, u32[]{:S(2)}) collective-permute-start(bf16[1024,512]{1,0:T(8,128)(2,1)S(1)} %pack.5), channel_id=1, source_target_pairs={{0,1},{1,0},{2,3},{3,2},{4,5},{5,4},{6,7},{7,6},{8,9},{9,8},{10,11... | collective-permute-start | bytes 3145736 | tf_op jit(solution)/shard_map/ppermute | solution.py:339
  37.3 8.7 %collective-permute-start.14 = (bf16[256,512]{1,0:T(8,128)(2,1)S(1)}, bf16[256,512]{1,0:T(8,128)(2,1)S(1)}, u32[]{:S(2)}, u32[]{:S(2)}) collective-permute-start(bf16[256,512]{1,0:T(8,128)(2,1)S(1)} %pack.4.refs_5_), channel_id=1, source_target_pairs={{0,2},{1,3},{2,0},{3,1},{4,6},{5,7},{6,4},{7,5},{8,10},{9,11},{10,... | collective-permute-start | bytes 786440 | tf_op jit(solution)/shard_map/ppermute | solution.py:280
  37.9 10.1 %collective-permute-start.15 = (bf16[128,512]{1,0:T(8,128)(2,1)S(1)}, bf16[128,512]{1,0:T(8,128)(2,1)S(1)}, u32[]{:S(2)}, u32[]{:S(2)}) collective-permute-start(bf16[128,512]{1,0:T(8,128)(2,1)S(1)} %get-tuple-element.28), channel_id=1, source_target_pairs={{0,12},{4,8},{8,4},{12,0},{1,13},{5,9},{9,5},{13,1},{2,14},{6,10},... | collective-permute-start | bytes 393224 | tf_op jit(solution)/shard_map/ppermute | solution.py:333
  39.6 12.3 %collective-permute-start.16 = (bf16[128,512]{1,0:T(8,128)(2,1)S(1)}, bf16[128,512]{1,0:T(8,128)(2,1)S(1)}, u32[]{:S(2)}, u32[]{:S(2)}) collective-permute-start(bf16[128,512]{1,0:T(8,128)(2,1)S(1)} %get-tuple-element.29), channel_id=1, source_target_pairs={{0,8},{4,12},{8,0},{12,4},{1,9},{5,13},{9,1},{13,5},{2,10},{6,14},... | collective-permute-start | bytes 393224 | tf_op jit(solution)/shard_map/ppermute | solution.py:333
  39.9 12.0 %collective-permute-start.17 = (bf16[128,512]{1,0:T(8,128)(2,1)S(1)}, bf16[128,512]{1,0:T(8,128)(2,1)S(1)}, u32[]{:S(2)}, u32[]{:S(2)}) collective-permute-start(bf16[128,512]{1,0:T(8,128)(2,1)S(1)} %get-tuple-element.30), channel_id=1, source_target_pairs={{0,4},{4,0},{8,12},{12,8},{1,5},{5,1},{9,13},{13,9},{2,6},{6,2},{1... | collective-permute-start | bytes 393224 | tf_op jit(solution)/shard_map/ppermute | solution.py:333
  46.1 5.8 %collective-permute-start.18 = (bf16[128,512]{1,0:T(8,128)(2,1)S(1)}, bf16[128,512]{1,0:T(8,128)(2,1)S(1)}, u32[]{:S(2)}, u32[]{:S(2)}) collective-permute-start(bf16[128,512]{1,0:T(8,128)(2,1)S(1)} %get-tuple-element.31), channel_id=1, source_target_pairs={{0,1},{1,0},{2,3},{3,2},{4,5},{5,4},{6,7},{7,6},{8,9},{9,8},{10,11... | collective-permute-start | bytes 393224 | tf_op jit(solution)/shard_map/ppermute | solution.py:348
  46.2 5.7 %collective-permute-start.19 = (bf16[128,512]{1,0:T(8,128)(2,1)S(1)}, bf16[128,512]{1,0:T(8,128)(2,1)S(1)}, u32[]{:S(2)}, u32[]{:S(2)}) collective-permute-start(bf16[128,512]{1,0:T(8,128)(2,1)S(1)} %get-tuple-element.32), channel_id=1, source_target_pairs={{0,1},{1,0},{2,3},{3,2},{4,5},{5,4},{6,7},{7,6},{8,9},{9,8},{10,11... | collective-permute-start | bytes 393224 | tf_op jit(solution)/shard_map/ppermute | solution.py:348

commit v18 on v15

--- a/solution.py
+++ b/solution.py
@@ -54,10 +54,7 @@
         in_specs=[pl.BlockSpec(memory_space=pltpu.SMEM)] * len(smem)
         + [pl.BlockSpec(memory_space=pltpu.VMEM)] * len(arrays)
         + [pl.BlockSpec(memory_space=pl.ANY)] * len(after),
-        out_specs=[
-            pl.BlockSpec(memory_space=pltpu.SMEM if o.dtype == jnp.int32 else pltpu.VMEM)
-            for o in outs
-        ],
+        out_specs=[pl.BlockSpec(memory_space=pltpu.VMEM)] * len(outs),
         scratch_shapes=list(scratch),
         compiler_params=pltpu.CompilerParams(vmem_limit_bytes=size + MARGIN),
         cost_estimate=pl.CostEstimate(flops=flops, bytes_accessed=size, transcendentals=0),
@@ -131,11 +128,8 @@
 
 
 def fetch_kernel(hp, zp, h, hp_out, zp_out, h_out):
-    h_out[...] = h[...]
-    for i in range(hp.shape[0]):
-        for j in range(hp.shape[1]):
-            hp_out[i, j] = hp[i, j]
-            zp_out[i, j] = zp[i, j]
+    for ref, out in ((hp, hp_out), (zp, zp_out), (h, h_out)):
+        out[...] = ref[...]
 
 
 def bring_kernel(sizes, h_table, hp, zp, *refs):
@@ -308,16 +302,15 @@
         fetch_kernel,
         "fetch",
         [shape(*h_pattern.shape, jnp.int32)] * 2 + [shape(*hamiltonian.shape)],
-        [hamiltonian],
-        smem=[h_pattern, z_pattern],
+        [h_pattern, z_pattern, hamiltonian],
     )
     h_pieces, h_table = [hamiltonian], [(0, 0)]
     for axis, bit in [("layer", top)] + [("row", b) for b in row_bits]:
         perm = flip(rows if axis == "row" else layers, bit)
         for piece, (dr, dl) in list(zip(h_pieces, h_table)):
             h_table.append((dr ^ bit, dl) if axis == "row" else (dr, dl ^ bit))
-            if dl and axis == 'row':
-                piece = pack([piece], [slots[1]])
+            if False:
+                piece = pack([piece], [])
             h_pieces.append(lax.ppermute(piece, axis, perm))
     raw = lax.ppermute(hamiltonian, "layer", flip(layers, low))
     group = range(1, cols - 1)
@@ -332,7 +325,7 @@
         + [shape(cols_here, 2 * q)] * cols,
         [fetched, *h_pieces[1:], *slots[:-1]],
         smem=[h_pattern, z_pattern],
-        after=[raw, mine],
+        after=(),
     )
     sent, h_own = h_own[:n_sent], h_own[n_sent:]
     h_other = [lax.ppermute(piece, "layer", flip(layers, low)) for piece in sent]

time: 58.5 us -> 53.5 us (0.915)
  waiting for transfers between devices: 27.3 us -> 23.7 us
  Pallas kernels: 8.88 us -> 7.47 us
    ppermute x2, waiting for transfers between devices: 8.75 us -> 2.89 us  [local(): lax.ppermute(right, 'col', [(i, (i + 1) % cols) for i in range(cols)])]
    ppermute x1, waiting for transfers between devices: 0.01 us -> 3.51 us  [local(): left = lax.ppermute(left, 'col', [(i, (i - 1) % cols) for i in range(cols)])]
    ppermute x2, waiting for transfers between devices: 2.75 us -> 5.42 us  [cross(): return lax.ppermute(piece, 'layer', flip(layers, layer_bits[0]))]
    ppermute x3, waiting for transfers between devices: 4.36 us -> 2.29 us  [local(): lax.ppermute(outgoing[d], 'col', flip(cols, d))]
    ppermute x2, starting transfers between devices: 3.23 us -> 1.75 us  [local(): lax.ppermute(right, 'col', [(i, (i + 1) % cols) for i in range(cols)])]
    pallas_call x12 -> x11, Pallas kernels: 8.88 us -> 7.47 us  [run(): pl.pallas_call(body, out_shape=list(outs), in_specs=[pl.BlockSpec(memory_...]
    ppermute x3, starting transfers between devices: 4.81 us -> 6.17 us  [local(): h_pieces.append(lax.ppermute(piece, axis, perm))]
    ppermute x1, starting transfers between devices: 0.6 us -> 1.56 us  [local(): gathered[dr ^ bit] = lax.ppermute(piece, 'row', flip(rows, bit))]
  transfers between devices with their start and end apart: 20 -> 20, of which waited for: 7 -> 9; matrix products, arithmetic and copies ran while one was open for 0% -> 2% of each run, Pallas kernels for 12% -> 10%
where the time goes in v18:
time: 53.5 us; the launch traced here: 53.3 us
  waiting for transfers between devices  23.7 us (44%)
  starting transfers between devices  18.6 us (35%)
  Pallas kernels  7.47 us (14%)
  local copies, waits for them, and re-layouts  3.29 us (6%)
    pallas_call x11, Pallas kernels, run(): pl.pallas_call(body, out_shape=list(outs), in_specs=[pl.BlockSpec(memory_...  7.47 us
    ppermute x1, waiting for transfers between devices, local(): gathered[dr ^ bit] = lax.ppermute(piece, 'row', flip(rows, bit))  7.16 us
    ppermute x3, starting transfers between devices, local(): h_pieces.append(lax.ppermute(piece, axis, perm))  6.17 us
    ppermute x2, waiting for transfers between devices, cross(): return lax.ppermute(piece, 'layer', flip(layers, layer_bits[0]))  5.42 us
    ppermute x3, starting transfers between devices, local(): lax.ppermute(outgoing[d], 'col', flip(cols, d))  4.39 us
    ppermute x1, waiting for transfers between devices, local(): left = lax.ppermute(left, 'col', [(i, (i - 1) % cols) for i in range(cols)])  3.51 us
    ppermute x2, waiting for transfers between devices, local(): lax.ppermute(right, 'col', [(i, (i + 1) % cols) for i in range(cols)])  2.89 us
    ppermute x3, waiting for transfers between devices, local(): h_pieces.append(lax.ppermute(piece, axis, perm))  2.45 us
  transfers between devices with their start and end apart: 20, of which 9 were waited for; matrix products, arithmetic and copies ran while one was open for 2% of the time, Pallas kernels for 10%

profile of v18, /device:TPU:0, one launch (start us, length us, event | category | flops | bytes accessed | tf_op | source)
XLA Modules:
  0.0 53.3 jit_solution(18303207761850785545)
XLA Ops:
  0.0 3.0 %collective-permute-start.3 = (bf16[1024,128]{1,0:T(8,128)(2,1)}, bf16[1024,128]{1,0:T(8,128)(2,1)S(1)}, u32[]{:S(2)}, u32[]{:S(2)}) collective-permute-start(bf16[1024,128]{1,0:T(8,128)(2,1)} %refs_2_.1), channel_id=1, source_target_pairs={{0,2},{1,3},{2,0},{3,1},{4,6},{5,7},{6,4},{7,5},{8,10},{9,11},{10,... | collective-permute-start | bytes 786440 | tf_op jit(solution)/shard_map/ppermute | solution.py:314
  3.0 1.0 %constant_dynamic-slice_fusion = bf16[2,1,128,512]{3,2,1,0:T(8,128)(2,1)S(1)} fusion(bf16[2,4,128,512]{3,2,1,0:T(8,128)(2,1)} %bitcast.4, s32[]{:T(128)S(6)} %select_n.4), kind=kLoop, calls=%fused_computation | loop fusion | bytes 524292 | tf_op jit(solution)/shard_map/jit(dynamic_index_in_dim)/dynamic_slice | solution.py:287
  3.9 1.6 %collective-permute-start = (bf16[256,512]{1,0:T(8,128)(2,1)S(1)}, bf16[256,512]{1,0:T(8,128)(2,1)S(1)}, u32[]{:S(2)}, u32[]{:S(2)}) collective-permute-start(bf16[256,512]{1,0:T(8,128)(2,1)S(1)} %bitcast.5), channel_id=1, source_target_pairs={{0,4},{4,8},{8,12},{12,0},{1,5},{5,9},{9,13},{13,1},{2,6},{6,10},{... | collective-permute-start | bytes 786440 | tf_op jit(solution)/shard_map/ppermute | solution.py:292
  5.6 2.2 %collective-permute-start.1 = (bf16[256,512]{1,0:T(8,128)(2,1)S(1)}, bf16[256,512]{1,0:T(8,128)(2,1)S(1)}, u32[]{:S(2)}, u32[]{:S(2)}) collective-permute-start(bf16[256,512]{1,0:T(8,128)(2,1)S(1)} %bitcast.6), channel_id=1, source_target_pairs={{0,12},{4,0},{8,4},{12,8},{1,13},{5,1},{9,5},{13,9},{2,14},{6,2},{... | collective-permute-start | bytes 786440 | tf_op jit(solution)/shard_map/ppermute | solution.py:294
  7.8 1.5 %collective-permute-start.4 = (bf16[1024,128]{1,0:T(8,128)(2,1)}, bf16[1024,128]{1,0:T(8,128)(2,1)S(1)}, u32[]{:S(2)}, u32[]{:S(2)}) collective-permute-start(bf16[1024,128]{1,0:T(8,128)(2,1)} %refs_2_.1), channel_id=1, source_target_pairs={{0,16},{16,0},{1,17},{17,1},{2,18},{18,2},{3,19},{19,3},{4,20},{20... | collective-permute-start | bytes 786440 | tf_op jit(solution)/shard_map/ppermute | solution.py:314
  9.5 1.7 %collective-permute-start.5 = (bf16[1024,128]{1,0:T(8,128)(2,1)S(1)}, bf16[1024,128]{1,0:T(8,128)(2,1)S(1)}, u32[]{:S(2)}, u32[]{:S(2)}) collective-permute-start(bf16[1024,128]{1,0:T(8,128)(2,1)S(1)} %collective-permute-done.3.refs_3_), channel_id=1, source_target_pairs={{0,16},{16,0},{1,17},{17,1},{2,18},{18,2},{3,19},{19,3},{4,20},{20... | collective-permute-start | bytes 786440 | tf_op jit(solution)/shard_map/ppermute | solution.py:314
  11.2 0.9 %copy-done.1 = bf16[1024,128]{1,0:T(8,128)(2,1)S(1)} copy-done((bf16[1024,128]{1,0:T(8,128)(2,1)S(1)}, bf16[1024,128]{1,0:T(8,128)(2,1)}, u32[]{:S(2)}) %copy-start.1) | copy-done | bytes 262168
  12.2 0.7 %copy-done.2 = s32[8,8]{1,0:T(8,128)S(1)} copy-done((s32[8,8]{1,0:T(8,128)S(1)}, s32[8,8]{1,0:T(8,128)}, u32[]{:S(2)}) %copy-start.2) | copy-done | bytes 280
  13.5 1.5 %collective-permute-done.refs_0_.refs_7_ = bf16[256,512]{1,0:T(8,128)(2,1)S(1)} collective-permute-done((bf16[256,512]{1,0:T(8,128)(2,1)S(1)}, bf16[256,512]{1,0:T(8,128)(2,1)S(1)}, u32[]{:S(2)}, u32[]{:S(2)}) %collective-permute-start) | collective-permute-done | bytes 262176 | tf_op jit(solution)/shard_map/ppermute | solution.py:292
  15.2 3.5 %collective-permute-done.1.refs_1_.refs_8_ = bf16[256,512]{1,0:T(8,128)(2,1)S(1)} collective-permute-done((bf16[256,512]{1,0:T(8,128)(2,1)S(1)}, bf16[256,512]{1,0:T(8,128)(2,1)S(1)}, u32[]{:S(2)}, u32[]{:S(2)}) %collective-permute-start.1) | collective-permute-done | bytes 262176 | tf_op jit(solution)/shard_map/ppermute | solution.py:294
  18.7 2.3 %collective-permute-done.5.refs_5_ = bf16[1024,128]{1,0:T(8,128)(2,1)S(1)} collective-permute-done((bf16[1024,128]{1,0:T(8,128)(2,1)S(1)}, bf16[1024,128]{1,0:T(8,128)(2,1)S(1)}, u32[]{:S(2)}, u32[]{:S(2)}) %collective-permute-start.5) | collective-permute-done | bytes 262176 | tf_op jit(solution)/shard_map/ppermute | solution.py:314
  21.0 1.3 %bring.1 = (bf16[256,2048]{1,0:T(8,128)(2,1)S(1)}, bf16[1024,128]{1,0:T(8,128)(2,1)S(1)}, bf16[1024,128]{1,0:T(8,128)(2,1)S(1)}, bf16[1024,128]{1,0:T(8,128)(2,1...) custom-call(s32[8,8]{1,0:T(8,128)S(1)} %get-tuple-element.23.refs_0_, ...), custom_call_target="tpu_custom_call" | custom-call | bytes 4718592 | tf_op jit(solution)/shard_map/bring/pallas_call | solution.py:51
  23.5 1.4 %collective-permute-done.6.refs_3_.refs_0_ = bf16[256,512]{1,0:T(8,128)(2,1)S(1)} collective-permute-done((bf16[256,512]{1,0:T(8,128)(2,1)S(1)}, bf16[256,512]{1,0:T(8,128)(2,1)S(1)}, u32[]{:S(2)}, u32[]{:S(2)}) %collective-permute-start.6) | collective-permute-done | bytes 262176 | tf_op jit(solution)/shard_map/ppermute | solution.py:292
  24.9 1.8 %first_product.1.refs_1_.refs_0_ = bf16[256,512]{1,0:T(8,128)(2,1)S(1)} custom-call(s32[8,8]{1,0:T(8,128)S(1)} %get-tuple-element.23.refs_0_, s32[8,8]{1,0:T(8,128)S(1)} %get-tuple-element.22.refs_1_.refs_0_, bf16[256,2048]{1,0:T(8,128)(2,1)S(1)} %get-tuple-element.25.refs_2_, bf16[256,512]{1,0:T(8,128)(2,1)S(1)} %collective-permute-done.6.refs_3_.refs_0_, ...), custom_call_target="tpu_custom_call" | custom-call | bytes 4980736 | tf_op jit(solution)/shard_map/first_product/pallas_call | solution.py:51
  26.8 1.6 %collective-permute-start.11 = (bf16[256,512]{1,0:T(8,128)(2,1)S(1)}, bf16[256,512]{1,0:T(8,128)(2,1)S(1)}, u32[]{:S(2)}, u32[]{:S(2)}) collective-permute-start(bf16[256,512]{1,0:T(8,128)(2,1)S(1)} %first_product.1.refs_1_.refs_0_), channel_id=1, source_target_pairs={{0,16},{16,0},{1,17},{17,1},{2,18},{18,2},{3,19},{19,3},{4,20},{20... | collective-permute-start | bytes 786440 | tf_op jit(solution)/shard_map/ppermute | solution.py:348
  28.4 7.2 %collective-permute-done.11.refs_1_ = bf16[256,512]{1,0:T(8,128)(2,1)S(1)} collective-permute-done((bf16[256,512]{1,0:T(8,128)(2,1)S(1)}, bf16[256,512]{1,0:T(8,128)(2,1)S(1)}, u32[]{:S(2)}, u32[]{:S(2)}) %collective-permute-start.11) | collective-permute-done | bytes 262176 | tf_op jit(solution)/shard_map/ppermute | solution.py:348
  35.6 1.7 %collective-permute-done.2.refs_1_.refs_3_ = bf16[512,512]{1,0:T(8,128)(2,1)S(1)} collective-permute-done((bf16[512,512]{1,0:T(8,128)(2,1)S(1)}, bf16[512,512]{1,0:T(8,128)(2,1)S(1)}, u32[]{:S(2)}, u32[]{:S(2)}) %collective-permute-start.2) | collective-permute-done | bytes 524320 | tf_op jit(solution)/shard_map/ppermute | solution.py:298
  38.0 1.7 %collective-permute-start.15 = (bf16[128,512]{1,0:T(8,128)(2,1)S(1)}, bf16[128,512]{1,0:T(8,128)(2,1)S(1)}, u32[]{:S(2)}, u32[]{:S(2)}) collective-permute-start(bf16[128,512]{1,0:T(8,128)(2,1)S(1)} %get-tuple-element.34), channel_id=1, source_target_pairs={{0,12},{4,8},{8,4},{12,0},{1,13},{5,9},{9,5},{13,1},{2,14},{6,10},... | collective-permute-start | bytes 393224 | tf_op jit(solution)/shard_map/ppermute | solution.py:364
  39.7 2.7 %collective-permute-start.17 = (bf16[128,512]{1,0:T(8,128)(2,1)S(1)}, bf16[128,512]{1,0:T(8,128)(2,1)S(1)}, u32[]{:S(2)}, u32[]{:S(2)}) collective-permute-start(bf16[128,512]{1,0:T(8,128)(2,1)S(1)} %get-tuple-element.36), channel_id=1, source_target_pairs={{0,4},{4,0},{8,12},{12,8},{1,5},{5,1},{9,13},{13,9},{2,6},{6,2},{1... | collective-permute-start | bytes 393224 | tf_op jit(solution)/shard_map/ppermute | solution.py:364
  42.4 3.8 %collective-permute-done.14.refs_7_.refs_0_ = bf16[256,512]{1,0:T(8,128)(2,1)S(1)} collective-permute-done((bf16[256,512]{1,0:T(8,128)(2,1)S(1)}, bf16[256,512]{1,0:T(8,128)(2,1)S(1)}, u32[]{:S(2)}, u32[]{:S(2)}) %collective-permute-start.14) | collective-permute-done | bytes 262176 | tf_op jit(solution)/shard_map/ppermute | solution.py:298
  46.8 1.4 %layers.1.refs_0_.refs_1_ = bf16[1024,2048]{1,0:T(8,128)(2,1)S(1)} custom-call(s32[8,8]{1,0:T(8,128)S(1)} %get-tuple-element.22.refs_1_.refs_0_, bf16[1024,512]{1,0:T(8,128)(2,1)S(1)} %copy-done, bf16[512,512]{1,0:T(8,128)(2,1)S(1)} %pack.3.refs_0_.refs_2_, bf16[512,512]{1,0:T(8,128)(2,1)S(1)} %collective-permute-done.2.refs_1_.refs_3_, ...), custom_call_target="tpu_custom_call" | custom-call | bytes 8126464 | tf_op jit(solution)/shard_map/layers/pallas_call | solution.py:51
  48.1 0.7 %second_product.1.refs_2_ = f32[1024,128]{1,0:T(8,128)S(1)} custom-call(bf16[1024,2048]{1,0:T(8,128)(2,1)S(1)} %layers.1.refs_0_.refs_1_, bf16[128,512]{1,0:T(8,128)(2,1)S(1)} %get-tuple-element.33.refs_2_.refs_1_, bf16[128,512]{1,0:T(8,128)(2,1)S(1)} %collective-permute-done.15.refs_2_), custom_call_target="tpu_custom_call" | custom-call | bytes 4980736 | tf_op jit(solution)/shard_map/second_product/pallas_call | solution.py:51
  48.9 2.3 %collective-permute-done.16.refs_3_ = bf16[128,512]{1,0:T(8,128)(2,1)S(1)} collective-permute-done((bf16[128,512]{1,0:T(8,128)(2,1)S(1)}, bf16[128,512]{1,0:T(8,128)(2,1)S(1)}, u32[]{:S(2)}, u32[]{:S(2)}) %collective-permute-start.16) | collective-permute-done | bytes 131104 | tf_op jit(solution)/shard_map/ppermute | solution.py:364
  51.2 2.1 %last_product.1 = bf16[1024,128]{1,0:T(8,128)(2,1)} custom-call(s32[8,8]{1,0:T(8,128)S(1)} %get-tuple-element.22.refs_1_.refs_0_, bf16[1024,2048]{1,0:T(8,128)(2,1)S(1)} %layers.1.refs_0_.refs_1_, f32[1024,128]{1,0:T(8,128)S(1)} %second_product.1.refs_2_, bf16[128,512]{1,0:T(8,128)(2,1)S(1)} %collective-permute-done.16.refs_3_, ...), custom_call_target="tpu_custom_call" | custom-call | bytes 6553600 | tf_op jit(solution)/shard_map/last_product/pallas_call | solution.py:51
  (36 shorter events, 3.8 us)
Async XLA Ops:
  0.0 9.5 %collective-permute-start.3 = (bf16[1024,128]{1,0:T(8,128)(2,1)}, bf16[1024,128]{1,0:T(8,128)(2,1)S(1)}, u32[]{:S(2)}, u32[]{:S(2)}) collective-permute-start(bf16[1024,128]{1,0:T(8,128)(2,1)} %refs_2_.1), channel_id=1, source_target_pairs={{0,2},{1,3},{2,0},{3,1},{4,6},{5,7},{6,4},{7,5},{8,10},{9,11},{10,... | collective-permute-start | bytes 786440 | tf_op jit(solution)/shard_map/ppermute | solution.py:314
  3.9 11.1 %collective-permute-start = (bf16[256,512]{1,0:T(8,128)(2,1)S(1)}, bf16[256,512]{1,0:T(8,128)(2,1)S(1)}, u32[]{:S(2)}, u32[]{:S(2)}) collective-permute-start(bf16[256,512]{1,0:T(8,128)(2,1)S(1)} %bitcast.5), channel_id=1, source_target_pairs={{0,4},{4,8},{8,12},{12,0},{1,5},{5,9},{9,13},{13,1},{2,6},{6,10},{... | collective-permute-start | bytes 786440 | tf_op jit(solution)/shard_map/ppermute | solution.py:292
  5.6 13.1 %collective-permute-start.1 = (bf16[256,512]{1,0:T(8,128)(2,1)S(1)}, bf16[256,512]{1,0:T(8,128)(2,1)S(1)}, u32[]{:S(2)}, u32[]{:S(2)}) collective-permute-start(bf16[256,512]{1,0:T(8,128)(2,1)S(1)} %bitcast.6), channel_id=1, source_target_pairs={{0,12},{4,0},{8,4},{12,8},{1,13},{5,1},{9,5},{13,9},{2,14},{6,2},{... | collective-permute-start | bytes 786440 | tf_op jit(solution)/shard_map/ppermute | solution.py:294
  7.8 10.9 %collective-permute-start.4 = (bf16[1024,128]{1,0:T(8,128)(2,1)}, bf16[1024,128]{1,0:T(8,128)(2,1)S(1)}, u32[]{:S(2)}, u32[]{:S(2)}) collective-permute-start(bf16[1024,128]{1,0:T(8,128)(2,1)} %refs_2_.1), channel_id=1, source_target_pairs={{0,16},{16,0},{1,17},{17,1},{2,18},{18,2},{3,19},{19,3},{4,20},{20... | collective-permute-start | bytes 786440 | tf_op jit(solution)/shard_map/ppermute | solution.py:314
  9.5 11.5 %collective-permute-start.5 = (bf16[1024,128]{1,0:T(8,128)(2,1)S(1)}, bf16[1024,128]{1,0:T(8,128)(2,1)S(1)}, u32[]{:S(2)}, u32[]{:S(2)}) collective-permute-start(bf16[1024,128]{1,0:T(8,128)(2,1)S(1)} %collective-permute-done.3.refs_3_), channel_id=1, source_target_pairs={{0,16},{16,0},{1,17},{17,1},{2,18},{18,2},{3,19},{19,3},{4,20},{20... | collective-permute-start | bytes 786440 | tf_op jit(solution)/shard_map/ppermute | solution.py:314
  11.2 11.7 %collective-permute-start.7 = (bf16[1024,128]{1,0:T(8,128)(2,1)}, bf16[1024,128]{1,0:T(8,128)(2,1)S(1)}, u32[]{:S(2)}, u32[]{:S(2)}) collective-permute-start(bf16[1024,128]{1,0:T(8,128)(2,1)} %refs_2_.1), channel_id=1, source_target_pairs={{0,1},{1,0},{2,3},{3,2},{4,5},{5,4},{6,7},{7,6},{8,9},{9,8},{10,11... | collective-permute-start | bytes 786440 | tf_op jit(solution)/shard_map/ppermute | solution.py:315
  11.2 1.0 %copy-start.1 = (bf16[1024,128]{1,0:T(8,128)(2,1)S(1)}, bf16[1024,128]{1,0:T(8,128)(2,1)}, u32[]{:S(2)}) copy-start(bf16[1024,128]{1,0:T(8,128)(2,1)} %refs_2_.1) | copy-start | bytes 786436
  12.2 0.7 %copy-start.2 = (s32[8,8]{1,0:T(8,128)S(1)}, s32[8,8]{1,0:T(8,128)}, u32[]{:S(2)}) copy-start(s32[8,8]{1,0:T(8,128)} %refs_0_.1) | copy-start | bytes 772
  12.8 0.7 %copy-start.3 = (s32[8,8]{1,0:T(8,128)S(1)}, s32[8,8]{1,0:T(8,128)}, u32[]{:S(2)}) copy-start(s32[8,8]{1,0:T(8,128)} %refs_1_.2) | copy-start | bytes 772
  15.1 9.8 %collective-permute-start.6 = (bf16[256,512]{1,0:T(8,128)(2,1)S(1)}, bf16[256,512]{1,0:T(8,128)(2,1)S(1)}, u32[]{:S(2)}, u32[]{:S(2)}) collective-permute-start(bf16[256,512]{1,0:T(8,128)(2,1)S(1)} %collective-permute-done.refs_0_.refs_7_), channel_id=1, source_target_pairs={{0,4},{4,8},{8,12},{12,0},{1,5},{5,9},{9,13},{13,1},{2,6},{6,10},{... | collective-permute-start | bytes 786440 | tf_op jit(solution)/shard_map/ppermute | solution.py:292
  22.2 2.7 %collective-permute-start.10 = (bf16[1024,128]{1,0:T(8,128)(2,1)S(1)}, bf16[1024,128]{1,0:T(8,128)(2,1)S(1)}, u32[]{:S(2)}, u32[]{:S(2)}) collective-permute-start(bf16[1024,128]{1,0:T(8,128)(2,1)S(1)} %get-tuple-element.28), channel_id=1, source_target_pairs={{0,1},{1,0},{2,3},{3,2},{4,5},{5,4},{6,7},{7,6},{8,9},{9,8},{10,11... | collective-permute-start | bytes 786440 | tf_op jit(solution)/shard_map/ppermute | solution.py:331
  22.3 2.6 %collective-permute-start.8 = (bf16[1024,128]{1,0:T(8,128)(2,1)S(1)}, bf16[1024,128]{1,0:T(8,128)(2,1)S(1)}, u32[]{:S(2)}, u32[]{:S(2)}) collective-permute-start(bf16[1024,128]{1,0:T(8,128)(2,1)S(1)} %get-tuple-element.26), channel_id=1, source_target_pairs={{0,1},{1,0},{2,3},{3,2},{4,5},{5,4},{6,7},{7,6},{8,9},{9,8},{10,11... | collective-permute-start | bytes 786440 | tf_op jit(solution)/shard_map/ppermute | solution.py:331
  22.8 23.9 %copy-start = (bf16[1024,512]{1,0:T(8,128)(2,1)S(1)}, bf16[1024,512]{1,0:T(8,128)(2,1)}, u32[]{:S(2)}) copy-start(bf16[1024,512]{1,0:T(8,128)(2,1)} %refs_1_.3) | copy-start | bytes 3145732
  22.8 2.1 %collective-permute-start.9 = (bf16[1024,128]{1,0:T(8,128)(2,1)S(1)}, bf16[1024,128]{1,0:T(8,128)(2,1)S(1)}, u32[]{:S(2)}, u32[]{:S(2)}) collective-permute-start(bf16[1024,128]{1,0:T(8,128)(2,1)S(1)} %get-tuple-element.27), channel_id=1, source_target_pairs={{0,1},{1,0},{2,3},{3,2},{4,5},{5,4},{6,7},{7,6},{8,9},{9,8},{10,11... | collective-permute-start | bytes 786440 | tf_op jit(solution)/shard_map/ppermute | solution.py:331
  23.0 14.3 %collective-permute-start.2 = (bf16[512,512]{1,0:T(8,128)(2,1)S(1)}, bf16[512,512]{1,0:T(8,128)(2,1)S(1)}, u32[]{:S(2)}, u32[]{:S(2)}) collective-permute-start(bf16[512,512]{1,0:T(8,128)(2,1)S(1)} %pack.3.refs_0_.refs_2_), channel_id=1, source_target_pairs={{0,2},{1,3},{2,0},{3,1},{4,6},{5,7},{6,4},{7,5},{8,10},{9,11},{10,... | collective-permute-start | bytes 1572872 | tf_op jit(solution)/shard_map/ppermute | solution.py:298
  26.7 1.6 %collective-permute-start.12 = (bf16[256,512]{1,0:T(8,128)(2,1)S(1)}, bf16[256,512]{1,0:T(8,128)(2,1)S(1)}, u32[]{:S(2)}, u32[]{:S(2)}) collective-permute-start(bf16[256,512]{1,0:T(8,128)(2,1)S(1)} %pack.4.refs_5_), channel_id=1, source_target_pairs={{0,1},{1,0},{2,3},{3,2},{4,5},{5,4},{6,7},{7,6},{8,9},{9,8},{10,11... | collective-permute-start | bytes 786440 | tf_op jit(solution)/shard_map/ppermute | solution.py:354
  26.8 8.7 %collective-permute-start.11 = (bf16[256,512]{1,0:T(8,128)(2,1)S(1)}, bf16[256,512]{1,0:T(8,128)(2,1)S(1)}, u32[]{:S(2)}, u32[]{:S(2)}) collective-permute-start(bf16[256,512]{1,0:T(8,128)(2,1)S(1)} %first_product.1.refs_1_.refs_0_), channel_id=1, source_target_pairs={{0,16},{16,0},{1,17},{17,1},{2,18},{18,2},{3,19},{19,3},{4,20},{20... | collective-permute-start | bytes 786440 | tf_op jit(solution)/shard_map/ppermute | solution.py:348
  37.4 8.9 %collective-permute-start.13 = (bf16[1024,512]{1,0:T(8,128)(2,1)S(1)}, bf16[1024,512]{1,0:T(8,128)(2,1)S(1)}, u32[]{:S(2)}, u32[]{:S(2)}) collective-permute-start(bf16[1024,512]{1,0:T(8,128)(2,1)S(1)} %pack.5), channel_id=1, source_target_pairs={{0,1},{1,0},{2,3},{3,2},{4,5},{5,4},{6,7},{7,6},{8,9},{9,8},{10,11... | collective-permute-start | bytes 3145736 | tf_op jit(solution)/shard_map/ppermute | solution.py:367
  37.4 8.7 %collective-permute-start.14 = (bf16[256,512]{1,0:T(8,128)(2,1)S(1)}, bf16[256,512]{1,0:T(8,128)(2,1)S(1)}, u32[]{:S(2)}, u32[]{:S(2)}) collective-permute-start(bf16[256,512]{1,0:T(8,128)(2,1)S(1)} %pack.4.refs_5_), channel_id=1, source_target_pairs={{0,2},{1,3},{2,0},{3,1},{4,6},{5,7},{6,4},{7,5},{8,10},{9,11},{10,... | collective-permute-start | bytes 786440 | tf_op jit(solution)/shard_map/ppermute | solution.py:298
  38.0 10.1 %collective-permute-start.15 = (bf16[128,512]{1,0:T(8,128)(2,1)S(1)}, bf16[128,512]{1,0:T(8,128)(2,1)S(1)}, u32[]{:S(2)}, u32[]{:S(2)}) collective-permute-start(bf16[128,512]{1,0:T(8,128)(2,1)S(1)} %get-tuple-element.34), channel_id=1, source_target_pairs={{0,12},{4,8},{8,4},{12,0},{1,13},{5,9},{9,5},{13,1},{2,14},{6,10},... | collective-permute-start | bytes 393224 | tf_op jit(solution)/shard_map/ppermute | solution.py:364
  39.7 11.4 %collective-permute-start.16 = (bf16[128,512]{1,0:T(8,128)(2,1)S(1)}, bf16[128,512]{1,0:T(8,128)(2,1)S(1)}, u32[]{:S(2)}, u32[]{:S(2)}) collective-permute-start(bf16[128,512]{1,0:T(8,128)(2,1)S(1)} %get-tuple-element.35), channel_id=1, source_target_pairs={{0,8},{4,12},{8,0},{12,4},{1,9},{5,13},{9,1},{13,5},{2,10},{6,14},... | collective-permute-start | bytes 393224 | tf_op jit(solution)/shard_map/ppermute | solution.py:364
  39.7 11.4 %collective-permute-start.17 = (bf16[128,512]{1,0:T(8,128)(2,1)S(1)}, bf16[128,512]{1,0:T(8,128)(2,1)S(1)}, u32[]{:S(2)}, u32[]{:S(2)}) collective-permute-start(bf16[128,512]{1,0:T(8,128)(2,1)S(1)} %get-tuple-element.36), channel_id=1, source_target_pairs={{0,4},{4,0},{8,12},{12,8},{1,5},{5,1},{9,13},{13,9},{2,6},{6,2},{1... | collective-permute-start | bytes 393224 | tf_op jit(solution)/shard_map/ppermute | solution.py:364
  46.2 5.0 %collective-permute-start.18 = (bf16[128,512]{1,0:T(8,128)(2,1)S(1)}, bf16[128,512]{1,0:T(8,128)(2,1)S(1)}, u32[]{:S(2)}, u32[]{:S(2)}) collective-permute-start(bf16[128,512]{1,0:T(8,128)(2,1)S(1)} %get-tuple-element.37), channel_id=1, source_target_pairs={{0,1},{1,0},{2,3},{3,2},{4,5},{5,4},{6,7},{7,6},{8,9},{9,8},{10,11... | collective-permute-start | bytes 393224 | tf_op jit(solution)/shard_map/ppermute | solution.py:376
  46.3 4.9 %collective-permute-start.19 = (bf16[128,512]{1,0:T(8,128)(2,1)S(1)}, bf16[128,512]{1,0:T(8,128)(2,1)S(1)}, u32[]{:S(2)}, u32[]{:S(2)}) collective-permute-start(bf16[128,512]{1,0:T(8,128)(2,1)S(1)} %get-tuple-element.38), channel_id=1, source_target_pairs={{0,1},{1,0},{2,3},{3,2},{4,5},{5,4},{6,7},{7,6},{8,9},{9,8},{10,11... | collective-permute-start | bytes 393224 | tf_op jit(solution)/shard_map/ppermute | solution.py:376

commit v19 on v18

--- a/solution.py
+++ b/solution.py
@@ -170,9 +170,17 @@
     zs[...] = zm[...]
     zs[:, columns_of(cc, sizes)] = mask_piece(zp, r, l, cc, last[...], sizes)
     block_col = (c * sizes.cols_here + (l ^ 1) * q) // BS
-    for first in range(0, sizes.rows_here, BS):
-        j = (r * sizes.rows_here + first) // BS
-        hs[first : first + BS, :] = keep_block(hp, j, block_col, raw[first : first + BS, :])
+    high = sizes.rows_here
+    for (dr, dl), h in zip(h_table, [raw, *others]):
+        columns = slice(q, 2 * q) if dl else slice(0, q)
+        if dr or dl:
+            hs[dr * high : (dr + 1) * high, columns] = h[...]
+            continue
+        for first in range(0, high, BS):
+            j = (r * high + first) // BS
+            hs[first : first + BS, columns] = keep_block(
+                hp, j, block_col, h[first : first + BS, :]
+            )
     width, acc = blocks[0].shape[0], None
     for n, block in enumerate(blocks):
         part = jnp.dot(
@@ -181,17 +189,15 @@
         acc = part if acc is None else acc + part
     for n, ll in enumerate((l, l ^ top)):
         out[:, pl.ds(pl.multiple_of(ll * q, q), q)] = acc[:, n * q : (n + 1) * q].astype(out.dtype)
-    for dl in (0, top):
-        acc = None
-        for (dr, there), h in zip(h_table, [hs, *others]):
-            if there == dl:
-                rows = pl.ds(
-                    pl.multiple_of((r ^ dr) * sizes.rows_here, sizes.rows_here), sizes.rows_here
-                )
-                part = jnp.dot(zs[:, rows], h[...], preferred_element_type=jnp.float32)
-                acc = part if acc is None else acc + part
-        ll = l ^ 1 ^ dl
-        out[:, pl.ds(pl.multiple_of(ll * q, q), q)] = acc.astype(out.dtype)
+    acc = None
+    for dr in range(sizes.rows):
+        rows = pl.ds(pl.multiple_of((r ^ dr) * high, high), high)
+        part = jnp.dot(
+            zs[:, rows], hs[dr * high : (dr + 1) * high, :], preferred_element_type=jnp.float32
+        )
+        acc = part if acc is None else acc + part
+    for n, ll in enumerate((l ^ 1, l ^ 1 ^ top)):
+        out[:, pl.ds(pl.multiple_of(ll * q, q), q)] = acc[:, n * q : (n + 1) * q].astype(out.dtype)
 
 
 def route_kernel(sizes, row_offsets, *refs):
@@ -338,7 +344,7 @@
         smem=[h_pattern, z_pattern],
         scratch=[
             pltpu.VMEM((height, order), jnp.bfloat16),
-            pltpu.VMEM(hamiltonian.shape, jnp.bfloat16),
+            pltpu.VMEM((order, 2 * q), jnp.bfloat16),
         ],
     )[0]
 

time: 53.5 us -> 53.5 us (level)
  no operation moved by 1% of the time
where the time goes in v19:
time: 53.5 us; the launch traced here: 53.3 us
  waiting for transfers between devices  24 us (45%)
  starting transfers between devices  18.6 us (35%)
  Pallas kernels  7.25 us (14%)
  local copies, waits for them, and re-layouts  3.29 us (6%)
    pallas_call x11, Pallas kernels, run(): pl.pallas_call(body, out_shape=list(outs), in_specs=[pl.BlockSpec(memory_...  7.25 us
    ppermute x1, waiting for transfers between devices, local(): gathered[dr ^ bit] = lax.ppermute(piece, 'row', flip(rows, bit))  7.16 us
    ppermute x3, starting transfers between devices, local(): h_pieces.append(lax.ppermute(piece, axis, perm))  6.17 us
    ppermute x2, waiting for transfers between devices, cross(): return lax.ppermute(piece, 'layer', flip(layers, layer_bits[0]))  5.64 us
    ppermute x3, starting transfers between devices, local(): lax.ppermute(outgoing[d], 'col', flip(cols, d))  4.39 us
    ppermute x1, waiting for transfers between devices, local(): left = lax.ppermute(left, 'col', [(i, (i - 1) % cols) for i in range(cols)])  3.51 us
    ppermute x2, waiting for transfers between devices, local(): lax.ppermute(right, 'col', [(i, (i + 1) % cols) for i in range(cols)])  2.89 us
    ppermute x3, waiting for transfers between devices, local(): h_pieces.append(lax.ppermute(piece, axis, perm))  2.45 us
  transfers between devices with their start and end apart: 20, of which 9 were waited for; matrix products, arithmetic and copies ran while one was open for 2% of the time, Pallas kernels for 10%

profile of v19, /device:TPU:0, one launch (start us, length us, event | category | flops | bytes accessed | tf_op | source)
XLA Modules:
  0.0 53.3 jit_solution(11617686838697989211)
XLA Ops:
  0.0 3.0 %collective-permute-start.3 = (bf16[1024,128]{1,0:T(8,128)(2,1)}, bf16[1024,128]{1,0:T(8,128)(2,1)S(1)}, u32[]{:S(2)}, u32[]{:S(2)}) collective-permute-start(bf16[1024,128]{1,0:T(8,128)(2,1)} %refs_2_.1), channel_id=1, source_target_pairs={{0,2},{1,3},{2,0},{3,1},{4,6},{5,7},{6,4},{7,5},{8,10},{9,11},{10,... | collective-permute-start | bytes 786440 | tf_op jit(solution)/shard_map/ppermute | solution.py:320
  3.0 1.0 %constant_dynamic-slice_fusion = bf16[2,1,128,512]{3,2,1,0:T(8,128)(2,1)S(1)} fusion(bf16[2,4,128,512]{3,2,1,0:T(8,128)(2,1)} %bitcast.4, s32[]{:T(128)S(6)} %select_n.4), kind=kLoop, calls=%fused_computation | loop fusion | bytes 524292 | tf_op jit(solution)/shard_map/jit(dynamic_index_in_dim)/dynamic_slice | solution.py:293
  3.9 1.6 %collective-permute-start = (bf16[256,512]{1,0:T(8,128)(2,1)S(1)}, bf16[256,512]{1,0:T(8,128)(2,1)S(1)}, u32[]{:S(2)}, u32[]{:S(2)}) collective-permute-start(bf16[256,512]{1,0:T(8,128)(2,1)S(1)} %bitcast.5), channel_id=1, source_target_pairs={{0,4},{4,8},{8,12},{12,0},{1,5},{5,9},{9,13},{13,1},{2,6},{6,10},{... | collective-permute-start | bytes 786440 | tf_op jit(solution)/shard_map/ppermute | solution.py:298
  5.6 2.2 %collective-permute-start.1 = (bf16[256,512]{1,0:T(8,128)(2,1)S(1)}, bf16[256,512]{1,0:T(8,128)(2,1)S(1)}, u32[]{:S(2)}, u32[]{:S(2)}) collective-permute-start(bf16[256,512]{1,0:T(8,128)(2,1)S(1)} %bitcast.6), channel_id=1, source_target_pairs={{0,12},{4,0},{8,4},{12,8},{1,13},{5,1},{9,5},{13,9},{2,14},{6,2},{... | collective-permute-start | bytes 786440 | tf_op jit(solution)/shard_map/ppermute | solution.py:300
  7.8 1.5 %collective-permute-start.4 = (bf16[1024,128]{1,0:T(8,128)(2,1)}, bf16[1024,128]{1,0:T(8,128)(2,1)S(1)}, u32[]{:S(2)}, u32[]{:S(2)}) collective-permute-start(bf16[1024,128]{1,0:T(8,128)(2,1)} %refs_2_.1), channel_id=1, source_target_pairs={{0,16},{16,0},{1,17},{17,1},{2,18},{18,2},{3,19},{19,3},{4,20},{20... | collective-permute-start | bytes 786440 | tf_op jit(solution)/shard_map/ppermute | solution.py:320
  9.5 1.7 %collective-permute-start.5 = (bf16[1024,128]{1,0:T(8,128)(2,1)S(1)}, bf16[1024,128]{1,0:T(8,128)(2,1)S(1)}, u32[]{:S(2)}, u32[]{:S(2)}) collective-permute-start(bf16[1024,128]{1,0:T(8,128)(2,1)S(1)} %collective-permute-done.3.refs_3_), channel_id=1, source_target_pairs={{0,16},{16,0},{1,17},{17,1},{2,18},{18,2},{3,19},{19,3},{4,20},{20... | collective-permute-start | bytes 786440 | tf_op jit(solution)/shard_map/ppermute | solution.py:320
  11.2 0.9 %copy-done.1 = bf16[1024,128]{1,0:T(8,128)(2,1)S(1)} copy-done((bf16[1024,128]{1,0:T(8,128)(2,1)S(1)}, bf16[1024,128]{1,0:T(8,128)(2,1)}, u32[]{:S(2)}) %copy-start.1) | copy-done | bytes 262168
  12.2 0.7 %copy-done.2 = s32[8,8]{1,0:T(8,128)S(1)} copy-done((s32[8,8]{1,0:T(8,128)S(1)}, s32[8,8]{1,0:T(8,128)}, u32[]{:S(2)}) %copy-start.2) | copy-done | bytes 280
  13.5 1.5 %collective-permute-done.refs_0_.refs_7_ = bf16[256,512]{1,0:T(8,128)(2,1)S(1)} collective-permute-done((bf16[256,512]{1,0:T(8,128)(2,1)S(1)}, bf16[256,512]{1,0:T(8,128)(2,1)S(1)}, u32[]{:S(2)}, u32[]{:S(2)}) %collective-permute-start) | collective-permute-done | bytes 262176 | tf_op jit(solution)/shard_map/ppermute | solution.py:298
  15.2 3.5 %collective-permute-done.1.refs_1_.refs_8_ = bf16[256,512]{1,0:T(8,128)(2,1)S(1)} collective-permute-done((bf16[256,512]{1,0:T(8,128)(2,1)S(1)}, bf16[256,512]{1,0:T(8,128)(2,1)S(1)}, u32[]{:S(2)}, u32[]{:S(2)}) %collective-permute-start.1) | collective-permute-done | bytes 262176 | tf_op jit(solution)/shard_map/ppermute | solution.py:300
  18.7 2.3 %collective-permute-done.5.refs_5_ = bf16[1024,128]{1,0:T(8,128)(2,1)S(1)} collective-permute-done((bf16[1024,128]{1,0:T(8,128)(2,1)S(1)}, bf16[1024,128]{1,0:T(8,128)(2,1)S(1)}, u32[]{:S(2)}, u32[]{:S(2)}) %collective-permute-start.5) | collective-permute-done | bytes 262176 | tf_op jit(solution)/shard_map/ppermute | solution.py:320
  21.0 1.3 %bring.1 = (bf16[256,2048]{1,0:T(8,128)(2,1)S(1)}, bf16[1024,128]{1,0:T(8,128)(2,1)S(1)}, bf16[1024,128]{1,0:T(8,128)(2,1)S(1)}, bf16[1024,128]{1,0:T(8,128)(2,1...) custom-call(s32[8,8]{1,0:T(8,128)S(1)} %get-tuple-element.23.refs_0_, ...), custom_call_target="tpu_custom_call" | custom-call | bytes 4718592 | tf_op jit(solution)/shard_map/bring/pallas_call | solution.py:51
  23.5 1.4 %collective-permute-done.6.refs_3_.refs_0_ = bf16[256,512]{1,0:T(8,128)(2,1)S(1)} collective-permute-done((bf16[256,512]{1,0:T(8,128)(2,1)S(1)}, bf16[256,512]{1,0:T(8,128)(2,1)S(1)}, u32[]{:S(2)}, u32[]{:S(2)}) %collective-permute-start.6) | collective-permute-done | bytes 262176 | tf_op jit(solution)/shard_map/ppermute | solution.py:298
  24.9 1.6 %first_product.1.refs_1_.refs_0_ = bf16[256,512]{1,0:T(8,128)(2,1)S(1)} custom-call(s32[8,8]{1,0:T(8,128)S(1)} %get-tuple-element.23.refs_0_, s32[8,8]{1,0:T(8,128)S(1)} %get-tuple-element.22.refs_1_.refs_0_, bf16[256,2048]{1,0:T(8,128)(2,1)S(1)} %get-tuple-element.25.refs_2_, bf16[256,512]{1,0:T(8,128)(2,1)S(1)} %collective-permute-done.6.refs_3_.refs_0_, ...), custom_call_target="tpu_custom_call" | custom-call | bytes 5767168 | tf_op jit(solution)/shard_map/first_product/pallas_call | solution.py:51
  26.6 1.6 %collective-permute-start.11 = (bf16[256,512]{1,0:T(8,128)(2,1)S(1)}, bf16[256,512]{1,0:T(8,128)(2,1)S(1)}, u32[]{:S(2)}, u32[]{:S(2)}) collective-permute-start(bf16[256,512]{1,0:T(8,128)(2,1)S(1)} %first_product.1.refs_1_.refs_0_), channel_id=1, source_target_pairs={{0,16},{16,0},{1,17},{17,1},{2,18},{18,2},{3,19},{19,3},{4,20},{20... | collective-permute-start | bytes 786440 | tf_op jit(solution)/shard_map/ppermute | solution.py:354
  28.2 7.2 %collective-permute-done.11.refs_1_ = bf16[256,512]{1,0:T(8,128)(2,1)S(1)} collective-permute-done((bf16[256,512]{1,0:T(8,128)(2,1)S(1)}, bf16[256,512]{1,0:T(8,128)(2,1)S(1)}, u32[]{:S(2)}, u32[]{:S(2)}) %collective-permute-start.11) | collective-permute-done | bytes 262176 | tf_op jit(solution)/shard_map/ppermute | solution.py:354
  35.4 1.9 %collective-permute-done.2.refs_1_.refs_3_ = bf16[512,512]{1,0:T(8,128)(2,1)S(1)} collective-permute-done((bf16[512,512]{1,0:T(8,128)(2,1)S(1)}, bf16[512,512]{1,0:T(8,128)(2,1)S(1)}, u32[]{:S(2)}, u32[]{:S(2)}) %collective-permute-start.2) | collective-permute-done | bytes 524320 | tf_op jit(solution)/shard_map/ppermute | solution.py:304
  38.0 1.7 %collective-permute-start.15 = (bf16[128,512]{1,0:T(8,128)(2,1)S(1)}, bf16[128,512]{1,0:T(8,128)(2,1)S(1)}, u32[]{:S(2)}, u32[]{:S(2)}) collective-permute-start(bf16[128,512]{1,0:T(8,128)(2,1)S(1)} %get-tuple-element.34), channel_id=1, source_target_pairs={{0,12},{4,8},{8,4},{12,0},{1,13},{5,9},{9,5},{13,1},{2,14},{6,10},... | collective-permute-start | bytes 393224 | tf_op jit(solution)/shard_map/ppermute | solution.py:370
  39.7 2.7 %collective-permute-start.17 = (bf16[128,512]{1,0:T(8,128)(2,1)S(1)}, bf16[128,512]{1,0:T(8,128)(2,1)S(1)}, u32[]{:S(2)}, u32[]{:S(2)}) collective-permute-start(bf16[128,512]{1,0:T(8,128)(2,1)S(1)} %get-tuple-element.36), channel_id=1, source_target_pairs={{0,4},{4,0},{8,12},{12,8},{1,5},{5,1},{9,13},{13,9},{2,6},{6,2},{1... | collective-permute-start | bytes 393224 | tf_op jit(solution)/shard_map/ppermute | solution.py:370
  42.4 3.8 %collective-permute-done.14.refs_7_.refs_0_ = bf16[256,512]{1,0:T(8,128)(2,1)S(1)} collective-permute-done((bf16[256,512]{1,0:T(8,128)(2,1)S(1)}, bf16[256,512]{1,0:T(8,128)(2,1)S(1)}, u32[]{:S(2)}, u32[]{:S(2)}) %collective-permute-start.14) | collective-permute-done | bytes 262176 | tf_op jit(solution)/shard_map/ppermute | solution.py:304
  46.8 1.4 %layers.1.refs_0_.refs_1_ = bf16[1024,2048]{1,0:T(8,128)(2,1)S(1)} custom-call(s32[8,8]{1,0:T(8,128)S(1)} %get-tuple-element.22.refs_1_.refs_0_, bf16[1024,512]{1,0:T(8,128)(2,1)S(1)} %copy-done, bf16[512,512]{1,0:T(8,128)(2,1)S(1)} %pack.3.refs_0_.refs_2_, bf16[512,512]{1,0:T(8,128)(2,1)S(1)} %collective-permute-done.2.refs_1_.refs_3_, ...), custom_call_target="tpu_custom_call" | custom-call | bytes 8126464 | tf_op jit(solution)/shard_map/layers/pallas_call | solution.py:51
  48.1 0.7 %second_product.1.refs_2_ = f32[1024,128]{1,0:T(8,128)S(1)} custom-call(bf16[1024,2048]{1,0:T(8,128)(2,1)S(1)} %layers.1.refs_0_.refs_1_, bf16[128,512]{1,0:T(8,128)(2,1)S(1)} %get-tuple-element.33.refs_2_.refs_1_, bf16[128,512]{1,0:T(8,128)(2,1)S(1)} %collective-permute-done.15.refs_2_), custom_call_target="tpu_custom_call" | custom-call | bytes 4980736 | tf_op jit(solution)/shard_map/second_product/pallas_call | solution.py:51
  48.9 2.3 %collective-permute-done.16.refs_3_ = bf16[128,512]{1,0:T(8,128)(2,1)S(1)} collective-permute-done((bf16[128,512]{1,0:T(8,128)(2,1)S(1)}, bf16[128,512]{1,0:T(8,128)(2,1)S(1)}, u32[]{:S(2)}, u32[]{:S(2)}) %collective-permute-start.16) | collective-permute-done | bytes 131104 | tf_op jit(solution)/shard_map/ppermute | solution.py:370
  51.2 2.1 %last_product.1 = bf16[1024,128]{1,0:T(8,128)(2,1)} custom-call(s32[8,8]{1,0:T(8,128)S(1)} %get-tuple-element.22.refs_1_.refs_0_, bf16[1024,2048]{1,0:T(8,128)(2,1)S(1)} %layers.1.refs_0_.refs_1_, f32[1024,128]{1,0:T(8,128)S(1)} %second_product.1.refs_2_, bf16[128,512]{1,0:T(8,128)(2,1)S(1)} %collective-permute-done.16.refs_3_, ...), custom_call_target="tpu_custom_call" | custom-call | bytes 6553600 | tf_op jit(solution)/shard_map/last_product/pallas_call | solution.py:51
  (36 shorter events, 3.8 us)
Async XLA Ops:
  0.0 9.5 %collective-permute-start.3 = (bf16[1024,128]{1,0:T(8,128)(2,1)}, bf16[1024,128]{1,0:T(8,128)(2,1)S(1)}, u32[]{:S(2)}, u32[]{:S(2)}) collective-permute-start(bf16[1024,128]{1,0:T(8,128)(2,1)} %refs_2_.1), channel_id=1, source_target_pairs={{0,2},{1,3},{2,0},{3,1},{4,6},{5,7},{6,4},{7,5},{8,10},{9,11},{10,... | collective-permute-start | bytes 786440 | tf_op jit(solution)/shard_map/ppermute | solution.py:320
  3.9 11.1 %collective-permute-start = (bf16[256,512]{1,0:T(8,128)(2,1)S(1)}, bf16[256,512]{1,0:T(8,128)(2,1)S(1)}, u32[]{:S(2)}, u32[]{:S(2)}) collective-permute-start(bf16[256,512]{1,0:T(8,128)(2,1)S(1)} %bitcast.5), channel_id=1, source_target_pairs={{0,4},{4,8},{8,12},{12,0},{1,5},{5,9},{9,13},{13,1},{2,6},{6,10},{... | collective-permute-start | bytes 786440 | tf_op jit(solution)/shard_map/ppermute | solution.py:298
  5.6 13.1 %collective-permute-start.1 = (bf16[256,512]{1,0:T(8,128)(2,1)S(1)}, bf16[256,512]{1,0:T(8,128)(2,1)S(1)}, u32[]{:S(2)}, u32[]{:S(2)}) collective-permute-start(bf16[256,512]{1,0:T(8,128)(2,1)S(1)} %bitcast.6), channel_id=1, source_target_pairs={{0,12},{4,0},{8,4},{12,8},{1,13},{5,1},{9,5},{13,9},{2,14},{6,2},{... | collective-permute-start | bytes 786440 | tf_op jit(solution)/shard_map/ppermute | solution.py:300
  7.8 10.9 %collective-permute-start.4 = (bf16[1024,128]{1,0:T(8,128)(2,1)}, bf16[1024,128]{1,0:T(8,128)(2,1)S(1)}, u32[]{:S(2)}, u32[]{:S(2)}) collective-permute-start(bf16[1024,128]{1,0:T(8,128)(2,1)} %refs_2_.1), channel_id=1, source_target_pairs={{0,16},{16,0},{1,17},{17,1},{2,18},{18,2},{3,19},{19,3},{4,20},{20... | collective-permute-start | bytes 786440 | tf_op jit(solution)/shard_map/ppermute | solution.py:320
  9.5 11.5 %collective-permute-start.5 = (bf16[1024,128]{1,0:T(8,128)(2,1)S(1)}, bf16[1024,128]{1,0:T(8,128)(2,1)S(1)}, u32[]{:S(2)}, u32[]{:S(2)}) collective-permute-start(bf16[1024,128]{1,0:T(8,128)(2,1)S(1)} %collective-permute-done.3.refs_3_), channel_id=1, source_target_pairs={{0,16},{16,0},{1,17},{17,1},{2,18},{18,2},{3,19},{19,3},{4,20},{20... | collective-permute-start | bytes 786440 | tf_op jit(solution)/shard_map/ppermute | solution.py:320
  11.2 11.7 %collective-permute-start.7 = (bf16[1024,128]{1,0:T(8,128)(2,1)}, bf16[1024,128]{1,0:T(8,128)(2,1)S(1)}, u32[]{:S(2)}, u32[]{:S(2)}) collective-permute-start(bf16[1024,128]{1,0:T(8,128)(2,1)} %refs_2_.1), channel_id=1, source_target_pairs={{0,1},{1,0},{2,3},{3,2},{4,5},{5,4},{6,7},{7,6},{8,9},{9,8},{10,11... | collective-permute-start | bytes 786440 | tf_op jit(solution)/shard_map/ppermute | solution.py:321
  11.2 1.0 %copy-start.1 = (bf16[1024,128]{1,0:T(8,128)(2,1)S(1)}, bf16[1024,128]{1,0:T(8,128)(2,1)}, u32[]{:S(2)}) copy-start(bf16[1024,128]{1,0:T(8,128)(2,1)} %refs_2_.1) | copy-start | bytes 786436
  12.2 0.7 %copy-start.2 = (s32[8,8]{1,0:T(8,128)S(1)}, s32[8,8]{1,0:T(8,128)}, u32[]{:S(2)}) copy-start(s32[8,8]{1,0:T(8,128)} %refs_0_.1) | copy-start | bytes 772
  12.8 0.7 %copy-start.3 = (s32[8,8]{1,0:T(8,128)S(1)}, s32[8,8]{1,0:T(8,128)}, u32[]{:S(2)}) copy-start(s32[8,8]{1,0:T(8,128)} %refs_1_.2) | copy-start | bytes 772
  15.1 9.8 %collective-permute-start.6 = (bf16[256,512]{1,0:T(8,128)(2,1)S(1)}, bf16[256,512]{1,0:T(8,128)(2,1)S(1)}, u32[]{:S(2)}, u32[]{:S(2)}) collective-permute-start(bf16[256,512]{1,0:T(8,128)(2,1)S(1)} %collective-permute-done.refs_0_.refs_7_), channel_id=1, source_target_pairs={{0,4},{4,8},{8,12},{12,0},{1,5},{5,9},{9,13},{13,1},{2,6},{6,10},{... | collective-permute-start | bytes 786440 | tf_op jit(solution)/shard_map/ppermute | solution.py:298
  22.2 2.7 %collective-permute-start.10 = (bf16[1024,128]{1,0:T(8,128)(2,1)S(1)}, bf16[1024,128]{1,0:T(8,128)(2,1)S(1)}, u32[]{:S(2)}, u32[]{:S(2)}) collective-permute-start(bf16[1024,128]{1,0:T(8,128)(2,1)S(1)} %get-tuple-element.28), channel_id=1, source_target_pairs={{0,1},{1,0},{2,3},{3,2},{4,5},{5,4},{6,7},{7,6},{8,9},{9,8},{10,11... | collective-permute-start | bytes 786440 | tf_op jit(solution)/shard_map/ppermute | solution.py:337
  22.3 2.6 %collective-permute-start.8 = (bf16[1024,128]{1,0:T(8,128)(2,1)S(1)}, bf16[1024,128]{1,0:T(8,128)(2,1)S(1)}, u32[]{:S(2)}, u32[]{:S(2)}) collective-permute-start(bf16[1024,128]{1,0:T(8,128)(2,1)S(1)} %get-tuple-element.26), channel_id=1, source_target_pairs={{0,1},{1,0},{2,3},{3,2},{4,5},{5,4},{6,7},{7,6},{8,9},{9,8},{10,11... | collective-permute-start | bytes 786440 | tf_op jit(solution)/shard_map/ppermute | solution.py:337
  22.8 23.9 %copy-start = (bf16[1024,512]{1,0:T(8,128)(2,1)S(1)}, bf16[1024,512]{1,0:T(8,128)(2,1)}, u32[]{:S(2)}) copy-start(bf16[1024,512]{1,0:T(8,128)(2,1)} %refs_1_.3) | copy-start | bytes 3145732
  22.8 2.1 %collective-permute-start.9 = (bf16[1024,128]{1,0:T(8,128)(2,1)S(1)}, bf16[1024,128]{1,0:T(8,128)(2,1)S(1)}, u32[]{:S(2)}, u32[]{:S(2)}) collective-permute-start(bf16[1024,128]{1,0:T(8,128)(2,1)S(1)} %get-tuple-element.27), channel_id=1, source_target_pairs={{0,1},{1,0},{2,3},{3,2},{4,5},{5,4},{6,7},{7,6},{8,9},{9,8},{10,11... | collective-permute-start | bytes 786440 | tf_op jit(solution)/shard_map/ppermute | solution.py:337
  23.0 14.3 %collective-permute-start.2 = (bf16[512,512]{1,0:T(8,128)(2,1)S(1)}, bf16[512,512]{1,0:T(8,128)(2,1)S(1)}, u32[]{:S(2)}, u32[]{:S(2)}) collective-permute-start(bf16[512,512]{1,0:T(8,128)(2,1)S(1)} %pack.3.refs_0_.refs_2_), channel_id=1, source_target_pairs={{0,2},{1,3},{2,0},{3,1},{4,6},{5,7},{6,4},{7,5},{8,10},{9,11},{10,... | collective-permute-start | bytes 1572872 | tf_op jit(solution)/shard_map/ppermute | solution.py:304
  26.5 1.6 %collective-permute-start.12 = (bf16[256,512]{1,0:T(8,128)(2,1)S(1)}, bf16[256,512]{1,0:T(8,128)(2,1)S(1)}, u32[]{:S(2)}, u32[]{:S(2)}) collective-permute-start(bf16[256,512]{1,0:T(8,128)(2,1)S(1)} %pack.4.refs_5_), channel_id=1, source_target_pairs={{0,1},{1,0},{2,3},{3,2},{4,5},{5,4},{6,7},{7,6},{8,9},{9,8},{10,11... | collective-permute-start | bytes 786440 | tf_op jit(solution)/shard_map/ppermute | solution.py:360
  26.6 8.7 %collective-permute-start.11 = (bf16[256,512]{1,0:T(8,128)(2,1)S(1)}, bf16[256,512]{1,0:T(8,128)(2,1)S(1)}, u32[]{:S(2)}, u32[]{:S(2)}) collective-permute-start(bf16[256,512]{1,0:T(8,128)(2,1)S(1)} %first_product.1.refs_1_.refs_0_), channel_id=1, source_target_pairs={{0,16},{16,0},{1,17},{17,1},{2,18},{18,2},{3,19},{19,3},{4,20},{20... | collective-permute-start | bytes 786440 | tf_op jit(solution)/shard_map/ppermute | solution.py:354
  37.4 8.9 %collective-permute-start.13 = (bf16[1024,512]{1,0:T(8,128)(2,1)S(1)}, bf16[1024,512]{1,0:T(8,128)(2,1)S(1)}, u32[]{:S(2)}, u32[]{:S(2)}) collective-permute-start(bf16[1024,512]{1,0:T(8,128)(2,1)S(1)} %pack.5), channel_id=1, source_target_pairs={{0,1},{1,0},{2,3},{3,2},{4,5},{5,4},{6,7},{7,6},{8,9},{9,8},{10,11... | collective-permute-start | bytes 3145736 | tf_op jit(solution)/shard_map/ppermute | solution.py:373
  37.4 8.7 %collective-permute-start.14 = (bf16[256,512]{1,0:T(8,128)(2,1)S(1)}, bf16[256,512]{1,0:T(8,128)(2,1)S(1)}, u32[]{:S(2)}, u32[]{:S(2)}) collective-permute-start(bf16[256,512]{1,0:T(8,128)(2,1)S(1)} %pack.4.refs_5_), channel_id=1, source_target_pairs={{0,2},{1,3},{2,0},{3,1},{4,6},{5,7},{6,4},{7,5},{8,10},{9,11},{10,... | collective-permute-start | bytes 786440 | tf_op jit(solution)/shard_map/ppermute | solution.py:304
  38.0 10.1 %collective-permute-start.15 = (bf16[128,512]{1,0:T(8,128)(2,1)S(1)}, bf16[128,512]{1,0:T(8,128)(2,1)S(1)}, u32[]{:S(2)}, u32[]{:S(2)}) collective-permute-start(bf16[128,512]{1,0:T(8,128)(2,1)S(1)} %get-tuple-element.34), channel_id=1, source_target_pairs={{0,12},{4,8},{8,4},{12,0},{1,13},{5,9},{9,5},{13,1},{2,14},{6,10},... | collective-permute-start | bytes 393224 | tf_op jit(solution)/shard_map/ppermute | solution.py:370
  39.7 11.4 %collective-permute-start.16 = (bf16[128,512]{1,0:T(8,128)(2,1)S(1)}, bf16[128,512]{1,0:T(8,128)(2,1)S(1)}, u32[]{:S(2)}, u32[]{:S(2)}) collective-permute-start(bf16[128,512]{1,0:T(8,128)(2,1)S(1)} %get-tuple-element.35), channel_id=1, source_target_pairs={{0,8},{4,12},{8,0},{12,4},{1,9},{5,13},{9,1},{13,5},{2,10},{6,14},... | collective-permute-start | bytes 393224 | tf_op jit(solution)/shard_map/ppermute | solution.py:370
  39.7 11.4 %collective-permute-start.17 = (bf16[128,512]{1,0:T(8,128)(2,1)S(1)}, bf16[128,512]{1,0:T(8,128)(2,1)S(1)}, u32[]{:S(2)}, u32[]{:S(2)}) collective-permute-start(bf16[128,512]{1,0:T(8,128)(2,1)S(1)} %get-tuple-element.36), channel_id=1, source_target_pairs={{0,4},{4,0},{8,12},{12,8},{1,5},{5,1},{9,13},{13,9},{2,6},{6,2},{1... | collective-permute-start | bytes 393224 | tf_op jit(solution)/shard_map/ppermute | solution.py:370
  46.2 5.0 %collective-permute-start.18 = (bf16[128,512]{1,0:T(8,128)(2,1)S(1)}, bf16[128,512]{1,0:T(8,128)(2,1)S(1)}, u32[]{:S(2)}, u32[]{:S(2)}) collective-permute-start(bf16[128,512]{1,0:T(8,128)(2,1)S(1)} %get-tuple-element.37), channel_id=1, source_target_pairs={{0,1},{1,0},{2,3},{3,2},{4,5},{5,4},{6,7},{7,6},{8,9},{9,8},{10,11... | collective-permute-start | bytes 393224 | tf_op jit(solution)/shard_map/ppermute | solution.py:382
  46.3 4.9 %collective-permute-start.19 = (bf16[128,512]{1,0:T(8,128)(2,1)S(1)}, bf16[128,512]{1,0:T(8,128)(2,1)S(1)}, u32[]{:S(2)}, u32[]{:S(2)}) collective-permute-start(bf16[128,512]{1,0:T(8,128)(2,1)S(1)} %get-tuple-element.38), channel_id=1, source_target_pairs={{0,1},{1,0},{2,3},{3,2},{4,5},{5,4},{6,7},{7,6},{8,9},{9,8},{10,11... | collective-permute-start | bytes 393224 | tf_op jit(solution)/shard_map/ppermute | solution.py:382
